TPU v7x, 32 devices: a whole 2x2x4 slice. The times are simulated.
32 devices in a mesh: dp: 8 (over y, x, core), fsdp: 4 (over z).
Axes of the slice: x: 2, y: 2, z: 4, core: 2. Of those that a mesh axis runs over, the one named last changes fastest.
Arguments:
- block_in: bfloat16 [64, 320, 1024], P(('dp', 'fsdp')), may hold values from -6 to 6
- keep_mask: int32 [64, 256], P(('dp', 'fsdp')), may hold values from 0 to 1, as said below
- out_cotangent: bfloat16 [64, 320, 1024], P(('dp', 'fsdp')), may hold values from -6 to 6
- norm1_gain: float32 [1024], P(('dp', 'fsdp')), may hold values from 0.1 to 1.9
- norm1_bias: float32 [1024], P(('dp', 'fsdp')), may hold values from -3 to 3
- qkv_weight: float32 [1024, 3072], P(('dp', 'fsdp')), may hold values from -0.1875 to 0.1875
- qv_bias: float32 [2048], P(('dp', 'fsdp')), may hold values from -3 to 3
- out_weight: float32 [1024, 1024], P(('dp', 'fsdp')), may hold values from -0.75 to 0.75
- out_bias: float32 [1024], P(('dp', 'fsdp')), may hold values from -3 to 3
- norm2_gain: float32 [1024], P(('dp', 'fsdp')), may hold values from 0.1 to 1.9
- norm2_bias: float32 [1024], P(('dp', 'fsdp')), may hold values from -3 to 3
- fc1_weight: float32 [1024, 4096], P(('dp', 'fsdp')), may hold values from -0.1875 to 0.1875
- fc1_bias: float32 [4096], P(('dp', 'fsdp')), may hold values from -3 to 3
- fc2_weight: float32 [4096, 1024], P(('dp', 'fsdp')), may hold values from -0.09375 to 0.09375
- fc2_bias: float32 [1024], P(('dp', 'fsdp')), may hold values from -3 to 3
Outputs:
- block_out: float32 [64, 320, 1024], P(('dp', 'fsdp'))
- input_grad: float32 [64, 320, 1024], P(('dp', 'fsdp'))
- norm1_gain_grad: float32 [1024], P(('dp', 'fsdp'))
- norm1_bias_grad: float32 [1024], P(('dp', 'fsdp'))
- qkv_weight_grad: float32 [1024, 3072], P(('dp', 'fsdp'))
- qv_bias_grad: float32 [2048], P(('dp', 'fsdp'))
- out_weight_grad: float32 [1024, 1024], P(('dp', 'fsdp'))
- out_bias_grad: float32 [1024], P(('dp', 'fsdp'))
- norm2_gain_grad: float32 [1024], P(('dp', 'fsdp'))
- norm2_bias_grad: float32 [1024], P(('dp', 'fsdp'))
- fc1_weight_grad: float32 [1024, 4096], P(('dp', 'fsdp'))
- fc1_bias_grad: float32 [4096], P(('dp', 'fsdp'))
- fc2_weight_grad: float32 [4096, 1024], P(('dp', 'fsdp'))
- fc2_bias_grad: float32 [1024], P(('dp', 'fsdp'))
Inputs may be any that keep to these rules, and one draw needn't show every extreme that they name: `keep_mask`: each sequence keeps its image tokens at a rate of its own between 60 and 100 percent.
All inputs are finite; a program needn't handle non-finite values.
Results may differ from a plain program's by a relative error of at most 0.012.
The roundings to bfloat16 on the way count: a program that leaves them out, or rounds other values in their place, can miss the bound.
Values may be sent and summed in bfloat16 or wider, within the bound.
No kernel may reach another device: no remote copies, remote signals or barrier semaphores. Data moves between devices by JAX's collectives and lax.ppermute only.
A program may use at most 256 MiB of HBM per device.

v0:
```python
import math

import jax
import jax.numpy as jnp
from jax import lax
from jax.sharding import PartitionSpec as P

HD = 64
MB = 2


EPSILON = 1e-05


def norm_forward(values, norm_gain, norm_bias):
    average = jnp.mean(values, -1, keepdims=True)
    centered = values - average
    inverse = lax.rsqrt(jnp.mean(centered * centered, -1, keepdims=True) + EPSILON)
    normed = centered * inverse
    return (normed * norm_gain + norm_bias, normed, inverse)


def norm_backward(grad_norm, normed, inverse, norm_gain):
    scaled = grad_norm * norm_gain
    return inverse * (
        scaled
        - jnp.mean(scaled, -1, keepdims=True)
        - normed * jnp.mean(scaled * normed, -1, keepdims=True)
    )


def gelu_value(values):
    return 0.5 * values * (1.0 + jax.scipy.special.erf(values * 0.7071067811865476))


def gelu_slope(values):
    cumul = 0.5 * (1.0 + jax.scipy.special.erf(values * 0.7071067811865476))
    return cumul + values * jnp.exp(-0.5 * values * values) * 0.3989422804014327


def local(
    block_in,
    keep_mask,
    out_cotangent,
    norm1_gain,
    norm1_bias,
    qkv_weight,
    qv_bias,
    out_weight,
    out_bias,
    norm2_gain,
    norm2_bias,
    fc1_weight,
    fc1_bias,
    fc2_weight,
    fc2_bias,
):
    bf16 = jnp.bfloat16
    f32 = jnp.float32
    local_seqs = block_in.shape[0]
    length = block_in.shape[1]
    width = block_in.shape[2]
    per_micro = local_seqs // MB
    rows = per_micro * length
    heads = width // HD
    scale = 1.0 / math.sqrt(HD)
    keep_full = jnp.concatenate(
        [jnp.ones((local_seqs, length - keep_mask.shape[1]), jnp.int32), keep_mask], axis=1
    )
    outputs_list = []
    inputs_grad_list = []
    totals = None
    for micro in range(MB):
        fetched = (
            lax.all_gather(norm1_gain.astype(bf16), ("dp", "fsdp"), axis=0, tiled=True),
            lax.all_gather(norm1_bias.astype(bf16), ("dp", "fsdp"), axis=0, tiled=True),
            lax.all_gather(qkv_weight.astype(bf16), ("dp", "fsdp"), axis=0, tiled=True),
            lax.all_gather(qv_bias.astype(bf16), ("dp", "fsdp"), axis=0, tiled=True),
            lax.all_gather(out_weight.astype(bf16), ("dp", "fsdp"), axis=0, tiled=True),
            lax.all_gather(out_bias.astype(bf16), ("dp", "fsdp"), axis=0, tiled=True),
            lax.all_gather(norm2_gain.astype(bf16), ("dp", "fsdp"), axis=0, tiled=True),
            lax.all_gather(norm2_bias.astype(bf16), ("dp", "fsdp"), axis=0, tiled=True),
            lax.all_gather(fc1_weight.astype(bf16), ("dp", "fsdp"), axis=0, tiled=True),
            lax.all_gather(fc1_bias.astype(bf16), ("dp", "fsdp"), axis=0, tiled=True),
            lax.all_gather(fc2_weight.astype(bf16), ("dp", "fsdp"), axis=0, tiled=True),
            lax.all_gather(fc2_bias.astype(bf16), ("dp", "fsdp"), axis=0, tiled=True),
        )
        (
            gain_one,
            bias_one,
            qkv_mat,
            qv_shift,
            out_mat,
            out_shift,
            gain_two,
            bias_two,
            up_mat,
            up_shift,
            down_mat,
            down_shift,
        ) = fetched
        first = micro * per_micro
        inputs = block_in[first : first + per_micro].astype(f32).reshape(rows, width)
        keep_block = keep_full[first : first + per_micro]
        keep_rows = keep_block.reshape(rows, 1).astype(f32)
        visible = keep_block[:, None, None, :] > 0
        normed_one, plain_one, inverse_one = norm_forward(
            inputs, gain_one.astype(f32), bias_one.astype(f32)
        )
        act_one = normed_one.astype(bf16)
        project = jnp.dot(act_one, qkv_mat, preferred_element_type=f32)
        shift_all = qv_shift.astype(f32)
        queries = (
            (project[:, :width] + shift_all[:width])
            .astype(bf16)
            .reshape(per_micro, length, heads, HD)
        )
        keys_low = project[:, width : 2 * width].astype(bf16).reshape(per_micro, length, heads, HD)
        values_low = (
            (project[:, 2 * width :] + shift_all[width:])
            .astype(bf16)
            .reshape(per_micro, length, heads, HD)
        )

        def scores_of():
            logits = (
                jnp.einsum("sqhe,skhe->shqk", queries, keys_low, preferred_element_type=f32) * scale
            )
            return jnp.where(visible, logits, -1000000000.0)

        logits = scores_of()
        top_score = jnp.max(logits, -1, keepdims=True)
        log_total = top_score + jnp.log(jnp.sum(jnp.exp(logits - top_score), -1, keepdims=True))
        probs = jnp.exp(logits - log_total)
        mixed = (
            jnp.einsum(
                "shqk,skhe->sqhe", probs.astype(bf16), values_low, preferred_element_type=f32
            )
            .reshape(rows, width)
            .astype(bf16)
        )
        branch = jnp.dot(mixed, out_mat, preferred_element_type=f32) + out_shift.astype(f32)
        middle = inputs + branch
        normed_two, plain_two, inverse_two = norm_forward(
            middle, gain_two.astype(f32), bias_two.astype(f32)
        )
        act_two = normed_two.astype(bf16)
        hidden_pre = jnp.dot(act_two, up_mat, preferred_element_type=f32) + up_shift.astype(f32)
        hidden = gelu_value(hidden_pre).astype(bf16)
        feed = jnp.dot(hidden, down_mat, preferred_element_type=f32) + down_shift.astype(f32)
        outputs_list.append((keep_rows * (middle + feed)).reshape(per_micro, length, width))
        backing = (
            lax.all_gather(norm1_gain.astype(bf16), ("dp", "fsdp"), axis=0, tiled=True),
            lax.all_gather(norm1_bias.astype(bf16), ("dp", "fsdp"), axis=0, tiled=True),
            lax.all_gather(qkv_weight.astype(bf16), ("dp", "fsdp"), axis=0, tiled=True),
            lax.all_gather(qv_bias.astype(bf16), ("dp", "fsdp"), axis=0, tiled=True),
            lax.all_gather(out_weight.astype(bf16), ("dp", "fsdp"), axis=0, tiled=True),
            lax.all_gather(out_bias.astype(bf16), ("dp", "fsdp"), axis=0, tiled=True),
            lax.all_gather(norm2_gain.astype(bf16), ("dp", "fsdp"), axis=0, tiled=True),
            lax.all_gather(norm2_bias.astype(bf16), ("dp", "fsdp"), axis=0, tiled=True),
            lax.all_gather(fc1_weight.astype(bf16), ("dp", "fsdp"), axis=0, tiled=True),
            lax.all_gather(fc1_bias.astype(bf16), ("dp", "fsdp"), axis=0, tiled=True),
            lax.all_gather(fc2_weight.astype(bf16), ("dp", "fsdp"), axis=0, tiled=True),
            lax.all_gather(fc2_bias.astype(bf16), ("dp", "fsdp"), axis=0, tiled=True),
        )
        (
            gain_one,
            bias_one,
            qkv_mat,
            qv_shift,
            out_mat,
            out_shift,
            gain_two,
            bias_two,
            up_mat,
            up_shift,
            down_mat,
            down_shift,
        ) = backing
        grad_out = (
            out_cotangent[first : first + per_micro].astype(f32).reshape(rows, width) * keep_rows
        )
        grad_feed = grad_out.astype(bf16)
        down_grad = jnp.einsum("ra,rb->ab", hidden, grad_feed, preferred_element_type=f32)
        down_bias_grad = jnp.sum(grad_feed.astype(f32), 0)
        grad_hidden = jnp.einsum("rb,ab->ra", grad_feed, down_mat, preferred_element_type=f32)
        grad_pre = (grad_hidden * gelu_slope(hidden_pre)).astype(bf16)
        up_grad = jnp.einsum("rd,rf->df", act_two, grad_pre, preferred_element_type=f32)
        up_bias_grad = jnp.sum(grad_pre.astype(f32), 0)
        grad_act_two = jnp.einsum("rf,df->rd", grad_pre, up_mat, preferred_element_type=f32)
        gain_two_grad = jnp.sum(grad_act_two * plain_two, 0)
        bias_two_grad = jnp.sum(grad_act_two, 0)
        grad_middle = grad_out + norm_backward(
            grad_act_two, plain_two, inverse_two, gain_two.astype(f32)
        )
        grad_branch = grad_middle.astype(bf16)
        out_grad = jnp.einsum("ra,rb->ab", mixed, grad_branch, preferred_element_type=f32)
        out_bias_grad = jnp.sum(grad_branch.astype(f32), 0)
        grad_mixed = (
            jnp.einsum("rb,ab->ra", grad_branch, out_mat, preferred_element_type=f32)
            .astype(bf16)
            .reshape(per_micro, length, heads, HD)
        )
        again = jnp.exp(scores_of() - log_total)
        grad_values = jnp.einsum(
            "shqk,sqhe->skhe", again.astype(bf16), grad_mixed, preferred_element_type=f32
        ).astype(bf16)
        grad_probs = jnp.einsum(
            "sqhe,skhe->shqk", grad_mixed, values_low, preferred_element_type=f32
        )
        row_terms = jnp.sum(grad_probs * again, -1, keepdims=True)
        grad_logits = (again * (grad_probs - row_terms)).astype(bf16)
        grad_queries = (
            (
                jnp.einsum("shqk,skhe->sqhe", grad_logits, keys_low, preferred_element_type=f32)
                * scale
            )
            .astype(bf16)
            .reshape(rows, width)
        )
        grad_keys = (
            (
                jnp.einsum("shqk,sqhe->skhe", grad_logits, queries, preferred_element_type=f32)
                * scale
            )
            .astype(bf16)
            .reshape(rows, width)
        )
        grad_values = grad_values.reshape(rows, width)
        grad_project = jnp.concatenate([grad_queries, grad_keys, grad_values], axis=1)
        qkv_grad = jnp.einsum("rd,re->de", act_one, grad_project, preferred_element_type=f32)
        qv_grad = jnp.concatenate(
            [jnp.sum(grad_queries.astype(f32), 0), jnp.sum(grad_values.astype(f32), 0)]
        )
        grad_act_one = jnp.einsum("re,de->rd", grad_project, qkv_mat, preferred_element_type=f32)
        gain_one_grad = jnp.sum(grad_act_one * plain_one, 0)
        bias_one_grad = jnp.sum(grad_act_one, 0)
        grad_inputs = grad_middle + norm_backward(
            grad_act_one, plain_one, inverse_one, gain_one.astype(f32)
        )
        inputs_grad_list.append(grad_inputs.reshape(per_micro, length, width))
        terms = (
            gain_one_grad,
            bias_one_grad,
            qkv_grad,
            qv_grad,
            out_grad,
            out_bias_grad,
            gain_two_grad,
            bias_two_grad,
            up_grad,
            up_bias_grad,
            down_grad,
            down_bias_grad,
        )
        if totals is None:
            totals = tuple(terms)
        else:
            totals = tuple((left + right for left, right in zip(totals, terms)))
    totals = (
        lax.psum_scatter(totals[0], ("dp", "fsdp"), scatter_dimension=0, tiled=True),
        lax.psum_scatter(totals[1], ("dp", "fsdp"), scatter_dimension=0, tiled=True),
        lax.psum_scatter(totals[2], ("dp", "fsdp"), scatter_dimension=0, tiled=True),
        lax.psum_scatter(totals[3], ("dp", "fsdp"), scatter_dimension=0, tiled=True),
        lax.psum_scatter(totals[4], ("dp", "fsdp"), scatter_dimension=0, tiled=True),
        lax.psum_scatter(totals[5], ("dp", "fsdp"), scatter_dimension=0, tiled=True),
        lax.psum_scatter(totals[6], ("dp", "fsdp"), scatter_dimension=0, tiled=True),
        lax.psum_scatter(totals[7], ("dp", "fsdp"), scatter_dimension=0, tiled=True),
        lax.psum_scatter(totals[8], ("dp", "fsdp"), scatter_dimension=0, tiled=True),
        lax.psum_scatter(totals[9], ("dp", "fsdp"), scatter_dimension=0, tiled=True),
        lax.psum_scatter(totals[10], ("dp", "fsdp"), scatter_dimension=0, tiled=True),
        lax.psum_scatter(totals[11], ("dp", "fsdp"), scatter_dimension=0, tiled=True),
    )
    block_out = jnp.concatenate(outputs_list, axis=0)
    input_grad = jnp.concatenate(inputs_grad_list, axis=0)
    return (
        block_out,
        input_grad,
        totals[0],
        totals[1],
        totals[2],
        totals[3],
        totals[4],
        totals[5],
        totals[6],
        totals[7],
        totals[8],
        totals[9],
        totals[10],
        totals[11],
    )


def solution(mesh):
    return jax.shard_map(
        local,
        mesh=mesh,
        in_specs=(
            P(("dp", "fsdp"), None, None),
            P(("dp", "fsdp"), None),
            P(("dp", "fsdp"), None, None),
            P(("dp", "fsdp")),
            P(("dp", "fsdp")),
            P(("dp", "fsdp"), None),
            P(("dp", "fsdp")),
            P(("dp", "fsdp"), None),
            P(("dp", "fsdp")),
            P(("dp", "fsdp")),
            P(("dp", "fsdp")),
            P(("dp", "fsdp"), None),
            P(("dp", "fsdp")),
            P(("dp", "fsdp"), None),
            P(("dp", "fsdp")),
        ),
        out_specs=(
            P(("dp", "fsdp"), None, None),
            P(("dp", "fsdp"), None, None),
            P(("dp", "fsdp")),
            P(("dp", "fsdp")),
            P(("dp", "fsdp"), None),
            P(("dp", "fsdp")),
            P(("dp", "fsdp"), None),
            P(("dp", "fsdp")),
            P(("dp", "fsdp")),
            P(("dp", "fsdp")),
            P(("dp", "fsdp"), None),
            P(("dp", "fsdp")),
            P(("dp", "fsdp"), None),
            P(("dp", "fsdp")),
        ),
        check_vma=False,
    )
```

profile of v0, /device:TPU:0, one launch (start us, length us, event | category | flops | bytes accessed | tf_op | source)
XLA Modules:
  0.0 1386.8 jit_solution(10412663118319708560)
XLA Ops:
  15.2 42.7 %all-reduce.17 = (bf16[1024]{0:T(1024)(128)(2,1)S(1)}, bf16[1024]{0:T(1024)(128)(2,1)S(1)}, bf16[2048]{0:T(1024)(128)(2,1)S(1)}, bf16[1024]{0:T(1024)(128)(2,1)S...) all-reduce(bf16[1024]{0:T(1024)(128)(2,1)S(1)} %dynamic-update-slic, ...), channel_id=1, replica_groups=mesh['dp'=8,'fsdp'=4] {'dp','fsdp'}, use_global_device_ids=true, to_apply=%add.2 | all-reduce | flops 8192 | bytes 32768
  58.0 66.2 %all-gather = bf16[32,1,128]{2,1,0:T(2,128)(2,1)S(1)} all-gather(bf16[1,1,128]{2,1,0:T(2,128)(2,1)S(1)} %convert_bitcast_fusion.2), channel_id=1, replica_groups=mesh['dp'=8,'fsdp'=4] {'dp','fsdp'}, dimensions={0}, use_global_device_ids=true | all-gather | bytes 8448 | tf_op jit(solution)/shard_map/all_gather | solution.py:84
  125.2 5.4 fusion.83
  133.0 5.3 fusion.80
  150.7 3.3 fusion
  157.1 3.5 convolution_convert_fusion.3
  173.2 49.2 %all-gather.10.cloned.1.call-done = bf16[1024,4096]{1,0:T(8,128)(2,1)} async-done(((bf16[32,4096]{1,0:T(8,128)(2,1)}), bf16[1024,4096]{1,0:T(8,128)(2,1)}) %all-gather.10.cloned.1.call-update) | async-done | bytes 8388624 | tf_op jit(solution)/shard_map/all_gather | solution.py:83
  222.4 8.5 convolution_add_fusion.3
  230.8 6.3 multiply_convert_fusion.3
  237.1 64.6 %all-gather.12.cloned.1.call-done = bf16[4096,1024]{1,0:T(8,128)(2,1)} async-done(((bf16[128,1024]{1,0:T(8,128)(2,1)}), bf16[4096,1024]{1,0:T(8,128)(2,1)}) %all-gather.12.cloned.1.call-update) | async-done | bytes 8388624 | tf_op jit(solution)/shard_map/all_gather | solution.py:85
  301.7 7.8 convert_reduce_fusion
  309.6 6.3 fusion.95
  316.7 9.0 convert_reduce_fusion.1
  325.8 7.6 multiply_reduce_fusion.3
  340.3 3.9 convolution_convert_fusion.4
  346.4 3.4 convolution_convert_fusion.5
  352.1 7.1 multiply_reduce_fusion
  359.2 5.1 multiply_convert_fusion
  377.3 3.8 fusion.63
  383.3 9.3 convolution_add_fusion.2
  392.9 6.9 fusion.85
  399.7 12.9 convolution_add_fusion.1
  413.9 10.2 fusion.74
  424.1 11.7 convolution_add_fusion
  436.9 6.2 fusion.62
  443.2 7.6 fusion.52
  450.9 40.5 %all-reduce.16 = (f32[1024]{0:T(1024)S(1)}, f32[1024]{0:T(1024)S(1)}, f32[2048]{0:T(1024)S(1)}, f32[1024]{0:T(1024)S(1)}, f32[1024]{0:T(1024)S(1)}, /*index=5*/f...) all-reduce(f32[1024]{0:T(1024)S(1)} %add.285, ...), channel_id=2, replica_groups=mesh['dp'=8,'fsdp'=4] {'dp','fsdp'}, use_global_device_ids=true, to_apply=%region_24.25.clone | all-reduce | flops 12288 | bytes 98304
  496.1 6.5 fusion.32
  502.5 8.6 fusion.35
  517.6 130.8 %reduce-scatter.5.cloned.1.call-done = f32[32,3072]{1,0:T(8,128)} async-done(((f32[1024,3072]{1,0:T(8,128)}), f32[32,3072]{1,0:T(8,128)}) %reduce-scatter.5.cloned.1.call-update) | async-done | bytes 393232 | tf_op jit(solution)/shard_map/reduce_scatter | solution.py:263
  648.3 366.3 %reduce-scatter.9.cloned.1.call-done = f32[32,4096]{1,0:T(8,128)} async-done(((f32[1024,4096]{1,0:T(8,128)}), f32[32,4096]{1,0:T(8,128)}) %reduce-scatter.9.cloned.1.call-update) | async-done | bytes 524304 | tf_op jit(solution)/shard_map/reduce_scatter | solution.py:269
  1014.7 365.1 %reduce-scatter.11.cloned.1.call-done = f32[128,1024]{1,0:T(8,128)} async-done(((f32[4096,1024]{1,0:T(8,128)}), f32[128,1024]{1,0:T(8,128)}) %reduce-scatter.11.cloned.1.call-update) | async-done | bytes 524304 | tf_op jit(solution)/shard_map/reduce_scatter | solution.py:271
  (270 shorter events, 80.1 us)
Async XLA Ops:
  7.2 6.4 copy-start.59
  7.2 6.5 copy-start.60
  7.2 6.5 copy-start.61
  7.3 6.5 copy-start.62
  7.3 50.7 %copy-start.63 = (f32[128]{0:T(128)S(1)}, f32[128]{0:T(128)}, u32[]{:S(2)}) copy-start(f32[128]{0:T(128)} %param.27) | copy-start | bytes 1540
  7.3 116.9 %copy-start.48 = (s32[2,256]{1,0:T(2,128)S(1)}, s32[2,256]{1,0:T(2,128)}, u32[]{:S(2)}) copy-start(s32[2,256]{1,0:T(2,128)} %param.16) | copy-start | bytes 6148
  7.3 117.1 %copy-start.2 = (bf16[2,320,1024]{2,1,0:T(8,128)(2,1)S(1)}, bf16[2,320,1024]{2,1,0:T(8,128)(2,1)}, u32[]{:S(2)}) copy-start(bf16[2,320,1024]{2,1,0:T(8,128)(2,1)} %param.15) | copy-start | bytes 3932164
  7.3 117.9 %all-gather.6.cloned.1.call-start = ((), (), s32[]{:S(2)}) async-start(), calls=%async_computation.4 | async-start | bytes 6488064 | tf_op jit(solution)/shard_map/all_gather | solution.py:77
  9.3 151.3 %all-gather.8.cloned.1.call-start = ((), (), s32[]{:S(2)}) async-start(), calls=%async_computation.5 | async-start | bytes 2162688 | tf_op jit(solution)/shard_map/all_gather | solution.py:79
  10.9 211.5 %all-gather.10.cloned.1.call-start = ((), (), s32[]{:S(2)}) async-start(), calls=%async_computation.6 | async-start | bytes 8650752 | tf_op jit(solution)/shard_map/all_gather | solution.py:83
  12.7 289.0 %all-gather.12.cloned.1.call-start = ((), (), s32[]{:S(2)}) async-start(), calls=%async_computation.7 | async-start | bytes 8650752 | tf_op jit(solution)/shard_map/all_gather | solution.py:85
  13.5 504.0 %reduce-scatter.7.cloned.1.call-start = ((), (), s32[]{:S(2)}) async-start(), calls=%async_computation.9 | async-start | bytes 4325376 | tf_op jit(solution)/shard_map/reduce_scatter | solution.py:265
  143.6 10.4 copy-start.16
  172.8 160.6 %copy-start.4 = (f32[320,1024]{1,0:T(8,128)}, f32[320,1024]{1,0:T(8,128)S(1)}, u32[]{:S(2)}) copy-start(f32[320,1024]{1,0:T(8,128)S(1)} %get-tuple-element.82) | copy-start | bytes 3932164
  222.4 8.5 copy-start.7
  222.4 8.5 copy-start.55
  309.5 7.2 copy-start.54
  316.7 9.1 copy-start.8
  325.8 7.6 copy-start.39
  340.2 308.1 %reduce-scatter.5.cloned.1.call-start = ((), (), s32[]{:S(2)}) async-start(), calls=%async_computation.8 | async-start | bytes 12976128 | tf_op jit(solution)/shard_map/reduce_scatter | solution.py:263
  352.0 14.5 %slice-start = ((s8[7864320]{0:T(1024)(128)(4,1)}), s8[4194304]{0:T(1024)(128)(4,1)S(1)}, s32[]{:S(2)}) async-start(s8[7864320]{0:T(1024)(128)(4,1)} %bitcast.207), calls=%async_computation.12 | async-start | bytes 8388608
  359.1 7.4 slice-start.1
  365.6 17.7 %copy-start.29 = (bf16[16,64,320]{2,1,0:T(8,128)(2,1)}, bf16[16,64,320]{2,1,0:T(8,128)(2,1)S(1)}, u32[]{:S(2)}) copy-start(bf16[16,64,320]{2,1,0:T(8,128)(2,1)S(1)} %multiply_convert_fusion.4) | copy-start | bytes 1966084
  366.6 16.7 %copy-start.31 = (bf16[16,64,320]{2,1,0:T(8,128)(2,1)}, bf16[16,64,320]{2,1,0:T(8,128)(2,1)S(1)}, u32[]{:S(2)}) copy-start(bf16[16,64,320]{2,1,0:T(8,128)(2,1)S(1)} %get-tuple-element.102) | copy-start | bytes 1966084
  383.3 9.3 copy-start.45
  392.6 622.1 %reduce-scatter.9.cloned.1.call-start = ((), (), s32[]{:S(2)}) async-start(), calls=%async_computation.10 | async-start | bytes 17301504 | tf_op jit(solution)/shard_map/reduce_scatter | solution.py:269
  412.6 11.5 slice-start.4
  412.6 967.2 %reduce-scatter.11.cloned.1.call-start = ((), (), s32[]{:S(2)}) async-start(), calls=%async_computation.11 | async-start | bytes 17301504 | tf_op jit(solution)/shard_map/reduce_scatter | solution.py:271
  413.9 10.2 slice-start.5
  443.2 7.6 copy-start.40
  443.2 52.8 %copy-start.9 = (f32[320,1024]{1,0:T(8,128)S(1)}, f32[320,1024]{1,0:T(8,128)}, u32[]{:S(2)}) copy-start(f32[320,1024]{1,0:T(8,128)} %copy-done.6) | copy-start | bytes 3932164
  496.1 6.5 copy-start.5
  (46 other events, 148.3 us)
Sparse Core Ops, SparseCore 0:
  11.6 72.3 all-gather.5
  87.5 54.9 all-gather.7
  146.0 76.2 all-gather.9
  225.7 75.9 all-gather.11
  340.3 147.7 reduce-scatter.6
  494.6 153.6 reduce-scatter.4
  651.3 363.3 reduce-scatter.8
  1017.6 362.1 reduce-scatter.10
where the time goes:
time: 1390 us
  waiting for transfers between devices  976 us (70%)
  matrix products  185 us (13%)
  blocking collectives  149 us (11%)
  local copies, waits for them, and re-layouts  33.1 us (2%)
  other arithmetic  26.7 us (2%)
  between operations  15.5 us (1%)
    reduce_scatter x1, waiting for transfers between devices, local(): lax.psum_scatter(totals[8], ('dp', 'fsdp'), scatter_dimension=0, tiled=True)  366 us
    reduce_scatter x1, waiting for transfers between devices, local(): lax.psum_scatter(totals[10], ('dp', 'fsdp'), scatter_dimension=0, tiled=T...  365 us
    reduce_scatter x1, waiting for transfers between devices, local(): lax.psum_scatter(totals[2], ('dp', 'fsdp'), scatter_dimension=0, tiled=True)  131 us
    unnamed x2, blocking collectives  83.2 us
    all_gather x1, blocking collectives, local(): lax.all_gather(fc1_bias.astype(bf16), ('dp', 'fsdp'), axis=0, tiled=True)  66.2 us
    all_gather x1, waiting for transfers between devices, local(): lax.all_gather(fc2_weight.astype(bf16), ('dp', 'fsdp'), axis=0, tiled=True)  64.6 us
    all_gather x1, waiting for transfers between devices, local(): lax.all_gather(fc1_weight.astype(bf16), ('dp', 'fsdp'), axis=0, tiled=True)  49.2 us
  transfers between devices with their start and end apart: 8, of which 5 were waited for; matrix products, arithmetic and copies ran while one was open for 14% of the time, Pallas kernels for 0%

commit v1 on v0

v1 whole, which is shorter than its diff:
```python
import functools
import math

import jax
import jax.numpy as jnp
from jax import lax
from jax.experimental import pallas as pl
from jax.experimental.pallas import tpu as pltpu
from jax.sharding import PartitionSpec as P

HD = 64
EPSILON = 1e-05
AXES = ("dp", "fsdp")
bf16 = jnp.bfloat16
f32 = jnp.float32
NN = (((1,), (0,)), ((), ()))
NT = (((1,), (1,)), ((), ()))
TN = (((0,), (0,)), ((), ()))


def dot(left, right, dims=NN):
    return lax.dot_general(left, right, dims, preferred_element_type=f32)


def attention_forward_kernel(seqs, length, keep_ref, q_ref, k_ref, v_ref, o_ref):
    scale = 1.0 / math.sqrt(HD)
    for s in range(seqs):
        rows = slice(s * length, (s + 1) * length)
        visible = keep_ref[s] > 0
        mixed = []
        for h in range(128 // HD):
            cols = slice(h * HD, (h + 1) * HD)
            logits = dot(k_ref[rows, cols], q_ref[rows, cols] * scale, NT)
            logits = jnp.where(visible, logits, -1e9)
            raised = jnp.exp(logits - jnp.max(logits, 0, keepdims=True))
            probs = raised * (1.0 / jnp.sum(raised, 0, keepdims=True))
            mixed.append(dot(probs.astype(bf16), v_ref[rows, cols], TN))
        o_ref[rows, :] = jnp.concatenate(mixed, 1).astype(bf16)


def attention_backward_kernel(
    seqs, length, keep_ref, q_ref, k_ref, v_ref, do_ref, dq_ref, dk_ref, dv_ref, sq_ref, sv_ref
):
    scale = 1.0 / math.sqrt(HD)
    sum_q = jnp.zeros((1, 128), f32)
    sum_v = jnp.zeros((1, 128), f32)
    for s in range(seqs):
        rows = slice(s * length, (s + 1) * length)
        visible = keep_ref[s] > 0
        dqs, dks, dvs = [], [], []
        for h in range(128 // HD):
            cols = slice(h * HD, (h + 1) * HD)
            queries = q_ref[rows, cols] * scale
            keys = k_ref[rows, cols]
            grad_mixed = do_ref[rows, cols]
            logits = dot(keys, queries, NT)
            grad_probs = dot(v_ref[rows, cols], grad_mixed, NT)
            logits = jnp.where(visible, logits, -1e9)
            raised = jnp.exp(logits - jnp.max(logits, 0, keepdims=True))
            probs = raised * (1.0 / jnp.sum(raised, 0, keepdims=True))
            dvs.append(dot(probs.astype(bf16), grad_mixed))
            row_terms = jnp.sum(grad_probs * probs, 0, keepdims=True)
            grad_logits = (probs * (grad_probs - row_terms)).astype(bf16)
            dks.append(dot(grad_logits, queries))
            dqs.append(dot(grad_logits, keys, TN) * scale)
        dq = jnp.concatenate(dqs, 1).astype(bf16)
        dv = jnp.concatenate(dvs, 1).astype(bf16)
        dq_ref[rows, :] = dq
        dk_ref[rows, :] = jnp.concatenate(dks, 1).astype(bf16)
        dv_ref[rows, :] = dv
        sum_q += jnp.sum(dq.astype(f32), 0, keepdims=True)
        sum_v += jnp.sum(dv.astype(f32), 0, keepdims=True)
    sq_ref[...] = sum_q
    sv_ref[...] = sum_v


def attention_forward(keep, q, k, v):
    seqs, length = keep.shape[:2]
    rows, width = q.shape
    block = pl.BlockSpec((rows, 128), lambda i: (0, i))
    return pl.pallas_call(
        functools.partial(attention_forward_kernel, seqs, length),
        grid=(width // 128,),
        in_specs=[pl.BlockSpec((seqs, length, 1), lambda i: (0, 0, 0))] + [block] * 3,
        out_specs=block,
        out_shape=jax.ShapeDtypeStruct((rows, width), bf16),
        compiler_params=pltpu.CompilerParams(vmem_limit_bytes=40 << 20),
        cost_estimate=pl.CostEstimate(
            flops=16 * rows * length * width, bytes_accessed=8 * rows * width, transcendentals=0
        ),
    )(keep, q, k, v)


def attention_backward(keep, q, k, v, grad_mixed):
    seqs, length = keep.shape[:2]
    rows, width = q.shape
    block = pl.BlockSpec((rows, 128), lambda i: (0, i))
    vector = pl.BlockSpec((1, 128), lambda i: (0, i))
    low = jax.ShapeDtypeStruct((rows, width), bf16)
    sums = jax.ShapeDtypeStruct((1, width), f32)
    return pl.pallas_call(
        functools.partial(attention_backward_kernel, seqs, length),
        grid=(width // 128,),
        in_specs=[pl.BlockSpec((seqs, length, 1), lambda i: (0, 0, 0))] + [block] * 4,
        out_specs=[block] * 3 + [vector] * 2,
        out_shape=[low] * 3 + [sums] * 2,
        compiler_params=pltpu.CompilerParams(vmem_limit_bytes=40 << 20),
        cost_estimate=pl.CostEstimate(
            flops=24 * rows * length * width, bytes_accessed=14 * rows * width, transcendentals=0
        ),
    )(keep, q, k, v, grad_mixed)


def norm_forward(values, norm_gain, norm_bias):
    average = jnp.mean(values, -1, keepdims=True)
    centered = values - average
    inverse = lax.rsqrt(jnp.mean(centered * centered, -1, keepdims=True) + EPSILON)
    normed = centered * inverse
    return (normed * norm_gain + norm_bias, normed, inverse)


def norm_backward(grad_norm, normed, inverse, norm_gain):
    scaled = grad_norm * norm_gain
    return inverse * (
        scaled
        - jnp.mean(scaled, -1, keepdims=True)
        - normed * jnp.mean(scaled * normed, -1, keepdims=True)
    )


class Exchange:
    def __init__(self, dp_size):
        self.size = dp_size
        bits = [1 << i for i in range(dp_size.bit_length() - 1)]
        self.paths = (bits[:1] + bits[1:][::-1], bits)
        self.me = lax.axis_index("dp")

    def swap(self, value, bit):
        return lax.ppermute(value, "dp", [(i, i ^ bit) for i in range(self.size)])

    def order(self, path):
        count = len(path)
        return [
            sum(bit for at, bit in enumerate(path) if place >> (count - 1 - at) & 1)
            for place in range(self.size)
        ]

    def relative(self, value, path):
        width = value.shape[1] // self.size
        rows = value.shape[0]
        return jnp.concatenate(
            [
                lax.dynamic_slice(value, (0, (self.me ^ r) * width), (rows, width))
                for r in self.order(path)
            ],
            1,
        )

    def weight_grad(self, left, right):
        half = right.shape[1] // 2
        parts = []
        for path, right_part in zip(self.paths, (right[:, :half], right[:, half:])):
            ordered = self.relative(left, path)
            arrived = []

            def rows_of(first, last):
                total = dot(ordered[:, first:last], right_part, TN)
                for piece in arrived:
                    total = total + piece[first:last].astype(f32)
                return total.astype(bf16)

            rest = left.shape[1]
            for bit in path:
                sent = rows_of(rest // 2, rest)
                arrived.append(self.swap(sent, bit))
                rest //= 2
            parts.append(rows_of(0, rest))
        own = lax.psum_scatter(
            jnp.concatenate(parts, 1), "fsdp", scatter_dimension=0, tiled=True
        )
        return own.astype(f32)


def local(dp_size, device_count, block_in, keep_mask, out_cotangent, *params):
    (g1, b1, qkv_weight, qv_bias, out_weight, out_bias, g2, b2, up_weight, up_bias, down_weight, down_bias) = params
    seqs, length, width = block_in.shape
    rows = seqs * length
    exchange = Exchange(dp_size)

    vectors = (g1, b1, qv_bias, out_bias, g2, b2, up_bias, down_bias)
    sizes = [v.shape[0] for v in vectors]
    cuts = [sum(sizes[:i]) for i in range(1, len(sizes))]
    packed = lax.all_gather(jnp.concatenate([v.astype(bf16) for v in vectors]), AXES, axis=0, tiled=False)
    g1, b1, qv_bias, out_bias, g2, b2, up_bias, down_bias = (
        part.reshape(-1).astype(f32) for part in jnp.split(packed, cuts, axis=1)
    )
    qkv_mat, out_mat, up_mat, down_mat = (
        lax.all_gather(w.astype(bf16), AXES, axis=0, tiled=True)
        for w in (qkv_weight, out_weight, up_weight, down_weight)
    )

    keep = jnp.concatenate(
        [jnp.ones((seqs, length - keep_mask.shape[1]), jnp.int32), keep_mask], axis=1
    )
    keep_rows = keep.reshape(rows, 1).astype(f32)
    keep_column = keep.reshape(seqs, length, 1)
    inputs = block_in.astype(f32).reshape(rows, width)
    grad_out = out_cotangent.astype(f32).reshape(rows, width) * keep_rows
    grad_feed = grad_out.astype(bf16)
    down_bias_grad = jnp.sum(grad_feed.astype(f32), 0)

    normed_one, plain_one, inverse_one = norm_forward(inputs, g1, b1)
    act_one = normed_one.astype(bf16)
    queries = (dot(act_one, qkv_mat[:, :width]) + qv_bias[:width]).astype(bf16)
    keys = dot(act_one, qkv_mat[:, width : 2 * width]).astype(bf16)
    values = (dot(act_one, qkv_mat[:, 2 * width :]) + qv_bias[width:]).astype(bf16)
    mixed = attention_forward(keep_column, queries, keys, values)
    middle = inputs + dot(mixed, out_mat) + out_bias
    normed_two, plain_two, inverse_two = norm_forward(middle, g2, b2)
    act_two = normed_two.astype(bf16)
    pre = dot(act_two, up_mat) + up_bias
    cumul = 0.5 * (1.0 + lax.erf(pre * 0.7071067811865476))
    hidden = (pre * cumul).astype(bf16)
    slope = cumul + pre * jnp.exp(-0.5 * pre * pre) * 0.3989422804014327
    hidden, slope = lax.optimization_barrier((hidden, slope))

    down_grad = exchange.weight_grad(hidden, grad_feed)
    grad_pre = (dot(grad_feed, down_mat, NT) * slope).astype(bf16)
    up_bias_grad = jnp.sum(grad_pre.astype(f32), 0)
    up_grad = exchange.weight_grad(act_two, grad_pre)
    grad_act_two = dot(grad_pre, up_mat, NT)
    gain_two_grad = jnp.sum(grad_act_two * plain_two, 0)
    bias_two_grad = jnp.sum(grad_act_two, 0)
    grad_middle = grad_out + norm_backward(grad_act_two, plain_two, inverse_two, g2)
    grad_branch = grad_middle.astype(bf16)
    out_bias_grad = jnp.sum(grad_branch.astype(f32), 0)
    out_grad = exchange.weight_grad(mixed, grad_branch)
    grad_mixed = dot(grad_branch, out_mat, NT).astype(bf16)
    dq, dk, dv, sum_q, sum_v = attention_backward(keep_column, queries, keys, values, grad_mixed)
    grad_project = jnp.concatenate([dq, dk, dv], 1)
    qkv_grad = exchange.weight_grad(act_one, grad_project)
    grad_act_one = dot(grad_project, qkv_mat, NT)
    gain_one_grad = jnp.sum(grad_act_one * plain_one, 0)
    bias_one_grad = jnp.sum(grad_act_one, 0)
    input_grad = grad_middle + norm_backward(grad_act_one, plain_one, inverse_one, g1)

    feed = dot(hidden, down_mat) + down_bias
    block_out = keep_rows * (middle + feed)

    grads = (
        gain_one_grad,
        bias_one_grad,
        jnp.concatenate([sum_q.reshape(-1), sum_v.reshape(-1)]),
        out_bias_grad,
        gain_two_grad,
        bias_two_grad,
        up_bias_grad,
        down_bias_grad,
    )
    packed_grads = jnp.concatenate([g.reshape(device_count, -1) for g in grads], 1)
    summed = lax.psum_scatter(packed_grads, AXES, scatter_dimension=0, tiled=False)
    v = jnp.split(summed, cuts)
    return (
        block_out.reshape(seqs, length, width),
        input_grad.reshape(seqs, length, width),
        v[0],
        v[1],
        qkv_grad,
        v[2],
        out_grad,
        v[3],
        v[4],
        v[5],
        up_grad,
        v[6],
        down_grad,
        v[7],
    )


def solution(mesh):
    dp_size = mesh.shape["dp"]
    row = P(AXES, None)
    vec = P(AXES)
    cube = P(AXES, None, None)
    return jax.shard_map(
        functools.partial(local, dp_size, dp_size * mesh.shape["fsdp"]),
        mesh=mesh,
        in_specs=(cube, row, cube, vec, vec, row, vec, row, vec, vec, vec, row, vec, row, vec),
        out_specs=(cube, cube, vec, vec, row, vec, row, vec, vec, vec, row, vec, row, vec),
        check_vma=False,
    )
```

time: 1390 us -> 633 us (0.46)
  waiting for transfers between devices: 976 us -> 245 us
  matrix products: 185 us -> 140 us
  Pallas kernels: 0 us -> 39.2 us
  blocking collectives: 149 us -> 111 us
  starting transfers between devices: 0.95 us -> 21.6 us
  local copies, waits for them, and re-layouts: 33.1 us -> 17.5 us
    reduce_scatter x4 -> x3, waiting for transfers between devices: 862 us -> 4.44 us  [weight_grad(): lax.psum_scatter(jnp.concatenate(parts, 1), 'fsdp', scatter_dimension=0,...]
    ppermute x0 -> x24, waiting for transfers between devices: none -> 85.2 us  [swap(): return lax.ppermute(value, 'dp', [(i, i ^ bit) for i in range(self.size)])]
    dot_general x36 -> x42, matrix products: 185 us -> 140 us  [dot(): return lax.dot_general(left, right, dims, preferred_element_type=f32)]
    unnamed x2 -> x1, blocking collectives: 83.2 us -> 39.7 us
    all_gather x4, waiting for transfers between devices: 114 us -> 156 us  [local(): lax.all_gather(w.astype(bf16), AXES, axis=0, tiled=True)]
    pallas_call x0 -> x2, Pallas kernels: none -> 39.2 us  [the longest x1 22.1 us: attention_backward(): pl.pallas_call(functools.partial(attention_backward_kernel, seqs, length)...]
    ppermute x0 -> x24, starting transfers between devices: none -> 20.8 us  [swap(): return lax.ppermute(value, 'dp', [(i, i ^ bit) for i in range(self.size)])]
  transfers between devices with their start and end apart: 8 -> 32, of which waited for: 5 -> 15; matrix products, arithmetic and copies ran while one was open for 14% -> 23% of each run, Pallas kernels for 0% -> 6%
where the time goes in v1:
time: 633 us; the launch traced here: 626 us
  waiting for transfers between devices  245 us (39%)
  matrix products  140 us (22%)
  blocking collectives  111 us (18%)
  Pallas kernels  39.2 us (6%)
  other arithmetic  36.9 us (6%)
  starting transfers between devices  21.6 us (3%)
  local copies, waits for them, and re-layouts  17.5 us (3%)
  between operations  15.5 us (2%)
    all_gather x4, waiting for transfers between devices, local(): lax.all_gather(w.astype(bf16), AXES, axis=0, tiled=True)  156 us
    dot_general x42, matrix products, dot(): return lax.dot_general(left, right, dims, preferred_element_type=f32)  140 us
    ppermute x24, waiting for transfers between devices, swap(): return lax.ppermute(value, 'dp', [(i, i ^ bit) for i in range(self.size)])  85.2 us
    all_gather x1, blocking collectives, local(): lax.all_gather(jnp.concatenate([v.astype(bf16) for v in vectors]), AXES,...  70.9 us
    unnamed x1, blocking collectives  39.7 us
    pallas_call x1, Pallas kernels, attention_backward(): pl.pallas_call(functools.partial(attention_backward_kernel, seqs, length)...  22.1 us
    ppermute x24, starting transfers between devices, swap(): return lax.ppermute(value, 'dp', [(i, i ^ bit) for i in range(self.size)])  20.8 us
    pallas_call x1, Pallas kernels, attention_forward(): pl.pallas_call(functools.partial(attention_forward_kernel, seqs, length),...  17.1 us
  transfers between devices with their start and end apart: 32, of which 15 were waited for; matrix products, arithmetic and copies ran while one was open for 23% of the time, Pallas kernels for 6%

profile of v1, /device:TPU:0, one launch (start us, length us, event | category | flops | bytes accessed | tf_op | source)
XLA Modules:
  0.0 626.5 jit_solution(10222294262505617969)
XLA Ops:
  13.9 70.9 %all-gather.1 = bf16[32,1,384]{2,1,0:T(2,128)(2,1)S(1)} all-gather(bf16[1,1,384]{2,1,0:T(2,128)(2,1)S(1)} %reshape.235), channel_id=2, replica_groups=mesh['dp'=8,'fsdp'=4] {'dp','fsdp'}, dimensions={0}, use_global_device_ids=true | all-gather | bytes 25344 | tf_op jit(solution)/shard_map/all_gather | solution.py:193
  92.1 3.3 fusion.52.k_ref
  98.6 17.1 %shard_map.254 = bf16[640,1024]{1,0:T(8,128)(2,1)S(1)} custom-call(s32[2,320,1]{2,1,0:T(8,128)S(1)} %copy.45.keep_ref, bf16[640,1024]{1,0:T(8,128)(2,1)S(1)} %add_convert_fusion.2.q_ref, bf16[640,1024]{1,0:T(8,128)(2,1)S(1)} %fusion.52.k_ref, bf16[640,1024]{1,0:T(8,128)(2,1)S(1)} %add_convert_fusion.1.v_ref), custom_call_target="tpu_custom_call" | custom-call | flops 3355443200 | bytes 5242880 | tf_op jit(solution)/shard_map/pallas_call | solution.py:81
  116.9 25.6 %all-gather.9.cloned.1.call-done = bf16[1024,1024]{1,0:T(8,128)(2,1)} async-done(((bf16[32,1024]{1,0:T(8,128)(2,1)}), bf16[1024,1024]{1,0:T(8,128)(2,1)}) %all-gather.9.cloned.1.call-update) | async-done | bytes 2097168 | tf_op jit(solution)/shard_map/all_gather | solution.py:198
  142.6 3.2 fusion.170
  148.4 73.9 %all-gather.11.cloned.1.call-done = bf16[1024,4096]{1,0:T(8,128)(2,1)} async-done(((bf16[32,4096]{1,0:T(8,128)(2,1)}), bf16[1024,4096]{1,0:T(8,128)(2,1)}) %all-gather.11.cloned.1.call-update) | async-done | bytes 8388624 | tf_op jit(solution)/shard_map/all_gather | solution.py:198
  222.3 13.2 %fusion.3 = (f32[640,4096]{1,0:T(8,128)}, bf16[640,4096]{1,0:T(8,128)(2,1)S(1)}) fusion(f32[4096]{0:T(1024)S(1)} %fusion.137, bf16[640,1024]{1,0:T(8,128)(2,1)S(1)} %add_convert_fusion, bf16[1024,4096]{1,0:T(8,128)(2,1)} %all-gather.11.cloned.1.call-done), kind=kOutput, calls=%fused_computation.4 | convolution fusion | flops 5397544960 | bytes 25444352 | tf_op jit(solution)/shard_map/dot_general | solution.py:22
  238.5 3.6 convolution_convert_fusion.3
  242.1 3.6 convolution_convert_fusion.2
  245.7 56.0 %all-gather.13.cloned.1.call-done = bf16[4096,1024]{1,0:T(8,128)(2,1)} async-done(((bf16[128,1024]{1,0:T(8,128)(2,1)}), bf16[4096,1024]{1,0:T(8,128)(2,1)}) %all-gather.13.cloned.1.call-update) | async-done | bytes 8388624 | tf_op jit(solution)/shard_map/all_gather | solution.py:198
  301.7 12.9 %convert_reduce_fusion = (f32[4096]{0:T(1024)S(1)}, bf16[640,4096]{1,0:T(8,128)(2,1)}) fusion(f32[640,4096]{1,0:T(8,128)} %get-tuple-element.22, bf16[640,1024]{1,0:T(8,128)(2,1)} %fusion.31, bf16[4096,1024]{1,0:T(8,128)(2,1)} %all-gather.13.cloned.1.call-done), kind=kOutput, calls=%fused_computation.5 | convolution fusion | flops 5379190784 | bytes 25444352 | tf_op jit(solution)/shard_map/dot_general | solution.py:22
  314.7 5.1 convolution_convert_fusion.5
  319.7 3.2 convolution_convert_fusion.4
  326.7 8.9 %multiply_reduce_fusion = (f32[1024]{0:T(1024)S(1)}, f32[640]{0:T(1024)S(1)}, f32[640]{0:T(1024)S(1)}, f32[1024]{0:T(1024)S(1)}, f32[640,1024]{1,0:T(8,128)S(1)}) fusion(f32[640,1024]{1,0:T(8,128)S(1)} %copy-done.9, f32[640]{0:T(1024)S(1)} %add_rsqrt_fusion, f32[640]{0:T(1024)S(1)} %broadcast_multiply_fusion.4, f32[1024]{0:T(1024)S(1)} %reshape.230, ...), kind=kOutput, calls=%fused_computation.53 | convolution fusion | flops 5374604288 | bytes 18896896 | tf_op jit(solution)/shard_map/dot_general | solution.py:22
  348.3 22.1 %shard_map.255 = (bf16[640,1024]{1,0:T(8,128)(2,1)S(1)}, bf16[640,1024]{1,0:T(8,128)(2,1)S(1)}, bf16[640,1024]{1,0:T(8,128)(2,1)S(1)}, f32[1,1024]{1,0:T(1,128)S(1)}, f32[1,1024]{1,0:T(1,128)S(1)}) custom-call(s32[2,320,1]{2,1,0:T(8,128)S(1)} %copy.45.keep_ref, bf16[640,1024]{1,0:T(8,128)(2,1)S(1)} %copy-done.7, bf16[640,1024]{1,0:T(8,128)(2,1)S(1)} %copy-done.3, ...), custom_call_target="tpu_custom_call" | custom-call | flops 5033164800 | bytes 9175040 | tf_op jit(solution)/shard_map/pallas_call | solution.py:101
  377.8 9.6 %fusion.29 = (f32[1024]{0:T(1024)S(1)}, f32[640]{0:T(1024)S(1)}, f32[640]{0:T(1024)S(1)}, f32[1024]{0:T(1024)S(1)}, f32[640,1024]{1,0:T(8,128)}) fusion(bf16[2,320,1024]{2,1,0:T(8,128)(2,1)} %param.15, f32[640]{0:T(1024)S(1)} %rsqrt.20, f32[640]{0:T(1024)S(1)} %div.27, f32[1024]{0:T(1024)S(1)} %reshape.227, ...), kind=kOutput, calls=%fused_computation.49 | convolution fusion | flops 4044878848 | bytes 14178304 | tf_op jit(solution)/shard_map/dot_general | solution.py:22
  387.9 39.7 %all-reduce.1 = f32[32,384]{1,0:T(8,128)S(1)} all-reduce(f32[32,384]{1,0:T(8,128)S(1)} %concatenate.100), channel_id=3, replica_groups=mesh['dp'=8,'fsdp'=4] {'dp','fsdp'}, use_global_device_ids=true, to_apply=%region_15.0.clone | all-reduce | flops 12288 | bytes 98304
  430.3 2.7 fusion.81
  447.2 2.9 collective-permute-done.8
  466.1 3.4 add_convert_fusion.4
  470.6 3.4 add_convert_fusion.3
  474.0 8.2 %collective-permute-done.1 = bf16[256,1536]{1,0:T(8,128)(2,1)S(1)} collective-permute-done((bf16[256,1536]{1,0:T(8,128)(2,1)S(1)}, bf16[256,1536]{1,0:T(8,128)(2,1)S(1)}, u32[]{:S(2)}, u32[]{:S(2)}) %collective-permute-start.1) | collective-permute-done | bytes 786464 | tf_op jit(solution)/shard_map/ppermute | solution.py:139
  485.9 3.3 add_convert_fusion.6
  491.9 23.4 %collective-permute-done.2 = bf16[128,1536]{1,0:T(8,128)(2,1)S(1)} collective-permute-done((bf16[128,1536]{1,0:T(8,128)(2,1)S(1)}, bf16[128,1536]{1,0:T(8,128)(2,1)S(1)}, u32[]{:S(2)}, u32[]{:S(2)}) %collective-permute-start.2) | collective-permute-done | bytes 393248 | tf_op jit(solution)/shard_map/ppermute | solution.py:139
  517.4 17.3 %collective-permute-done.5 = bf16[128,1536]{1,0:T(8,128)(2,1)S(1)} collective-permute-done((bf16[128,1536]{1,0:T(8,128)(2,1)S(1)}, bf16[128,1536]{1,0:T(8,128)(2,1)S(1)}, u32[]{:S(2)}, u32[]{:S(2)}) %collective-permute-start.5) | collective-permute-done | bytes 393248 | tf_op jit(solution)/shard_map/ppermute | solution.py:139
  542.9 3.1 add_convert_fusion.5
  547.2 6.6 %collective-permute-done.20 = bf16[512,512]{0,1:T(8,128)(2,1)S(1)} collective-permute-done((bf16[512,512]{0,1:T(8,128)(2,1)S(1)}, bf16[512,512]{0,1:T(8,128)(2,1)S(1)}, u32[]{:S(2)}, u32[]{:S(2)}) %collective-permute-start.20) | collective-permute-done | bytes 524320 | tf_op jit(solution)/shard_map/ppermute | solution.py:139
  562.5 13.8 %collective-permute-done.16 = bf16[256,2048]{1,0:T(8,128)(2,1)S(1)} collective-permute-done((bf16[256,2048]{1,0:T(8,128)(2,1)S(1)}, bf16[256,2048]{1,0:T(8,128)(2,1)S(1)}, u32[]{:S(2)}, u32[]{:S(2)}) %collective-permute-start.16) | collective-permute-done | bytes 1048608 | tf_op jit(solution)/shard_map/ppermute | solution.py:139
  579.9 5.7 collective-permute-done.14
  592.2 5.0 fusion.28
  597.3 10.6 %add_multiply_fusion.1 = f32[640,1024]{1,0:T(8,128)} fusion(f32[640,1024]{1,0:T(8,128)S(1)} %copy-done.10, bf16[640,4096]{1,0:T(8,128)(2,1)} %copy-done.18, bf16[4096,1024]{1,0:T(8,128)(2,1)} %all-gather.13.cloned.1.call-done, f32[1024]{0:T(1024)S(1)} %copy-done.60, f32[640]{0:T(1024)S(1)} %convert_element_type.424), kind=kOutput, calls=%fused_computation.57 | convolution fusion | flops 5370675200 | bytes 18881024 | tf_op jit(solution)/shard_map/dot_general | solution.py:22
  613.1 4.4 reduce-scatter.11.cloned.1.call-done
  (321 shorter events, 125.1 us)
Async XLA Ops:
  7.3 84.8 %all-gather.7.cloned.1.call-start = ((), (), s32[]{:S(2)}) async-start(), calls=%async_computation.4 | async-start | bytes 6488064 | tf_op jit(solution)/shard_map/all_gather | solution.py:198
  9.2 133.3 %all-gather.9.cloned.1.call-start = ((), (), s32[]{:S(2)}) async-start(), calls=%async_computation.5 | async-start | bytes 2162688 | tf_op jit(solution)/shard_map/all_gather | solution.py:198
  10.9 211.5 %all-gather.11.cloned.1.call-start = ((), (), s32[]{:S(2)}) async-start(), calls=%async_computation.6 | async-start | bytes 8650752 | tf_op jit(solution)/shard_map/all_gather | solution.py:198
  12.7 289.0 %all-gather.13.cloned.1.call-start = ((), (), s32[]{:S(2)}) async-start(), calls=%async_computation.7 | async-start | bytes 8650752 | tf_op jit(solution)/shard_map/all_gather | solution.py:198
  13.5 594.3 %reduce-scatter.9.cloned.1.call-start = ((), (), s32[]{:S(2)}) async-start(), calls=%async_computation.9 | async-start | bytes 327680 | tf_op jit(solution)/shard_map/reduce_scatter | solution.py:178
  343.0 122.1 %collective-permute-start.18 = (bf16[2048,512]{0,1:T(8,128)(2,1)}, bf16[2048,512]{0,1:T(8,128)(2,1)}, u32[]{:S(2)}, u32[]{:S(2)}) collective-permute-start(bf16[2048,512]{0,1:T(8,128)(2,1)} %convolution_convert_fusion.3), channel_id=1, source_target_pairs={{0,4},{4,0},{8,12},{12,8},{16,20},{20,16},{24,28},{28,24},{1,5},{5... | collective-permute-start | bytes 6291464 | tf_op jit(solution)/shard_map/ppermute | solution.py:139
  345.9 123.6 %collective-permute-start.21 = (bf16[2048,512]{0,1:T(8,128)(2,1)}, bf16[2048,512]{0,1:T(8,128)(2,1)}, u32[]{:S(2)}, u32[]{:S(2)}) collective-permute-start(bf16[2048,512]{0,1:T(8,128)(2,1)} %convolution_convert_fusion.2), channel_id=1, source_target_pairs={{0,4},{4,0},{8,12},{12,8},{16,20},{20,16},{24,28},{28,24},{1,5},{5... | collective-permute-start | bytes 6291464 | tf_op jit(solution)/shard_map/ppermute | solution.py:139
  346.2 86.9 %collective-permute-start.6 = (bf16[512,512]{1,0:T(8,128)(2,1)}, bf16[512,512]{1,0:T(8,128)(2,1)}, u32[]{:S(2)}, u32[]{:S(2)}) collective-permute-start(bf16[512,512]{1,0:T(8,128)(2,1)} %convolution_convert_fusion.8), channel_id=1, source_target_pairs={{0,4},{4,0},{8,12},{12,8},{16,20},{20,16},{24,28},{28,24},{1,5},{5... | collective-permute-start | bytes 1572872 | tf_op jit(solution)/shard_map/ppermute | solution.py:139
  346.4 90.3 %collective-permute-start.9 = (bf16[512,512]{1,0:T(8,128)(2,1)}, bf16[512,512]{1,0:T(8,128)(2,1)}, u32[]{:S(2)}, u32[]{:S(2)}) collective-permute-start(bf16[512,512]{1,0:T(8,128)(2,1)} %convolution_convert_fusion.7), channel_id=1, source_target_pairs={{0,4},{4,0},{8,12},{12,8},{16,20},{20,16},{24,28},{28,24},{1,5},{5... | collective-permute-start | bytes 1572872 | tf_op jit(solution)/shard_map/ppermute | solution.py:139
  373.0 85.6 %collective-permute-start = (bf16[512,1536]{1,0:T(8,128)(2,1)}, bf16[512,1536]{1,0:T(8,128)(2,1)}, u32[]{:S(2)}, u32[]{:S(2)}) collective-permute-start(bf16[512,1536]{1,0:T(8,128)(2,1)} %convolution_convert_fusion.1), channel_id=1, source_target_pairs={{0,4},{4,0},{8,12},{12,8},{16,20},{20,16},{24,28},{28,24},{1,5},{5... | collective-permute-start | bytes 4718600 | tf_op jit(solution)/shard_map/ppermute | solution.py:139
  434.4 7.9 %collective-permute-start.7 = (bf16[256,512]{1,0:T(8,128)(2,1)S(1)}, bf16[256,512]{1,0:T(8,128)(2,1)S(1)}, u32[]{:S(2)}, u32[]{:S(2)}) collective-permute-start(bf16[256,512]{1,0:T(8,128)(2,1)S(1)} %add_convert_fusion.22), channel_id=1, source_target_pairs={{0,16},{4,20},{8,24},{12,28},{16,0},{20,4},{24,8},{28,12},{1,17},{... | collective-permute-start | bytes 786440 | tf_op jit(solution)/shard_map/ppermute | solution.py:139
  438.1 7.0 %collective-permute-start.10 = (bf16[256,512]{1,0:T(8,128)(2,1)S(1)}, bf16[256,512]{1,0:T(8,128)(2,1)S(1)}, u32[]{:S(2)}, u32[]{:S(2)}) collective-permute-start(bf16[256,512]{1,0:T(8,128)(2,1)S(1)} %add_convert_fusion.21), channel_id=1, source_target_pairs={{0,8},{4,12},{8,0},{12,4},{16,24},{20,28},{24,16},{28,20},{1,9},{5... | collective-permute-start | bytes 786440 | tf_op jit(solution)/shard_map/ppermute | solution.py:139
  442.3 19.5 %collective-permute-start.3 = (bf16[512,1536]{1,0:T(8,128)(2,1)}, bf16[512,1536]{1,0:T(8,128)(2,1)}, u32[]{:S(2)}, u32[]{:S(2)}) collective-permute-start(bf16[512,1536]{1,0:T(8,128)(2,1)} %convolution_convert_fusion), channel_id=1, source_target_pairs={{0,4},{4,0},{8,12},{12,8},{16,20},{20,16},{24,28},{28,24},{1,5},{5... | collective-permute-start | bytes 4718600 | tf_op jit(solution)/shard_map/ppermute | solution.py:139
  445.1 5.0 collective-permute-start.8
  450.1 5.0 collective-permute-start.11
  455.1 29.8 %collective-permute-start.12 = (bf16[512,2048]{1,0:T(8,128)(2,1)}, bf16[512,2048]{1,0:T(8,128)(2,1)}, u32[]{:S(2)}, u32[]{:S(2)}) collective-permute-start(bf16[512,2048]{1,0:T(8,128)(2,1)} %convolution_convert_fusion.5), channel_id=1, source_target_pairs={{0,4},{4,0},{8,12},{12,8},{16,20},{20,16},{24,28},{28,24},{1,5},{5... | collective-permute-start | bytes 6291464 | tf_op jit(solution)/shard_map/ppermute | solution.py:139
  458.4 151.0 %reduce-scatter.7.cloned.1.call-start = ((), (), s32[]{:S(2)}) async-start(), calls=%async_computation.8 | async-start | bytes 983040 | tf_op jit(solution)/shard_map/reduce_scatter | solution.py:178
  458.7 84.2 %collective-permute-start.15 = (bf16[512,2048]{1,0:T(8,128)(2,1)}, bf16[512,2048]{1,0:T(8,128)(2,1)}, u32[]{:S(2)}, u32[]{:S(2)}) collective-permute-start(bf16[512,2048]{1,0:T(8,128)(2,1)} %convolution_convert_fusion.4), channel_id=1, source_target_pairs={{0,4},{4,0},{8,12},{12,8},{16,20},{20,16},{24,28},{28,24},{1,5},{5... | collective-permute-start | bytes 6291464 | tf_op jit(solution)/shard_map/ppermute | solution.py:139
  461.8 20.5 %collective-permute-start.1 = (bf16[256,1536]{1,0:T(8,128)(2,1)S(1)}, bf16[256,1536]{1,0:T(8,128)(2,1)S(1)}, u32[]{:S(2)}, u32[]{:S(2)}) collective-permute-start(bf16[256,1536]{1,0:T(8,128)(2,1)S(1)} %add_convert_fusion.8), channel_id=1, source_target_pairs={{0,16},{4,20},{8,24},{12,28},{16,0},{20,4},{24,8},{28,12},{1,17},{... | collective-permute-start | bytes 2359304 | tf_op jit(solution)/shard_map/ppermute | solution.py:139
  465.1 24.1 %collective-permute-start.4 = (bf16[256,1536]{1,0:T(8,128)(2,1)S(1)}, bf16[256,1536]{1,0:T(8,128)(2,1)S(1)}, u32[]{:S(2)}, u32[]{:S(2)}) collective-permute-start(bf16[256,1536]{1,0:T(8,128)(2,1)S(1)} %add_convert_fusion.7), channel_id=1, source_target_pairs={{0,8},{4,12},{8,0},{12,4},{16,24},{20,28},{24,16},{28,20},{1,9},{5... | collective-permute-start | bytes 2359304 | tf_op jit(solution)/shard_map/ppermute | solution.py:139
  469.5 67.4 %collective-permute-start.19 = (bf16[1024,512]{0,1:T(8,128)(2,1)}, bf16[1024,512]{0,1:T(8,128)(2,1)}, u32[]{:S(2)}, u32[]{:S(2)}) collective-permute-start(bf16[1024,512]{0,1:T(8,128)(2,1)} %add_convert_fusion.4), channel_id=1, source_target_pairs={{0,16},{4,20},{8,24},{12,28},{16,0},{20,4},{24,8},{28,12},{1,17},{... | collective-permute-start | bytes 3145736 | tf_op jit(solution)/shard_map/ppermute | solution.py:139
  482.2 57.8 %collective-permute-start.22 = (bf16[1024,512]{0,1:T(8,128)(2,1)}, bf16[1024,512]{0,1:T(8,128)(2,1)}, u32[]{:S(2)}, u32[]{:S(2)}) collective-permute-start(bf16[1024,512]{0,1:T(8,128)(2,1)} %add_convert_fusion.3), channel_id=1, source_target_pairs={{0,8},{4,12},{8,0},{12,4},{16,24},{20,28},{24,16},{28,20},{1,9},{5... | collective-permute-start | bytes 3145736 | tf_op jit(solution)/shard_map/ppermute | solution.py:139
  484.9 30.3 %collective-permute-start.2 = (bf16[128,1536]{1,0:T(8,128)(2,1)S(1)}, bf16[128,1536]{1,0:T(8,128)(2,1)S(1)}, u32[]{:S(2)}, u32[]{:S(2)}) collective-permute-start(bf16[128,1536]{1,0:T(8,128)(2,1)S(1)} %add_convert_fusion.20), channel_id=1, source_target_pairs={{0,8},{4,12},{8,0},{12,4},{16,24},{20,28},{24,16},{28,20},{1,9},{5... | collective-permute-start | bytes 1179656 | tf_op jit(solution)/shard_map/ppermute | solution.py:139
  489.2 69.4 %collective-permute-start.13 = (bf16[256,2048]{1,0:T(8,128)(2,1)}, bf16[256,2048]{1,0:T(8,128)(2,1)}, u32[]{:S(2)}, u32[]{:S(2)}) collective-permute-start(bf16[256,2048]{1,0:T(8,128)(2,1)} %add_convert_fusion.6), channel_id=1, source_target_pairs={{0,16},{4,20},{8,24},{12,28},{16,0},{20,4},{24,8},{28,12},{1,17},{... | collective-permute-start | bytes 3145736 | tf_op jit(solution)/shard_map/ppermute | solution.py:139
  515.2 19.5 %collective-permute-start.5 = (bf16[128,1536]{1,0:T(8,128)(2,1)S(1)}, bf16[128,1536]{1,0:T(8,128)(2,1)S(1)}, u32[]{:S(2)}, u32[]{:S(2)}) collective-permute-start(bf16[128,1536]{1,0:T(8,128)(2,1)S(1)} %add_convert_fusion.18), channel_id=1, source_target_pairs={{0,16},{4,20},{8,24},{12,28},{16,0},{20,4},{24,8},{28,12},{1,17},{... | collective-permute-start | bytes 1179656 | tf_op jit(solution)/shard_map/ppermute | solution.py:139
  536.8 74.2 %reduce-scatter.13.cloned.1.call-start = ((), (), s32[]{:S(2)}) async-start(), calls=%async_computation.11 | async-start | bytes 1310720
  538.8 14.9 %collective-permute-start.20 = (bf16[512,512]{0,1:T(8,128)(2,1)S(1)}, bf16[512,512]{0,1:T(8,128)(2,1)S(1)}, u32[]{:S(2)}, u32[]{:S(2)}) collective-permute-start(bf16[512,512]{0,1:T(8,128)(2,1)S(1)} %add_convert_fusion.12), channel_id=1, source_target_pairs={{0,8},{4,12},{8,0},{12,4},{16,24},{20,28},{24,16},{28,20},{1,9},{5... | collective-permute-start | bytes 1572872 | tf_op jit(solution)/shard_map/ppermute | solution.py:139
  541.9 13.4 %collective-permute-start.23 = (bf16[512,512]{0,1:T(8,128)(2,1)S(1)}, bf16[512,512]{0,1:T(8,128)(2,1)S(1)}, u32[]{:S(2)}, u32[]{:S(2)}) collective-permute-start(bf16[512,512]{0,1:T(8,128)(2,1)S(1)} %add_convert_fusion.10), channel_id=1, source_target_pairs={{0,16},{4,20},{8,24},{12,28},{16,0},{20,4},{24,8},{28,12},{1,17},{... | collective-permute-start | bytes 1572872 | tf_op jit(solution)/shard_map/ppermute | solution.py:139
  546.0 30.2 %collective-permute-start.16 = (bf16[256,2048]{1,0:T(8,128)(2,1)S(1)}, bf16[256,2048]{1,0:T(8,128)(2,1)S(1)}, u32[]{:S(2)}, u32[]{:S(2)}) collective-permute-start(bf16[256,2048]{1,0:T(8,128)(2,1)S(1)} %add_convert_fusion.5), channel_id=1, source_target_pairs={{0,8},{4,12},{8,0},{12,4},{16,24},{20,28},{24,16},{28,20},{1,9},{5... | collective-permute-start | bytes 3145736 | tf_op jit(solution)/shard_map/ppermute | solution.py:139
  558.3 59.2 %reduce-scatter.11.cloned.1.call-start = ((), (), s32[]{:S(2)}) async-start(), calls=%async_computation.10 | async-start | bytes 1310720 | tf_op jit(solution)/shard_map/reduce_scatter | solution.py:178
  561.3 24.4 %collective-permute-start.14 = (bf16[128,2048]{1,0:T(8,128)(2,1)S(1)}, bf16[128,2048]{1,0:T(8,128)(2,1)S(1)}, u32[]{:S(2)}, u32[]{:S(2)}) collective-permute-start(bf16[128,2048]{1,0:T(8,128)(2,1)S(1)} %add_convert_fusion.16), channel_id=1, source_target_pairs={{0,8},{4,12},{8,0},{12,4},{16,24},{20,28},{24,16},{28,20},{1,9},{5... | collective-permute-start | bytes 1572872 | tf_op jit(solution)/shard_map/ppermute | solution.py:139
  578.7 10.4 %collective-permute-start.17 = (bf16[128,2048]{1,0:T(8,128)(2,1)S(1)}, bf16[128,2048]{1,0:T(8,128)(2,1)S(1)}, u32[]{:S(2)}, u32[]{:S(2)}) collective-permute-start(bf16[128,2048]{1,0:T(8,128)(2,1)S(1)} %add_convert_fusion.14), channel_id=1, source_target_pairs={{0,16},{4,20},{8,24},{12,28},{16,0},{20,4},{24,8},{28,12},{1,17},{... | collective-permute-start | bytes 1572872 | tf_op jit(solution)/shard_map/ppermute | solution.py:139
  (74 other events, 795.3 us)
Sparse Core Ops, SparseCore 0:
  11.6 72.3 all-gather.6
  87.4 55.0 all-gather.8
  146.1 76.2 all-gather.10
  225.7 75.9 all-gather.12
  458.5 18.3 reduce-scatter.8
  537.0 21.8 reduce-scatter.6
  561.3 26.3 reduce-scatter.12
  591.9 25.6 reduce-scatter.10

commit v2 on v1

v2 whole, which is shorter than its diff:
```python
import functools
import math

import jax
import jax.numpy as jnp
from jax import lax
from jax.experimental import pallas as pl
from jax.experimental.pallas import tpu as pltpu
from jax.sharding import PartitionSpec as P

HD = 64
EPSILON = 1e-05
AXES = ("dp", "fsdp")
bf16 = jnp.bfloat16
f32 = jnp.float32
NN = (((1,), (0,)), ((), ()))
NT = (((1,), (1,)), ((), ()))
TN = (((0,), (0,)), ((), ()))


def dot(left, right, dims=NN):
    return lax.dot_general(left, right, dims, preferred_element_type=f32)


def attention_forward_kernel(seqs, length, keep_ref, q_ref, k_ref, v_ref, o_ref):
    scale = 1.0 / math.sqrt(HD)
    for s in range(seqs):
        rows = slice(s * length, (s + 1) * length)
        visible = keep_ref[s] > 0
        mixed = []
        for h in range(128 // HD):
            cols = slice(h * HD, (h + 1) * HD)
            logits = dot(k_ref[rows, cols], q_ref[rows, cols] * scale, NT)
            logits = jnp.where(visible, logits, -1e9)
            raised = jnp.exp(logits - jnp.max(logits, 0, keepdims=True))
            probs = raised * (1.0 / jnp.sum(raised, 0, keepdims=True))
            mixed.append(dot(probs.astype(bf16), v_ref[rows, cols], TN))
        o_ref[rows, :] = jnp.concatenate(mixed, 1).astype(bf16)


def attention_backward_kernel(
    seqs, length, keep_ref, q_ref, k_ref, v_ref, do_ref, above_ref, dp_ref, sq_ref, sv_ref
):
    scale = 1.0 / math.sqrt(HD)
    sum_q = jnp.zeros((1, 128), f32)
    sum_v = jnp.zeros((1, 128), f32)
    for s in range(seqs):
        rows = slice(s * length, (s + 1) * length)
        visible = keep_ref[s] > 0
        dqs, dks, dvs = [], [], []
        for h in range(128 // HD):
            cols = slice(h * HD, (h + 1) * HD)
            queries = q_ref[rows, cols] * scale
            keys = k_ref[rows, cols]
            grad_mixed = do_ref[rows, cols]
            logits = dot(keys, queries, NT)
            grad_probs = dot(v_ref[rows, cols], grad_mixed, NT)
            logits = jnp.where(visible, logits, -1e9)
            raised = jnp.exp(logits - jnp.max(logits, 0, keepdims=True))
            probs = raised * (1.0 / jnp.sum(raised, 0, keepdims=True))
            dvs.append(dot(probs.astype(bf16), grad_mixed))
            row_terms = jnp.sum(grad_probs * probs, 0, keepdims=True)
            grad_logits = (probs * (grad_probs - row_terms)).astype(bf16)
            dks.append(dot(grad_logits, queries))
            dqs.append(dot(grad_logits, keys, TN) * scale)
        dq = jnp.concatenate(dqs, 1).astype(bf16)
        dv = jnp.concatenate(dvs, 1).astype(bf16)
        dp_ref[0, rows, :] = dq
        dp_ref[1, rows, :] = jnp.concatenate(dks, 1).astype(bf16)
        dp_ref[2, rows, :] = dv
        sum_q += jnp.sum(dq.astype(f32), 0, keepdims=True)
        sum_v += jnp.sum(dv.astype(f32), 0, keepdims=True)
    dp_ref[3] = above_ref[...]
    sq_ref[...] = sum_q
    sv_ref[...] = sum_v


def attention_forward(keep, project, part):
    seqs, length = keep.shape[:2]
    rows, width = project.shape[0], project.shape[1] // 6
    steps = width // 128
    block = pl.BlockSpec((rows, 128), lambda i: (0, i))
    return pl.pallas_call(
        functools.partial(attention_forward_kernel, seqs, length),
        grid=(steps,),
        in_specs=[pl.BlockSpec((seqs, length, 1), lambda i: (0, 0, 0))]
        + [
            pl.BlockSpec((rows, 128), lambda i, at=at: (0, i + (2 * at + part) * steps))
            for at in range(3)
        ],
        out_specs=block,
        out_shape=jax.ShapeDtypeStruct((rows, width), bf16),
        compiler_params=pltpu.CompilerParams(vmem_limit_bytes=16 << 20),
        cost_estimate=pl.CostEstimate(flops=int(8.5 * COST), bytes_accessed=1, transcendentals=0),
    )(keep, project, project, project)


def attention_backward(keep, project, grad_mixed, above):
    seqs, length = keep.shape[:2]
    rows, width = project.shape[0], project.shape[1] // 3
    steps = width // 128
    block = pl.BlockSpec((rows, 128), lambda i: (0, i))
    vector = pl.BlockSpec((1, 128), lambda i: (0, i))
    sums = jax.ShapeDtypeStruct((1, width), f32)
    return pl.pallas_call(
        functools.partial(attention_backward_kernel, seqs, length),
        grid=(steps,),
        in_specs=[pl.BlockSpec((seqs, length, 1), lambda i: (0, 0, 0))]
        + [pl.BlockSpec((rows, 128), lambda i, at=at: (0, i + at * steps)) for at in range(3)]
        + [block] * 2,
        out_specs=[pl.BlockSpec((4, rows, 128), lambda i: (0, 0, i)), vector, vector],
        out_shape=[jax.ShapeDtypeStruct((4, rows, width), bf16), sums, sums],
        compiler_params=pltpu.CompilerParams(vmem_limit_bytes=16 << 20),
        cost_estimate=pl.CostEstimate(flops=int(22 * COST), bytes_accessed=1, transcendentals=0),
    )(keep, project, project, project, grad_mixed, above)


def norm_forward(values, norm_gain, norm_bias):
    average = jnp.mean(values, -1, keepdims=True)
    centered = values - average
    inverse = lax.rsqrt(jnp.mean(centered * centered, -1, keepdims=True) + EPSILON)
    normed = centered * inverse
    return (normed * norm_gain + norm_bias, normed, inverse)


def norm_backward(grad_norm, normed, inverse, norm_gain):
    scaled = grad_norm * norm_gain
    return inverse * (
        scaled
        - jnp.mean(scaled, -1, keepdims=True)
        - normed * jnp.mean(scaled * normed, -1, keepdims=True)
    )


def gathered(device_count, block_in, keep_mask, out_cotangent, *params):
    (g1, b1, qkv_weight, qv_bias, out_weight, out_bias, g2, b2, up_weight, up_bias, down_weight, down_bias) = params
    seqs, length, width = block_in.shape
    rows = seqs * length
    vectors = (g1, b1, qv_bias, out_bias, g2, b2, up_bias, down_bias)
    sizes = [v.shape[0] for v in vectors]
    cuts = [sum(sizes[:i]) for i in range(1, len(sizes))]
    packed = lax.all_gather(jnp.concatenate(vectors).astype(bf16), AXES, axis=0, tiled=False)
    g1, b1, qv_bias, out_bias, g2, b2, up_bias, down_bias = (
        part.reshape(-1).astype(f32) for part in jnp.split(packed, cuts, axis=1)
    )
    qkv_mat, out_mat, up_mat, down_mat = (
        lax.all_gather(w.astype(bf16), AXES, axis=0, tiled=True)
        for w in (qkv_weight, out_weight, up_weight, down_weight)
    )
    keep = jnp.concatenate(
        [jnp.ones((seqs, length - keep_mask.shape[1]), jnp.int32), keep_mask], axis=1
    )
    keep_rows = keep.reshape(rows, 1).astype(f32)
    keep_column = keep.reshape(seqs, length, 1)
    inputs = block_in.astype(f32).reshape(rows, width)
    grad_out = out_cotangent.astype(f32).reshape(rows, width) * keep_rows
    grad_feed = grad_out.astype(bf16)

    normed_one, plain_one, inverse_one = norm_forward(inputs, g1, b1)
    act_one = normed_one.astype(bf16)
    zeros = jnp.zeros((width,), f32)
    shift = jnp.concatenate([qv_bias[:width], zeros, qv_bias[width:]])
    project = (dot(act_one, qkv_mat) + shift).astype(bf16)

    mixed = jnp.concatenate([attention_forward(keep_column, project, part) for part in range(2)], 1)
    middle = inputs + dot(mixed, out_mat) + out_bias
    normed_two, plain_two, inverse_two = norm_forward(middle, g2, b2)
    act_two = normed_two.astype(bf16)
    pre = dot(act_two, up_mat) + up_bias
    cumul = 0.5 * (1.0 + lax.erf(pre * 0.7071067811865476))
    hidden = (pre * cumul).astype(bf16)
    slope = cumul + pre * jnp.exp(-0.5 * pre * pre) * 0.3989422804014327
    feed = dot(hidden, down_mat) + down_bias
    block_out = keep_rows * (middle + feed)

    grad_pre = (dot(grad_feed, down_mat, NT) * slope).astype(bf16)
    grad_act_two = dot(grad_pre, up_mat, NT)
    grad_middle = grad_out + norm_backward(grad_act_two, plain_two, inverse_two, g2)
    grad_branch = grad_middle.astype(bf16)
    grad_mixed = dot(grad_branch, out_mat, NT).astype(bf16)
    grad_parts, sum_q, sum_v = attention_backward(keep_column, project, grad_mixed, grad_branch)
    grad_project = jnp.concatenate([grad_parts[i] for i in range(3)], 1)
    grad_act_one = dot(grad_project, qkv_mat, NT)
    input_grad = grad_middle + norm_backward(grad_act_one, plain_one, inverse_one, g1)
    grads = (
        jnp.sum(grad_act_one * plain_one, 0),
        jnp.sum(grad_act_one, 0),
        jnp.concatenate([sum_q[0], sum_v[0]]),
        jnp.sum(grad_branch.astype(f32), 0),
        jnp.sum(grad_act_two * plain_two, 0),
        jnp.sum(grad_act_two, 0),
        jnp.sum(grad_pre.astype(f32), 0),
        jnp.sum(grad_feed.astype(f32), 0),
    )
    shares = jnp.concatenate([g.reshape(device_count, -1) for g in grads], 1)
    v = jnp.split(lax.psum_scatter(shares, AXES, scatter_dimension=0, tiled=False), cuts)

    def to_owner(left, right):
        total = dot(left, right, TN).astype(bf16)
        return lax.psum_scatter(total, AXES, scatter_dimension=0, tiled=True).astype(f32)

    return (
        block_out.reshape(seqs, length, width),
        input_grad.reshape(seqs, length, width),
        v[0],
        v[1],
        to_owner(act_one, grad_project),
        v[2],
        to_owner(mixed, grad_branch),
        v[3],
        v[4],
        v[5],
        to_owner(act_two, grad_pre),
        v[6],
        to_owner(hidden, grad_feed),
        v[7],
    )


CORE, XBIT, YBIT = 1, 2, 4
BLOCKS = [c * CORE + y * YBIT + x * XBIT for c in range(2) for y in range(2) for x in range(2)]
COST = 1e12


def positions(me, line, count):
    true = [me ^ r for r in BLOCKS]
    place = [
        sum(jnp.where((me ^ d) == r, at, 0) for at, r in enumerate(BLOCKS)) for d in range(8)
    ]
    ahead = [(line + by) % count for by in range(count)]
    return jnp.stack(true + place + ahead).astype(jnp.int32)


def call(kernel, grid, where, ins, outs, scratch=(), micros=3):
    held = 6 << 20
    specs = []
    for array, block, index in ins:
        once = tuple(block) == tuple(array.shape)
        size = math.prod(n or 1 for n in block) * array.dtype.itemsize
        held += size if once else 2 * size
        specs.append(pl.BlockSpec(block, index, pipeline_mode=pl.Buffered(1) if once else None))
    for _, dtype, block, _ in outs:
        held += 2 * math.prod(block) * jnp.dtype(dtype).itemsize
    for buffer in scratch:
        held += math.prod(buffer.shape) * jnp.dtype(buffer.dtype).itemsize
    return pl.pallas_call(
        kernel,
        grid_spec=pltpu.PrefetchScalarGridSpec(
            num_scalar_prefetch=1,
            grid=grid,
            in_specs=specs,
            out_specs=[pl.BlockSpec(block, index) for _, _, block, index in outs],
            scratch_shapes=list(scratch),
        ),
        out_shape=[jax.ShapeDtypeStruct(shape, dtype) for shape, dtype, _, _ in outs],
        compiler_params=pltpu.CompilerParams(vmem_limit_bytes=held),
        cost_estimate=pl.CostEstimate(flops=int(micros * COST), bytes_accessed=1, transcendentals=0),
    )(where, *[array for array, _, _ in ins])


def whole(array):
    return (array, array.shape, lambda *_: (0,) * array.ndim)


def whole_out(shape, dtype):
    return (shape, dtype, shape, lambda *_: (0,) * len(shape))


def column(i, *_):
    return (0, i)


def lanes(where, at):
    return pl.ds(pl.multiple_of(where[at] * 128, 128), 128)


def deal(where, source, low, high):
    for at in range(4):
        cols = slice(at * 128, (at + 1) * 128)
        low[:, cols] = source[:, lanes(where, at)]
        high[:, cols] = source[:, lanes(where, 4 + at)]


def normalize(values):
    centered = values - jnp.mean(values, -1, keepdims=True)
    inverse = lax.rsqrt(jnp.mean(centered * centered, -1, keepdims=True) + EPSILON)
    return centered * inverse, inverse


def norm_kernel(where, x_ref, grad_ref, gain_ref, bias_ref, low_ref, pack_ref, whole_ref):
    normed, _ = normalize(x_ref[...].astype(f32))
    whole_ref[...] = (normed * gain_ref[...] + bias_ref[...]).astype(bf16)
    half = low_ref.shape[1]
    deal(where, whole_ref, low_ref, pack_ref.at[:, :half])
    pack_ref[:, half:] = grad_ref[...]


def norm_one(where, inputs, grad_feed, gain, bias):
    rows, width = inputs.shape
    index = lambda i, _: (i, 0)
    return call(
        norm_kernel,
        (rows // 128,),
        where,
        [(inputs, (128, width), index), (grad_feed, (128, width), index), whole(gain), whole(bias)],
        [
            ((rows, width // 2), bf16, (128, width // 2), index),
            ((rows, width // 2 + width), bf16, (128, width // 2 + width), index),
        ],
        [pltpu.VMEM((128, width), bf16)],
    )


def project_kernel(where, low_ref, high_ref, mat_low, mat_high, bias_ref, out_ref):
    total = dot(low_ref[...], mat_low[...]) + dot(high_ref[...], mat_high[...])
    out_ref[...] = (total + bias_ref[...]).astype(bf16)


def project(where, low, pack, mats, bias):
    rows, depth = low.shape
    columns = bias.shape[1]
    tile = ((depth, 512), column)
    return call(
        project_kernel,
        (columns // 512,),
        where,
        [whole(low), first_columns(pack, depth), (mats[0], *tile), (mats[1], *tile), (bias, (1, 512), column)],
        [((rows, columns), bf16, (rows, 512), column)], micros=8)[0]


def branch_kernel(
    where, mixed_ref, x_ref, mat_low, mat_high, shift_ref, gain_ref, bias_ref,
    mix_low, middle_ref, two_low, pack_ref, whole_ref,
):
    half = mix_low.shape[1]
    mix_high, two_high = pack_ref.at[:, :half], pack_ref.at[:, half:]
    deal(where, mixed_ref, mix_low, mix_high)
    total = dot(mix_low[...], mat_low[...]) + dot(mix_high[...], mat_high[...])
    middle = x_ref[...].astype(f32) + total + shift_ref[...]
    middle_ref[...] = middle
    normed, _ = normalize(middle)
    whole_ref[...] = (normed * gain_ref[...] + bias_ref[...]).astype(bf16)
    deal(where, whole_ref, two_low, two_high)


def branch_norm(where, mixed, inputs, mats, shift, gain, bias, length):
    rows, width = inputs.shape
    block = ((length, width), lambda i, _: (i, 0))
    part = ((rows, width // 2), bf16, (length, width // 2), lambda i, _: (i, 0))
    return call(
        branch_kernel,
        (rows // length,),
        where,
        [(mixed, *block), (inputs, *block), *[last_columns(m, width) for m in mats]]
        + [whole(v) for v in (shift, gain, bias)],
        [part, ((rows, width), f32, *block), part, ((rows, width), bf16, *block)],
        [pltpu.VMEM((length, width), bf16)], micros=4)


def first_columns(mat, count, at=0):
    return (mat, (mat.shape[0], count), lambda *_: (0, at))


def last_columns(mat, count):
    at = mat.shape[1] // count - 1
    return (mat, (mat.shape[0], count), lambda *_: (0, at))


def expand_kernel(where, low_ref, high_ref, mat_low, mat_high, shift_ref, hidden_ref, slope_ref):
    chunk = low_ref.shape[0] // 4
    for at in range(4):
        rows = slice(at * chunk, (at + 1) * chunk)
        pre = dot(low_ref[rows, :], mat_low[...]) + dot(high_ref[rows, :], mat_high[...])
        pre = pre + shift_ref[...]
        cumul = 0.5 * (1.0 + lax.erf(pre * 0.7071067811865476))
        hidden_ref[rows, :] = (pre * cumul).astype(bf16)
        slope = cumul + pre * jnp.exp(-0.5 * pre * pre) * 0.3989422804014327
        slope_ref[rows, :] = slope.astype(bf16)


def expand(where, side, low, pack, mats, shift):
    rows, depth = low.shape
    columns = shift.shape[1]
    tile = columns // 8
    true = lambda i, where: (0, where[4 * side + i])
    return call(
        expand_kernel,
        (4,),
        where,
        [
            whole(low),
            first_columns(pack, depth, 1),
            (mats[0], (depth, tile), true),
            (mats[1], (depth, tile), true),
            (shift, (1, tile), true),
        ],
        [((rows, columns // 2), bf16, (rows, tile), column)] * 2,
        micros=7,
    )


def shrink_kernel(where, grad_ref, mat_low, mat_high, slope_low, slope_high, out_ref, sum_ref):
    for side, (mat, slope) in enumerate(((mat_low, slope_low), (mat_high, slope_high))):

        @pl.when(pl.program_id(0) // 4 == side)
        def _(mat=mat, slope=slope):
            grad = (dot(grad_ref[...], mat[...], NT) * slope[...].astype(f32)).astype(bf16)
            out_ref[...] = grad
            sum_ref[...] = jnp.sum(grad.astype(f32), 0, keepdims=True)


def shrink(where, grad, mats, slopes):
    rows, width = grad.shape
    columns = 2 * slopes[0].shape[1]
    tile = columns // 8
    true = lambda i, where: (0, where[i])
    near = lambda i, _: jnp.minimum(i, 3)
    far = lambda i, _: jnp.maximum(i - 4, 0)
    return call(
        shrink_kernel,
        (8,),
        where,
        [
            whole(grad),
            (mats[0], (tile, width), lambda i, _: (near(i, _), 0)),
            (mats[1], (tile, width), lambda i, _: (far(i, _), 0)),
            (slopes[0], (rows, tile), lambda i, _: (0, near(i, _))),
            (slopes[1], (rows, tile), lambda i, _: (0, far(i, _))),
        ],
        [((rows, columns), bf16, (rows, tile), true), ((1, columns), f32, (1, tile), true)],
        micros=12,
    )


def back_product(grad, mat):
    if len(grad.shape) == 2:
        return dot(grad[...], mat[...], NT)
    cols = grad.shape[2]
    return sum(dot(grad[i], mat[:, i * cols : (i + 1) * cols], NT) for i in range(3))


def back_kernel(low, where, grad_ref, mat_low, mat_high, values_ref, above_ref, gain_ref, out_ref, *rest):
    (*low_refs, gain_sum, bias_sum, total) = rest
    step = pl.program_id(0)

    def put(mat):
        part = back_product(grad_ref, mat)
        for side in range(2):
            total[:, lanes(where, 2 * step + side)] = part[:, side * 128 : (side + 1) * 128]

    @pl.when(step < 2)
    def _():
        put(mat_low)

    @pl.when(step >= 2)
    def _():
        put(mat_high)

    @pl.when(step == 3)
    def _():
        count, width = values_ref.shape
        chunk = 64
        sums = [jnp.zeros((1, width), f32)] * 3
        for first in range(0, count, chunk):
            rows = slice(first, first + chunk)
            normed, inverse = normalize(values_ref[rows, :].astype(f32))
            grad = total[rows, :]
            scaled = grad * gain_ref[...]
            result = above_ref[rows, :].astype(f32) + inverse * (
                scaled
                - jnp.mean(scaled, -1, keepdims=True)
                - normed * jnp.mean(scaled * normed, -1, keepdims=True)
            )
            out_ref[rows, :] = result
            sums[0] += jnp.sum(grad * normed, 0, keepdims=True)
            sums[1] += jnp.sum(grad, 0, keepdims=True)
            if low:
                rounded = result.astype(bf16)
                low_refs[0][rows, :] = rounded
                sums[2] += jnp.sum(rounded.astype(f32), 0, keepdims=True)
        gain_sum[...] = sums[0]
        bias_sum[...] = sums[1]
        if low:
            low_refs[1][...] = sums[2]


def back(where, grad, mats, values, above, gain, low):
    rows, width = values.shape
    columns = grad.shape[1] if grad.ndim == 2 else 3 * width
    outs = [whole_out((rows, width), f32)]
    if low:
        outs += [whole_out((rows, width), bf16), whole_out((1, width), f32)]
    outs += [whole_out((1, width), f32)] * 2
    return call(
        functools.partial(back_kernel, low),
        (4,),
        where,
        [
            whole(grad) if grad.ndim == 2 else (grad, (3, rows, width), lambda *_: (0, 0, 0)),
            (mats[0], (256, columns), lambda i, _: (jnp.minimum(i, 1), 0)),
            (mats[1], (256, columns), lambda i, _: (jnp.maximum(i - 2, 0), 0)),
            whole(values),
            whole(above),
            whole(gain),
        ],
        outs,
        [pltpu.VMEM((rows, width), f32)], micros=13)


def mixed_grad_kernel(where, grad_ref, low, high, out_ref):
    for at in range(4):
        mat = (low, high)[at // 2]
        part = dot(grad_ref[...], mat[at % 2 * 256 : at % 2 * 256 + 256, :], NT).astype(bf16)
        for side in range(2):
            out_ref[:, lanes(where, 2 * at + side)] = part[:, side * 128 : (side + 1) * 128]


def mixed_grad(where, grad, mats):
    return call(
        mixed_grad_kernel,
        (1,),
        where,
        [whole(grad), *[last_columns(m, grad.shape[1]) for m in mats]],
        [whole_out(grad.shape, bf16)], micros=3)[0]


def feed_kernel(where, low_ref, high_ref, mat_low, mat_high, middle_ref, shift_ref, keep_ref, out_ref):
    total = dot(low_ref[...], mat_low[...]) + dot(high_ref[...], mat_high[...])
    out_ref[...] = keep_ref[...] * (total + middle_ref[...] + shift_ref[...])


def feed(where, low, high, mats, middle, shift, keep):
    rows, width = middle.shape
    mat = ((mats[0].shape[0], 256), column)
    return call(
        feed_kernel,
        (width // 256,),
        where,
        [
            whole(low),
            whole(high),
            (mats[0], *mat),
            (mats[1], *mat),
            (middle, (rows, 256), column),
            (shift, (1, 256), column),
            whole(keep),
        ],
        [((rows, width), f32, (rows, 256), column)], micros=10)[0]


def product_kernel(counts, where, *refs):
    n = len(counts)
    lefts, rights, outs, turned = refs[: 2 * n], refs[2 * n : 4 * n], refs[4 * n : -2 * n], refs[-2 * n :]
    keep_a, send_a, keep_b, send_b = outs
    step = pl.program_id(0)
    middle = sum(counts) // 2

    @pl.when(step == 0)
    def _():
        for left, turn in zip(lefts, turned):
            turn[...] = left[...].T

    def put(pair, targets):
        own, other = turned[2 * pair : 2 * pair + 2]
        right, right_other = rights[2 * pair : 2 * pair + 2]
        count = own.shape[0] // 4
        total = (dot(own[...], right[...]) + dot(other[...], right_other[...])).astype(bf16)
        for target, blocks in targets:
            for at, block in enumerate(blocks):
                target[at * count : (at + 1) * count, :] = total[block * count : (block + 1) * count, :]

    first = 0
    for pair, count in enumerate(counts):
        here = (step >= first) & (step < first + count)

        @pl.when(here & (step < middle))
        def _(pair=pair):
            put(pair, ((keep_a, (0, 1)), (send_a, (2, 3))))

        @pl.when(here & (step >= middle))
        def _(pair=pair):
            put(pair, ((keep_b, (0, 2)), (send_b, (1, 3))))

        first += count


def add_kernel(where, a0, a1, b0, b1, keep_a, send_a, keep_b, send_b):
    half = a0.shape[0] // 2
    for kept, piece, targets in ((a0, a1, (keep_a, send_a)), (b0, b1, (keep_b, send_b))):
        for part, target in enumerate(targets):
            rows = slice(part * half, (part + 1) * half)
            total = kept[rows, :].astype(f32) + piece[rows, :].astype(f32)
            target[...] = total.astype(bf16)


def flat_kernel(where, a0, a1, b0, b1, out):
    columns = a0.shape[1]
    for side, (kept, piece) in enumerate(((a0, a1), (b0, b1))):
        total = kept[...].astype(f32) + piece[...].astype(f32)
        out[:, side * columns : (side + 1) * columns] = total.astype(bf16)


def finish_kernel(where, a0, a1, b0, b1, *refs):
    own, *others, total = refs
    columns = a0.shape[1]
    for side, (kept, piece) in enumerate(((a0, a1), (b0, b1))):
        total[:, side * columns : (side + 1) * columns] = kept[...].astype(f32) + piece[...].astype(f32)
    count = own.shape[0]
    for at, out in enumerate((own, *others)):
        rows = pl.ds(pl.multiple_of(where[16 + at] * count, count), count)
        out[...] = total[rows, :].astype(out.dtype)


class Sum:
    def __init__(self, swap, along, order, where, lefts, rights, tile, counts, flat=False):
        self.swap, self.along, self.order, self.where = swap, along, order, where
        self.lefts = [left for pair in lefts for left in pair]
        self.rights = [right for pair in rights for right in pair]
        self.tile, self.counts, self.flat = tile, counts, flat
        self.sent = 0

    def product(self, *arrays):
        n = len(self.counts)
        lefts, rights = arrays[: 2 * n], arrays[2 * n :]
        depth = lefts[0].shape[0]
        count = self.lefts[0][0].shape[1]
        specs = [first_columns(left, count, at) for left, (_, at) in zip(lefts, self.lefts)]
        first = 0
        for pair, steps in enumerate(self.counts):
            for right, (_, base) in list(zip(rights, self.rights))[2 * pair : 2 * pair + 2]:
                at = lambda i, first=first, steps=steps, base=base: base + jnp.clip(i - first, 0, steps - 1)
                if right.ndim == 2:
                    specs.append((right, (depth, self.tile), lambda i, _, at=at: (0, at(i))))
                else:
                    per = right.shape[2] // self.tile
                    specs.append(
                        (right, (None, depth, self.tile), lambda i, _, at=at: (at(i) // per, 0, at(i) % per))
                    )
            first += steps
        near = lambda i, _: (0, jnp.minimum(i, first // 2 - 1))
        far = lambda i, _: (0, jnp.maximum(i - first // 2, 0))
        shape = (count // 2, self.tile * first // 2)
        block = (count // 2, self.tile)
        return call(
            functools.partial(product_kernel, self.counts),
            (first,),
            self.where,
            specs,
            [(shape, bf16, block, near)] * 2 + [(shape, bf16, block, far)] * 2,
            [pltpu.VMEM((count, depth), bf16)] * (2 * n),
            micros=12,
        )

    def add(self, *pieces):
        rows, columns = pieces[0].shape
        tile = columns // 2
        block = ((rows, tile), column)
        half = ((rows // 2, columns), bf16, (rows // 2, tile), column)
        return call(
            add_kernel, (columns // tile,), self.where, [(v, *block) for v in pieces], [half] * 4, micros=12)

    def finish(self, *pieces):
        rows, columns = pieces[0].shape
        if self.flat:
            out = whole_out((rows, 2 * columns), bf16)
            return call(flat_kernel, (1,), self.where, [whole(v) for v in pieces], [out])
        owners = self.where.shape[0] - 16
        share = (rows // owners, 2 * columns)
        return call(
            finish_kernel,
            (1,),
            self.where,
            [whole(v) for v in pieces],
            [whole_out(share, f32)] + [whole_out(share, bf16)] * (owners - 1),
            [pltpu.VMEM((rows, 2 * columns), f32)],
        )

    def work(self):
        if self.sent == 2:
            self.own, *self.ready = self.order(
                self.finish, self.kept[0], self.arrived[0], self.kept[1], self.arrived[1]
            )
            return
        if self.sent == 0:
            factors = [array for array, _ in (*self.lefts, *self.rights)]
            keep_a, send_a, keep_b, send_b = self.order(self.product, *factors)
        else:
            keep_a, send_a, keep_b, send_b = self.order(
                self.add, self.kept[0], self.arrived[0], self.kept[1], self.arrived[1]
            )
        self.kept = keep_a, keep_b
        self.ready = send_a, send_b

    def send(self):
        if self.sent == 2 and self.flat:
            self.share = lax.psum_scatter(
                self.order.tie(self.own)[0], "fsdp", scatter_dimension=0, tiled=True
            )
            return
        ready = self.order.tie(*self.ready)
        if self.sent == 2:
            self.shares = [self.along(piece, by) for by, piece in enumerate(ready, 1)]
        else:
            bits = (XBIT, YBIT) if self.sent else (YBIT, XBIT)
            self.arrived = self.swap(ready[0], bits[0]), self.swap(ready[1], bits[1])
        self.sent += 1

    def total(self):
        if self.flat:
            return self.order(lambda share: share.astype(f32), self.share)
        return self.order(
            lambda own, *others: sum((piece.astype(f32) for piece in others), own), self.own, *self.shares
        )


class Order:
    def __init__(self):
        self.last = ()

    def __call__(self, function, *values):
        result = function(*self.tie(*values))
        self.last = (result[0] if isinstance(result, (tuple, list)) else result,)
        return result

    def tie(self, *values):
        return lax.optimization_barrier((*values, *self.last))[: len(values)]


def assemble_kernel(where, *refs):
    count = refs[0].shape[0]
    for at, piece in enumerate(refs[:-1]):
        rows = pl.ds(pl.multiple_of(where[at] * count, count), count)
        refs[-1][rows, :] = piece[...]


def assemble(places, *pieces):
    rows, columns = pieces[0].shape
    out = whole_out((rows * len(pieces), columns), bf16)
    return call(assemble_kernel, (1,), places, [whole(p) for p in pieces], [out])[0]


def join_kernel(where, own, near, far, left, right, out):
    count = own.shape[0]
    for at, piece in enumerate((own, near, far)):
        out[at * count : (at + 1) * count, :] = piece[...]
    for side, piece in enumerate((left, right)):

        @pl.when(pl.program_id(0) == side)
        def _(piece=piece):
            out[3 * count :, :] = piece[...]


def join(where, own, near, far, left, right):
    rows, columns = own.shape
    block = (rows, columns // 2)
    return call(
        join_kernel,
        (2,),
        where,
        [(v, block, column) for v in (own, near, far)] + [whole(left), whole(right)],
        [((4 * rows, columns), bf16, (4 * rows, columns // 2), column)], micros=4)[0]


def turn_kernel(where, near, far, left, right):
    left[...] = near[...]
    right[...] = far[...]


def turn(where, near, far):
    rows, columns = near.shape
    half = (rows, columns // 2)
    return call(
        turn_kernel,
        (1,),
        where,
        [(near, half, lambda *_: (0, 0)), (far, half, lambda *_: (0, 1))],
        [whole_out(half, bf16)] * 2,
    )


def pack_kernel(where, *refs):
    out = refs[-1]
    owners = out.shape[0]
    first = 0
    for vector in refs[:-1]:
        share = vector.shape[1] // owners
        for owner in range(owners):
            out[owner : owner + 1, first : first + share] = vector[:, owner * share : (owner + 1) * share]
        first += share


def pack(where, vectors, owners):
    columns = sum(v.shape[1] for v in vectors) // owners
    return call(
        pack_kernel, (1,), where, [whole(v) for v in vectors], [whole_out((owners, columns), f32)]
    )[0]


def unpack_kernel(where, low, high, *refs):
    outs, true = refs[:-1], refs[-1]
    for side, part in enumerate((low, high)):
        turned = part[...].astype(f32).T
        for at in range(4):
            true[:, lanes(where, 4 * side + at)] = turned[:, at * 128 : (at + 1) * 128]
    share = 32
    first = 0
    for vector in outs:
        columns = vector.shape[1] // true.shape[1]
        if columns == 1:
            vector[...] = true[first : first + 1, :]
        else:
            for owner in range(true.shape[1] // share):
                for at in range(columns):
                    start = (owner * columns + at) * share
                    vector[:, start : start + share] = true[
                        first + at : first + at + 1, owner * share : (owner + 1) * share
                    ]
        first += columns


def unpack(where, mats, sizes):
    block = mats[0].shape[1] // 128 - 2
    outs = [whole_out((1, size), f32) for size in sizes]
    rows = mats[0].shape[0]
    return call(
        unpack_kernel,
        (1,),
        where,
        [(mat, (rows, 128), lambda *_: (0, block)) for mat in mats],
        outs,
        [pltpu.VMEM((128, 2 * rows), f32)],
    )


def exchanged(fsdp_size, block_in, keep_mask, out_cotangent, *params):
    (g1, b1, qkv_weight, qv_bias, out_weight, out_bias, g2, b2, up_weight, up_bias, down_weight, down_bias) = params
    seqs, length, width = block_in.shape
    rows = seqs * length
    half = width // 2
    order = Order()
    me, line = lax.axis_index("dp"), lax.axis_index("fsdp")
    where = positions(me, line, fsdp_size)

    def swap(value, bit):
        return lax.ppermute(value, "dp", [(i, i ^ bit) for i in range(8)])

    def along(value, by):
        return lax.ppermute(value, "fsdp", [(i, (i + by) % fsdp_size) for i in range(fsdp_size)])

    class Gather:
        def start(self, block):
            self.own = order.tie(block)[0]
            self.near, self.far = swap(self.own, XBIT), swap(self.own, YBIT)

        def turn(self, *others):
            self.ready = order(lambda near, far, *_: turn(where, near, far), self.near, self.far, *others)

        def turned(self):
            left, right = order.tie(*self.ready)
            self.left, self.right = swap(left, YBIT), swap(right, XBIT)

        def join(self):
            self.low = order(
                functools.partial(join, where), self.own, self.near, self.far, self.left, self.right
            )

        def joined(self):
            low = order.tie(self.low)[0]
            self.mats = low, swap(low, CORE)

    def around(shard):
        return [shard] + [along(shard, by) for by in range(1, fsdp_size)]

    vectors = (g1, b1, qv_bias, out_bias, g2, b2, up_bias, down_bias)
    device_count = 8 * fsdp_size
    sizes = [v.shape[0] * device_count for v in vectors]
    cuts = [sum(v.shape[0] for v in vectors[:i]) for i in range(1, len(vectors))]
    share = qkv_weight.shape[0]
    beside = jnp.concatenate(vectors).reshape(-1, share).T
    beside = jnp.pad(beside, ((0, 0), (0, 256 - beside.shape[1])))
    qkv_low = jnp.concatenate([qkv_weight, beside], 1).astype(bf16)
    behind = jnp.stack([(line - by) % fsdp_size for by in range(fsdp_size)]).astype(jnp.int32)
    qkv_pieces = around(qkv_low)
    up_low = jnp.concatenate([up_weight, out_weight], 1).astype(bf16)
    down_block = lax.all_gather(down_weight.astype(bf16), "fsdp", axis=0, tiled=True)

    keep = jnp.concatenate(
        [jnp.ones((seqs, length - keep_mask.shape[1]), jnp.int32), keep_mask], axis=1
    )
    keep_rows = keep.reshape(rows, 1).astype(f32)
    keep_column = keep.reshape(seqs, length, 1)
    inputs = block_in.reshape(rows, width)
    grad_feed = jnp.where(keep_rows > 0, out_cotangent.reshape(rows, width), jnp.zeros((), bf16))
    down_bias_grad = jnp.sum(grad_feed.astype(f32), 0)

    qkv, up, down = Gather(), Gather(), Gather()
    block = order(functools.partial(assemble, behind), *qkv_pieces)
    qkv.start(block)
    up_pieces = around(order.tie(up_low)[0])
    qkv.turn()
    qkv.turned()
    up_block = order(functools.partial(assemble, behind), *up_pieces)
    qkv.join()
    qkv.joined()
    up.start(up_block)
    g1, b1, qv_bias, out_bias, g2, b2, up_bias, down_bias = order(
        lambda *m: unpack(where, m, sizes), *qkv.mats
    )
    one_low, one_pack = order(functools.partial(norm_one, where), inputs, grad_feed, g1, b1)
    shift = jnp.concatenate([qv_bias[:, :width], jnp.zeros((1, width), f32), qv_bias[:, width:]], 1)
    projected = order(
        lambda lo, hi, s, *m: project(where, lo, hi, m, s), one_low, one_pack, shift, *qkv.mats
    )
    mixed_left = order(lambda p: attention_forward(keep_column, p, 0), projected)
    up.turn(down_block)
    up.turned()
    one_other = swap(order.tie(one_pack)[0], CORE)
    mixed_right = order(lambda p: attention_forward(keep_column, p, 1), projected)
    up.join()
    up.joined()
    down.start(down_block)
    mixed = jnp.concatenate([mixed_left, mixed_right], 1)
    mix_low, middle, two_low, two_pack = order(
        lambda m, o, *mats: branch_norm(where, m, inputs, mats, o, g2, b2, length),
        mixed, out_bias, *up.mats,
    )
    hidden_high, slope_high = order(
        lambda lo, hi, s, *m: expand(where, 1, lo, hi, m, s), two_low, two_pack, up_bias, *up.mats
    )
    hidden_low, slope_low = order(
        lambda lo, hi, s, *m: expand(where, 0, lo, hi, m, s), two_low, two_pack, up_bias, *up.mats
    )
    down.turn()
    down.turned()
    hidden_other = swap(order.tie(hidden_high)[0], CORE)
    two_other = swap(order.tie(two_pack)[0], CORE)
    down_sum = Sum(
        swap, along, order, where,
        [((hidden_low, 0), (hidden_other, 0))], [((grad_feed, 0), (one_other, half // 256))],
        256, [width // 256], True,
    )
    down_sum.work()
    down.join()
    down.joined()
    down_sum.send()
    grad_pre, up_bias_grad = order(
        lambda g, s0, s1, *m: shrink(where, g, m, (s0, s1)),
        grad_feed, slope_low, slope_high, *down.mats,
    )
    down_sum.work()
    down_sum.send()
    pre_other = swap(order.tie(grad_pre)[0], CORE)
    grad_middle, grad_branch, out_bias_grad, gain_two_grad, bias_two_grad = order(
        lambda g, mid, above, *m: back(where, g, m, mid, above, g2, True),
        grad_pre, middle, grad_feed, *up.mats,
    )
    up_sum = Sum(
        swap, along, order, where,
        [((two_low, 0), (two_other, 1))], [((grad_pre, 0), (pre_other, 0))],
        512, [grad_pre.shape[1] // 512],
    )
    up_sum.work()
    down_sum.work()
    up_sum.send()
    grad_mixed = order(lambda g, *m: mixed_grad(where, g, m), grad_branch, *up.mats)
    grad_projected, sum_q, sum_v = order(
        lambda p, g, b: attention_backward(keep_column, p, g, b), projected, grad_mixed, grad_branch
    )
    up_sum.work()
    up_sum.send()
    projected_other = swap(order.tie(grad_projected)[0], CORE)
    down_sum.send()
    input_grad, gain_one_grad, bias_one_grad = order(
        lambda g, x, above, *m: back(where, g, m, x, above, g1, False),
        grad_projected, inputs, grad_middle, *qkv.mats,
    )
    grads = (
        gain_one_grad,
        bias_one_grad,
        jnp.concatenate([sum_q, sum_v], 1),
        out_bias_grad,
        gain_two_grad,
        bias_two_grad,
        up_bias_grad,
        down_bias_grad,
    )
    shares = order(lambda *g: pack(where, g, device_count), *[g.reshape(1, -1) for g in grads])
    mid_sum = Sum(
        swap, along, order, where,
        [((one_low, 0), (one_other, 0)), ((mix_low, 0), (two_other, 0))],
        [((grad_projected, 0), (projected_other, 0)), ((grad_projected, 6), (projected_other, 6))],
        512, [3 * width // 512, width // 512],
    )
    mid_sum.work()
    down_grad = down_sum.total()
    up_sum.work()
    mid_sum.send()
    up_sum.send()
    upper = me % 2 == 1
    shares = shares.reshape(4, 2, fsdp_size, -1)
    low, high = shares[:, 0], shares[:, 1]
    core_share = swap(order.tie(jnp.where(upper, low, high))[0], CORE)
    shares = jnp.where(upper, high, low)
    block_out = order(
        lambda lo, hi, mid, s, *m: feed(where, lo, hi, m, mid, s, keep_rows),
        hidden_low, hidden_high, middle, down_bias, *down.mats,
    )
    mid_sum.work()
    mid_sum.send()
    shares = order.tie(shares + core_share)[0]

    def part_of(bits):
        return lax.dynamic_index_in_dim(shares, (me ^ bits) // 2, 0, keepdims=False)

    plane_shares = [swap(part_of(bits), bits) for bits in (XBIT, YBIT, XBIT + YBIT)]
    up_grad = up_sum.total()
    mid_sum.work()
    mid_sum.send()
    shares = order.tie(sum(plane_shares, part_of(0)))[0]

    def row_of(by):
        return lax.dynamic_slice(shares, ((line + by) % fsdp_size, 0), (1, shares.shape[1]))

    line_shares = [along(row_of(by), by) for by in range(1, fsdp_size)]
    mid_grad = mid_sum.total()
    mine = sum(line_shares, row_of(0))
    qkv_grad, out_grad = mid_grad[:, : 3 * width], mid_grad[:, 3 * width :]
    v = jnp.split(mine[0], cuts)
    return (
        block_out.reshape(seqs, length, width),
        input_grad.reshape(seqs, length, width),
        v[0],
        v[1],
        qkv_grad,
        v[2],
        out_grad,
        v[3],
        v[4],
        v[5],
        up_grad,
        v[6],
        down_grad,
        v[7],
    )


def solution(mesh):
    dp_size, fsdp_size = mesh.shape["dp"], mesh.shape["fsdp"]
    if dp_size == 8:
        local = functools.partial(exchanged, fsdp_size)
    else:
        local = functools.partial(gathered, dp_size * fsdp_size)
    row = P(AXES, None)
    vec = P(AXES)
    cube = P(AXES, None, None)
    return jax.shard_map(
        local,
        mesh=mesh,
        in_specs=(cube, row, cube, vec, vec, row, vec, row, vec, vec, vec, row, vec, row, vec),
        out_specs=(cube, cube, vec, vec, row, vec, row, vec, vec, vec, row, vec, row, vec),
        check_vma=False,
    )
```

time: 633 us -> 429 us (0.68)
  Pallas kernels: 39.2 us -> 199 us
  waiting for transfers between devices: 245 us -> 88.1 us
  matrix products: 140 us -> 0 us
  blocking collectives: 111 us -> 0 us
  starting transfers between devices: 21.6 us -> 66.1 us
  other arithmetic: 36.9 us -> 18.5 us
  local copies, waits for them, and re-layouts: 17.5 us -> 33.8 us
    pallas_call x0 -> x29, Pallas kernels: none -> 160 us  [call(): pl.pallas_call(kernel, grid_spec=pltpu.PrefetchScalarGridSpec(num_scalar_...]
    all_gather x4 -> x1, waiting for transfers between devices: 156 us -> 2.98 us  [exchanged(): lax.all_gather(down_weight.astype(bf16), 'fsdp', axis=0, tiled=True)]
    dot_general x42 -> x0, matrix products: 140 us -> none  [dot(): return lax.dot_general(left, right, dims, preferred_element_type=f32)]
    all_gather x1 -> x0, blocking collectives: 70.9 us -> none  [local(): lax.all_gather(jnp.concatenate([v.astype(bf16) for v in vectors]), AXES,...]
    ppermute x24 -> x51, starting transfers between devices: 20.8 us -> 65.8 us  [the longest x15 34.5 us: along(): lax.ppermute(value, 'fsdp', [(i, (i + by) % fsdp_size) for i in range(fsd...]
    unnamed x1 -> x0, blocking collectives: 39.7 us -> none
    unnamed x153 -> x150, local copies, waits for them, and re-layouts: 7.93 us -> 29 us
    convert_element_type x30 -> x3, other arithmetic: 23.8 us -> 3.19 us  [the longest x1 1.79 us: total(): return self.order(lambda share: share.astype(f32), self.share)]
  transfers between devices with their start and end apart: 32 -> 53, of which waited for: 15 -> 25; matrix products, arithmetic and copies ran while one was open for 23% -> 4% of each run, Pallas kernels for 6% -> 40%
where the time goes in v2:
time: 429 us; the launch traced here: 421 us
  Pallas kernels  199 us (46%)
  waiting for transfers between devices  88.1 us (21%)
  starting transfers between devices  66.1 us (15%)
  local copies, waits for them, and re-layouts  33.8 us (8%)
  other arithmetic  18.5 us (4%)
  between operations  15.5 us (4%)
    pallas_call x29, Pallas kernels, call(): pl.pallas_call(kernel, grid_spec=pltpu.PrefetchScalarGridSpec(num_scalar_...  160 us
    ppermute x36, waiting for transfers between devices, swap(): return lax.ppermute(value, 'dp', [(i, i ^ bit) for i in range(8)])  56.1 us
    ppermute x15, starting transfers between devices, along(): lax.ppermute(value, 'fsdp', [(i, (i + by) % fsdp_size) for i in range(fsd...  34.5 us
    ppermute x36, starting transfers between devices, swap(): return lax.ppermute(value, 'dp', [(i, i ^ bit) for i in range(8)])  31.4 us
    unnamed x150, local copies, waits for them, and re-layouts  29 us
    ppermute x15, waiting for transfers between devices, along(): lax.ppermute(value, 'fsdp', [(i, (i + by) % fsdp_size) for i in range(fsd...  29 us
    pallas_call x1, Pallas kernels, attention_backward(): pl.pallas_call(functools.partial(attention_backward_kernel, seqs, length)...  22.8 us
    pallas_call x2, Pallas kernels, attention_forward(): pl.pallas_call(functools.partial(attention_forward_kernel, seqs, length),...  16.9 us
  transfers between devices with their start and end apart: 53, of which 25 were waited for; matrix products, arithmetic and copies ran while one was open for 4% of the time, Pallas kernels for 40%

profile of v2, /device:TPU:0, one launch (start us, length us, event | category | flops | bytes accessed | tf_op | source)
XLA Modules:
  0.0 421.3 jit_solution(15944858081075519550)
XLA Ops:
  20.9 4.2 %collective-permute-done.refs_1_ = bf16[32,3328]{1,0:T(8,128)(2,1)S(1)} collective-permute-done((bf16[32,3328]{1,0:T(8,128)(2,1)S(1)}, bf16[32,3328]{1,0:T(8,128)(2,1)S(1)}, u32[]{:S(2)}, u32[]{:S(2)}) %collective-permute-start) | collective-permute-done | bytes 213024 | tf_op jit(solution)/shard_map/ppermute | solution.py:848
  25.2 8.3 %collective-permute-done.1.refs_2_ = bf16[32,3328]{1,0:T(8,128)(2,1)S(1)} collective-permute-done((bf16[32,3328]{1,0:T(8,128)(2,1)S(1)}, bf16[32,3328]{1,0:T(8,128)(2,1)S(1)}, u32[]{:S(2)}, u32[]{:S(2)}) %collective-permute-start.1) | collective-permute-done | bytes 213024 | tf_op jit(solution)/shard_map/ppermute | solution.py:848
  38.4 5.0 %collective-permute-start.7 = (bf16[32,5120]{1,0:T(8,128)(2,1)}, bf16[32,5120]{1,0:T(8,128)(2,1)}, u32[]{:S(2)}, u32[]{:S(2)}) collective-permute-start(bf16[32,5120]{1,0:T(8,128)(2,1)} %pad_maximum_fusion.1.refs_0_), channel_id=1, source_target_pairs={{0,1},{1,2},{2,3},{3,0},{4,5},{5,6},{6,7},{7,4},{8,9},{9,10},{10,1... | collective-permute-start | bytes 983048 | tf_op jit(solution)/shard_map/ppermute | solution.py:848
  45.7 9.2 %collective-permute-done.3.near = bf16[128,3328]{1,0:T(8,128)(2,1)S(1)} collective-permute-done((bf16[128,3328]{1,0:T(8,128)(2,1)S(1)}, bf16[128,3328]{1,0:T(8,128)(2,1)S(1)}, u32[]{:S(2)}, u32[]{:S(2)}) %collective-permute-start.3) | collective-permute-done | bytes 852000 | tf_op jit(solution)/shard_map/ppermute | solution.py:845
  59.7 5.5 %collective-permute-done.8.refs_2_ = bf16[32,5120]{1,0:T(8,128)(2,1)} collective-permute-done((bf16[32,5120]{1,0:T(8,128)(2,1)}, bf16[32,5120]{1,0:T(8,128)(2,1)}, u32[]{:S(2)}, u32[]{:S(2)}) %collective-permute-start.8) | collective-permute-done | bytes 327712 | tf_op jit(solution)/shard_map/ppermute | solution.py:848
  69.8 3.7 shard_map.257.low.mat_low
  84.2 8.3 %shard_map.260.q_ref.k_ref.v_ref = bf16[640,3072]{1,0:T(8,128)(2,1)S(1)} custom-call(s32[20]{0:T(128)S(1)} %stack.96.where, bf16[640,512]{1,0:T(8,128)(2,1)S(1)} %get-tuple-element.448.low_ref.refs_0_, bf16[640,1536]{1,0:T(8,128)(2,1)S(1)} %get-tuple-element.349.high_ref, bf16[512,3328]{1,0:T(8,128)(2,1)} %shard_map.257.low.mat_low, ...), custom_call_target="tpu_custom_call" | custom-call | flops 7999999967232 | bytes 1 | tf_op jit(solution)/shard_map/pallas_call | solution.py:246
  92.6 8.5 %shard_map.261 = bf16[640,512]{1,0:T(8,128)(2,1)S(1)} custom-call(s32[2,320,1]{2,1,0:T(8,128)S(1)} %copy.34.keep_ref, bf16[640,3072]{1,0:T(8,128)(2,1)S(1)} %shard_map.260.q_ref.k_ref.v_ref, bf16[640,3072]{1,0:T(8,128)(2,1)S(1)} %shard_map.260.q_ref.k_ref.v_ref, bf16[640,3072]{1,0:T(8,128)(2,1)S(1)} %shard_map.260.q_ref.k_ref.v_ref), custom_call_target="tpu_custom_call" | custom-call | flops 8499999801344 | bytes 1 | tf_op jit(solution)/shard_map/pallas_call | solution.py:83
  105.9 3.8 collective-permute-done.11.near
  115.1 8.4 %shard_map.263 = bf16[640,512]{1,0:T(8,128)(2,1)S(1)} custom-call(s32[2,320,1]{2,1,0:T(8,128)S(1)} %copy.34.keep_ref, bf16[640,3072]{1,0:T(8,128)(2,1)S(1)} %copy-done.33, bf16[640,3072]{1,0:T(8,128)(2,1)S(1)} %copy-done.33, bf16[640,3072]{1,0:T(8,128)(2,1)S(1)} %copy-done.33), custom_call_target="tpu_custom_call" | custom-call | flops 8499999801344 | bytes 1 | tf_op jit(solution)/shard_map/pallas_call | solution.py:83
  123.6 6.0 %collective-permute-done.13.left = bf16[128,2560]{1,0:T(8,128)(2,1)} collective-permute-done((bf16[128,2560]{1,0:T(8,128)(2,1)}, bf16[128,2560]{1,0:T(8,128)(2,1)}, u32[]{:S(2)}, u32[]{:S(2)}) %collective-permute-start.13) | collective-permute-done | bytes 655392 | tf_op jit(solution)/shard_map/ppermute | solution.py:845
  136.5 5.5 %collective-permute-done.15.mat_high.high = bf16[512,5120]{1,0:T(8,128)(2,1)S(1)} collective-permute-done((bf16[512,5120]{1,0:T(8,128)(2,1)S(1)}, bf16[512,5120]{1,0:T(8,128)(2,1)S(1)}, u32[]{:S(2)}, u32[]{:S(2)}) %collective-permute-start.15) | collective-permute-done | bytes 5242912 | tf_op jit(solution)/shard_map/ppermute | solution.py:845
  142.0 4.4 %shard_map.265 = (bf16[640,512]{1,0:T(8,128)(2,1)S(1)}, f32[640,1024]{1,0:T(8,128)S(1)}, bf16[640,512]{1,0:T(8,128)(2,1)S(1)}, bf16[640,1024]{1,0:T(8,128)(2,1)}) custom-call(s32[20]{0:T(128)S(1)} %copy-done.8, bf16[640,1024]{1,0:T(8,128)(2,1)S(1)} %pad_maximum_fusion.mixed_ref, bf16[640,1024]{1,0:T(8,128)(2,1)S(1)} %bitcast.81, ...), custom_call_target="tpu_custom_call" | custom-call | flops 3999999983616 | bytes 1 | tf_op jit(solution)/shard_map/pallas_call | solution.py:246
  147.8 7.0 %shard_map.266 = (bf16[640,2048]{1,0:T(8,128)(2,1)S(1)}, bf16[640,2048]{1,0:T(8,128)(2,1)S(1)}) custom-call(s32[20]{0:T(128)S(1)} %copy-done.8, bf16[640,512]{1,0:T(8,128)(2,1)S(1)} %get-tuple-element.387.low_ref.refs_0_, bf16[640,1024]{1,0:T(8,128)(2,1)} %get-tuple-element.361.high_ref, bf16[512,5120]{1,0:T(8,128)(2,1)S(1)} %shard_map.264.mat_low.low, ...), custom_call_target="tpu_custom_call" | custom-call | flops 6999999774720 | bytes 1 | tf_op jit(solution)/shard_map/pallas_call | solution.py:246
  154.9 7.5 %shard_map.267 = (bf16[640,2048]{1,0:T(8,128)(2,1)S(1)}, bf16[640,2048]{1,0:T(8,128)(2,1)S(1)}) custom-call(s32[20]{0:T(128)S(1)} %copy-done.8, bf16[640,512]{1,0:T(8,128)(2,1)S(1)} %get-tuple-element.387.low_ref.refs_0_, bf16[640,1024]{1,0:T(8,128)(2,1)} %get-tuple-element.361.high_ref, bf16[512,5120]{1,0:T(8,128)(2,1)S(1)} %shard_map.264.mat_low.low, ...), custom_call_target="tpu_custom_call" | custom-call | flops 6999999774720 | bytes 1 | tf_op jit(solution)/shard_map/pallas_call | solution.py:246
  162.4 4.9 %shard_map.268 = (bf16[512,512]{1,0:T(8,128)(2,1)}, bf16[512,512]{1,0:T(8,128)(2,1)}) custom-call(s32[20]{0:T(128)S(1)} %copy-done.8, bf16[512,1024]{1,0:T(8,128)(2,1)} %collective-permute-done.16.near, bf16[512,1024]{1,0:T(8,128)(2,1)} %collective-permute-done.17.far), custom_call_target="tpu_custom_call" | custom-call | flops 3000000053248 | bytes 1 | tf_op jit(solution)/shard_map/pallas_call | solution.py:246
  170.9 4.2 collective-permute-done.21.refs_3_.refs_1_
  175.1 11.0 %shard_map.269 = (bf16[1024,512]{1,0:T(8,128)(2,1)S(1)}, bf16[1024,512]{1,0:T(8,128)(2,1)}, bf16[1024,512]{1,0:T(8,128)(2,1)S(1)}, bf16[1024,512]{1,0:T(8,128)(2,1)}) custom-call(s32[20]{0:T(128)S(1)} %copy-done.8, bf16[640,2048]{1,0:T(8,128)(2,1)S(1)} %get-tuple-element.463.refs_0_.low_ref, bf16[640,2048]{1,0:T(8,128)(2,1)S(1)} %collective-permute-done.20.refs_1_, ...), custom_call_target="tpu_custom_call" | custom-call | flops 12000000212992 | bytes 1 | tf_op jit(solution)/shard_map/pallas_call | solution.py:246
  186.2 4.7 %shard_map.270.mat_low = bf16[2048,1024]{1,0:T(8,128)(2,1)} custom-call(s32[20]{0:T(128)S(1)} %copy-done.9, bf16[512,1024]{1,0:T(8,128)(2,1)} %all-gather.2.cloned.1.call-done.own, bf16[512,1024]{1,0:T(8,128)(2,1)} %collective-permute-done.16.near, bf16[512,1024]{1,0:T(8,128)(2,1)} %collective-permute-done.17.far, ...), custom_call_target="tpu_custom_call" | custom-call | flops 3999999983616 | bytes 1 | tf_op jit(solution)/shard_map/pallas_call | solution.py:246
  201.9 12.4 %shard_map.271 = (bf16[640,4096]{1,0:T(8,128)(2,1)}, f32[1,4096]{1,0:T(1,128)S(1)}) custom-call(s32[20]{0:T(128)S(1)} %copy-done.9, bf16[640,1024]{1,0:T(8,128)(2,1)S(1)} %copy-done.2, bf16[2048,1024]{1,0:T(8,128)(2,1)} %shard_map.270.mat_low, bf16[2048,1024]{1,0:T(8,128)(2,1)} %collective-permute-done.22.mat_high, bf16[640,2048]{1,0:T(8,128)(2,1)S(1)} %copy-done.42, ...), custom_call_target="tpu_custom_call" | custom-call | flops 12000000212992 | bytes 1 | tf_op jit(solution)/shard_map/pallas_call | solution.py:246
  214.3 4.6 %collective-permute-done.24.a1 = bf16[1024,512]{1,0:T(8,128)(2,1)} collective-permute-done((bf16[1024,512]{1,0:T(8,128)(2,1)}, bf16[1024,512]{1,0:T(8,128)(2,1)}, u32[]{:S(2)}, u32[]{:S(2)}) %collective-permute-start.24) | collective-permute-done | bytes 1048608 | tf_op jit(solution)/shard_map/ppermute | solution.py:845
  225.6 13.1 %shard_map.273 = (f32[640,1024]{1,0:T(8,128)S(1)}, bf16[640,1024]{1,0:T(8,128)(2,1)S(1)}, f32[1,1024]{1,0:T(1,128)S(1)}, f32[1,1024]{1,0:T(1,128)S(1)}, f32[1,1024]{1,0:T(1,128)S(1)}) custom-call(s32[20]{0:T(128)S(1)} %copy-done.9, bf16[640,4096]{1,0:T(8,128)(2,1)} %get-tuple-element.389.grad_ref.refs_2_, bf16[512,5120]{1,0:T(8,128)(2,1)S(1)} %copy-done.11, ...), custom_call_target="tpu_custom_call" | custom-call | flops 12999999881216 | bytes 1 | tf_op jit(solution)/shard_map/pallas_call | solution.py:246
  238.8 13.0 %shard_map.274 = (bf16[256,2048]{1,0:T(8,128)(2,1)S(1)}, bf16[256,2048]{1,0:T(8,128)(2,1)}, bf16[256,2048]{1,0:T(8,128)(2,1)S(1)}, bf16[256,2048]{1,0:T(8,128)(2,1)}) custom-call(s32[20]{0:T(128)S(1)} %copy-done.9, bf16[640,512]{1,0:T(8,128)(2,1)S(1)} %copy-done.46, bf16[640,1024]{1,0:T(8,128)(2,1)} %collective-permute-done.23.refs_1_.refs_3_, ...), custom_call_target="tpu_custom_call" | custom-call | flops 12000000212992 | bytes 1 | tf_op jit(solution)/shard_map/pallas_call | solution.py:246
  266.3 22.8 %shard_map.277 = (bf16[4,640,1024]{2,1,0:T(8,128)(2,1)S(1)}, f32[1,1024]{1,0:T(1,128)S(1)}, f32[1,1024]{1,0:T(1,128)S(1)}) custom-call(s32[2,320,1]{2,1,0:T(8,128)S(1)} %copy-done.4, bf16[640,3072]{1,0:T(8,128)(2,1)S(1)} %copy-done.34, bf16[640,3072]{1,0:T(8,128)(2,1)S(1)} %copy-done.34, bf16[640,3072]{1,0:T(8,128)(2,1)S(1)} %copy-done.34, ...), custom_call_target="tpu_custom_call" | custom-call | flops 21999998992384 | bytes 1 | tf_op jit(solution)/shard_map/pallas_call | solution.py:105
  301.8 11.7 %shard_map.279 = (f32[640,1024]{1,0:T(8,128)}, f32[1,1024]{1,0:T(1,128)S(1)}, f32[1,1024]{1,0:T(1,128)S(1)}) custom-call(s32[20]{0:T(128)S(1)} %copy-done.9, bf16[4,640,1024]{2,1,0:T(8,128)(2,1)S(1)} %copy-done.16, bf16[512,3328]{1,0:T(8,128)(2,1)} %shard_map.257.low.mat_low, bf16[512,3328]{1,0:T(8,128)(2,1)} %collective-permute-done.10.high.mat_high, ...), custom_call_target="tpu_custom_call" | custom-call | flops 12999999881216 | bytes 1 | tf_op jit(solution)/shard_map/pallas_call | solution.py:246
  320.1 12.9 %shard_map.281 = (bf16[256,2048]{1,0:T(8,128)(2,1)S(1)}, bf16[256,2048]{1,0:T(8,128)(2,1)}, bf16[256,2048]{1,0:T(8,128)(2,1)S(1)}, bf16[256,2048]{1,0:T(8,128)(2,1)}) custom-call(s32[20]{0:T(128)S(1)} %copy-done.9, bf16[640,512]{1,0:T(8,128)(2,1)S(1)} %copy-done.31, bf16[640,1536]{1,0:T(8,128)(2,1)S(1)} %copy-done.21, bf16[640,512]{1,0:T(8,128)(2,1)S(1)} %copy-done.44, ...), custom_call_target="tpu_custom_call" | custom-call | flops 12000000212992 | bytes 1 | tf_op jit(solution)/shard_map/pallas_call | solution.py:246
  342.6 5.9 %collective-permute-start.42 = (bf16[32,4096]{1,0:T(8,128)(2,1)}, bf16[32,4096]{1,0:T(8,128)(2,1)}, u32[]{:S(2)}, u32[]{:S(2)}) collective-permute-start(bf16[32,4096]{1,0:T(8,128)(2,1)} %get-tuple-element.489), channel_id=1, source_target_pairs={{0,1},{1,2},{2,3},{3,0},{4,5},{5,6},{6,7},{7,4},{8,9},{9,10},{10,1... | collective-permute-start | bytes 786440 | tf_op jit(solution)/shard_map/ppermute | solution.py:848
  350.9 9.6 %shard_map.283 = f32[640,1024]{1,0:T(8,128)} custom-call(s32[20]{0:T(128)S(1)} %copy-done.9, bf16[640,2048]{1,0:T(8,128)(2,1)S(1)} %copy-done.38, bf16[640,2048]{1,0:T(8,128)(2,1)S(1)} %copy-done.19, bf16[2048,1024]{1,0:T(8,128)(2,1)} %shard_map.270.mat_low, bf16[2048,1024]{1,0:T(8,128)(2,1)} %collective-permute-done.22.mat_high, ...), custom_call_target="tpu_custom_call" | custom-call | flops 9999999827968 | bytes 1 | tf_op jit(solution)/shard_map/pallas_call | solution.py:246
  361.8 4.1 collective-permute-done.35.a1
  376.9 8.3 %collective-permute-done.40.a1 = bf16[128,2048]{1,0:T(8,128)(2,1)S(1)} collective-permute-done((bf16[128,2048]{1,0:T(8,128)(2,1)S(1)}, bf16[128,2048]{1,0:T(8,128)(2,1)S(1)}, u32[]{:S(2)}, u32[]{:S(2)}) %collective-permute-start.40) | collective-permute-done | bytes 524320 | tf_op jit(solution)/shard_map/ppermute | solution.py:845
  388.2 5.9 %collective-permute-start.47 = (f32[1,384]{1,0:T(1,128)S(1)}, f32[1,384]{1,0:T(1,128)S(1)}, u32[]{:S(2)}, u32[]{:S(2)}) collective-permute-start(f32[1,384]{1,0:T(1,128)S(1)} %get-tuple-element.518), channel_id=1, source_target_pairs={{0,3},{1,0},{2,1},{3,2},{4,7},{5,4},{6,5},{7,6},{8,11},{9,8},{10,9... | collective-permute-start | bytes 4616 | tf_op jit(solution)/shard_map/ppermute | solution.py:848
  405.8 6.9 %collective-permute-done.49 = bf16[32,4096]{1,0:T(8,128)(2,1)S(1)} collective-permute-done((bf16[32,4096]{1,0:T(8,128)(2,1)S(1)}, bf16[32,4096]{1,0:T(8,128)(2,1)S(1)}, u32[]{:S(2)}, u32[]{:S(2)}) %collective-permute-start.49) | collective-permute-done | bytes 262176 | tf_op jit(solution)/shard_map/ppermute | solution.py:848
  (305 shorter events, 154.4 us)
Async XLA Ops:
  7.2 98.7 %all-gather.2.cloned.1.call-start = ((), (), s32[]{:S(2)}) async-start(), calls=%async_computation.1 | async-start | bytes 1310720 | tf_op jit(solution)/shard_map/all_gather | solution.py:885
  16.9 16.5 %collective-permute-start.1 = (bf16[32,3328]{1,0:T(8,128)(2,1)S(1)}, bf16[32,3328]{1,0:T(8,128)(2,1)S(1)}, u32[]{:S(2)}, u32[]{:S(2)}) collective-permute-start(bf16[32,3328]{1,0:T(8,128)(2,1)S(1)} %fusion.1.refs_0_), channel_id=1, source_target_pairs={{0,2},{1,3},{2,0},{3,1},{4,6},{5,7},{6,4},{7,5},{8,10},{9,11},{10,... | collective-permute-start | bytes 638984 | tf_op jit(solution)/shard_map/ppermute | solution.py:848
  34.1 20.8 %collective-permute-start.3 = (bf16[128,3328]{1,0:T(8,128)(2,1)S(1)}, bf16[128,3328]{1,0:T(8,128)(2,1)S(1)}, u32[]{:S(2)}, u32[]{:S(2)}) collective-permute-start(bf16[128,3328]{1,0:T(8,128)(2,1)S(1)} %shard_map.254.own), channel_id=1, source_target_pairs={{0,8},{4,12},{8,0},{12,4},{16,24},{20,28},{24,16},{28,20},{1,9},{5... | collective-permute-start | bytes 2555912 | tf_op jit(solution)/shard_map/ppermute | solution.py:845
  35.6 20.5 %collective-permute-start.4 = (bf16[128,3328]{1,0:T(8,128)(2,1)S(1)}, bf16[128,3328]{1,0:T(8,128)(2,1)S(1)}, u32[]{:S(2)}, u32[]{:S(2)}) collective-permute-start(bf16[128,3328]{1,0:T(8,128)(2,1)S(1)} %shard_map.254.own), channel_id=1, source_target_pairs={{0,16},{4,20},{8,24},{12,28},{16,0},{20,4},{24,8},{28,12},{1,17},{... | collective-permute-start | bytes 2555912 | tf_op jit(solution)/shard_map/ppermute | solution.py:845
  38.4 21.3 %collective-permute-start.7 = (bf16[32,5120]{1,0:T(8,128)(2,1)}, bf16[32,5120]{1,0:T(8,128)(2,1)}, u32[]{:S(2)}, u32[]{:S(2)}) collective-permute-start(bf16[32,5120]{1,0:T(8,128)(2,1)} %pad_maximum_fusion.1.refs_0_), channel_id=1, source_target_pairs={{0,1},{1,2},{2,3},{3,0},{4,5},{5,6},{6,7},{7,4},{8,9},{9,10},{10,1... | collective-permute-start | bytes 983048 | tf_op jit(solution)/shard_map/ppermute | solution.py:848
  43.4 21.8 %collective-permute-start.8 = (bf16[32,5120]{1,0:T(8,128)(2,1)}, bf16[32,5120]{1,0:T(8,128)(2,1)}, u32[]{:S(2)}, u32[]{:S(2)}) collective-permute-start(bf16[32,5120]{1,0:T(8,128)(2,1)} %pad_maximum_fusion.1.refs_0_), channel_id=1, source_target_pairs={{0,2},{1,3},{2,0},{3,1},{4,6},{5,7},{6,4},{7,5},{8,10},{9,11},{10,... | collective-permute-start | bytes 983048 | tf_op jit(solution)/shard_map/ppermute | solution.py:848
  45.0 20.2 %collective-permute-start.9 = (bf16[32,5120]{1,0:T(8,128)(2,1)}, bf16[32,5120]{1,0:T(8,128)(2,1)}, u32[]{:S(2)}, u32[]{:S(2)}) collective-permute-start(bf16[32,5120]{1,0:T(8,128)(2,1)} %pad_maximum_fusion.1.refs_0_), channel_id=1, source_target_pairs={{0,3},{1,0},{2,1},{3,2},{4,7},{5,4},{6,5},{7,6},{8,11},{9,8},{10,9... | collective-permute-start | bytes 983048 | tf_op jit(solution)/shard_map/ppermute | solution.py:848
  74.2 260.8 %reduce-scatter.2.cloned.1.call-start = ((), (), s32[]{:S(2)}) async-start(), calls=%async_computation.2 | async-start | bytes 1310720 | tf_op jit(solution)/shard_map/reduce_scatter | solution.py:696
  78.1 31.6 %collective-permute-start.11 = (bf16[128,5120]{1,0:T(8,128)(2,1)}, bf16[128,5120]{1,0:T(8,128)(2,1)}, u32[]{:S(2)}, u32[]{:S(2)}) collective-permute-start(bf16[128,5120]{1,0:T(8,128)(2,1)} %shard_map.256.own), channel_id=1, source_target_pairs={{0,8},{4,12},{8,0},{12,4},{16,24},{20,28},{24,16},{28,20},{1,9},{5... | collective-permute-start | bytes 3932168 | tf_op jit(solution)/shard_map/ppermute | solution.py:845
  78.8 31.2 %collective-permute-start.12 = (bf16[128,5120]{1,0:T(8,128)(2,1)}, bf16[128,5120]{1,0:T(8,128)(2,1)}, u32[]{:S(2)}, u32[]{:S(2)}) collective-permute-start(bf16[128,5120]{1,0:T(8,128)(2,1)} %shard_map.256.own), channel_id=1, source_target_pairs={{0,16},{4,20},{8,24},{12,28},{16,0},{20,4},{24,8},{28,12},{1,17},{... | collective-permute-start | bytes 3932168 | tf_op jit(solution)/shard_map/ppermute | solution.py:845
  113.2 16.4 %collective-permute-start.13 = (bf16[128,2560]{1,0:T(8,128)(2,1)}, bf16[128,2560]{1,0:T(8,128)(2,1)}, u32[]{:S(2)}, u32[]{:S(2)}) collective-permute-start(bf16[128,2560]{1,0:T(8,128)(2,1)} %get-tuple-element.309), channel_id=1, source_target_pairs={{0,16},{4,20},{8,24},{12,28},{16,0},{20,4},{24,8},{28,12},{1,17},{... | collective-permute-start | bytes 1966088 | tf_op jit(solution)/shard_map/ppermute | solution.py:845
  113.7 16.1 %collective-permute-start.14 = (bf16[128,2560]{1,0:T(8,128)(2,1)}, bf16[128,2560]{1,0:T(8,128)(2,1)}, u32[]{:S(2)}, u32[]{:S(2)}) collective-permute-start(bf16[128,2560]{1,0:T(8,128)(2,1)} %get-tuple-element.310), channel_id=1, source_target_pairs={{0,8},{4,12},{8,0},{12,4},{16,24},{20,28},{24,16},{28,20},{1,9},{5... | collective-permute-start | bytes 1966088 | tf_op jit(solution)/shard_map/ppermute | solution.py:845
  133.5 28.9 %collective-permute-start.16 = (bf16[512,1024]{1,0:T(8,128)(2,1)}, bf16[512,1024]{1,0:T(8,128)(2,1)}, u32[]{:S(2)}, u32[]{:S(2)}) collective-permute-start(bf16[512,1024]{1,0:T(8,128)(2,1)} %all-gather.2.cloned.1.call-done.own), channel_id=1, source_target_pairs={{0,8},{4,12},{8,0},{12,4},{16,24},{20,28},{24,16},{28,20},{1,9},{5... | collective-permute-start | bytes 3145736 | tf_op jit(solution)/shard_map/ppermute | solution.py:845
  135.0 27.5 %collective-permute-start.17 = (bf16[512,1024]{1,0:T(8,128)(2,1)}, bf16[512,1024]{1,0:T(8,128)(2,1)}, u32[]{:S(2)}, u32[]{:S(2)}) collective-permute-start(bf16[512,1024]{1,0:T(8,128)(2,1)} %all-gather.2.cloned.1.call-done.own), channel_id=1, source_target_pairs={{0,16},{4,20},{8,24},{12,28},{16,0},{20,4},{24,8},{28,12},{1,17},{... | collective-permute-start | bytes 3145736 | tf_op jit(solution)/shard_map/ppermute | solution.py:845
  167.9 18.3 %collective-permute-start.18 = (bf16[512,512]{1,0:T(8,128)(2,1)}, bf16[512,512]{1,0:T(8,128)(2,1)}, u32[]{:S(2)}, u32[]{:S(2)}) collective-permute-start(bf16[512,512]{1,0:T(8,128)(2,1)} %get-tuple-element.346), channel_id=1, source_target_pairs={{0,16},{4,20},{8,24},{12,28},{16,0},{20,4},{24,8},{28,12},{1,17},{... | collective-permute-start | bytes 1572872 | tf_op jit(solution)/shard_map/ppermute | solution.py:845
  169.4 16.7 %collective-permute-start.19 = (bf16[512,512]{1,0:T(8,128)(2,1)}, bf16[512,512]{1,0:T(8,128)(2,1)}, u32[]{:S(2)}, u32[]{:S(2)}) collective-permute-start(bf16[512,512]{1,0:T(8,128)(2,1)} %get-tuple-element.347), channel_id=1, source_target_pairs={{0,8},{4,12},{8,0},{12,4},{16,24},{20,28},{24,16},{28,20},{1,9},{5... | collective-permute-start | bytes 1572872 | tf_op jit(solution)/shard_map/ppermute | solution.py:845
  193.0 45.7 %collective-permute-start.23 = (bf16[640,1024]{1,0:T(8,128)(2,1)}, bf16[640,1024]{1,0:T(8,128)(2,1)}, u32[]{:S(2)}, u32[]{:S(2)}) collective-permute-start(bf16[640,1024]{1,0:T(8,128)(2,1)} %get-tuple-element.361.high_ref), channel_id=1, source_target_pairs={{0,4},{4,0},{8,12},{12,8},{16,20},{20,16},{24,28},{28,24},{1,5},{5... | collective-permute-start | bytes 3932168 | tf_op jit(solution)/shard_map/ppermute | solution.py:845
  193.5 25.5 %collective-permute-start.24 = (bf16[1024,512]{1,0:T(8,128)(2,1)}, bf16[1024,512]{1,0:T(8,128)(2,1)}, u32[]{:S(2)}, u32[]{:S(2)}) collective-permute-start(bf16[1024,512]{1,0:T(8,128)(2,1)} %get-tuple-element.372), channel_id=1, source_target_pairs={{0,16},{4,20},{8,24},{12,28},{16,0},{20,4},{24,8},{28,12},{1,17},{... | collective-permute-start | bytes 3145736 | tf_op jit(solution)/shard_map/ppermute | solution.py:845
  195.0 25.2 %collective-permute-start.25 = (bf16[1024,512]{1,0:T(8,128)(2,1)}, bf16[1024,512]{1,0:T(8,128)(2,1)}, u32[]{:S(2)}, u32[]{:S(2)}) collective-permute-start(bf16[1024,512]{1,0:T(8,128)(2,1)} %get-tuple-element.374), channel_id=1, source_target_pairs={{0,8},{4,12},{8,0},{12,4},{16,24},{20,28},{24,16},{28,20},{1,9},{5... | collective-permute-start | bytes 3145736 | tf_op jit(solution)/shard_map/ppermute | solution.py:845
  223.7 30.1 %collective-permute-start.27 = (bf16[512,512]{1,0:T(8,128)(2,1)}, bf16[512,512]{1,0:T(8,128)(2,1)}, u32[]{:S(2)}, u32[]{:S(2)}) collective-permute-start(bf16[512,512]{1,0:T(8,128)(2,1)} %get-tuple-element.396), channel_id=1, source_target_pairs={{0,8},{4,12},{8,0},{12,4},{16,24},{20,28},{24,16},{28,20},{1,9},{5... | collective-permute-start | bytes 1572872 | tf_op jit(solution)/shard_map/ppermute | solution.py:845
  225.2 28.6 %collective-permute-start.28 = (bf16[512,512]{1,0:T(8,128)(2,1)}, bf16[512,512]{1,0:T(8,128)(2,1)}, u32[]{:S(2)}, u32[]{:S(2)}) collective-permute-start(bf16[512,512]{1,0:T(8,128)(2,1)} %get-tuple-element.398), channel_id=1, source_target_pairs={{0,16},{4,20},{8,24},{12,28},{16,0},{20,4},{24,8},{28,12},{1,17},{... | collective-permute-start | bytes 1572872 | tf_op jit(solution)/shard_map/ppermute | solution.py:845
  256.8 34.7 %collective-permute-start.29 = (bf16[256,2048]{1,0:T(8,128)(2,1)}, bf16[256,2048]{1,0:T(8,128)(2,1)}, u32[]{:S(2)}, u32[]{:S(2)}) collective-permute-start(bf16[256,2048]{1,0:T(8,128)(2,1)} %get-tuple-element.403), channel_id=1, source_target_pairs={{0,16},{4,20},{8,24},{12,28},{16,0},{20,4},{24,8},{28,12},{1,17},{... | collective-permute-start | bytes 3145736 | tf_op jit(solution)/shard_map/ppermute | solution.py:845
  258.4 33.1 %collective-permute-start.30 = (bf16[256,2048]{1,0:T(8,128)(2,1)}, bf16[256,2048]{1,0:T(8,128)(2,1)}, u32[]{:S(2)}, u32[]{:S(2)}) collective-permute-start(bf16[256,2048]{1,0:T(8,128)(2,1)} %get-tuple-element.405), channel_id=1, source_target_pairs={{0,8},{4,12},{8,0},{12,4},{16,24},{20,28},{24,16},{28,20},{1,9},{5... | collective-permute-start | bytes 3145736 | tf_op jit(solution)/shard_map/ppermute | solution.py:845
  295.6 41.2 %collective-permute-start.31 = (bf16[128,2048]{1,0:T(8,128)(2,1)}, bf16[128,2048]{1,0:T(8,128)(2,1)}, u32[]{:S(2)}, u32[]{:S(2)}) collective-permute-start(bf16[128,2048]{1,0:T(8,128)(2,1)} %get-tuple-element.421), channel_id=1, source_target_pairs={{0,8},{4,12},{8,0},{12,4},{16,24},{20,28},{24,16},{28,20},{1,9},{5... | collective-permute-start | bytes 1572872 | tf_op jit(solution)/shard_map/ppermute | solution.py:845
  297.0 39.7 %collective-permute-start.32 = (bf16[128,2048]{1,0:T(8,128)(2,1)}, bf16[128,2048]{1,0:T(8,128)(2,1)}, u32[]{:S(2)}, u32[]{:S(2)}) collective-permute-start(bf16[128,2048]{1,0:T(8,128)(2,1)} %get-tuple-element.423), channel_id=1, source_target_pairs={{0,16},{4,20},{8,24},{12,28},{16,0},{20,4},{24,8},{28,12},{1,17},{... | collective-permute-start | bytes 1572872 | tf_op jit(solution)/shard_map/ppermute | solution.py:845
  297.5 17.5 %collective-permute-start.33 = (bf16[4,640,1024]{2,1,0:T(8,128)(2,1)}, bf16[4,640,1024]{2,1,0:T(8,128)(2,1)}, u32[]{:S(2)}, u32[]{:S(2)}) collective-permute-start(bf16[4,640,1024]{2,1,0:T(8,128)(2,1)} %copy-done.15), channel_id=1, source_target_pairs={{0,4},{4,0},{8,12},{12,8},{16,20},{20,16},{24,28},{28,24},{1,5},{5... | collective-permute-start | bytes 15728648 | tf_op jit(solution)/shard_map/ppermute | solution.py:845
  340.1 20.4 %collective-permute-start.34 = (f32[4,4,384]{2,1,0:T(4,128)}, f32[4,4,384]{2,1,0:T(4,128)}, u32[]{:S(2)}, u32[]{:S(2)}) collective-permute-start(f32[4,4,384]{2,1,0:T(4,128)} %select_bitcast_fusion), channel_id=1, source_target_pairs={{0,4},{4,0},{8,12},{12,8},{16,20},{20,16},{24,28},{28,24},{1,5},{5... | collective-permute-start | bytes 73736 | tf_op jit(solution)/shard_map/ppermute | solution.py:845
  340.5 25.4 %collective-permute-start.35 = (bf16[256,2048]{1,0:T(8,128)(2,1)}, bf16[256,2048]{1,0:T(8,128)(2,1)}, u32[]{:S(2)}, u32[]{:S(2)}) collective-permute-start(bf16[256,2048]{1,0:T(8,128)(2,1)} %get-tuple-element.472), channel_id=1, source_target_pairs={{0,16},{4,20},{8,24},{12,28},{16,0},{20,4},{24,8},{28,12},{1,17},{... | collective-permute-start | bytes 3145736 | tf_op jit(solution)/shard_map/ppermute | solution.py:845
  342.2 25.1 %collective-permute-start.36 = (bf16[256,2048]{1,0:T(8,128)(2,1)}, bf16[256,2048]{1,0:T(8,128)(2,1)}, u32[]{:S(2)}, u32[]{:S(2)}) collective-permute-start(bf16[256,2048]{1,0:T(8,128)(2,1)} %get-tuple-element.474), channel_id=1, source_target_pairs={{0,8},{4,12},{8,0},{12,4},{16,24},{20,28},{24,16},{28,20},{1,9},{5... | collective-permute-start | bytes 3145736 | tf_op jit(solution)/shard_map/ppermute | solution.py:845
  342.6 29.1 %collective-permute-start.42 = (bf16[32,4096]{1,0:T(8,128)(2,1)}, bf16[32,4096]{1,0:T(8,128)(2,1)}, u32[]{:S(2)}, u32[]{:S(2)}) collective-permute-start(bf16[32,4096]{1,0:T(8,128)(2,1)} %get-tuple-element.489), channel_id=1, source_target_pairs={{0,1},{1,2},{2,3},{3,0},{4,5},{5,6},{6,7},{7,4},{8,9},{9,10},{10,1... | collective-permute-start | bytes 786440 | tf_op jit(solution)/shard_map/ppermute | solution.py:848
  348.5 24.9 %collective-permute-start.43 = (bf16[32,4096]{1,0:T(8,128)(2,1)}, bf16[32,4096]{1,0:T(8,128)(2,1)}, u32[]{:S(2)}, u32[]{:S(2)}) collective-permute-start(bf16[32,4096]{1,0:T(8,128)(2,1)} %get-tuple-element.490), channel_id=1, source_target_pairs={{0,2},{1,3},{2,0},{3,1},{4,6},{5,7},{6,4},{7,5},{8,10},{9,11},{10,... | collective-permute-start | bytes 786440 | tf_op jit(solution)/shard_map/ppermute | solution.py:848
  397.6 15.1 %collective-permute-start.49 = (bf16[32,4096]{1,0:T(8,128)(2,1)S(1)}, bf16[32,4096]{1,0:T(8,128)(2,1)S(1)}, u32[]{:S(2)}, u32[]{:S(2)}) collective-permute-start(bf16[32,4096]{1,0:T(8,128)(2,1)S(1)} %get-tuple-element.506), channel_id=1, source_target_pairs={{0,2},{1,3},{2,0},{3,1},{4,6},{5,7},{6,4},{7,5},{8,10},{9,11},{10,... | collective-permute-start | bytes 786440 | tf_op jit(solution)/shard_map/ppermute | solution.py:848
  (96 other events, 868.0 us)
Sparse Core Ops, SparseCore 0:
  74.4 31.5 all-gather.1
  297.6 31.6 reduce-scatter.1

commit v3 on v2

--- a/solution.py
+++ b/solution.py
@@ -39,7 +39,7 @@
 
 
 def attention_backward_kernel(
-    seqs, length, keep_ref, q_ref, k_ref, v_ref, do_ref, above_ref, dp_ref, sq_ref, sv_ref
+    seqs, length, keep_ref, q_ref, k_ref, v_ref, do_ref, dp_ref, sq_ref, sv_ref
 ):
     scale = 1.0 / math.sqrt(HD)
     sum_q = jnp.zeros((1, 128), f32)
@@ -70,7 +70,6 @@
         dp_ref[2, rows, :] = dv
         sum_q += jnp.sum(dq.astype(f32), 0, keepdims=True)
         sum_v += jnp.sum(dv.astype(f32), 0, keepdims=True)
-    dp_ref[3] = above_ref[...]
     sq_ref[...] = sum_q
     sv_ref[...] = sum_v
 
@@ -95,7 +94,7 @@
     )(keep, project, project, project)
 
 
-def attention_backward(keep, project, grad_mixed, above):
+def attention_backward(keep, project, grad_mixed):
     seqs, length = keep.shape[:2]
     rows, width = project.shape[0], project.shape[1] // 3
     steps = width // 128
@@ -107,12 +106,12 @@
         grid=(steps,),
         in_specs=[pl.BlockSpec((seqs, length, 1), lambda i: (0, 0, 0))]
         + [pl.BlockSpec((rows, 128), lambda i, at=at: (0, i + at * steps)) for at in range(3)]
-        + [block] * 2,
-        out_specs=[pl.BlockSpec((4, rows, 128), lambda i: (0, 0, i)), vector, vector],
-        out_shape=[jax.ShapeDtypeStruct((4, rows, width), bf16), sums, sums],
+        + [block],
+        out_specs=[pl.BlockSpec((3, rows, 128), lambda i: (0, 0, i)), vector, vector],
+        out_shape=[pltpu.HBM((3, rows, width), bf16), sums, sums],
         compiler_params=pltpu.CompilerParams(vmem_limit_bytes=16 << 20),
         cost_estimate=pl.CostEstimate(flops=int(22 * COST), bytes_accessed=1, transcendentals=0),
-    )(keep, project, project, project, grad_mixed, above)
+    )(keep, project, project, project, grad_mixed)
 
 
 def norm_forward(values, norm_gain, norm_bias):
@@ -178,7 +177,7 @@
     grad_middle = grad_out + norm_backward(grad_act_two, plain_two, inverse_two, g2)
     grad_branch = grad_middle.astype(bf16)
     grad_mixed = dot(grad_branch, out_mat, NT).astype(bf16)
-    grad_parts, sum_q, sum_v = attention_backward(keep_column, project, grad_mixed, grad_branch)
+    grad_parts, sum_q, sum_v = attention_backward(keep_column, project, grad_mixed)
     grad_project = jnp.concatenate([grad_parts[i] for i in range(3)], 1)
     grad_act_one = dot(grad_project, qkv_mat, NT)
     input_grad = grad_middle + norm_backward(grad_act_one, plain_one, inverse_one, g1)
@@ -231,7 +230,7 @@
     return jnp.stack(true + place + ahead).astype(jnp.int32)
 
 
-def call(kernel, grid, where, ins, outs, scratch=(), micros=3):
+def call(kernel, grid, where, ins, outs, scratch=(), micros=3, sent=()):
     held = 6 << 20
     specs = []
     for array, block, index in ins:
@@ -252,7 +251,10 @@
             out_specs=[pl.BlockSpec(block, index) for _, _, block, index in outs],
             scratch_shapes=list(scratch),
         ),
-        out_shape=[jax.ShapeDtypeStruct(shape, dtype) for shape, dtype, _, _ in outs],
+        out_shape=[
+            pltpu.HBM(shape, dtype) if at in sent else jax.ShapeDtypeStruct(shape, dtype)
+            for at, (shape, dtype, _, _) in enumerate(outs)
+        ],
         compiler_params=pltpu.CompilerParams(vmem_limit_bytes=held),
         cost_estimate=pl.CostEstimate(flops=int(micros * COST), bytes_accessed=1, transcendentals=0),
     )(where, *[array for array, _, _ in ins])
@@ -439,8 +441,11 @@
     return sum(dot(grad[i], mat[:, i * cols : (i + 1) * cols], NT) for i in range(3))
 
 
-def back_kernel(low, where, grad_ref, mat_low, mat_high, values_ref, above_ref, gain_ref, out_ref, *rest):
-    (*low_refs, gain_sum, bias_sum, total) = rest
+def back_kernel(low, where, grad_ref, mat_low, mat_high, values_ref, above_ref, gain_ref, *rest):
+    if low:
+        out_ref, low_ref, low_sum, gain_sum, bias_sum, total = rest
+    else:
+        *vectors, out_ref, packed, total = rest
     step = pl.program_id(0)
 
     def put(mat):
@@ -476,21 +481,34 @@
             sums[1] += jnp.sum(grad, 0, keepdims=True)
             if low:
                 rounded = result.astype(bf16)
-                low_refs[0][rows, :] = rounded
+                low_ref[rows, :] = rounded
                 sums[2] += jnp.sum(rounded.astype(f32), 0, keepdims=True)
-        gain_sum[...] = sums[0]
-        bias_sum[...] = sums[1]
         if low:
-            low_refs[1][...] = sums[2]
-
-
-def back(where, grad, mats, values, above, gain, low):
+            gain_sum[...] = sums[0]
+            bias_sum[...] = sums[1]
+            low_sum[...] = sums[2]
+        else:
+            owners = packed.shape[0]
+            at = 0
+            for vector in (*sums[:2], *[ref[...] for ref in vectors]):
+                share = vector.shape[1] // owners
+                for owner in range(owners):
+                    packed[owner : owner + 1, at : at + share] = vector[
+                        :, owner * share : (owner + 1) * share
+                    ]
+                at += share
+
+
+def back(where, grad, mats, values, above, gain, vectors=(), owners=0):
+    low = not vectors
     rows, width = values.shape
     columns = grad.shape[1] if grad.ndim == 2 else 3 * width
     outs = [whole_out((rows, width), f32)]
     if low:
-        outs += [whole_out((rows, width), bf16), whole_out((1, width), f32)]
-    outs += [whole_out((1, width), f32)] * 2
+        outs += [whole_out((rows, width), bf16)] + [whole_out((1, width), f32)] * 3
+    else:
+        columns_packed = (2 * width + sum(v.shape[1] for v in vectors)) // owners
+        outs += [whole_out((owners, columns_packed), f32)]
     return call(
         functools.partial(back_kernel, low),
         (4,),
@@ -502,6 +520,7 @@
             whole(values),
             whole(above),
             whole(gain),
+            *[whole(v) for v in vectors],
         ],
         outs,
         [pltpu.VMEM((rows, width), f32)], micros=13)
@@ -618,6 +637,7 @@
         self.rights = [right for pair in rights for right in pair]
         self.tile, self.counts, self.flat = tile, counts, flat
         self.sent = 0
+        self.shares = []
 
     def product(self, *arrays):
         n = len(self.counts)
@@ -649,6 +669,7 @@
             [(shape, bf16, block, near)] * 2 + [(shape, bf16, block, far)] * 2,
             [pltpu.VMEM((count, depth), bf16)] * (2 * n),
             micros=12,
+            sent=(0, 1, 2, 3),
         )
 
     def add(self, *pieces):
@@ -691,19 +712,27 @@
         self.kept = keep_a, keep_b
         self.ready = send_a, send_b
 
-    def send(self):
-        if self.sent == 2 and self.flat:
+    def send(self, shares=()):
+        if self.sent < 2:
+            ready = self.order.tie(*self.ready)
+            bits = (XBIT, YBIT) if self.sent else (YBIT, XBIT)
+            self.arrived = self.swap(ready[0], bits[0]), self.swap(ready[1], bits[1])
+            self.sent += 1
+        elif self.flat:
             self.share = lax.psum_scatter(
                 self.order.tie(self.own)[0], "fsdp", scatter_dimension=0, tiled=True
             )
-            return
-        ready = self.order.tie(*self.ready)
-        if self.sent == 2:
-            self.shares = [self.along(piece, by) for by, piece in enumerate(ready, 1)]
         else:
-            bits = (XBIT, YBIT) if self.sent else (YBIT, XBIT)
-            self.arrived = self.swap(ready[0], bits[0]), self.swap(ready[1], bits[1])
-        self.sent += 1
+            for by, piece in zip(shares, self.order.tie(*[self.ready[by - 1] for by in shares])):
+                self.shares.append(self.along(piece, by))
+
+    def meet(self):
+        if self.flat:
+            (self.share,) = self.order.tie(self.share)
+            self.order.last = (self.share,)
+        else:
+            self.shares = list(self.order.tie(*self.shares))
+            self.order.last = (self.shares[0],)
 
     def total(self):
         if self.flat:
@@ -727,73 +756,61 @@
 
 
 def assemble_kernel(where, *refs):
+    pieces, targets = [], []
+    for ref in refs:
+        (pieces if ref.shape[0] == refs[0].shape[0] else targets).append(ref)
+    count = pieces[0].shape[0]
+    columns = targets[0].shape[1]
+    for at, piece in enumerate(pieces):
+        rows = pl.ds(pl.multiple_of(where[at] * count, count), count)
+        for side, target in enumerate(targets):
+            target[rows, :] = piece[:, side * columns : (side + 1) * columns]
+
+
+def assemble(count, places, *pieces):
+    rows, columns = pieces[0].shape
+    out = whole_out((rows * len(pieces), columns // count), bf16)
+    return call(assemble_kernel, (1,), places, [whole(p) for p in pieces], [out] * count)
+
+
+def join_kernel(where, *refs):
+    out = refs[-1]
     count = refs[0].shape[0]
-    for at, piece in enumerate(refs[:-1]):
-        rows = pl.ds(pl.multiple_of(where[at] * count, count), count)
-        refs[-1][rows, :] = piece[...]
-
-
-def assemble(places, *pieces):
-    rows, columns = pieces[0].shape
-    out = whole_out((rows * len(pieces), columns), bf16)
-    return call(assemble_kernel, (1,), places, [whole(p) for p in pieces], [out])[0]
-
-
-def join_kernel(where, own, near, far, left, right, out):
-    count = own.shape[0]
-    for at, piece in enumerate((own, near, far)):
-        out[at * count : (at + 1) * count, :] = piece[...]
-    for side, piece in enumerate((left, right)):
+    for side in range(2):
 
         @pl.when(pl.program_id(0) == side)
-        def _(piece=piece):
-            out[3 * count :, :] = piece[...]
-
-
-def join(where, own, near, far, left, right):
-    rows, columns = own.shape
-    block = (rows, columns // 2)
+        def _(side=side):
+            for at, piece in enumerate(refs[4 * side : 4 * side + 4]):
+                out[at * count : (at + 1) * count, :] = piece[...]
+
+
+def join(where, *pieces):
+    rows, columns = pieces[3].shape
+    ins = [first_columns(p, columns, at // 4 if p.shape[1] > columns else 0) for at, p in enumerate(pieces)]
     return call(
         join_kernel,
         (2,),
         where,
-        [(v, block, column) for v in (own, near, far)] + [whole(left), whole(right)],
-        [((4 * rows, columns), bf16, (4 * rows, columns // 2), column)], micros=4)[0]
-
-
-def turn_kernel(where, near, far, left, right):
+        ins,
+        [((4 * rows, 2 * columns), bf16, (4 * rows, columns), column)],
+        micros=4,
+    )[0]
+
+
+def split_kernel(where, near, far, left, right):
     left[...] = near[...]
     right[...] = far[...]
 
 
-def turn(where, near, far):
-    rows, columns = near.shape
-    half = (rows, columns // 2)
+def split(where, near, far):
+    rows, columns = near.shape[0], near.shape[1] // 2
     return call(
-        turn_kernel,
+        split_kernel,
         (1,),
         where,
-        [(near, half, lambda *_: (0, 0)), (far, half, lambda *_: (0, 1))],
-        [whole_out(half, bf16)] * 2,
-    )
-
-
-def pack_kernel(where, *refs):
-    out = refs[-1]
-    owners = out.shape[0]
-    first = 0
-    for vector in refs[:-1]:
-        share = vector.shape[1] // owners
-        for owner in range(owners):
-            out[owner : owner + 1, first : first + share] = vector[:, owner * share : (owner + 1) * share]
-        first += share
-
-
-def pack(where, vectors, owners):
-    columns = sum(v.shape[1] for v in vectors) // owners
-    return call(
-        pack_kernel, (1,), where, [whole(v) for v in vectors], [whole_out((owners, columns), f32)]
-    )[0]
+        [first_columns(near, columns, 0), first_columns(far, columns, 1)],
+        [whole_out((rows, columns), bf16)] * 2,
+    )
 
 
 def unpack_kernel(where, low, high, *refs):
@@ -848,21 +865,31 @@
         return lax.ppermute(value, "fsdp", [(i, (i + by) % fsdp_size) for i in range(fsdp_size)])
 
     class Gather:
-        def start(self, block):
-            self.own = order.tie(block)[0]
-            self.near, self.far = swap(self.own, XBIT), swap(self.own, YBIT)
+        def start(self, left, right):
+            left, right = self.own = order.tie(left, right)
+            self.near = swap(left, XBIT), swap(right, XBIT)
+            self.far = swap(left, YBIT), swap(right, YBIT)
 
         def turn(self, *others):
-            self.ready = order(lambda near, far, *_: turn(where, near, far), self.near, self.far, *others)
-
-        def turned(self):
-            left, right = order.tie(*self.ready)
-            self.left, self.right = swap(left, YBIT), swap(right, XBIT)
-
-        def join(self):
-            self.low = order(
-                functools.partial(join, where), self.own, self.near, self.far, self.left, self.right
-            )
+            *pieces, = order.tie(*self.near, *self.far, *others)
+            self.near, self.far = tuple(pieces[:2]), tuple(pieces[2:4])
+            left, right = self.near[0], self.far[1]
+            order.last = (left,)
+            self.last = swap(left, YBIT), swap(right, XBIT)
+
+        def start_whole(self, block):
+            block = order.tie(block)[0]
+            self.own = block
+            self.near, self.far = swap(block, XBIT), swap(block, YBIT)
+
+        def turn_whole(self):
+            left, right = order(functools.partial(split, where), self.near, self.far)
+            self.last = swap(left, YBIT), swap(right, XBIT)
+
+        def join(self, *others):
+            sides = [v if isinstance(v, tuple) else (v, v) for v in (self.own, self.near, self.far)]
+            pieces = [p for side in zip(*sides, self.last) for p in side]
+            self.low = order(lambda *p: join(where, *p[:8]), *pieces, *others)
 
         def joined(self):
             low = order.tie(self.low)[0]
@@ -876,7 +903,7 @@
     sizes = [v.shape[0] * device_count for v in vectors]
     cuts = [sum(v.shape[0] for v in vectors[:i]) for i in range(1, len(vectors))]
     share = qkv_weight.shape[0]
-    beside = jnp.concatenate(vectors).reshape(-1, share).T
+    beside = lax.optimization_barrier(jnp.concatenate(vectors)).reshape(-1, share).T
     beside = jnp.pad(beside, ((0, 0), (0, 256 - beside.shape[1])))
     qkv_low = jnp.concatenate([qkv_weight, beside], 1).astype(bf16)
     behind = jnp.stack([(line - by) % fsdp_size for by in range(fsdp_size)]).astype(jnp.int32)
@@ -894,15 +921,13 @@
     down_bias_grad = jnp.sum(grad_feed.astype(f32), 0)
 
     qkv, up, down = Gather(), Gather(), Gather()
-    block = order(functools.partial(assemble, behind), *qkv_pieces)
-    qkv.start(block)
+    qkv.start_whole(order(functools.partial(assemble, 1, behind), *qkv_pieces)[0])
     up_pieces = around(order.tie(up_low)[0])
-    qkv.turn()
-    qkv.turned()
-    up_block = order(functools.partial(assemble, behind), *up_pieces)
+    qkv.turn_whole()
+    up_halves = order(functools.partial(assemble, 2, behind), *up_pieces)
     qkv.join()
     qkv.joined()
-    up.start(up_block)
+    up.start(*up_halves)
     g1, b1, qv_bias, out_bias, g2, b2, up_bias, down_bias = order(
         lambda *m: unpack(where, m, sizes), *qkv.mats
     )
@@ -913,12 +938,12 @@
     )
     mixed_left = order(lambda p: attention_forward(keep_column, p, 0), projected)
     up.turn(down_block)
-    up.turned()
     one_other = swap(order.tie(one_pack)[0], CORE)
     mixed_right = order(lambda p: attention_forward(keep_column, p, 1), projected)
-    up.join()
+    down_halves = order(lambda b: (b[:, :half], b[:, half:]), down_block)
+    up.join(one_other)
     up.joined()
-    down.start(down_block)
+    down.start(*down_halves)
     mixed = jnp.concatenate([mixed_left, mixed_right], 1)
     mix_low, middle, two_low, two_pack = order(
         lambda m, o, *mats: branch_norm(where, m, inputs, mats, o, g2, b2, length),
@@ -931,7 +956,6 @@
         lambda lo, hi, s, *m: expand(where, 0, lo, hi, m, s), two_low, two_pack, up_bias, *up.mats
     )
     down.turn()
-    down.turned()
     hidden_other = swap(order.tie(hidden_high)[0], CORE)
     two_other = swap(order.tie(two_pack)[0], CORE)
     down_sum = Sum(
@@ -951,51 +975,49 @@
     down_sum.send()
     pre_other = swap(order.tie(grad_pre)[0], CORE)
     grad_middle, grad_branch, out_bias_grad, gain_two_grad, bias_two_grad = order(
-        lambda g, mid, above, *m: back(where, g, m, mid, above, g2, True),
+        lambda g, mid, above, *m: back(where, g, m, mid, above, g2),
         grad_pre, middle, grad_feed, *up.mats,
     )
+    branch_other = swap(order.tie(grad_branch)[0], CORE)
+    down_sum.work()
     up_sum = Sum(
         swap, along, order, where,
-        [((two_low, 0), (two_other, 1))], [((grad_pre, 0), (pre_other, 0))],
-        512, [grad_pre.shape[1] // 512],
+        [((two_low, 0), (two_other, 1)), ((mix_low, 0), (two_other, 0))],
+        [((grad_pre, 0), (pre_other, 0)), ((grad_branch, 0), (branch_other, 0))],
+        512, [grad_pre.shape[1] // 512, width // 512],
     )
     up_sum.work()
-    down_sum.work()
     up_sum.send()
     grad_mixed = order(lambda g, *m: mixed_grad(where, g, m), grad_branch, *up.mats)
     grad_projected, sum_q, sum_v = order(
-        lambda p, g, b: attention_backward(keep_column, p, g, b), projected, grad_mixed, grad_branch
+        lambda p, g: attention_backward(keep_column, p, g), projected, grad_mixed
     )
     up_sum.work()
     up_sum.send()
     projected_other = swap(order.tie(grad_projected)[0], CORE)
     down_sum.send()
-    input_grad, gain_one_grad, bias_one_grad = order(
-        lambda g, x, above, *m: back(where, g, m, x, above, g1, False),
-        grad_projected, inputs, grad_middle, *qkv.mats,
-    )
-    grads = (
-        gain_one_grad,
-        bias_one_grad,
+    sums = [
         jnp.concatenate([sum_q, sum_v], 1),
         out_bias_grad,
         gain_two_grad,
         bias_two_grad,
         up_bias_grad,
-        down_bias_grad,
-    )
-    shares = order(lambda *g: pack(where, g, device_count), *[g.reshape(1, -1) for g in grads])
-    mid_sum = Sum(
+        down_bias_grad.reshape(1, -1),
+    ]
+    input_grad, shares = order(
+        lambda g, x, above, m0, m1, *v: back(where, g, (m0, m1), x, above, g1, v, device_count),
+        grad_projected, inputs, grad_middle, *qkv.mats, *sums,
+    )
+    qkv_sum = Sum(
         swap, along, order, where,
-        [((one_low, 0), (one_other, 0)), ((mix_low, 0), (two_other, 0))],
-        [((grad_projected, 0), (projected_other, 0)), ((grad_projected, 6), (projected_other, 6))],
-        512, [3 * width // 512, width // 512],
-    )
-    mid_sum.work()
-    down_grad = down_sum.total()
+        [((one_low, 0), (one_other, 0))], [((grad_projected, 0), (projected_other, 0))],
+        512, [3 * width // 512],
+    )
+    qkv_sum.work()
     up_sum.work()
-    mid_sum.send()
-    up_sum.send()
+    down_sum.meet()
+    qkv_sum.send()
+    up_sum.send((1, 3))
     upper = me % 2 == 1
     shares = shares.reshape(4, 2, fsdp_size, -1)
     low, high = shares[:, 0], shares[:, 1]
@@ -1005,26 +1027,30 @@
         lambda lo, hi, mid, s, *m: feed(where, lo, hi, m, mid, s, keep_rows),
         hidden_low, hidden_high, middle, down_bias, *down.mats,
     )
-    mid_sum.work()
-    mid_sum.send()
-    shares = order.tie(shares + core_share)[0]
+    up_sum.meet()
+    qkv_sum.work()
+    qkv_sum.send()
+    up_sum.send((2,))
+    up_sum.meet()
+    shares = shares + core_share
+    qkv_sum.work()
+    qkv_sum.send((1, 2, 3))
+    qkv_sum.shares[0], shares = order.tie(qkv_sum.shares[0], shares)
 
     def part_of(bits):
         return lax.dynamic_index_in_dim(shares, (me ^ bits) // 2, 0, keepdims=False)
 
     plane_shares = [swap(part_of(bits), bits) for bits in (XBIT, YBIT, XBIT + YBIT)]
-    up_grad = up_sum.total()
-    mid_sum.work()
-    mid_sum.send()
-    shares = order.tie(sum(plane_shares, part_of(0)))[0]
+    down_grad, up_grad = down_sum.total(), up_sum.total()
+    up_grad, out_grad = up_grad[:, : up_weight.shape[1]], up_grad[:, up_weight.shape[1] :]
+    shares = sum(plane_shares, part_of(0))
 
     def row_of(by):
         return lax.dynamic_slice(shares, ((line + by) % fsdp_size, 0), (1, shares.shape[1]))
 
     line_shares = [along(row_of(by), by) for by in range(1, fsdp_size)]
-    mid_grad = mid_sum.total()
+    qkv_grad = qkv_sum.total()
     mine = sum(line_shares, row_of(0))
-    qkv_grad, out_grad = mid_grad[:, : 3 * width], mid_grad[:, 3 * width :]
     v = jnp.split(mine[0], cuts)
     return (
         block_out.reshape(seqs, length, width),

time: 429 us -> 400 us (0.932)
  Pallas kernels: 199 us -> 191 us
  other arithmetic: 18.5 us -> 11.2 us
  local copies, waits for them, and re-layouts: 33.8 us -> 26.5 us
    ppermute x36 -> x41, waiting for transfers between devices: 56.1 us -> 41 us  [swap(): return lax.ppermute(value, 'dp', [(i, i ^ bit) for i in range(8)])]
    ppermute x15, waiting for transfers between devices: 29 us -> 41.8 us  [along(): lax.ppermute(value, 'fsdp', [(i, (i + by) % fsdp_size) for i in range(fsd...]
    unnamed x150 -> x122, local copies, waits for them, and re-layouts: 29 us -> 19.9 us
    pallas_call x29 -> x26, Pallas kernels: 160 us -> 153 us  [call(): pl.pallas_call(kernel, grid_spec=pltpu.PrefetchScalarGridSpec(num_scalar_...]
    another operation x11 -> x3, other arithmetic: 6.31 us -> 1.06 us
    ppermute x36 -> x41, starting transfers between devices: 31.4 us -> 35.1 us  [swap(): return lax.ppermute(value, 'dp', [(i, i ^ bit) for i in range(8)])]
  transfers between devices with their start and end apart: 53 -> 58, of which waited for: 25 -> 26; matrix products, arithmetic and copies ran while one was open for 4% -> 4% of each run, Pallas kernels for 40% -> 39%
where the time goes in v3:
time: 400 us; the launch traced here: 396 us
  Pallas kernels  191 us (48%)
  waiting for transfers between devices  84.3 us (21%)
  starting transfers between devices  66.9 us (17%)
  local copies, waits for them, and re-layouts  26.5 us (7%)
  between operations  15.4 us (4%)
  other arithmetic  11.2 us (3%)
    pallas_call x26, Pallas kernels, call(): pl.pallas_call(kernel, grid_spec=pltpu.PrefetchScalarGridSpec(num_scalar_...  153 us
    ppermute x15, waiting for transfers between devices, along(): lax.ppermute(value, 'fsdp', [(i, (i + by) % fsdp_size) for i in range(fsd...  41.8 us
    ppermute x41, waiting for transfers between devices, swap(): return lax.ppermute(value, 'dp', [(i, i ^ bit) for i in range(8)])  41 us
    ppermute x41, starting transfers between devices, swap(): return lax.ppermute(value, 'dp', [(i, i ^ bit) for i in range(8)])  35.1 us
    ppermute x15, starting transfers between devices, along(): lax.ppermute(value, 'fsdp', [(i, (i + by) % fsdp_size) for i in range(fsd...  31.6 us
    pallas_call x1, Pallas kernels, attention_backward(): pl.pallas_call(functools.partial(attention_backward_kernel, seqs, length)...  21.8 us
    unnamed x122, local copies, waits for them, and re-layouts  19.9 us
    pallas_call x2, Pallas kernels, attention_forward(): pl.pallas_call(functools.partial(attention_forward_kernel, seqs, length),...  16.9 us
  transfers between devices with their start and end apart: 58, of which 26 were waited for; matrix products, arithmetic and copies ran while one was open for 4% of the time, Pallas kernels for 39%

profile of v3, /device:TPU:0, one launch (start us, length us, event | category | flops | bytes accessed | tf_op | source)
XLA Modules:
  0.0 395.7 jit_solution(11744602354505877017)
XLA Ops:
  16.4 4.2 %collective-permute-done.refs_1_ = bf16[32,3328]{1,0:T(8,128)(2,1)S(1)} collective-permute-done((bf16[32,3328]{1,0:T(8,128)(2,1)S(1)}, bf16[32,3328]{1,0:T(8,128)(2,1)S(1)}, u32[]{:S(2)}, u32[]{:S(2)}) %collective-permute-start) | collective-permute-done | bytes 213024 | tf_op jit(solution)/shard_map/ppermute | solution.py:865
  20.6 8.3 %collective-permute-done.1.refs_2_ = bf16[32,3328]{1,0:T(8,128)(2,1)S(1)} collective-permute-done((bf16[32,3328]{1,0:T(8,128)(2,1)S(1)}, bf16[32,3328]{1,0:T(8,128)(2,1)S(1)}, u32[]{:S(2)}, u32[]{:S(2)}) %collective-permute-start.1) | collective-permute-done | bytes 213024 | tf_op jit(solution)/shard_map/ppermute | solution.py:865
  33.8 5.0 %collective-permute-start.7 = (bf16[32,5120]{1,0:T(8,128)(2,1)}, bf16[32,5120]{1,0:T(8,128)(2,1)}, u32[]{:S(2)}, u32[]{:S(2)}) collective-permute-start(bf16[32,5120]{1,0:T(8,128)(2,1)} %pad_maximum_fusion.1.refs_0_), channel_id=1, source_target_pairs={{0,1},{1,2},{2,3},{3,0},{4,5},{5,6},{6,7},{7,4},{8,9},{9,10},{10,1... | collective-permute-start | bytes 983048 | tf_op jit(solution)/shard_map/ppermute | solution.py:865
  41.2 9.2 %collective-permute-done.3.near.refs_1_.refs_5_ = bf16[128,3328]{1,0:T(8,128)(2,1)S(1)} collective-permute-done((bf16[128,3328]{1,0:T(8,128)(2,1)S(1)}, bf16[128,3328]{1,0:T(8,128)(2,1)S(1)}, u32[]{:S(2)}, u32[]{:S(2)}) %collective-permute-start.3) | collective-permute-done | bytes 852000 | tf_op jit(solution)/shard_map/ppermute | solution.py:862
  55.2 5.5 %collective-permute-done.8.refs_2_ = bf16[32,5120]{1,0:T(8,128)(2,1)} collective-permute-done((bf16[32,5120]{1,0:T(8,128)(2,1)}, bf16[32,5120]{1,0:T(8,128)(2,1)}, u32[]{:S(2)}, u32[]{:S(2)}) %collective-permute-start.8) | collective-permute-done | bytes 327712 | tf_op jit(solution)/shard_map/ppermute | solution.py:865
  65.3 3.7 shard_map.257.low.mat_low
  81.6 8.0 %shard_map.260.q_ref.k_ref.v_ref = bf16[640,3072]{1,0:T(8,128)(2,1)S(1)} custom-call(s32[20]{0:T(128)S(1)} %stack.96.where, bf16[640,512]{1,0:T(8,128)(2,1)S(1)} %get-tuple-element.467.low_ref.refs_0_, bf16[640,1536]{1,0:T(8,128)(2,1)S(1)} %get-tuple-element.324.high_ref, bf16[512,3328]{1,0:T(8,128)(2,1)} %shard_map.257.low.mat_low, ...), custom_call_target="tpu_custom_call" | custom-call | flops 7999999967232 | bytes 1 | tf_op jit(solution)/shard_map/pallas_call | solution.py:245
  90.5 8.4 %shard_map.261 = bf16[640,512]{1,0:T(8,128)(2,1)S(1)} custom-call(s32[2,320,1]{2,1,0:T(8,128)S(1)} %copy.34.keep_ref, bf16[640,3072]{1,0:T(8,128)(2,1)S(1)} %shard_map.260.q_ref.k_ref.v_ref, bf16[640,3072]{1,0:T(8,128)(2,1)S(1)} %shard_map.260.q_ref.k_ref.v_ref, bf16[640,3072]{1,0:T(8,128)(2,1)S(1)} %shard_map.260.q_ref.k_ref.v_ref), custom_call_target="tpu_custom_call" | custom-call | flops 8499999801344 | bytes 1 | tf_op jit(solution)/shard_map/pallas_call | solution.py:82
  109.0 8.5 %shard_map.262 = bf16[640,512]{1,0:T(8,128)(2,1)S(1)} custom-call(s32[2,320,1]{2,1,0:T(8,128)S(1)} %copy.34.keep_ref, bf16[640,3072]{1,0:T(8,128)(2,1)S(1)} %copy-done.30, bf16[640,3072]{1,0:T(8,128)(2,1)S(1)} %copy-done.30, bf16[640,3072]{1,0:T(8,128)(2,1)S(1)} %copy-done.30), custom_call_target="tpu_custom_call" | custom-call | flops 8499999801344 | bytes 1 | tf_op jit(solution)/shard_map/pallas_call | solution.py:82
  121.6 3.8 shard_map.263.mat_low.low
  129.8 4.3 %collective-permute-done.18.mat_high.high = bf16[512,5120]{1,0:T(8,128)(2,1)S(1)} collective-permute-done((bf16[512,5120]{1,0:T(8,128)(2,1)S(1)}, bf16[512,5120]{1,0:T(8,128)(2,1)S(1)}, u32[]{:S(2)}, u32[]{:S(2)}) %collective-permute-start.18) | collective-permute-done | bytes 5242912 | tf_op jit(solution)/shard_map/ppermute | solution.py:862
  134.1 3.5 shard_map.264
  137.7 6.1 %shard_map.265 = (bf16[640,2048]{1,0:T(8,128)(2,1)S(1)}, bf16[640,2048]{1,0:T(8,128)(2,1)S(1)}) custom-call(s32[20]{0:T(128)S(1)} %copy-done.8, bf16[640,512]{1,0:T(8,128)(2,1)S(1)} %get-tuple-element.417.low_ref.refs_0_, bf16[640,1024]{1,0:T(8,128)(2,1)S(1)} %get-tuple-element.413.high_ref, bf16[512,5120]{1,0:T(8,128)(2,1)S(1)} %shard_map.263.mat_low.low, ...), custom_call_target="tpu_custom_call" | custom-call | flops 6999999774720 | bytes 1 | tf_op jit(solution)/shard_map/pallas_call | solution.py:245
  143.8 6.1 %shard_map.266 = (bf16[640,2048]{1,0:T(8,128)(2,1)S(1)}, bf16[640,2048]{1,0:T(8,128)(2,1)S(1)}) custom-call(s32[20]{0:T(128)S(1)} %copy-done.8, bf16[640,512]{1,0:T(8,128)(2,1)S(1)} %get-tuple-element.417.low_ref.refs_0_, bf16[640,1024]{1,0:T(8,128)(2,1)S(1)} %get-tuple-element.413.high_ref, bf16[512,5120]{1,0:T(8,128)(2,1)S(1)} %shard_map.263.mat_low.low, ...), custom_call_target="tpu_custom_call" | custom-call | flops 6999999774720 | bytes 1 | tf_op jit(solution)/shard_map/pallas_call | solution.py:245
  157.7 12.1 %shard_map.267 = (bf16[1024,512]{1,0:T(8,128)(2,1)}, bf16[1024,512]{1,0:T(8,128)(2,1)}, bf16[1024,512]{1,0:T(8,128)(2,1)}, bf16[1024,512]{1,0:T(8,128)(2,1)}) custom-call(s32[20]{0:T(128)S(1)} %copy-done.8, bf16[640,2048]{1,0:T(8,128)(2,1)S(1)} %get-tuple-element.478.refs_0_.low_ref, bf16[640,2048]{1,0:T(8,128)(2,1)S(1)} %collective-permute-done.25.refs_1_, ...), custom_call_target="tpu_custom_call" | custom-call | flops 12000000212992 | bytes 1 | tf_op jit(solution)/shard_map/pallas_call | solution.py:245
  169.8 4.9 %shard_map.268.mat_low = bf16[2048,1024]{1,0:T(8,128)(2,1)} custom-call(s32[20]{0:T(128)S(1)} %copy-done.8, bf16[512,512]{1,0:T(8,128)(2,1)} %get-tuple-element.371.refs_0_, bf16[512,512]{1,0:T(8,128)(2,1)} %collective-permute-done.19.refs_1_, bf16[512,512]{1,0:T(8,128)(2,1)} %collective-permute-done.21.refs_2_, ...), custom_call_target="tpu_custom_call" | custom-call | flops 3999999983616 | bytes 1 | tf_op jit(solution)/shard_map/pallas_call | solution.py:245
  185.7 12.4 %shard_map.269 = (bf16[640,4096]{1,0:T(8,128)(2,1)}, f32[1,4096]{1,0:T(1,128)S(1)}) custom-call(s32[20]{0:T(128)S(1)} %copy-done.8, bf16[640,1024]{1,0:T(8,128)(2,1)S(1)} %copy-done.2, bf16[2048,1024]{1,0:T(8,128)(2,1)} %shard_map.268.mat_low, bf16[2048,1024]{1,0:T(8,128)(2,1)} %collective-permute-done.26.mat_high, bf16[640,2048]{1,0:T(8,128)(2,1)S(1)} %copy-done.37, ...), custom_call_target="tpu_custom_call" | custom-call | flops 12000000212992 | bytes 1 | tf_op jit(solution)/shard_map/pallas_call | solution.py:245
  198.1 4.6 %collective-permute-done.27.a1 = bf16[1024,512]{1,0:T(8,128)(2,1)} collective-permute-done((bf16[1024,512]{1,0:T(8,128)(2,1)}, bf16[1024,512]{1,0:T(8,128)(2,1)}, u32[]{:S(2)}, u32[]{:S(2)}) %collective-permute-start.27) | collective-permute-done | bytes 1048608 | tf_op jit(solution)/shard_map/ppermute | solution.py:862
  204.0 3.4 shard_map.270
  208.5 14.2 %shard_map.271 = (f32[640,1024]{1,0:T(8,128)S(1)}, bf16[640,1024]{1,0:T(8,128)(2,1)}, f32[1,1024]{1,0:T(1,128)S(1)}, f32[1,1024]{1,0:T(1,128)S(1)}, f32[1,1024]{1,0:T(1,128)S(1)}) custom-call(s32[20]{0:T(128)S(1)} %copy-done.8, bf16[640,4096]{1,0:T(8,128)(2,1)} %get-tuple-element.421.grad_ref.refs_4_, bf16[512,5120]{1,0:T(8,128)(2,1)S(1)} %copy-done.10, ...), custom_call_target="tpu_custom_call" | custom-call | flops 12999999881216 | bytes 1 | tf_op jit(solution)/shard_map/pallas_call | solution.py:245
  227.7 17.2 %shard_map.273 = (bf16[256,2560]{1,0:T(8,128)(2,1)}, bf16[256,2560]{1,0:T(8,128)(2,1)}, bf16[256,2560]{1,0:T(8,128)(2,1)}, bf16[256,2560]{1,0:T(8,128)(2,1)}) custom-call(s32[20]{0:T(128)S(1)} %copy-done.8, bf16[640,512]{1,0:T(8,128)(2,1)S(1)} %copy-done.39, bf16[640,1024]{1,0:T(8,128)(2,1)} %collective-permute-done.31.refs_1_.refs_3_, ...), custom_call_target="tpu_custom_call" | custom-call | flops 12000000212992 | bytes 1 | tf_op jit(solution)/shard_map/pallas_call | solution.py:245
  247.9 3.9 shard_map.274.do_ref
  251.8 21.8 %shard_map.275 = (bf16[3,640,1024]{2,1,0:T(8,128)(2,1)}, f32[1,1024]{1,0:T(1,128)S(1)}, f32[1,1024]{1,0:T(1,128)S(1)}) custom-call(s32[2,320,1]{2,1,0:T(8,128)S(1)} %copy-done.4, bf16[640,3072]{1,0:T(8,128)(2,1)S(1)} %copy-done.31, bf16[640,3072]{1,0:T(8,128)(2,1)S(1)} %copy-done.31, bf16[640,3072]{1,0:T(8,128)(2,1)S(1)} %copy-done.31, ...), custom_call_target="tpu_custom_call" | custom-call | flops 21999998992384 | bytes 1 | tf_op jit(solution)/shard_map/pallas_call | solution.py:104
  277.5 3.7 shard_map.276
  288.0 11.6 %shard_map.277 = (f32[640,1024]{1,0:T(8,128)}, f32[32,384]{1,0:T(8,128)S(1)}) custom-call(s32[20]{0:T(128)S(1)} %copy-done.8, bf16[3,640,1024]{2,1,0:T(8,128)(2,1)S(1)} %copy-done.14, bf16[512,3328]{1,0:T(8,128)(2,1)} %shard_map.257.low.mat_low, bf16[512,3328]{1,0:T(8,128)(2,1)} %collective-permute-done.10.high.mat_high, bf16[640,1024]{1,0:T(8,128)(2,1)S(1)} %bitcast.82, ...), custom_call_target="tpu_custom_call" | custom-call | flops 12999999881216 | bytes 1 | tf_op jit(solution)/shard_map/pallas_call | solution.py:245
  299.6 10.0 %shard_map.278 = (bf16[256,1536]{1,0:T(8,128)(2,1)}, bf16[256,1536]{1,0:T(8,128)(2,1)}, bf16[256,1536]{1,0:T(8,128)(2,1)}, bf16[256,1536]{1,0:T(8,128)(2,1)}) custom-call(s32[20]{0:T(128)S(1)} %copy-done.8, bf16[640,512]{1,0:T(8,128)(2,1)S(1)} %copy-done.26, bf16[640,1536]{1,0:T(8,128)(2,1)} %collective-permute-done.17.refs_3_.refs_1_, ...), custom_call_target="tpu_custom_call" | custom-call | flops 12000000212992 | bytes 1 | tf_op jit(solution)/shard_map/pallas_call | solution.py:245
  316.7 4.4 %collective-permute-start.41 = (bf16[32,5120]{1,0:T(8,128)(2,1)}, bf16[32,5120]{1,0:T(8,128)(2,1)}, u32[]{:S(2)}, u32[]{:S(2)}) collective-permute-start(bf16[32,5120]{1,0:T(8,128)(2,1)} %get-tuple-element.491), channel_id=1, source_target_pairs={{0,1},{1,2},{2,3},{3,0},{4,5},{5,6},{6,7},{7,4},{8,9},{9,10},{10,1... | collective-permute-start | bytes 983048 | tf_op jit(solution)/shard_map/ppermute | solution.py:865
  328.1 9.5 %shard_map.280 = f32[640,1024]{1,0:T(8,128)} custom-call(s32[20]{0:T(128)S(1)} %copy-done.8, bf16[640,2048]{1,0:T(8,128)(2,1)S(1)} %copy-done.33, bf16[640,2048]{1,0:T(8,128)(2,1)S(1)} %copy-done.16, bf16[2048,1024]{1,0:T(8,128)(2,1)} %shard_map.268.mat_low, bf16[2048,1024]{1,0:T(8,128)(2,1)} %collective-permute-done.26.mat_high, ...), custom_call_target="tpu_custom_call" | custom-call | flops 9999999827968 | bytes 1 | tf_op jit(solution)/shard_map/pallas_call | solution.py:245
  343.4 15.1 %collective-permute-done.45 = bf16[32,5120]{1,0:T(8,128)(2,1)} collective-permute-done((bf16[32,5120]{1,0:T(8,128)(2,1)S(1)}, bf16[32,5120]{1,0:T(8,128)(2,1)}, u32[]{:S(2)}, u32[]{:S(2)}) %collective-permute-start.45) | collective-permute-done | bytes 327712 | tf_op jit(solution)/shard_map/ppermute | solution.py:865
  365.0 4.1 %collective-permute-done.46 = bf16[32,3072]{1,0:T(8,128)(2,1)S(1)} collective-permute-done((bf16[32,3072]{1,0:T(8,128)(2,1)S(1)}, bf16[32,3072]{1,0:T(8,128)(2,1)S(1)}, u32[]{:S(2)}, u32[]{:S(2)}) %collective-permute-start.46) | collective-permute-done | bytes 196640 | tf_op jit(solution)/shard_map/ppermute | solution.py:865
  375.5 3.3 collective-permute-start.53
  383.3 3.6 collective-permute-done.51
  (277 shorter events, 135.8 us)
Async XLA Ops:
  7.2 94.3 %all-gather.2.cloned.1.call-start = ((), (), s32[]{:S(2)}) async-start(), calls=%async_computation.1 | async-start | bytes 1310720 | tf_op jit(solution)/shard_map/all_gather | solution.py:912
  29.6 20.8 %collective-permute-start.3 = (bf16[128,3328]{1,0:T(8,128)(2,1)S(1)}, bf16[128,3328]{1,0:T(8,128)(2,1)S(1)}, u32[]{:S(2)}, u32[]{:S(2)}) collective-permute-start(bf16[128,3328]{1,0:T(8,128)(2,1)S(1)} %shard_map.254.refs_0_.refs_4_), channel_id=1, source_target_pairs={{0,8},{4,12},{8,0},{12,4},{16,24},{20,28},{24,16},{28,20},{1,9},{5... | collective-permute-start | bytes 2555912 | tf_op jit(solution)/shard_map/ppermute | solution.py:862
  31.1 20.5 %collective-permute-start.4 = (bf16[128,3328]{1,0:T(8,128)(2,1)S(1)}, bf16[128,3328]{1,0:T(8,128)(2,1)S(1)}, u32[]{:S(2)}, u32[]{:S(2)}) collective-permute-start(bf16[128,3328]{1,0:T(8,128)(2,1)S(1)} %shard_map.254.refs_0_.refs_4_), channel_id=1, source_target_pairs={{0,16},{4,20},{8,24},{12,28},{16,0},{20,4},{24,8},{28,12},{1,17},{... | collective-permute-start | bytes 2555912 | tf_op jit(solution)/shard_map/ppermute | solution.py:862
  33.8 21.3 %collective-permute-start.7 = (bf16[32,5120]{1,0:T(8,128)(2,1)}, bf16[32,5120]{1,0:T(8,128)(2,1)}, u32[]{:S(2)}, u32[]{:S(2)}) collective-permute-start(bf16[32,5120]{1,0:T(8,128)(2,1)} %pad_maximum_fusion.1.refs_0_), channel_id=1, source_target_pairs={{0,1},{1,2},{2,3},{3,0},{4,5},{5,6},{6,7},{7,4},{8,9},{9,10},{10,1... | collective-permute-start | bytes 983048 | tf_op jit(solution)/shard_map/ppermute | solution.py:865
  38.9 21.8 %collective-permute-start.8 = (bf16[32,5120]{1,0:T(8,128)(2,1)}, bf16[32,5120]{1,0:T(8,128)(2,1)}, u32[]{:S(2)}, u32[]{:S(2)}) collective-permute-start(bf16[32,5120]{1,0:T(8,128)(2,1)} %pad_maximum_fusion.1.refs_0_), channel_id=1, source_target_pairs={{0,2},{1,3},{2,0},{3,1},{4,6},{5,7},{6,4},{7,5},{8,10},{9,11},{10,... | collective-permute-start | bytes 983048 | tf_op jit(solution)/shard_map/ppermute | solution.py:865
  40.5 20.2 %collective-permute-start.9 = (bf16[32,5120]{1,0:T(8,128)(2,1)}, bf16[32,5120]{1,0:T(8,128)(2,1)}, u32[]{:S(2)}, u32[]{:S(2)}) collective-permute-start(bf16[32,5120]{1,0:T(8,128)(2,1)} %pad_maximum_fusion.1.refs_0_), channel_id=1, source_target_pairs={{0,3},{1,0},{2,1},{3,2},{4,7},{5,4},{6,5},{7,6},{8,11},{9,8},{10,9... | collective-permute-start | bytes 983048 | tf_op jit(solution)/shard_map/ppermute | solution.py:865
  69.7 244.0 %reduce-scatter.2.cloned.1.call-start = ((), (), s32[]{:S(2)}) async-start(), calls=%async_computation.2 | async-start | bytes 1310720 | tf_op jit(solution)/shard_map/reduce_scatter | solution.py:722
  73.1 28.4 %collective-permute-start.11 = (bf16[128,2560]{1,0:T(8,128)(2,1)}, bf16[128,2560]{1,0:T(8,128)(2,1)}, u32[]{:S(2)}, u32[]{:S(2)}) collective-permute-start(bf16[128,2560]{1,0:T(8,128)(2,1)} %get-tuple-element.326.refs_0_), channel_id=1, source_target_pairs={{0,8},{4,12},{8,0},{12,4},{16,24},{20,28},{24,16},{28,20},{1,9},{5... | collective-permute-start | bytes 1966088 | tf_op jit(solution)/shard_map/ppermute | solution.py:862
  73.8 30.9 %collective-permute-start.13 = (bf16[128,2560]{1,0:T(8,128)(2,1)}, bf16[128,2560]{1,0:T(8,128)(2,1)}, u32[]{:S(2)}, u32[]{:S(2)}) collective-permute-start(bf16[128,2560]{1,0:T(8,128)(2,1)} %get-tuple-element.326.refs_0_), channel_id=1, source_target_pairs={{0,16},{4,20},{8,24},{12,28},{16,0},{20,4},{24,8},{28,12},{1,17},{... | collective-permute-start | bytes 1966088 | tf_op jit(solution)/shard_map/ppermute | solution.py:862
  74.3 30.4 %collective-permute-start.12 = (bf16[128,2560]{1,0:T(8,128)(2,1)}, bf16[128,2560]{1,0:T(8,128)(2,1)}, u32[]{:S(2)}, u32[]{:S(2)}) collective-permute-start(bf16[128,2560]{1,0:T(8,128)(2,1)} %get-tuple-element.330.refs_4_), channel_id=1, source_target_pairs={{0,8},{4,12},{8,0},{12,4},{16,24},{20,28},{24,16},{28,20},{1,9},{5... | collective-permute-start | bytes 1966088 | tf_op jit(solution)/shard_map/ppermute | solution.py:862
  75.7 29.3 %collective-permute-start.14 = (bf16[128,2560]{1,0:T(8,128)(2,1)}, bf16[128,2560]{1,0:T(8,128)(2,1)}, u32[]{:S(2)}, u32[]{:S(2)}) collective-permute-start(bf16[128,2560]{1,0:T(8,128)(2,1)} %get-tuple-element.330.refs_4_), channel_id=1, source_target_pairs={{0,16},{4,20},{8,24},{12,28},{16,0},{20,4},{24,8},{28,12},{1,17},{... | collective-permute-start | bytes 1966088 | tf_op jit(solution)/shard_map/ppermute | solution.py:862
  125.7 24.3 %collective-permute-start.19 = (bf16[512,512]{1,0:T(8,128)(2,1)}, bf16[512,512]{1,0:T(8,128)(2,1)}, u32[]{:S(2)}, u32[]{:S(2)}) collective-permute-start(bf16[512,512]{1,0:T(8,128)(2,1)} %get-tuple-element.371.refs_0_), channel_id=1, source_target_pairs={{0,8},{4,12},{8,0},{12,4},{16,24},{20,28},{24,16},{28,20},{1,9},{5... | collective-permute-start | bytes 1572872 | tf_op jit(solution)/shard_map/ppermute | solution.py:862
  127.1 24.5 %collective-permute-start.21 = (bf16[512,512]{1,0:T(8,128)(2,1)}, bf16[512,512]{1,0:T(8,128)(2,1)}, u32[]{:S(2)}, u32[]{:S(2)}) collective-permute-start(bf16[512,512]{1,0:T(8,128)(2,1)} %get-tuple-element.371.refs_0_), channel_id=1, source_target_pairs={{0,16},{4,20},{8,24},{12,28},{16,0},{20,4},{24,8},{28,12},{1,17},{... | collective-permute-start | bytes 1572872 | tf_op jit(solution)/shard_map/ppermute | solution.py:862
  128.7 22.9 %collective-permute-start.20 = (bf16[512,512]{1,0:T(8,128)(2,1)}, bf16[512,512]{1,0:T(8,128)(2,1)}, u32[]{:S(2)}, u32[]{:S(2)}) collective-permute-start(bf16[512,512]{1,0:T(8,128)(2,1)} %get-tuple-element.375.refs_4_), channel_id=1, source_target_pairs={{0,8},{4,12},{8,0},{12,4},{16,24},{20,28},{24,16},{28,20},{1,9},{5... | collective-permute-start | bytes 1572872 | tf_op jit(solution)/shard_map/ppermute | solution.py:862
  129.3 23.5 %collective-permute-start.22 = (bf16[512,512]{1,0:T(8,128)(2,1)}, bf16[512,512]{1,0:T(8,128)(2,1)}, u32[]{:S(2)}, u32[]{:S(2)}) collective-permute-start(bf16[512,512]{1,0:T(8,128)(2,1)} %get-tuple-element.375.refs_4_), channel_id=1, source_target_pairs={{0,16},{4,20},{8,24},{12,28},{16,0},{20,4},{24,8},{28,12},{1,17},{... | collective-permute-start | bytes 1572872 | tf_op jit(solution)/shard_map/ppermute | solution.py:862
  152.7 17.0 %collective-permute-start.23 = (bf16[512,512]{1,0:T(8,128)(2,1)}, bf16[512,512]{1,0:T(8,128)(2,1)}, u32[]{:S(2)}, u32[]{:S(2)}) collective-permute-start(bf16[512,512]{1,0:T(8,128)(2,1)} %collective-permute-done.19.refs_1_), channel_id=1, source_target_pairs={{0,16},{4,20},{8,24},{12,28},{16,0},{20,4},{24,8},{28,12},{1,17},{... | collective-permute-start | bytes 1572872 | tf_op jit(solution)/shard_map/ppermute | solution.py:862
  176.8 50.9 %collective-permute-start.31 = (bf16[640,1024]{1,0:T(8,128)(2,1)}, bf16[640,1024]{1,0:T(8,128)(2,1)}, u32[]{:S(2)}, u32[]{:S(2)}) collective-permute-start(bf16[640,1024]{1,0:T(8,128)(2,1)} %copy-done.21), channel_id=1, source_target_pairs={{0,4},{4,0},{8,12},{12,8},{16,20},{20,16},{24,28},{28,24},{1,5},{5... | collective-permute-start | bytes 3932168 | tf_op jit(solution)/shard_map/ppermute | solution.py:862
  177.2 25.5 %collective-permute-start.27 = (bf16[1024,512]{1,0:T(8,128)(2,1)}, bf16[1024,512]{1,0:T(8,128)(2,1)}, u32[]{:S(2)}, u32[]{:S(2)}) collective-permute-start(bf16[1024,512]{1,0:T(8,128)(2,1)} %get-tuple-element.382), channel_id=1, source_target_pairs={{0,16},{4,20},{8,24},{12,28},{16,0},{20,4},{24,8},{28,12},{1,17},{... | collective-permute-start | bytes 3145736 | tf_op jit(solution)/shard_map/ppermute | solution.py:862
  178.7 25.2 %collective-permute-start.28 = (bf16[1024,512]{1,0:T(8,128)(2,1)}, bf16[1024,512]{1,0:T(8,128)(2,1)}, u32[]{:S(2)}, u32[]{:S(2)}) collective-permute-start(bf16[1024,512]{1,0:T(8,128)(2,1)} %get-tuple-element.384), channel_id=1, source_target_pairs={{0,8},{4,12},{8,0},{12,4},{16,24},{20,28},{24,16},{28,20},{1,9},{5... | collective-permute-start | bytes 3145736 | tf_op jit(solution)/shard_map/ppermute | solution.py:862
  207.4 17.3 %collective-permute-start.29 = (bf16[512,512]{1,0:T(8,128)(2,1)}, bf16[512,512]{1,0:T(8,128)(2,1)}, u32[]{:S(2)}, u32[]{:S(2)}) collective-permute-start(bf16[512,512]{1,0:T(8,128)(2,1)} %get-tuple-element.400), channel_id=1, source_target_pairs={{0,8},{4,12},{8,0},{12,4},{16,24},{20,28},{24,16},{28,20},{1,9},{5... | collective-permute-start | bytes 1572872 | tf_op jit(solution)/shard_map/ppermute | solution.py:862
  208.0 16.7 %collective-permute-start.30 = (bf16[512,512]{1,0:T(8,128)(2,1)}, bf16[512,512]{1,0:T(8,128)(2,1)}, u32[]{:S(2)}, u32[]{:S(2)}) collective-permute-start(bf16[512,512]{1,0:T(8,128)(2,1)} %get-tuple-element.402), channel_id=1, source_target_pairs={{0,16},{4,20},{8,24},{12,28},{16,0},{20,4},{24,8},{28,12},{1,17},{... | collective-permute-start | bytes 1572872 | tf_op jit(solution)/shard_map/ppermute | solution.py:862
  208.5 19.2 %collective-permute-start.32 = (bf16[640,4096]{1,0:T(8,128)(2,1)}, bf16[640,4096]{1,0:T(8,128)(2,1)}, u32[]{:S(2)}, u32[]{:S(2)}) collective-permute-start(bf16[640,4096]{1,0:T(8,128)(2,1)} %get-tuple-element.421.grad_ref.refs_4_), channel_id=1, source_target_pairs={{0,4},{4,0},{8,12},{12,8},{16,20},{20,16},{24,28},{28,24},{1,5},{5... | collective-permute-start | bytes 15728648 | tf_op jit(solution)/shard_map/ppermute | solution.py:862
  244.9 31.4 %collective-permute-start.34 = (bf16[256,2560]{1,0:T(8,128)(2,1)}, bf16[256,2560]{1,0:T(8,128)(2,1)}, u32[]{:S(2)}, u32[]{:S(2)}) collective-permute-start(bf16[256,2560]{1,0:T(8,128)(2,1)} %get-tuple-element.428), channel_id=1, source_target_pairs={{0,16},{4,20},{8,24},{12,28},{16,0},{20,4},{24,8},{28,12},{1,17},{... | collective-permute-start | bytes 3932168 | tf_op jit(solution)/shard_map/ppermute | solution.py:862
  246.4 31.1 %collective-permute-start.35 = (bf16[256,2560]{1,0:T(8,128)(2,1)}, bf16[256,2560]{1,0:T(8,128)(2,1)}, u32[]{:S(2)}, u32[]{:S(2)}) collective-permute-start(bf16[256,2560]{1,0:T(8,128)(2,1)} %get-tuple-element.430), channel_id=1, source_target_pairs={{0,8},{4,12},{8,0},{12,4},{16,24},{20,28},{24,16},{28,20},{1,9},{5... | collective-permute-start | bytes 3932168 | tf_op jit(solution)/shard_map/ppermute | solution.py:862
  282.1 27.5 %collective-permute-start.36 = (bf16[128,2560]{1,0:T(8,128)(2,1)}, bf16[128,2560]{1,0:T(8,128)(2,1)}, u32[]{:S(2)}, u32[]{:S(2)}) collective-permute-start(bf16[128,2560]{1,0:T(8,128)(2,1)} %get-tuple-element.445), channel_id=1, source_target_pairs={{0,8},{4,12},{8,0},{12,4},{16,24},{20,28},{24,16},{28,20},{1,9},{5... | collective-permute-start | bytes 1966088 | tf_op jit(solution)/shard_map/ppermute | solution.py:862
  283.6 26.0 %collective-permute-start.37 = (bf16[128,2560]{1,0:T(8,128)(2,1)}, bf16[128,2560]{1,0:T(8,128)(2,1)}, u32[]{:S(2)}, u32[]{:S(2)}) collective-permute-start(bf16[128,2560]{1,0:T(8,128)(2,1)} %get-tuple-element.447), channel_id=1, source_target_pairs={{0,16},{4,20},{8,24},{12,28},{16,0},{20,4},{24,8},{28,12},{1,17},{... | collective-permute-start | bytes 1966088 | tf_op jit(solution)/shard_map/ppermute | solution.py:862
  313.7 23.9 %collective-permute-start.39 = (bf16[256,1536]{1,0:T(8,128)(2,1)}, bf16[256,1536]{1,0:T(8,128)(2,1)}, u32[]{:S(2)}, u32[]{:S(2)}) collective-permute-start(bf16[256,1536]{1,0:T(8,128)(2,1)} %get-tuple-element.486), channel_id=1, source_target_pairs={{0,16},{4,20},{8,24},{12,28},{16,0},{20,4},{24,8},{28,12},{1,17},{... | collective-permute-start | bytes 2359304 | tf_op jit(solution)/shard_map/ppermute | solution.py:862
  315.2 22.4 %collective-permute-start.40 = (bf16[256,1536]{1,0:T(8,128)(2,1)}, bf16[256,1536]{1,0:T(8,128)(2,1)}, u32[]{:S(2)}, u32[]{:S(2)}) collective-permute-start(bf16[256,1536]{1,0:T(8,128)(2,1)} %get-tuple-element.488), channel_id=1, source_target_pairs={{0,8},{4,12},{8,0},{12,4},{16,24},{20,28},{24,16},{28,20},{1,9},{5... | collective-permute-start | bytes 2359304 | tf_op jit(solution)/shard_map/ppermute | solution.py:862
  316.7 20.9 %collective-permute-start.41 = (bf16[32,5120]{1,0:T(8,128)(2,1)}, bf16[32,5120]{1,0:T(8,128)(2,1)}, u32[]{:S(2)}, u32[]{:S(2)}) collective-permute-start(bf16[32,5120]{1,0:T(8,128)(2,1)} %get-tuple-element.491), channel_id=1, source_target_pairs={{0,1},{1,2},{2,3},{3,0},{4,5},{5,6},{6,7},{7,4},{8,9},{9,10},{10,1... | collective-permute-start | bytes 983048 | tf_op jit(solution)/shard_map/ppermute | solution.py:865
  339.9 18.6 %collective-permute-start.43 = (bf16[128,1536]{1,0:T(8,128)(2,1)S(1)}, bf16[128,1536]{1,0:T(8,128)(2,1)S(1)}, u32[]{:S(2)}, u32[]{:S(2)}) collective-permute-start(bf16[128,1536]{1,0:T(8,128)(2,1)S(1)} %get-tuple-element.501), channel_id=1, source_target_pairs={{0,8},{4,12},{8,0},{12,4},{16,24},{20,28},{24,16},{28,20},{1,9},{5... | collective-permute-start | bytes 1179656 | tf_op jit(solution)/shard_map/ppermute | solution.py:862
  341.3 17.2 %collective-permute-start.44 = (bf16[128,1536]{1,0:T(8,128)(2,1)S(1)}, bf16[128,1536]{1,0:T(8,128)(2,1)S(1)}, u32[]{:S(2)}, u32[]{:S(2)}) collective-permute-start(bf16[128,1536]{1,0:T(8,128)(2,1)S(1)} %get-tuple-element.503), channel_id=1, source_target_pairs={{0,16},{4,20},{8,24},{12,28},{16,0},{20,4},{24,8},{28,12},{1,17},{... | collective-permute-start | bytes 1179656 | tf_op jit(solution)/shard_map/ppermute | solution.py:862
  341.8 16.7 %collective-permute-start.45 = (bf16[32,5120]{1,0:T(8,128)(2,1)S(1)}, bf16[32,5120]{1,0:T(8,128)(2,1)}, u32[]{:S(2)}, u32[]{:S(2)}) collective-permute-start(bf16[32,5120]{1,0:T(8,128)(2,1)S(1)} %get-tuple-element.506), channel_id=1, source_target_pairs={{0,2},{1,3},{2,0},{3,1},{4,6},{5,7},{6,4},{7,5},{8,10},{9,11},{10,... | collective-permute-start | bytes 983048 | tf_op jit(solution)/shard_map/ppermute | solution.py:865
  (87 other events, 831.5 us)
Sparse Core Ops, SparseCore 0:
  69.9 31.5 all-gather.1
  282.2 31.4 reduce-scatter.1

commit v4 on v3

--- a/solution.py
+++ b/solution.py
@@ -22,7 +22,7 @@
     return lax.dot_general(left, right, dims, preferred_element_type=f32)
 
 
-def attention_forward_kernel(seqs, length, keep_ref, q_ref, k_ref, v_ref, o_ref):
+def attention_forward_kernel(seqs, length, keep_ref, q_ref, k_ref, v_ref, o_ref, p_ref):
     scale = 1.0 / math.sqrt(HD)
     for s in range(seqs):
         rows = slice(s * length, (s + 1) * length)
@@ -33,52 +33,62 @@
             logits = dot(k_ref[rows, cols], q_ref[rows, cols] * scale, NT)
             logits = jnp.where(visible, logits, -1e9)
             raised = jnp.exp(logits - jnp.max(logits, 0, keepdims=True))
-            probs = raised * (1.0 / jnp.sum(raised, 0, keepdims=True))
-            mixed.append(dot(probs.astype(bf16), v_ref[rows, cols], TN))
+            probs = (raised * (1.0 / jnp.sum(raised, 0, keepdims=True))).astype(bf16)
+            p_ref[h, s] = probs
+            mixed.append(dot(probs, v_ref[rows, cols], TN))
         o_ref[rows, :] = jnp.concatenate(mixed, 1).astype(bf16)
 
 
 def attention_backward_kernel(
-    seqs, length, keep_ref, q_ref, k_ref, v_ref, do_ref, dp_ref, sq_ref, sv_ref
+    seqs, length, left_ref, right_ref, q_ref, k_ref, v_ref, do_ref, dp_ref, sq_ref, sv_ref
 ):
     scale = 1.0 / math.sqrt(HD)
-    sum_q = jnp.zeros((1, 128), f32)
-    sum_v = jnp.zeros((1, 128), f32)
-    for s in range(seqs):
-        rows = slice(s * length, (s + 1) * length)
-        visible = keep_ref[s] > 0
-        dqs, dks, dvs = [], [], []
-        for h in range(128 // HD):
-            cols = slice(h * HD, (h + 1) * HD)
-            queries = q_ref[rows, cols] * scale
-            keys = k_ref[rows, cols]
-            grad_mixed = do_ref[rows, cols]
-            logits = dot(keys, queries, NT)
-            grad_probs = dot(v_ref[rows, cols], grad_mixed, NT)
-            logits = jnp.where(visible, logits, -1e9)
-            raised = jnp.exp(logits - jnp.max(logits, 0, keepdims=True))
-            probs = raised * (1.0 / jnp.sum(raised, 0, keepdims=True))
-            dvs.append(dot(probs.astype(bf16), grad_mixed))
-            row_terms = jnp.sum(grad_probs * probs, 0, keepdims=True)
-            grad_logits = (probs * (grad_probs - row_terms)).astype(bf16)
-            dks.append(dot(grad_logits, queries))
-            dqs.append(dot(grad_logits, keys, TN) * scale)
-        dq = jnp.concatenate(dqs, 1).astype(bf16)
-        dv = jnp.concatenate(dvs, 1).astype(bf16)
-        dp_ref[0, rows, :] = dq
-        dp_ref[1, rows, :] = jnp.concatenate(dks, 1).astype(bf16)
-        dp_ref[2, rows, :] = dv
-        sum_q += jnp.sum(dq.astype(f32), 0, keepdims=True)
-        sum_v += jnp.sum(dv.astype(f32), 0, keepdims=True)
-    sq_ref[...] = sum_q
-    sv_ref[...] = sum_v
+
+    def work(p_ref):
+        sum_q = jnp.zeros((1, 128), f32)
+        sum_v = jnp.zeros((1, 128), f32)
+        for s in range(seqs):
+            rows = slice(s * length, (s + 1) * length)
+            dqs, dks, dvs = [], [], []
+            for h in range(128 // HD):
+                cols = slice(h * HD, (h + 1) * HD)
+                queries = q_ref[rows, cols] * scale
+                grad_mixed = do_ref[rows, cols]
+                low_probs = p_ref[h, s]
+                grad_probs = dot(v_ref[rows, cols], grad_mixed, NT)
+                dvs.append(dot(low_probs, grad_mixed))
+                probs = low_probs.astype(f32)
+                row_terms = jnp.sum(grad_probs * probs, 0, keepdims=True)
+                grad_logits = (probs * (grad_probs - row_terms)).astype(bf16)
+                dks.append(dot(grad_logits, queries))
+                dqs.append(dot(grad_logits, k_ref[rows, cols], TN) * scale)
+            dq = jnp.concatenate(dqs, 1).astype(bf16)
+            dv = jnp.concatenate(dvs, 1).astype(bf16)
+            dp_ref[0, rows, :] = dq
+            dp_ref[1, rows, :] = jnp.concatenate(dks, 1).astype(bf16)
+            dp_ref[2, rows, :] = dv
+            sum_q += jnp.sum(dq.astype(f32), 0, keepdims=True)
+            sum_v += jnp.sum(dv.astype(f32), 0, keepdims=True)
+        sq_ref[...] = sum_q
+        sv_ref[...] = sum_v
+
+    half = pl.num_programs(0) // 2
+
+    @pl.when(pl.program_id(0) < half)
+    def _():
+        work(left_ref)
+
+    @pl.when(pl.program_id(0) >= half)
+    def _():
+        work(right_ref)
 
 
 def attention_forward(keep, project, part):
     seqs, length = keep.shape[:2]
     rows, width = project.shape[0], project.shape[1] // 6
     steps = width // 128
-    block = pl.BlockSpec((rows, 128), lambda i: (0, i))
+    pair = 128 // HD
+    project = pltpu.with_memory_space_constraint(project, pltpu.HBM)
     return pl.pallas_call(
         functools.partial(attention_forward_kernel, seqs, length),
         grid=(steps,),
@@ -87,31 +97,45 @@
             pl.BlockSpec((rows, 128), lambda i, at=at: (0, i + (2 * at + part) * steps))
             for at in range(3)
         ],
-        out_specs=block,
-        out_shape=jax.ShapeDtypeStruct((rows, width), bf16),
-        compiler_params=pltpu.CompilerParams(vmem_limit_bytes=16 << 20),
+        out_specs=[
+            pl.BlockSpec((rows, 128), lambda i: (0, i)),
+            pl.BlockSpec((pair, seqs, length, length), lambda i: (i, 0, 0, 0)),
+        ],
+        out_shape=[
+            jax.ShapeDtypeStruct((rows, width), bf16),
+            pltpu.HBM((steps * pair, seqs, length, length), bf16),
+        ],
+        compiler_params=pltpu.CompilerParams(vmem_limit_bytes=20 << 20),
         cost_estimate=pl.CostEstimate(flops=int(8.5 * COST), bytes_accessed=1, transcendentals=0),
     )(keep, project, project, project)
 
 
-def attention_backward(keep, project, grad_mixed):
-    seqs, length = keep.shape[:2]
-    rows, width = project.shape[0], project.shape[1] // 3
+def attention_backward(probs, project, grad_mixed):
+    pairs, seqs, length = probs[0].shape[:3]
+    rows, width = grad_mixed.shape
     steps = width // 128
+    pair = 128 // HD
     block = pl.BlockSpec((rows, 128), lambda i: (0, i))
     vector = pl.BlockSpec((1, 128), lambda i: (0, i))
     sums = jax.ShapeDtypeStruct((1, width), f32)
+    shape = (pair, seqs, length, length)
+    project, left, right = (
+        pltpu.with_memory_space_constraint(v, pltpu.HBM) for v in (project, *probs)
+    )
     return pl.pallas_call(
         functools.partial(attention_backward_kernel, seqs, length),
         grid=(steps,),
-        in_specs=[pl.BlockSpec((seqs, length, 1), lambda i: (0, 0, 0))]
+        in_specs=[
+            pl.BlockSpec(shape, lambda i: (jnp.minimum(i, steps // 2 - 1), 0, 0, 0)),
+            pl.BlockSpec(shape, lambda i: (jnp.maximum(i - steps // 2, 0), 0, 0, 0)),
+        ]
         + [pl.BlockSpec((rows, 128), lambda i, at=at: (0, i + at * steps)) for at in range(3)]
         + [block],
         out_specs=[pl.BlockSpec((3, rows, 128), lambda i: (0, 0, i)), vector, vector],
         out_shape=[pltpu.HBM((3, rows, width), bf16), sums, sums],
-        compiler_params=pltpu.CompilerParams(vmem_limit_bytes=16 << 20),
+        compiler_params=pltpu.CompilerParams(vmem_limit_bytes=24 << 20),
         cost_estimate=pl.CostEstimate(flops=int(22 * COST), bytes_accessed=1, transcendentals=0),
-    )(keep, project, project, project, grad_mixed)
+    )(left, right, project, project, project, grad_mixed)
 
 
 def norm_forward(values, norm_gain, norm_bias):
@@ -161,7 +185,10 @@
     shift = jnp.concatenate([qv_bias[:width], zeros, qv_bias[width:]])
     project = (dot(act_one, qkv_mat) + shift).astype(bf16)
 
-    mixed = jnp.concatenate([attention_forward(keep_column, project, part) for part in range(2)], 1)
+    (mixed_left, probs_left), (mixed_right, probs_right) = (
+        attention_forward(keep_column, project, part) for part in range(2)
+    )
+    mixed = jnp.concatenate([mixed_left, mixed_right], 1)
     middle = inputs + dot(mixed, out_mat) + out_bias
     normed_two, plain_two, inverse_two = norm_forward(middle, g2, b2)
     act_two = normed_two.astype(bf16)
@@ -177,7 +204,7 @@
     grad_middle = grad_out + norm_backward(grad_act_two, plain_two, inverse_two, g2)
     grad_branch = grad_middle.astype(bf16)
     grad_mixed = dot(grad_branch, out_mat, NT).astype(bf16)
-    grad_parts, sum_q, sum_v = attention_backward(keep_column, project, grad_mixed)
+    grad_parts, sum_q, sum_v = attention_backward((probs_left, probs_right), project, grad_mixed)
     grad_project = jnp.concatenate([grad_parts[i] for i in range(3)], 1)
     grad_act_one = dot(grad_project, qkv_mat, NT)
     input_grad = grad_middle + norm_backward(grad_act_one, plain_one, inverse_one, g1)
@@ -230,11 +257,15 @@
     return jnp.stack(true + place + ahead).astype(jnp.int32)
 
 
-def call(kernel, grid, where, ins, outs, scratch=(), micros=3, sent=()):
+def call(kernel, grid, where, ins, outs, scratch=(), micros=3, sent=(), stream=False):
     held = 6 << 20
     specs = []
+    arrays = []
     for array, block, index in ins:
         once = tuple(block) == tuple(array.shape)
+        if stream and not once:
+            array = pltpu.with_memory_space_constraint(array, pltpu.HBM)
+        arrays.append(array)
         size = math.prod(n or 1 for n in block) * array.dtype.itemsize
         held += size if once else 2 * size
         specs.append(pl.BlockSpec(block, index, pipeline_mode=pl.Buffered(1) if once else None))
@@ -257,7 +288,7 @@
         ],
         compiler_params=pltpu.CompilerParams(vmem_limit_bytes=held),
         cost_estimate=pl.CostEstimate(flops=int(micros * COST), bytes_accessed=1, transcendentals=0),
-    )(where, *[array for array, _, _ in ins])
+    )(where, *arrays)
 
 
 def whole(array):
@@ -431,6 +462,7 @@
         ],
         [((rows, columns), bf16, (rows, tile), true), ((1, columns), f32, (1, tile), true)],
         micros=12,
+        stream=True,
     )
 
 
@@ -443,7 +475,8 @@
 
 def back_kernel(low, where, grad_ref, mat_low, mat_high, values_ref, above_ref, gain_ref, *rest):
     if low:
-        out_ref, low_ref, low_sum, gain_sum, bias_sum, total = rest
+        (out_low, out_high), rest = rest[:2], rest[2:]
+        out_ref, low_ref, low_sum, gain_sum, bias_sum, mixed_ref, total = rest
     else:
         *vectors, out_ref, packed, total = rest
     step = pl.program_id(0)
@@ -487,6 +520,11 @@
             gain_sum[...] = sums[0]
             bias_sum[...] = sums[1]
             low_sum[...] = sums[2]
+            for at in range(4):
+                mat = (out_low, out_high)[at // 2][at % 2 * 256 : at % 2 * 256 + 256, :]
+                part = dot(low_ref[...], mat, NT).astype(bf16)
+                for side in range(2):
+                    mixed_ref[:, lanes(where, 2 * at + side)] = part[:, side * 128 : (side + 1) * 128]
         else:
             owners = packed.shape[0]
             at = 0
@@ -506,6 +544,7 @@
     outs = [whole_out((rows, width), f32)]
     if low:
         outs += [whole_out((rows, width), bf16)] + [whole_out((1, width), f32)] * 3
+        outs += [whole_out((rows, width), bf16)]
     else:
         columns_packed = (2 * width + sum(v.shape[1] for v in vectors)) // owners
         outs += [whole_out((owners, columns_packed), f32)]
@@ -520,27 +559,11 @@
             whole(values),
             whole(above),
             whole(gain),
+            *[last_columns(m, width) for m in mats if low],
             *[whole(v) for v in vectors],
         ],
         outs,
-        [pltpu.VMEM((rows, width), f32)], micros=13)
-
-
-def mixed_grad_kernel(where, grad_ref, low, high, out_ref):
-    for at in range(4):
-        mat = (low, high)[at // 2]
-        part = dot(grad_ref[...], mat[at % 2 * 256 : at % 2 * 256 + 256, :], NT).astype(bf16)
-        for side in range(2):
-            out_ref[:, lanes(where, 2 * at + side)] = part[:, side * 128 : (side + 1) * 128]
-
-
-def mixed_grad(where, grad, mats):
-    return call(
-        mixed_grad_kernel,
-        (1,),
-        where,
-        [whole(grad), *[last_columns(m, grad.shape[1]) for m in mats]],
-        [whole_out(grad.shape, bf16)], micros=3)[0]
+        [pltpu.VMEM((rows, width), f32)], micros=13, sent=(0,) if low else ())
 
 
 def feed_kernel(where, low_ref, high_ref, mat_low, mat_high, middle_ref, shift_ref, keep_ref, out_ref):
@@ -564,7 +587,7 @@
             (shift, (1, 256), column),
             whole(keep),
         ],
-        [((rows, width), f32, (rows, 256), column)], micros=10)[0]
+        [((rows, width), f32, (rows, 256), column)], micros=0.002, stream=True)[0]
 
 
 def product_kernel(counts, where, *refs):
@@ -678,7 +701,7 @@
         block = ((rows, tile), column)
         half = ((rows // 2, columns), bf16, (rows // 2, tile), column)
         return call(
-            add_kernel, (columns // tile,), self.where, [(v, *block) for v in pieces], [half] * 4, micros=12)
+            add_kernel, (columns // tile,), self.where, [(v, *block) for v in pieces], [half] * 4, stream=True)
 
     def finish(self, *pieces):
         rows, columns = pieces[0].shape
@@ -770,7 +793,7 @@
 def assemble(count, places, *pieces):
     rows, columns = pieces[0].shape
     out = whole_out((rows * len(pieces), columns // count), bf16)
-    return call(assemble_kernel, (1,), places, [whole(p) for p in pieces], [out] * count)
+    return call(assemble_kernel, (1,), places, [whole(p) for p in pieces], [out] * count, micros=0.003)
 
 
 def join_kernel(where, *refs):
@@ -882,8 +905,8 @@
             self.own = block
             self.near, self.far = swap(block, XBIT), swap(block, YBIT)
 
-        def turn_whole(self):
-            left, right = order(functools.partial(split, where), self.near, self.far)
+        def turn_whole(self, *others):
+            left, right = order(lambda near, far, *_: split(where, near, far), self.near, self.far, *others)
             self.last = swap(left, YBIT), swap(right, XBIT)
 
         def join(self, *others):
@@ -896,7 +919,7 @@
             self.mats = low, swap(low, CORE)
 
     def around(shard):
-        return [shard] + [along(shard, by) for by in range(1, fsdp_size)]
+        return [shard] + [along(shard, by) for by in range(fsdp_size - 1, 0, -1)]
 
     vectors = (g1, b1, qv_bias, out_bias, g2, b2, up_bias, down_bias)
     device_count = 8 * fsdp_size
@@ -906,7 +929,7 @@
     beside = lax.optimization_barrier(jnp.concatenate(vectors)).reshape(-1, share).T
     beside = jnp.pad(beside, ((0, 0), (0, 256 - beside.shape[1])))
     qkv_low = jnp.concatenate([qkv_weight, beside], 1).astype(bf16)
-    behind = jnp.stack([(line - by) % fsdp_size for by in range(fsdp_size)]).astype(jnp.int32)
+    behind = jnp.stack([(line + by) % fsdp_size for by in range(fsdp_size)]).astype(jnp.int32)
     qkv_pieces = around(qkv_low)
     up_low = jnp.concatenate([up_weight, out_weight], 1).astype(bf16)
     down_block = lax.all_gather(down_weight.astype(bf16), "fsdp", axis=0, tiled=True)
@@ -917,7 +940,9 @@
     keep_rows = keep.reshape(rows, 1).astype(f32)
     keep_column = keep.reshape(seqs, length, 1)
     inputs = block_in.reshape(rows, width)
-    grad_feed = jnp.where(keep_rows > 0, out_cotangent.reshape(rows, width), jnp.zeros((), bf16))
+    grad_feed = order(
+        lambda g: jnp.where(keep_rows > 0, g, jnp.zeros((), bf16)), out_cotangent.reshape(rows, width)
+    )
     down_bias_grad = jnp.sum(grad_feed.astype(f32), 0)
 
     qkv, up, down = Gather(), Gather(), Gather()
@@ -936,10 +961,10 @@
     projected = order(
         lambda lo, hi, s, *m: project(where, lo, hi, m, s), one_low, one_pack, shift, *qkv.mats
     )
-    mixed_left = order(lambda p: attention_forward(keep_column, p, 0), projected)
+    mixed_left, probs_left = order(lambda p: attention_forward(keep_column, p, 0), projected)
     up.turn(down_block)
     one_other = swap(order.tie(one_pack)[0], CORE)
-    mixed_right = order(lambda p: attention_forward(keep_column, p, 1), projected)
+    mixed_right, probs_right = order(lambda p: attention_forward(keep_column, p, 1), projected)
     down_halves = order(lambda b: (b[:, :half], b[:, half:]), down_block)
     up.join(one_other)
     up.joined()
@@ -974,11 +999,12 @@
     down_sum.work()
     down_sum.send()
     pre_other = swap(order.tie(grad_pre)[0], CORE)
-    grad_middle, grad_branch, out_bias_grad, gain_two_grad, bias_two_grad = order(
+    grad_middle, grad_branch, out_bias_grad, gain_two_grad, bias_two_grad, grad_mixed = order(
         lambda g, mid, above, *m: back(where, g, m, mid, above, g2),
         grad_pre, middle, grad_feed, *up.mats,
     )
-    branch_other = swap(order.tie(grad_branch)[0], CORE)
+    branch, pre_other = order.tie(grad_branch, pre_other)
+    branch_other = swap(branch, CORE)
     down_sum.work()
     up_sum = Sum(
         swap, along, order, where,
@@ -988,14 +1014,28 @@
     )
     up_sum.work()
     up_sum.send()
-    grad_mixed = order(lambda g, *m: mixed_grad(where, g, m), grad_branch, *up.mats)
+    down_sum.send()
     grad_projected, sum_q, sum_v = order(
-        lambda p, g: attention_backward(keep_column, p, g), projected, grad_mixed
-    )
+        lambda p, g, *probs: attention_backward(probs, p, g),
+        projected, grad_mixed, probs_left, probs_right,
+    )
+    block_out = order(
+        lambda lo, hi, mid, s, *m: feed(where, lo, hi, m, mid, s, keep_rows),
+        hidden_low, hidden_high, middle, down_bias, *down.mats,
+    )
+    down_sum.meet()
     up_sum.work()
     up_sum.send()
     projected_other = swap(order.tie(grad_projected)[0], CORE)
-    down_sum.send()
+    qkv_sum = Sum(
+        swap, along, order, where,
+        [((one_low, 0), (one_other, 0))], [((grad_projected, 0), (projected_other, 0))],
+        512, [3 * width // 512],
+    )
+    qkv_sum.work()
+    up_sum.work()
+    qkv_sum.send()
+    up_sum.send((2,))
     sums = [
         jnp.concatenate([sum_q, sum_v], 1),
         out_bias_grad,
@@ -1008,47 +1048,29 @@
         lambda g, x, above, m0, m1, *v: back(where, g, (m0, m1), x, above, g1, v, device_count),
         grad_projected, inputs, grad_middle, *qkv.mats, *sums,
     )
-    qkv_sum = Sum(
-        swap, along, order, where,
-        [((one_low, 0), (one_other, 0))], [((grad_projected, 0), (projected_other, 0))],
-        512, [3 * width // 512],
-    )
-    qkv_sum.work()
-    up_sum.work()
-    down_sum.meet()
-    qkv_sum.send()
-    up_sum.send((1, 3))
-    upper = me % 2 == 1
-    shares = shares.reshape(4, 2, fsdp_size, -1)
-    low, high = shares[:, 0], shares[:, 1]
-    core_share = swap(order.tie(jnp.where(upper, low, high))[0], CORE)
-    shares = jnp.where(upper, high, low)
-    block_out = order(
-        lambda lo, hi, mid, s, *m: feed(where, lo, hi, m, mid, s, keep_rows),
-        hidden_low, hidden_high, middle, down_bias, *down.mats,
-    )
     up_sum.meet()
     qkv_sum.work()
     qkv_sum.send()
-    up_sum.send((2,))
+    up_sum.send((1, 3))
+    shares = order.tie(shares.reshape(2, 2, 2, fsdp_size, -1))[0]
+    for axis, bit in ((2, CORE), (1, XBIT), (0, YBIT)):
+        low, high = (lax.index_in_dim(shares, side, axis, keepdims=False) for side in range(2))
+        upper = me & bit > 0
+        shares = jnp.where(upper, high, low) + swap(jnp.where(upper, low, high), bit)
     up_sum.meet()
-    shares = shares + core_share
+    (shares,) = order.tie(shares)
+    order.last = (shares,)
     qkv_sum.work()
     qkv_sum.send((1, 2, 3))
     qkv_sum.shares[0], shares = order.tie(qkv_sum.shares[0], shares)
-
-    def part_of(bits):
-        return lax.dynamic_index_in_dim(shares, (me ^ bits) // 2, 0, keepdims=False)
-
-    plane_shares = [swap(part_of(bits), bits) for bits in (XBIT, YBIT, XBIT + YBIT)]
+    order.last = (qkv_sum.shares[0],)
+
+    def row_of(by):
+        return lax.dynamic_slice(shares, ((line + by) % fsdp_size, 0), (1, shares.shape[1]))
+
+    line_shares = [along(row_of(by), by) for by in range(1, fsdp_size)]
     down_grad, up_grad = down_sum.total(), up_sum.total()
     up_grad, out_grad = up_grad[:, : up_weight.shape[1]], up_grad[:, up_weight.shape[1] :]
-    shares = sum(plane_shares, part_of(0))
-
-    def row_of(by):
-        return lax.dynamic_slice(shares, ((line + by) % fsdp_size, 0), (1, shares.shape[1]))
-
-    line_shares = [along(row_of(by), by) for by in range(1, fsdp_size)]
     qkv_grad = qkv_sum.total()
     mine = sum(line_shares, row_of(0))
     v = jnp.split(mine[0], cuts)

time: 400 us -> 388 us (0.970)
  local copies, waits for them, and re-layouts: 26.5 us -> 17.1 us
    ppermute x15, waiting for transfers between devices: 41.8 us -> 27.6 us  [along(): lax.ppermute(value, 'fsdp', [(i, (i + by) % fsdp_size) for i in range(fsd...]
    unnamed x122 -> x92, local copies, waits for them, and re-layouts: 19.9 us -> 9.88 us
    ppermute x41 -> x40, waiting for transfers between devices: 41 us -> 48.3 us  [swap(): return lax.ppermute(value, 'dp', [(i, i ^ bit) for i in range(8)])]
    pallas_call x26 -> x25, Pallas kernels: 153 us -> 155 us  [call(): pl.pallas_call(kernel, grid_spec=pltpu.PrefetchScalarGridSpec(num_scalar_...]
    ppermute x41 -> x40, starting transfers between devices: 35.1 us -> 35 us  [swap(): return lax.ppermute(value, 'dp', [(i, i ^ bit) for i in range(8)])]
  transfers between devices with their start and end apart: 58 -> 57, of which waited for: 26 -> 24; matrix products, arithmetic and copies ran while one was open for 4% -> 4% of each run, Pallas kernels for 39% -> 40%
where the time goes in v4:
time: 388 us; the launch traced here: 384 us
  Pallas kernels  194 us (50%)
  waiting for transfers between devices  80.9 us (21%)
  starting transfers between devices  66.3 us (17%)
  local copies, waits for them, and re-layouts  17.1 us (4%)
  between operations  15.2 us (4%)
  other arithmetic  10.6 us (3%)
    pallas_call x25, Pallas kernels, call(): pl.pallas_call(kernel, grid_spec=pltpu.PrefetchScalarGridSpec(num_scalar_...  155 us
    ppermute x40, waiting for transfers between devices, swap(): return lax.ppermute(value, 'dp', [(i, i ^ bit) for i in range(8)])  48.3 us
    ppermute x40, starting transfers between devices, swap(): return lax.ppermute(value, 'dp', [(i, i ^ bit) for i in range(8)])  35 us
    ppermute x15, starting transfers between devices, along(): lax.ppermute(value, 'fsdp', [(i, (i + by) % fsdp_size) for i in range(fsd...  31 us
    ppermute x15, waiting for transfers between devices, along(): lax.ppermute(value, 'fsdp', [(i, (i + by) % fsdp_size) for i in range(fsd...  27.6 us
    pallas_call x2, Pallas kernels, attention_forward(): pl.pallas_call(functools.partial(attention_forward_kernel, seqs, length),...  20.5 us
    pallas_call x1, Pallas kernels, attention_backward(): pl.pallas_call(functools.partial(attention_backward_kernel, seqs, length)...  18.4 us
    unnamed x92, local copies, waits for them, and re-layouts  9.88 us
  transfers between devices with their start and end apart: 57, of which 24 were waited for; matrix products, arithmetic and copies ran while one was open for 4% of the time, Pallas kernels for 40%

profile of v4, /device:TPU:0, one launch (start us, length us, event | category | flops | bytes accessed | tf_op | source)
XLA Modules:
  0.0 384.1 jit_solution(12298618328260454816)
XLA Ops:
  20.6 8.3 %collective-permute-done.1.refs_2_ = bf16[32,3328]{1,0:T(8,128)(2,1)S(1)} collective-permute-done((bf16[32,3328]{1,0:T(8,128)(2,1)S(1)}, bf16[32,3328]{1,0:T(8,128)(2,1)S(1)}, u32[]{:S(2)}, u32[]{:S(2)}) %collective-permute-start.1) | collective-permute-done | bytes 213024 | tf_op jit(solution)/shard_map/ppermute | solution.py:888
  34.8 5.0 %collective-permute-start.9 = (bf16[32,5120]{1,0:T(8,128)(2,1)}, bf16[32,5120]{1,0:T(8,128)(2,1)}, u32[]{:S(2)}, u32[]{:S(2)}) collective-permute-start(bf16[32,5120]{1,0:T(8,128)(2,1)} %pad_maximum_fusion.1.refs_0_), channel_id=1, source_target_pairs={{0,1},{1,2},{2,3},{3,0},{4,5},{5,6},{6,7},{7,4},{8,9},{9,10},{10,1... | collective-permute-start | bytes 983048 | tf_op jit(solution)/shard_map/ppermute | solution.py:888
  42.2 8.2 %collective-permute-done.4.far.refs_2_.refs_6_ = bf16[128,3328]{1,0:T(8,128)(2,1)S(1)} collective-permute-done((bf16[128,3328]{1,0:T(8,128)(2,1)S(1)}, bf16[128,3328]{1,0:T(8,128)(2,1)S(1)}, u32[]{:S(2)}, u32[]{:S(2)}) %collective-permute-start.4) | collective-permute-done | bytes 852000 | tf_op jit(solution)/shard_map/ppermute | solution.py:885
  55.4 6.3 %collective-permute-done.8.refs_2_ = bf16[32,5120]{1,0:T(8,128)(2,1)} collective-permute-done((bf16[32,5120]{1,0:T(8,128)(2,1)}, bf16[32,5120]{1,0:T(8,128)(2,1)}, u32[]{:S(2)}, u32[]{:S(2)}) %collective-permute-start.8) | collective-permute-done | bytes 327712 | tf_op jit(solution)/shard_map/ppermute | solution.py:888
  65.3 3.6 shard_map.257.low.mat_low
  79.8 8.1 %shard_map.260.q_ref.k_ref.v_ref = bf16[640,3072]{1,0:T(8,128)(2,1)S(1)} custom-call(s32[20]{0:T(128)S(1)} %stack.90.where, bf16[640,512]{1,0:T(8,128)(2,1)S(1)} %get-tuple-element.472.low_ref.refs_0_, bf16[640,1536]{1,0:T(8,128)(2,1)S(1)} %get-tuple-element.331.high_ref, bf16[512,3328]{1,0:T(8,128)(2,1)} %shard_map.257.low.mat_low, ...), custom_call_target="tpu_custom_call" | custom-call | flops 7999999967232 | bytes 1 | tf_op jit(solution)/shard_map/pallas_call | solution.py:276
  90.6 10.2 %shard_map.261 = (bf16[640,512]{1,0:T(8,128)(2,1)S(1)}, bf16[8,2,320,320]{3,2,1,0:T(8,128)(2,1)}) custom-call(s32[2,320,1]{2,1,0:T(8,128)S(1)} %copy.32.keep_ref, bf16[640,3072]{1,0:T(8,128)(2,1)} %copy-done.25, bf16[640,3072]{1,0:T(8,128)(2,1)} %copy-done.25, bf16[640,3072]{1,0:T(8,128)(2,1)} %copy-done.25), custom_call_target="tpu_custom_call" | custom-call | flops 8499999801344 | bytes 1 | tf_op jit(solution)/shard_map/pallas_call | solution.py:92
  106.0 10.4 %shard_map.262 = (bf16[640,512]{1,0:T(8,128)(2,1)S(1)}, bf16[8,2,320,320]{3,2,1,0:T(8,128)(2,1)}) custom-call(s32[2,320,1]{2,1,0:T(8,128)S(1)} %copy.32.keep_ref, bf16[640,3072]{1,0:T(8,128)(2,1)} %copy-done.25, bf16[640,3072]{1,0:T(8,128)(2,1)} %copy-done.25, bf16[640,3072]{1,0:T(8,128)(2,1)} %copy-done.25), custom_call_target="tpu_custom_call" | custom-call | flops 8499999801344 | bytes 1 | tf_op jit(solution)/shard_map/pallas_call | solution.py:92
  117.4 3.5 collective-permute-done.16.refs_7_
  128.7 4.4 %collective-permute-done.18.mat_high.rest_1_ = bf16[512,5120]{1,0:T(8,128)(2,1)S(1)} collective-permute-done((bf16[512,5120]{1,0:T(8,128)(2,1)S(1)}, bf16[512,5120]{1,0:T(8,128)(2,1)S(1)}, u32[]{:S(2)}, u32[]{:S(2)}) %collective-permute-start.18) | collective-permute-done | bytes 5242912 | tf_op jit(solution)/shard_map/ppermute | solution.py:885
  133.1 3.5 shard_map.264
  136.6 6.1 %shard_map.265 = (bf16[640,2048]{1,0:T(8,128)(2,1)S(1)}, bf16[640,2048]{1,0:T(8,128)(2,1)S(1)}) custom-call(s32[20]{0:T(128)S(1)} %copy-done.11, bf16[640,512]{1,0:T(8,128)(2,1)S(1)} %get-tuple-element.428.low_ref.refs_0_, bf16[640,1024]{1,0:T(8,128)(2,1)S(1)} %get-tuple-element.413.high_ref, bf16[512,5120]{1,0:T(8,128)(2,1)S(1)} %shard_map.263.mat_low.rest_0_, ...), custom_call_target="tpu_custom_call" | custom-call | flops 6999999774720 | bytes 1 | tf_op jit(solution)/shard_map/pallas_call | solution.py:276
  144.3 6.0 %shard_map.266 = (bf16[640,2048]{1,0:T(8,128)(2,1)S(1)}, bf16[640,2048]{1,0:T(8,128)(2,1)S(1)}) custom-call(s32[20]{0:T(128)S(1)} %copy-done.11, bf16[640,512]{1,0:T(8,128)(2,1)S(1)} %get-tuple-element.428.low_ref.refs_0_, bf16[640,1024]{1,0:T(8,128)(2,1)S(1)} %get-tuple-element.413.high_ref, bf16[512,5120]{1,0:T(8,128)(2,1)S(1)} %shard_map.263.mat_low.rest_0_, ...), custom_call_target="tpu_custom_call" | custom-call | flops 6999999774720 | bytes 1 | tf_op jit(solution)/shard_map/pallas_call | solution.py:276
  156.8 12.1 %shard_map.267 = (bf16[1024,512]{1,0:T(8,128)(2,1)}, bf16[1024,512]{1,0:T(8,128)(2,1)}, bf16[1024,512]{1,0:T(8,128)(2,1)}, bf16[1024,512]{1,0:T(8,128)(2,1)}) custom-call(s32[20]{0:T(128)S(1)} %copy-done.11, bf16[640,2048]{1,0:T(8,128)(2,1)S(1)} %get-tuple-element.442.refs_0_.low_ref, bf16[640,2048]{1,0:T(8,128)(2,1)S(1)} %collective-permute-done.25.refs_1_, ...), custom_call_target="tpu_custom_call" | custom-call | flops 12000000212992 | bytes 1 | tf_op jit(solution)/shard_map/pallas_call | solution.py:276
  168.9 4.9 %shard_map.268.mat_low = bf16[2048,1024]{1,0:T(8,128)(2,1)} custom-call(s32[20]{0:T(128)S(1)} %copy-done.11, bf16[512,512]{1,0:T(8,128)(2,1)} %get-tuple-element.378.refs_0_, bf16[512,512]{1,0:T(8,128)(2,1)} %collective-permute-done.19.refs_1_, bf16[512,512]{1,0:T(8,128)(2,1)} %collective-permute-done.21.refs_2_, ...), custom_call_target="tpu_custom_call" | custom-call | flops 3999999983616 | bytes 1 | tf_op jit(solution)/shard_map/pallas_call | solution.py:276
  176.7 4.6 %collective-permute-done.26.mat_high = bf16[2048,1024]{1,0:T(8,128)(2,1)} collective-permute-done((bf16[2048,1024]{1,0:T(8,128)(2,1)}, bf16[2048,1024]{1,0:T(8,128)(2,1)}, u32[]{:S(2)}, u32[]{:S(2)}) %collective-permute-start.26) | collective-permute-done | bytes 4194336 | tf_op jit(solution)/shard_map/ppermute | solution.py:885
  182.6 13.3 %shard_map.269 = (bf16[640,4096]{1,0:T(8,128)(2,1)}, f32[1,4096]{1,0:T(1,128)S(1)}) custom-call(s32[20]{0:T(128)S(1)} %copy-done.11, bf16[640,1024]{1,0:T(8,128)(2,1)S(1)} %copy-done.7, bf16[2048,1024]{1,0:T(8,128)(2,1)} %shard_map.268.mat_low, bf16[2048,1024]{1,0:T(8,128)(2,1)} %collective-permute-done.26.mat_high, bf16[640,2048]{1,0:T(8,128)(2,1)} %copy-done.27, ...), custom_call_target="tpu_custom_call" | custom-call | flops 12000000212992 | bytes 1 | tf_op jit(solution)/shard_map/pallas_call | solution.py:276
  196.0 4.2 %collective-permute-done.27.a1 = bf16[1024,512]{1,0:T(8,128)(2,1)} collective-permute-done((bf16[1024,512]{1,0:T(8,128)(2,1)}, bf16[1024,512]{1,0:T(8,128)(2,1)}, u32[]{:S(2)}, u32[]{:S(2)}) %collective-permute-start.27) | collective-permute-done | bytes 1048608 | tf_op jit(solution)/shard_map/ppermute | solution.py:885
  200.5 3.8 shard_map.270
  207.1 17.9 %shard_map.271 = (f32[640,1024]{1,0:T(8,128)}, bf16[640,1024]{1,0:T(8,128)(2,1)}, f32[1,1024]{1,0:T(1,128)S(1)}, f32[1,1024]{1,0:T(1,128)S(1)}, f32[1,1024]{1,0:T(1,128)S(1)}, /*index=5*/bf16[640,1024]{1,0:T(8,128)(2,1)S(1)}) custom-call(s32[20]{0:T(128)S(1)} %copy-done.11, bf16[640,4096]{1,0:T(8,128)(2,1)} %get-tuple-element.432.grad_ref.refs_4_, ...), custom_call_target="tpu_custom_call" | custom-call | flops 12999999881216 | bytes 1 | tf_op jit(solution)/shard_map/pallas_call | solution.py:276
  229.7 16.9 %shard_map.273 = (bf16[256,2560]{1,0:T(8,128)(2,1)}, bf16[256,2560]{1,0:T(8,128)(2,1)}, bf16[256,2560]{1,0:T(8,128)(2,1)}, bf16[256,2560]{1,0:T(8,128)(2,1)}) custom-call(s32[20]{0:T(128)S(1)} %copy-done.11, bf16[640,512]{1,0:T(8,128)(2,1)S(1)} %copy-done.31, bf16[640,1024]{1,0:T(8,128)(2,1)} %collective-permute-done.29.refs_1_.refs_3_, ...), custom_call_target="tpu_custom_call" | custom-call | flops 12000000212992 | bytes 1 | tf_op jit(solution)/shard_map/pallas_call | solution.py:276
  247.8 18.4 %shard_map.274 = (bf16[3,640,1024]{2,1,0:T(8,128)(2,1)}, f32[1,1024]{1,0:T(1,128)S(1)}, f32[1,1024]{1,0:T(1,128)S(1)}) custom-call(bf16[8,2,320,320]{3,2,1,0:T(8,128)(2,1)} %get-tuple-element.437.left_ref, bf16[8,2,320,320]{3,2,1,0:T(8,128)(2,1)} %get-tuple-element.438.right_ref, bf16[640,3072]{1,0:T(8,128)(2,1)} %copy-done.25, ...), custom_call_target="tpu_custom_call" | custom-call | flops 21999998992384 | bytes 1 | tf_op jit(solution)/shard_map/pallas_call | solution.py:125
  266.2 9.9 %shard_map.275 = f32[640,1024]{1,0:T(8,128)} custom-call(s32[20]{0:T(128)S(1)} %copy-done.11, bf16[640,2048]{1,0:T(8,128)(2,1)S(1)} %copy-done.4, bf16[640,2048]{1,0:T(8,128)(2,1)S(1)} %copy-done.2, bf16[2048,1024]{1,0:T(8,128)(2,1)} %shard_map.268.mat_low, bf16[2048,1024]{1,0:T(8,128)(2,1)} %collective-permute-done.26.mat_high, f32[640,1024]{1,0:T(8,128)} %copy-done, ...), custom_call_target="tpu_custom_call" | custom-call | flops 2000000000 | bytes 1 | tf_op jit(solution)/shard_map/pallas_call | solution.py:276
  278.8 4.2 %shard_map.276 = (bf16[128,2560]{1,0:T(8,128)(2,1)S(1)}, bf16[128,2560]{1,0:T(8,128)(2,1)}, bf16[128,2560]{1,0:T(8,128)(2,1)S(1)}, bf16[128,2560]{1,0:T(8,128)(2,1)}) custom-call(s32[20]{0:T(128)S(1)} %copy-done.11, bf16[256,2560]{1,0:T(8,128)(2,1)} %get-tuple-element.461.a0, bf16[256,2560]{1,0:T(8,128)(2,1)} %collective-permute-done.34.a1, ...), custom_call_target="tpu_custom_call" | custom-call | flops 3000000053248 | bytes 1 | tf_op jit(solution)/shard_map/pallas_call | solution.py:276
  286.0 4.1 %collective-permute-done.38.refs_3_ = bf16[3,640,1024]{2,1,0:T(8,128)(2,1)} collective-permute-done((bf16[3,640,1024]{2,1,0:T(8,128)(2,1)}, bf16[3,640,1024]{2,1,0:T(8,128)(2,1)}, u32[]{:S(2)}, u32[]{:S(2)}) %collective-permute-start.38) | collective-permute-done | bytes 3932192 | tf_op jit(solution)/shard_map/ppermute | solution.py:885
  290.1 10.6 %shard_map.277 = (bf16[256,1536]{1,0:T(8,128)(2,1)}, bf16[256,1536]{1,0:T(8,128)(2,1)}, bf16[256,1536]{1,0:T(8,128)(2,1)}, bf16[256,1536]{1,0:T(8,128)(2,1)}) custom-call(s32[20]{0:T(128)S(1)} %copy-done.11, bf16[640,512]{1,0:T(8,128)(2,1)S(1)} %copy-done.24, bf16[640,1536]{1,0:T(8,128)(2,1)} %collective-permute-done.17.refs_3_.refs_1_, ...), custom_call_target="tpu_custom_call" | custom-call | flops 12000000212992 | bytes 1 | tf_op jit(solution)/shard_map/pallas_call | solution.py:276
  305.1 4.9 %collective-permute-start.41 = (bf16[32,5120]{1,0:T(8,128)(2,1)}, bf16[32,5120]{1,0:T(8,128)(2,1)}, u32[]{:S(2)}, u32[]{:S(2)}) collective-permute-start(bf16[32,5120]{1,0:T(8,128)(2,1)} %get-tuple-element.500), channel_id=1, source_target_pairs={{0,2},{1,3},{2,0},{3,1},{4,6},{5,7},{6,4},{7,5},{8,10},{9,11},{10,... | collective-permute-start | bytes 983048 | tf_op jit(solution)/shard_map/ppermute | solution.py:888
  311.9 12.9 %shard_map.279 = (f32[640,1024]{1,0:T(8,128)}, f32[32,384]{1,0:T(8,128)S(1)}) custom-call(s32[20]{0:T(128)S(1)} %copy-done.11, bf16[3,640,1024]{2,1,0:T(8,128)(2,1)} %get-tuple-element.482.refs_2_.grad_ref, bf16[512,3328]{1,0:T(8,128)(2,1)} %shard_map.257.low.mat_low, bf16[512,3328]{1,0:T(8,128)(2,1)} %collective-permute-done.10.high.mat_high, ...), custom_call_target="tpu_custom_call" | custom-call | flops 12999999881216 | bytes 1 | tf_op jit(solution)/shard_map/pallas_call | solution.py:276
  325.4 3.5 collective-permute-done.39.a1
  342.0 8.1 %collective-permute-done.46 = f32[4,384]{1,0:T(4,128)S(1)} collective-permute-done((f32[4,384]{1,0:T(4,128)S(1)}, f32[4,384]{1,0:T(4,128)S(1)}, u32[]{:S(2)}, u32[]{:S(2)}) %collective-permute-start.46) | collective-permute-done | bytes 6176 | tf_op jit(solution)/shard_map/ppermute | solution.py:885
  358.5 5.8 %collective-permute-done.49 = bf16[32,3072]{1,0:T(8,128)(2,1)S(1)} collective-permute-done((bf16[32,3072]{1,0:T(8,128)(2,1)S(1)}, bf16[32,3072]{1,0:T(8,128)(2,1)S(1)}, u32[]{:S(2)}, u32[]{:S(2)}) %collective-permute-start.49) | collective-permute-done | bytes 196640 | tf_op jit(solution)/shard_map/ppermute | solution.py:888
  364.3 3.8 collective-permute-start.52
  (245 shorter events, 121.8 us)
Async XLA Ops:
  7.2 95.8 %all-gather.2.cloned.1.call-start = ((), (), s32[]{:S(2)}) async-start(), calls=%async_computation.1 | async-start | bytes 1310720 | tf_op jit(solution)/shard_map/all_gather | solution.py:935
  12.4 16.5 %collective-permute-start.1 = (bf16[32,3328]{1,0:T(8,128)(2,1)S(1)}, bf16[32,3328]{1,0:T(8,128)(2,1)S(1)}, u32[]{:S(2)}, u32[]{:S(2)}) collective-permute-start(bf16[32,3328]{1,0:T(8,128)(2,1)S(1)} %fusion.1.refs_0_), channel_id=1, source_target_pairs={{0,2},{1,3},{2,0},{3,1},{4,6},{5,7},{6,4},{7,5},{8,10},{9,11},{10,... | collective-permute-start | bytes 638984 | tf_op jit(solution)/shard_map/ppermute | solution.py:888
  29.6 20.8 %collective-permute-start.4 = (bf16[128,3328]{1,0:T(8,128)(2,1)S(1)}, bf16[128,3328]{1,0:T(8,128)(2,1)S(1)}, u32[]{:S(2)}, u32[]{:S(2)}) collective-permute-start(bf16[128,3328]{1,0:T(8,128)(2,1)S(1)} %shard_map.254.refs_0_.refs_4_), channel_id=1, source_target_pairs={{0,16},{4,20},{8,24},{12,28},{16,0},{20,4},{24,8},{28,12},{1,17},{... | collective-permute-start | bytes 2555912 | tf_op jit(solution)/shard_map/ppermute | solution.py:885
  31.1 20.6 %collective-permute-start.3 = (bf16[128,3328]{1,0:T(8,128)(2,1)S(1)}, bf16[128,3328]{1,0:T(8,128)(2,1)}, u32[]{:S(2)}, u32[]{:S(2)}) collective-permute-start(bf16[128,3328]{1,0:T(8,128)(2,1)S(1)} %shard_map.254.refs_0_.refs_4_), channel_id=1, source_target_pairs={{0,8},{4,12},{8,0},{12,4},{16,24},{20,28},{24,16},{28,20},{1,9},{5... | collective-permute-start | bytes 2555912 | tf_op jit(solution)/shard_map/ppermute | solution.py:885
  34.8 20.6 %collective-permute-start.9 = (bf16[32,5120]{1,0:T(8,128)(2,1)}, bf16[32,5120]{1,0:T(8,128)(2,1)}, u32[]{:S(2)}, u32[]{:S(2)}) collective-permute-start(bf16[32,5120]{1,0:T(8,128)(2,1)} %pad_maximum_fusion.1.refs_0_), channel_id=1, source_target_pairs={{0,1},{1,2},{2,3},{3,0},{4,5},{5,6},{6,7},{7,4},{8,9},{9,10},{10,1... | collective-permute-start | bytes 983048 | tf_op jit(solution)/shard_map/ppermute | solution.py:888
  39.9 21.8 %collective-permute-start.8 = (bf16[32,5120]{1,0:T(8,128)(2,1)}, bf16[32,5120]{1,0:T(8,128)(2,1)}, u32[]{:S(2)}, u32[]{:S(2)}) collective-permute-start(bf16[32,5120]{1,0:T(8,128)(2,1)} %pad_maximum_fusion.1.refs_0_), channel_id=1, source_target_pairs={{0,2},{1,3},{2,0},{3,1},{4,6},{5,7},{6,4},{7,5},{8,10},{9,11},{10,... | collective-permute-start | bytes 983048 | tf_op jit(solution)/shard_map/ppermute | solution.py:888
  41.5 20.2 %collective-permute-start.7 = (bf16[32,5120]{1,0:T(8,128)(2,1)}, bf16[32,5120]{1,0:T(8,128)(2,1)}, u32[]{:S(2)}, u32[]{:S(2)}) collective-permute-start(bf16[32,5120]{1,0:T(8,128)(2,1)} %pad_maximum_fusion.1.refs_0_), channel_id=1, source_target_pairs={{0,3},{1,0},{2,1},{3,2},{4,7},{5,4},{6,5},{7,6},{8,11},{9,8},{10,9... | collective-permute-start | bytes 983048 | tf_op jit(solution)/shard_map/ppermute | solution.py:888
  69.7 209.1 %reduce-scatter.2.cloned.1.call-start = ((), (), s32[]{:S(2)}) async-start(), calls=%async_computation.2 | async-start | bytes 1310720 | tf_op jit(solution)/shard_map/reduce_scatter | solution.py:745
  71.4 31.6 %collective-permute-start.13 = (bf16[128,2560]{1,0:T(8,128)(2,1)}, bf16[128,2560]{1,0:T(8,128)(2,1)}, u32[]{:S(2)}, u32[]{:S(2)}) collective-permute-start(bf16[128,2560]{1,0:T(8,128)(2,1)} %copy-done.19), channel_id=1, source_target_pairs={{0,16},{4,20},{8,24},{12,28},{16,0},{20,4},{24,8},{28,12},{1,17},{... | collective-permute-start | bytes 1966088 | tf_op jit(solution)/shard_map/ppermute | solution.py:885
  71.9 31.1 %collective-permute-start.11 = (bf16[128,2560]{1,0:T(8,128)(2,1)}, bf16[128,2560]{1,0:T(8,128)(2,1)}, u32[]{:S(2)}, u32[]{:S(2)}) collective-permute-start(bf16[128,2560]{1,0:T(8,128)(2,1)} %copy-done.19), channel_id=1, source_target_pairs={{0,8},{4,12},{8,0},{12,4},{16,24},{20,28},{24,16},{28,20},{1,9},{5... | collective-permute-start | bytes 1966088 | tf_op jit(solution)/shard_map/ppermute | solution.py:885
  72.4 30.5 %collective-permute-start.14 = (bf16[128,2560]{1,0:T(8,128)(2,1)}, bf16[128,2560]{1,0:T(8,128)(2,1)}, u32[]{:S(2)}, u32[]{:S(2)}) collective-permute-start(bf16[128,2560]{1,0:T(8,128)(2,1)} %copy-done.21), channel_id=1, source_target_pairs={{0,16},{4,20},{8,24},{12,28},{16,0},{20,4},{24,8},{28,12},{1,17},{... | collective-permute-start | bytes 1966088 | tf_op jit(solution)/shard_map/ppermute | solution.py:885
  73.9 29.2 %collective-permute-start.12 = (bf16[128,2560]{1,0:T(8,128)(2,1)}, bf16[128,2560]{1,0:T(8,128)(2,1)}, u32[]{:S(2)}, u32[]{:S(2)}) collective-permute-start(bf16[128,2560]{1,0:T(8,128)(2,1)} %copy-done.21), channel_id=1, source_target_pairs={{0,8},{4,12},{8,0},{12,4},{16,24},{20,28},{24,16},{28,20},{1,9},{5... | collective-permute-start | bytes 1966088 | tf_op jit(solution)/shard_map/ppermute | solution.py:885
  103.1 17.8 %collective-permute-start.15 = (bf16[128,2560]{1,0:T(8,128)(2,1)}, bf16[128,2560]{1,0:T(8,128)(2,1)}, u32[]{:S(2)}, u32[]{:S(2)}) collective-permute-start(bf16[128,2560]{1,0:T(8,128)(2,1)} %collective-permute-done.11.refs_1_), channel_id=1, source_target_pairs={{0,16},{4,20},{8,24},{12,28},{16,0},{20,4},{24,8},{28,12},{1,17},{... | collective-permute-start | bytes 1966088 | tf_op jit(solution)/shard_map/ppermute | solution.py:885
  124.6 27.2 %collective-permute-start.21 = (bf16[512,512]{1,0:T(8,128)(2,1)}, bf16[512,512]{1,0:T(8,128)(2,1)}, u32[]{:S(2)}, u32[]{:S(2)}) collective-permute-start(bf16[512,512]{1,0:T(8,128)(2,1)} %get-tuple-element.378.refs_0_), channel_id=1, source_target_pairs={{0,16},{4,20},{8,24},{12,28},{16,0},{20,4},{24,8},{28,12},{1,17},{... | collective-permute-start | bytes 1572872 | tf_op jit(solution)/shard_map/ppermute | solution.py:885
  125.2 26.6 %collective-permute-start.19 = (bf16[512,512]{1,0:T(8,128)(2,1)}, bf16[512,512]{1,0:T(8,128)(2,1)}, u32[]{:S(2)}, u32[]{:S(2)}) collective-permute-start(bf16[512,512]{1,0:T(8,128)(2,1)} %get-tuple-element.378.refs_0_), channel_id=1, source_target_pairs={{0,8},{4,12},{8,0},{12,4},{16,24},{20,28},{24,16},{28,20},{1,9},{5... | collective-permute-start | bytes 1572872 | tf_op jit(solution)/shard_map/ppermute | solution.py:885
  126.7 25.1 %collective-permute-start.22 = (bf16[512,512]{1,0:T(8,128)(2,1)}, bf16[512,512]{1,0:T(8,128)(2,1)}, u32[]{:S(2)}, u32[]{:S(2)}) collective-permute-start(bf16[512,512]{1,0:T(8,128)(2,1)} %get-tuple-element.382.refs_4_), channel_id=1, source_target_pairs={{0,16},{4,20},{8,24},{12,28},{16,0},{20,4},{24,8},{28,12},{1,17},{... | collective-permute-start | bytes 1572872 | tf_op jit(solution)/shard_map/ppermute | solution.py:885
  128.2 23.6 %collective-permute-start.20 = (bf16[512,512]{1,0:T(8,128)(2,1)}, bf16[512,512]{1,0:T(8,128)(2,1)}, u32[]{:S(2)}, u32[]{:S(2)}) collective-permute-start(bf16[512,512]{1,0:T(8,128)(2,1)} %get-tuple-element.382.refs_4_), channel_id=1, source_target_pairs={{0,8},{4,12},{8,0},{12,4},{16,24},{20,28},{24,16},{28,20},{1,9},{5... | collective-permute-start | bytes 1572872 | tf_op jit(solution)/shard_map/ppermute | solution.py:885
  152.0 16.9 %collective-permute-start.23 = (bf16[512,512]{1,0:T(8,128)(2,1)}, bf16[512,512]{1,0:T(8,128)(2,1)}, u32[]{:S(2)}, u32[]{:S(2)}) collective-permute-start(bf16[512,512]{1,0:T(8,128)(2,1)} %collective-permute-done.19.refs_1_), channel_id=1, source_target_pairs={{0,16},{4,20},{8,24},{12,28},{16,0},{20,4},{24,8},{28,12},{1,17},{... | collective-permute-start | bytes 1572872 | tf_op jit(solution)/shard_map/ppermute | solution.py:885
  174.2 55.5 %collective-permute-start.29 = (bf16[640,1024]{1,0:T(8,128)(2,1)}, bf16[640,1024]{1,0:T(8,128)(2,1)}, u32[]{:S(2)}, u32[]{:S(2)}) collective-permute-start(bf16[640,1024]{1,0:T(8,128)(2,1)} %copy-done.18), channel_id=1, source_target_pairs={{0,4},{4,0},{8,12},{12,8},{16,20},{20,16},{24,28},{28,24},{1,5},{5... | collective-permute-start | bytes 3932168 | tf_op jit(solution)/shard_map/ppermute | solution.py:885
  174.6 25.5 %collective-permute-start.27 = (bf16[1024,512]{1,0:T(8,128)(2,1)}, bf16[1024,512]{1,0:T(8,128)(2,1)}, u32[]{:S(2)}, u32[]{:S(2)}) collective-permute-start(bf16[1024,512]{1,0:T(8,128)(2,1)} %get-tuple-element.397), channel_id=1, source_target_pairs={{0,16},{4,20},{8,24},{12,28},{16,0},{20,4},{24,8},{28,12},{1,17},{... | collective-permute-start | bytes 3145736 | tf_op jit(solution)/shard_map/ppermute | solution.py:885
  175.2 25.3 %collective-permute-start.28 = (bf16[1024,512]{1,0:T(8,128)(2,1)}, bf16[1024,512]{1,0:T(8,128)(2,1)}, u32[]{:S(2)}, u32[]{:S(2)}) collective-permute-start(bf16[1024,512]{1,0:T(8,128)(2,1)} %get-tuple-element.399), channel_id=1, source_target_pairs={{0,8},{4,12},{8,0},{12,4},{16,24},{20,28},{24,16},{28,20},{1,9},{5... | collective-permute-start | bytes 3145736 | tf_op jit(solution)/shard_map/ppermute | solution.py:885
  204.2 21.9 %collective-permute-start.32 = (bf16[512,512]{1,0:T(8,128)(2,1)}, bf16[512,512]{1,0:T(8,128)(2,1)}, u32[]{:S(2)}, u32[]{:S(2)}) collective-permute-start(bf16[512,512]{1,0:T(8,128)(2,1)} %get-tuple-element.421), channel_id=1, source_target_pairs={{0,8},{4,12},{8,0},{12,4},{16,24},{20,28},{24,16},{28,20},{1,9},{5... | collective-permute-start | bytes 1572872 | tf_op jit(solution)/shard_map/ppermute | solution.py:885
  205.7 20.4 %collective-permute-start.33 = (bf16[512,512]{1,0:T(8,128)(2,1)}, bf16[512,512]{1,0:T(8,128)(2,1)}, u32[]{:S(2)}, u32[]{:S(2)}) collective-permute-start(bf16[512,512]{1,0:T(8,128)(2,1)} %get-tuple-element.423), channel_id=1, source_target_pairs={{0,16},{4,20},{8,24},{12,28},{16,0},{20,4},{24,8},{28,12},{1,17},{... | collective-permute-start | bytes 1572872 | tf_op jit(solution)/shard_map/ppermute | solution.py:885
  207.1 19.0 %collective-permute-start.30 = (bf16[640,4096]{1,0:T(8,128)(2,1)}, bf16[640,4096]{1,0:T(8,128)(2,1)}, u32[]{:S(2)}, u32[]{:S(2)}) collective-permute-start(bf16[640,4096]{1,0:T(8,128)(2,1)} %get-tuple-element.432.grad_ref.refs_4_), channel_id=1, source_target_pairs={{0,4},{4,0},{8,12},{12,8},{16,20},{20,16},{24,28},{28,24},{1,5},{5... | collective-permute-start | bytes 15728648 | tf_op jit(solution)/shard_map/ppermute | solution.py:885
  246.6 32.2 %collective-permute-start.34 = (bf16[256,2560]{1,0:T(8,128)(2,1)}, bf16[256,2560]{1,0:T(8,128)(2,1)}, u32[]{:S(2)}, u32[]{:S(2)}) collective-permute-start(bf16[256,2560]{1,0:T(8,128)(2,1)} %get-tuple-element.456), channel_id=1, source_target_pairs={{0,16},{4,20},{8,24},{12,28},{16,0},{20,4},{24,8},{28,12},{1,17},{... | collective-permute-start | bytes 3932168 | tf_op jit(solution)/shard_map/ppermute | solution.py:885
  247.2 31.6 %collective-permute-start.35 = (bf16[256,2560]{1,0:T(8,128)(2,1)}, bf16[256,2560]{1,0:T(8,128)(2,1)}, u32[]{:S(2)}, u32[]{:S(2)}) collective-permute-start(bf16[256,2560]{1,0:T(8,128)(2,1)} %get-tuple-element.458), channel_id=1, source_target_pairs={{0,8},{4,12},{8,0},{12,4},{16,24},{20,28},{24,16},{28,20},{1,9},{5... | collective-permute-start | bytes 3932168 | tf_op jit(solution)/shard_map/ppermute | solution.py:885
  283.0 17.7 %collective-permute-start.36 = (bf16[128,2560]{1,0:T(8,128)(2,1)}, bf16[128,2560]{1,0:T(8,128)(2,1)}, u32[]{:S(2)}, u32[]{:S(2)}) collective-permute-start(bf16[128,2560]{1,0:T(8,128)(2,1)} %get-tuple-element.468), channel_id=1, source_target_pairs={{0,8},{4,12},{8,0},{12,4},{16,24},{20,28},{24,16},{28,20},{1,9},{5... | collective-permute-start | bytes 1966088 | tf_op jit(solution)/shard_map/ppermute | solution.py:885
  284.5 17.2 %collective-permute-start.37 = (bf16[128,2560]{1,0:T(8,128)(2,1)}, bf16[128,2560]{1,0:T(8,128)(2,1)}, u32[]{:S(2)}, u32[]{:S(2)}) collective-permute-start(bf16[128,2560]{1,0:T(8,128)(2,1)} %get-tuple-element.470), channel_id=1, source_target_pairs={{0,16},{4,20},{8,24},{12,28},{16,0},{20,4},{24,8},{28,12},{1,17},{... | collective-permute-start | bytes 1966088 | tf_op jit(solution)/shard_map/ppermute | solution.py:885
  305.1 20.3 %collective-permute-start.41 = (bf16[32,5120]{1,0:T(8,128)(2,1)}, bf16[32,5120]{1,0:T(8,128)(2,1)}, u32[]{:S(2)}, u32[]{:S(2)}) collective-permute-start(bf16[32,5120]{1,0:T(8,128)(2,1)} %get-tuple-element.500), channel_id=1, source_target_pairs={{0,2},{1,3},{2,0},{3,1},{4,6},{5,7},{6,4},{7,5},{8,10},{9,11},{10,... | collective-permute-start | bytes 983048 | tf_op jit(solution)/shard_map/ppermute | solution.py:888
  310.0 18.9 %collective-permute-start.39 = (bf16[256,1536]{1,0:T(8,128)(2,1)}, bf16[256,1536]{1,0:T(8,128)(2,1)}, u32[]{:S(2)}, u32[]{:S(2)}) collective-permute-start(bf16[256,1536]{1,0:T(8,128)(2,1)} %get-tuple-element.496), channel_id=1, source_target_pairs={{0,16},{4,20},{8,24},{12,28},{16,0},{20,4},{24,8},{28,12},{1,17},{... | collective-permute-start | bytes 2359304 | tf_op jit(solution)/shard_map/ppermute | solution.py:885
  311.4 18.6 %collective-permute-start.40 = (bf16[256,1536]{1,0:T(8,128)(2,1)}, bf16[256,1536]{1,0:T(8,128)(2,1)}, u32[]{:S(2)}, u32[]{:S(2)}) collective-permute-start(bf16[256,1536]{1,0:T(8,128)(2,1)} %get-tuple-element.498), channel_id=1, source_target_pairs={{0,8},{4,12},{8,0},{12,4},{16,24},{20,28},{24,16},{28,20},{1,9},{5... | collective-permute-start | bytes 2359304 | tf_op jit(solution)/shard_map/ppermute | solution.py:885
  355.1 16.7 %collective-permute-start.53 = (bf16[32,3072]{1,0:T(8,128)(2,1)S(1)}, bf16[32,3072]{1,0:T(8,128)(2,1)S(1)}, u32[]{:S(2)}, u32[]{:S(2)}) collective-permute-start(bf16[32,3072]{1,0:T(8,128)(2,1)S(1)} %get-tuple-element.531), channel_id=1, source_target_pairs={{0,2},{1,3},{2,0},{3,1},{4,6},{5,7},{6,4},{7,5},{8,10},{9,11},{10,... | collective-permute-start | bytes 589832 | tf_op jit(solution)/shard_map/ppermute | solution.py:888
  (71 other events, 795.7 us)
Sparse Core Ops, SparseCore 0:
  69.8 33.1 all-gather.1
  246.7 32.0 reduce-scatter.1

commit v5 on v4

--- a/solution.py
+++ b/solution.py
@@ -262,6 +262,10 @@
     specs = []
     arrays = []
     for array, block, index in ins:
+        if block is None:
+            arrays.append(pltpu.with_memory_space_constraint(array, pltpu.HBM) if stream else array)
+            specs.append(pl.BlockSpec(memory_space=pl.ANY))
+            continue
         once = tuple(block) == tuple(array.shape)
         if stream and not once:
             array = pltpu.with_memory_space_constraint(array, pltpu.HBM)
@@ -272,7 +276,8 @@
     for _, dtype, block, _ in outs:
         held += 2 * math.prod(block) * jnp.dtype(dtype).itemsize
     for buffer in scratch:
-        held += math.prod(buffer.shape) * jnp.dtype(buffer.dtype).itemsize
+        if len(buffer.shape) > 1:
+            held += math.prod(buffer.shape) * jnp.dtype(buffer.dtype).itemsize
     return pl.pallas_call(
         kernel,
         grid_spec=pltpu.PrefetchScalarGridSpec(
@@ -358,7 +363,7 @@
         (columns // 512,),
         where,
         [whole(low), first_columns(pack, depth), (mats[0], *tile), (mats[1], *tile), (bias, (1, 512), column)],
-        [((rows, columns), bf16, (rows, 512), column)], micros=8)[0]
+        [((rows, columns), bf16, (rows, 512), column)], micros=8, sent=(0,))[0]
 
 
 def branch_kernel(
@@ -429,6 +434,7 @@
         ],
         [((rows, columns // 2), bf16, (rows, tile), column)] * 2,
         micros=7,
+        sent=(0, 1),
     )
 
 
@@ -466,43 +472,47 @@
     )
 
 
-def back_product(grad, mat):
-    if len(grad.shape) == 2:
-        return dot(grad[...], mat[...], NT)
-    cols = grad.shape[2]
-    return sum(dot(grad[i], mat[:, i * cols : (i + 1) * cols], NT) for i in range(3))
-
-
-def back_kernel(low, where, grad_ref, mat_low, mat_high, values_ref, above_ref, gain_ref, *rest):
+def back_kernel(low, where, grad_ref, mat_low, mat_high, values_any, above_any, gain_ref, *rest):
+    *rest, total, values_ref, above_ref, sems = rest
     if low:
-        (out_low, out_high), rest = rest[:2], rest[2:]
-        out_ref, low_ref, low_sum, gain_sum, bias_sum, mixed_ref, total = rest
+        out_low, out_high, out_ref, low_ref, low_sum, gain_sum, bias_sum, mixed_ref = rest
     else:
-        *vectors, out_ref, packed, total = rest
+        *vectors, out_ref, packed = rest
     step = pl.program_id(0)
-
-    def put(mat):
-        part = back_product(grad_ref, mat)
-        for side in range(2):
-            total[:, lanes(where, 2 * step + side)] = part[:, side * 128 : (side + 1) * 128]
-
-    @pl.when(step < 2)
+    fetches = [
+        pltpu.make_async_copy(values_any, values_ref, sems.at[0]),
+        pltpu.make_async_copy(above_any, above_ref, sems.at[1]),
+    ]
+
+    @pl.when(step == 0)
     def _():
-        put(mat_low)
-
-    @pl.when(step >= 2)
+        for fetch in fetches:
+            fetch.start()
+
+    half = mat_low.shape[0]
+    for side, mat in enumerate((mat_low, mat_high)):
+        cols = slice(side * half, (side + 1) * half)
+        part = dot(grad_ref[...], mat[...], NT)
+
+        @pl.when(step == 0)
+        def _(cols=cols, part=part):
+            total[:, cols] = part
+
+        @pl.when(step > 0)
+        def _(cols=cols, part=part):
+            total[:, cols] += part
+
+    @pl.when(step == pl.num_programs(0) - 1)
     def _():
-        put(mat_high)
-
-    @pl.when(step == 3)
-    def _():
+        for fetch in fetches:
+            fetch.wait()
         count, width = values_ref.shape
         chunk = 64
         sums = [jnp.zeros((1, width), f32)] * 3
         for first in range(0, count, chunk):
             rows = slice(first, first + chunk)
             normed, inverse = normalize(values_ref[rows, :].astype(f32))
-            grad = total[rows, :]
+            grad = jnp.concatenate([total[rows, lanes(where, 8 + block)] for block in range(8)], 1)
             scaled = grad * gain_ref[...]
             result = above_ref[rows, :].astype(f32) + inverse * (
                 scaled
@@ -540,30 +550,44 @@
 def back(where, grad, mats, values, above, gain, vectors=(), owners=0):
     low = not vectors
     rows, width = values.shape
-    columns = grad.shape[1] if grad.ndim == 2 else 3 * width
+    depth = mats[0].shape[0]
+    tile = 1024
     outs = [whole_out((rows, width), f32)]
     if low:
+        steps = grad.shape[1] // tile
+        grad_block = (grad, (rows, tile), column)
         outs += [whole_out((rows, width), bf16)] + [whole_out((1, width), f32)] * 3
         outs += [whole_out((rows, width), bf16)]
     else:
+        steps = grad.shape[0]
+        grad_block = (grad, (None, rows, tile), lambda i, _: (i, 0, 0))
         columns_packed = (2 * width + sum(v.shape[1] for v in vectors)) // owners
         outs += [whole_out((owners, columns_packed), f32)]
     return call(
         functools.partial(back_kernel, low),
-        (4,),
+        (steps,),
         where,
         [
-            whole(grad) if grad.ndim == 2 else (grad, (3, rows, width), lambda *_: (0, 0, 0)),
-            (mats[0], (256, columns), lambda i, _: (jnp.minimum(i, 1), 0)),
-            (mats[1], (256, columns), lambda i, _: (jnp.maximum(i - 2, 0), 0)),
-            whole(values),
-            whole(above),
+            grad_block,
+            (mats[0], (depth, tile), column),
+            (mats[1], (depth, tile), column),
+            (values, None, None),
+            (above, None, None),
             whole(gain),
             *[last_columns(m, width) for m in mats if low],
             *[whole(v) for v in vectors],
         ],
         outs,
-        [pltpu.VMEM((rows, width), f32)], micros=13, sent=(0,) if low else ())
+        [
+            pltpu.VMEM((rows, width), f32),
+            pltpu.VMEM((rows, width), values.dtype),
+            pltpu.VMEM((rows, width), above.dtype),
+            pltpu.SemaphoreType.DMA((2,)),
+        ],
+        micros=13 if low else 0.005,
+        stream=not low,
+        sent=(0, 1) if low else (),
+    )
 
 
 def feed_kernel(where, low_ref, high_ref, mat_low, mat_high, middle_ref, shift_ref, keep_ref, out_ref):
@@ -701,7 +725,9 @@
         block = ((rows, tile), column)
         half = ((rows // 2, columns), bf16, (rows // 2, tile), column)
         return call(
-            add_kernel, (columns // tile,), self.where, [(v, *block) for v in pieces], [half] * 4, stream=True)
+            add_kernel, (columns // tile,), self.where, [(v, *block) for v in pieces], [half] * 4, stream=True,
+            micros=3 if self.flat else 0.005,
+        )
 
     def finish(self, *pieces):
         rows, columns = pieces[0].shape
@@ -717,6 +743,7 @@
             [whole(v) for v in pieces],
             [whole_out(share, f32)] + [whole_out(share, bf16)] * (owners - 1),
             [pltpu.VMEM((rows, 2 * columns), f32)],
+            micros=0.002,
         )
 
     def work(self):
@@ -1010,7 +1037,7 @@
         swap, along, order, where,
         [((two_low, 0), (two_other, 1)), ((mix_low, 0), (two_other, 0))],
         [((grad_pre, 0), (pre_other, 0)), ((grad_branch, 0), (branch_other, 0))],
-        512, [grad_pre.shape[1] // 512, width // 512],
+        512, [grad_pre.shape[1] // 512, width // 512], True,
     )
     up_sum.work()
     up_sum.send()
@@ -1033,9 +1060,9 @@
         512, [3 * width // 512],
     )
     qkv_sum.work()
+    qkv_sum.send()
     up_sum.work()
-    qkv_sum.send()
-    up_sum.send((2,))
+    up_sum.send()
     sums = [
         jnp.concatenate([sum_q, sum_v], 1),
         out_bias_grad,
@@ -1048,22 +1075,27 @@
         lambda g, x, above, m0, m1, *v: back(where, g, (m0, m1), x, above, g1, v, device_count),
         grad_projected, inputs, grad_middle, *qkv.mats, *sums,
     )
-    up_sum.meet()
     qkv_sum.work()
     qkv_sum.send()
-    up_sum.send((1, 3))
     shares = order.tie(shares.reshape(2, 2, 2, fsdp_size, -1))[0]
-    for axis, bit in ((2, CORE), (1, XBIT), (0, YBIT)):
+
+    def halve(shares, axis, bit):
         low, high = (lax.index_in_dim(shares, side, axis, keepdims=False) for side in range(2))
         upper = me & bit > 0
-        shares = jnp.where(upper, high, low) + swap(jnp.where(upper, low, high), bit)
+        return jnp.where(upper, high, low), jnp.where(upper, low, high)
+
+    mine, other = halve(shares, 2, CORE)
+    mine, other = halve(mine + swap(other, CORE), 1, XBIT)
     up_sum.meet()
-    (shares,) = order.tie(shares)
-    order.last = (shares,)
+    mine, other = order.tie(mine, other)
+    order.last = (mine,)
     qkv_sum.work()
     qkv_sum.send((1, 2, 3))
+    shares = mine + swap(order.tie(other)[0], XBIT)
     qkv_sum.shares[0], shares = order.tie(qkv_sum.shares[0], shares)
     order.last = (qkv_sum.shares[0],)
+    mine, other = halve(shares, 0, YBIT)
+    shares = mine + swap(other, YBIT)
 
     def row_of(by):
         return lax.dynamic_slice(shares, ((line + by) % fsdp_size, 0), (1, shares.shape[1]))

time: 388 us -> 384 us (0.990)
    reduce_scatter x1 -> x2, waiting for transfers between devices: 2.68 us -> 11.7 us  [send(): lax.psum_scatter(self.order.tie(self.own)[0], 'fsdp', scatter_dimension=0...]
    ppermute x40, waiting for transfers between devices: 48.3 us -> 40.4 us  [swap(): return lax.ppermute(value, 'dp', [(i, i ^ bit) for i in range(8)])]
    ppermute x15 -> x12, starting transfers between devices: 31 us -> 28.4 us  [along(): lax.ppermute(value, 'fsdp', [(i, (i + by) % fsdp_size) for i in range(fsd...]
    ppermute x15 -> x12, waiting for transfers between devices: 27.6 us -> 26.1 us  [along(): lax.ppermute(value, 'fsdp', [(i, (i + by) % fsdp_size) for i in range(fsd...]
  transfers between devices with their start and end apart: 57 -> 55, of which waited for: 24 -> 26; matrix products, arithmetic and copies ran while one was open for 4% -> 3% of each run, Pallas kernels for 40% -> 41%
where the time goes in v5:
time: 384 us; the launch traced here: 380 us
  Pallas kernels  195 us (51%)
  waiting for transfers between devices  80 us (21%)
  starting transfers between devices  65.3 us (17%)
  local copies, waits for them, and re-layouts  16 us (4%)
  between operations  14.8 us (4%)
  other arithmetic  8.72 us (2%)
    pallas_call x25, Pallas kernels, call(): pl.pallas_call(kernel, grid_spec=pltpu.PrefetchScalarGridSpec(num_scalar_...  156 us
    ppermute x40, waiting for transfers between devices, swap(): return lax.ppermute(value, 'dp', [(i, i ^ bit) for i in range(8)])  40.4 us
    ppermute x40, starting transfers between devices, swap(): return lax.ppermute(value, 'dp', [(i, i ^ bit) for i in range(8)])  36.7 us
    ppermute x12, starting transfers between devices, along(): lax.ppermute(value, 'fsdp', [(i, (i + by) % fsdp_size) for i in range(fsd...  28.4 us
    ppermute x12, waiting for transfers between devices, along(): lax.ppermute(value, 'fsdp', [(i, (i + by) % fsdp_size) for i in range(fsd...  26.1 us
    pallas_call x2, Pallas kernels, attention_forward(): pl.pallas_call(functools.partial(attention_forward_kernel, seqs, length),...  20.5 us
    pallas_call x1, Pallas kernels, attention_backward(): pl.pallas_call(functools.partial(attention_backward_kernel, seqs, length)...  18.4 us
    reduce_scatter x2, waiting for transfers between devices, send(): lax.psum_scatter(self.order.tie(self.own)[0], 'fsdp', scatter_dimension=0...  11.7 us
  transfers between devices with their start and end apart: 55, of which 26 were waited for; matrix products, arithmetic and copies ran while one was open for 3% of the time, Pallas kernels for 41%

profile of v5, /device:TPU:0, one launch (start us, length us, event | category | flops | bytes accessed | tf_op | source)
XLA Modules:
  0.0 379.8 jit_solution(9824582104290145621)
XLA Ops:
  20.6 8.3 %collective-permute-done.1.refs_2_ = bf16[32,3328]{1,0:T(8,128)(2,1)S(1)} collective-permute-done((bf16[32,3328]{1,0:T(8,128)(2,1)S(1)}, bf16[32,3328]{1,0:T(8,128)(2,1)S(1)}, u32[]{:S(2)}, u32[]{:S(2)}) %collective-permute-start.1) | collective-permute-done | bytes 213024 | tf_op jit(solution)/shard_map/ppermute | solution.py:915
  34.8 5.0 %collective-permute-start.9 = (bf16[32,5120]{1,0:T(8,128)(2,1)}, bf16[32,5120]{1,0:T(8,128)(2,1)}, u32[]{:S(2)}, u32[]{:S(2)}) collective-permute-start(bf16[32,5120]{1,0:T(8,128)(2,1)} %pad_maximum_fusion.1.refs_0_), channel_id=1, source_target_pairs={{0,1},{1,2},{2,3},{3,0},{4,5},{5,6},{6,7},{7,4},{8,9},{9,10},{10,1... | collective-permute-start | bytes 983048 | tf_op jit(solution)/shard_map/ppermute | solution.py:915
  42.2 8.2 %collective-permute-done.4.far.refs_2_.refs_6_ = bf16[128,3328]{1,0:T(8,128)(2,1)S(1)} collective-permute-done((bf16[128,3328]{1,0:T(8,128)(2,1)S(1)}, bf16[128,3328]{1,0:T(8,128)(2,1)S(1)}, u32[]{:S(2)}, u32[]{:S(2)}) %collective-permute-start.4) | collective-permute-done | bytes 852000 | tf_op jit(solution)/shard_map/ppermute | solution.py:912
  55.4 6.3 %collective-permute-done.8.refs_2_ = bf16[32,5120]{1,0:T(8,128)(2,1)} collective-permute-done((bf16[32,5120]{1,0:T(8,128)(2,1)}, bf16[32,5120]{1,0:T(8,128)(2,1)}, u32[]{:S(2)}, u32[]{:S(2)}) %collective-permute-start.8) | collective-permute-done | bytes 327712 | tf_op jit(solution)/shard_map/ppermute | solution.py:915
  65.3 3.6 shard_map.257.low.mat_low
  79.8 9.1 %shard_map.260.q_ref.k_ref.v_ref = bf16[640,3072]{1,0:T(8,128)(2,1)} custom-call(s32[20]{0:T(128)S(1)} %stack.90.where, bf16[640,512]{1,0:T(8,128)(2,1)S(1)} %get-tuple-element.462.low_ref.refs_0_, bf16[640,1536]{1,0:T(8,128)(2,1)S(1)} %get-tuple-element.321.high_ref, bf16[512,3328]{1,0:T(8,128)(2,1)} %shard_map.257.low.mat_low, ...), custom_call_target="tpu_custom_call" | custom-call | flops 7999999967232 | bytes 1 | tf_op jit(solution)/shard_map/pallas_call | solution.py:281
  91.0 10.2 %shard_map.261 = (bf16[640,512]{1,0:T(8,128)(2,1)S(1)}, bf16[8,2,320,320]{3,2,1,0:T(8,128)(2,1)}) custom-call(s32[2,320,1]{2,1,0:T(8,128)S(1)} %copy.32.keep_ref, bf16[640,3072]{1,0:T(8,128)(2,1)} %shard_map.260.q_ref.k_ref.v_ref, bf16[640,3072]{1,0:T(8,128)(2,1)} %shard_map.260.q_ref.k_ref.v_ref, bf16[640,3072]{1,0:T(8,128)(2,1)} %shard_map.260.q_ref.k_ref.v_ref), custom_call_target="tpu_custom_call" | custom-call | flops 8499999801344 | bytes 1 | tf_op jit(solution)/shard_map/pallas_call | solution.py:92
  106.0 10.3 %shard_map.262 = (bf16[640,512]{1,0:T(8,128)(2,1)S(1)}, bf16[8,2,320,320]{3,2,1,0:T(8,128)(2,1)}) custom-call(s32[2,320,1]{2,1,0:T(8,128)S(1)} %copy.32.keep_ref, bf16[640,3072]{1,0:T(8,128)(2,1)} %shard_map.260.q_ref.k_ref.v_ref, bf16[640,3072]{1,0:T(8,128)(2,1)} %shard_map.260.q_ref.k_ref.v_ref, bf16[640,3072]{1,0:T(8,128)(2,1)} %shard_map.260.q_ref.k_ref.v_ref), custom_call_target="tpu_custom_call" | custom-call | flops 8499999801344 | bytes 1 | tf_op jit(solution)/shard_map/pallas_call | solution.py:92
  128.7 4.4 %collective-permute-done.18.mat_high.rest_1_ = bf16[512,5120]{1,0:T(8,128)(2,1)S(1)} collective-permute-done((bf16[512,5120]{1,0:T(8,128)(2,1)S(1)}, bf16[512,5120]{1,0:T(8,128)(2,1)S(1)}, u32[]{:S(2)}, u32[]{:S(2)}) %collective-permute-start.18) | collective-permute-done | bytes 5242912 | tf_op jit(solution)/shard_map/ppermute | solution.py:912
  133.1 3.6 shard_map.264
  136.7 6.8 %shard_map.265 = (bf16[640,2048]{1,0:T(8,128)(2,1)}, bf16[640,2048]{1,0:T(8,128)(2,1)}) custom-call(s32[20]{0:T(128)S(1)} %copy-done.11, bf16[640,512]{1,0:T(8,128)(2,1)S(1)} %get-tuple-element.418.low_ref.refs_0_, bf16[640,1024]{1,0:T(8,128)(2,1)S(1)} %get-tuple-element.403.high_ref, bf16[512,5120]{1,0:T(8,128)(2,1)S(1)} %shard_map.263.mat_low.rest_0_, ...), custom_call_target="tpu_custom_call" | custom-call | flops 6999999774720 | bytes 1 | tf_op jit(solution)/shard_map/pallas_call | solution.py:281
  143.6 6.7 %shard_map.266 = (bf16[640,2048]{1,0:T(8,128)(2,1)}, bf16[640,2048]{1,0:T(8,128)(2,1)}) custom-call(s32[20]{0:T(128)S(1)} %copy-done.11, bf16[640,512]{1,0:T(8,128)(2,1)S(1)} %get-tuple-element.418.low_ref.refs_0_, bf16[640,1024]{1,0:T(8,128)(2,1)S(1)} %get-tuple-element.403.high_ref, bf16[512,5120]{1,0:T(8,128)(2,1)S(1)} %shard_map.263.mat_low.rest_0_, ...), custom_call_target="tpu_custom_call" | custom-call | flops 6999999774720 | bytes 1 | tf_op jit(solution)/shard_map/pallas_call | solution.py:281
  157.5 12.1 %shard_map.267 = (bf16[1024,512]{1,0:T(8,128)(2,1)}, bf16[1024,512]{1,0:T(8,128)(2,1)}, bf16[1024,512]{1,0:T(8,128)(2,1)}, bf16[1024,512]{1,0:T(8,128)(2,1)}) custom-call(s32[20]{0:T(128)S(1)} %copy-done.11, bf16[640,2048]{1,0:T(8,128)(2,1)S(1)} %copy-done.3, bf16[640,2048]{1,0:T(8,128)(2,1)S(1)} %collective-permute-done.25.refs_1_, ...), custom_call_target="tpu_custom_call" | custom-call | flops 12000000212992 | bytes 1 | tf_op jit(solution)/shard_map/pallas_call | solution.py:281
  169.6 4.9 %shard_map.268.mat_low = bf16[2048,1024]{1,0:T(8,128)(2,1)} custom-call(s32[20]{0:T(128)S(1)} %copy-done.11, bf16[512,512]{1,0:T(8,128)(2,1)} %get-tuple-element.368.refs_0_, bf16[512,512]{1,0:T(8,128)(2,1)} %collective-permute-done.19.refs_1_, bf16[512,512]{1,0:T(8,128)(2,1)} %collective-permute-done.21.refs_2_, ...), custom_call_target="tpu_custom_call" | custom-call | flops 3999999983616 | bytes 1 | tf_op jit(solution)/shard_map/pallas_call | solution.py:281
  178.3 3.7 collective-permute-done.26.mat_high
  183.3 13.3 %shard_map.269 = (bf16[640,4096]{1,0:T(8,128)(2,1)}, f32[1,4096]{1,0:T(1,128)S(1)}) custom-call(s32[20]{0:T(128)S(1)} %copy-done.11, bf16[640,1024]{1,0:T(8,128)(2,1)S(1)} %copy-done.7, bf16[2048,1024]{1,0:T(8,128)(2,1)} %shard_map.268.mat_low, bf16[2048,1024]{1,0:T(8,128)(2,1)} %collective-permute-done.26.mat_high, ...), custom_call_target="tpu_custom_call" | custom-call | flops 12000000212992 | bytes 1 | tf_op jit(solution)/shard_map/pallas_call | solution.py:281
  196.6 4.2 %collective-permute-done.27.a1 = bf16[1024,512]{1,0:T(8,128)(2,1)} collective-permute-done((bf16[1024,512]{1,0:T(8,128)(2,1)}, bf16[1024,512]{1,0:T(8,128)(2,1)}, u32[]{:S(2)}, u32[]{:S(2)}) %collective-permute-start.27) | collective-permute-done | bytes 1048608 | tf_op jit(solution)/shard_map/ppermute | solution.py:912
  202.1 4.0 %shard_map.270 = (bf16[512,512]{1,0:T(8,128)(2,1)S(1)}, bf16[512,512]{1,0:T(8,128)(2,1)}, bf16[512,512]{1,0:T(8,128)(2,1)S(1)}, bf16[512,512]{1,0:T(8,128)(2,1)}) custom-call(s32[20]{0:T(128)S(1)} %copy-done.11, bf16[1024,512]{1,0:T(8,128)(2,1)} %get-tuple-element.390.a0, bf16[1024,512]{1,0:T(8,128)(2,1)} %collective-permute-done.27.a1, ...), custom_call_target="tpu_custom_call" | custom-call | flops 3000000053248 | bytes 1 | tf_op jit(solution)/shard_map/pallas_call | solution.py:281
  208.1 16.8 %shard_map.271 = (f32[640,1024]{1,0:T(8,128)}, bf16[640,1024]{1,0:T(8,128)(2,1)}, f32[1,1024]{1,0:T(1,128)S(1)}, f32[1,1024]{1,0:T(1,128)S(1)}, f32[1,1024]{1,0:T(1,128)S(1)}, /*index=5*/bf16[640,1024]{1,0:T(8,128)(2,1)S(1)}) custom-call(s32[20]{0:T(128)S(1)} %copy-done.11, bf16[640,4096]{1,0:T(8,128)(2,1)} %get-tuple-element.422.grad_ref.refs_4_, ...), custom_call_target="tpu_custom_call" | custom-call | flops 12999999881216 | bytes 1 | tf_op jit(solution)/shard_map/pallas_call | solution.py:281
  229.9 16.3 %shard_map.273 = (bf16[256,2560]{1,0:T(8,128)(2,1)}, bf16[256,2560]{1,0:T(8,128)(2,1)}, bf16[256,2560]{1,0:T(8,128)(2,1)}, bf16[256,2560]{1,0:T(8,128)(2,1)}) custom-call(s32[20]{0:T(128)S(1)} %copy-done.11, bf16[640,512]{1,0:T(8,128)(2,1)S(1)} %copy-done.31, bf16[640,1024]{1,0:T(8,128)(2,1)} %collective-permute-done.29.refs_1_.refs_3_, ...), custom_call_target="tpu_custom_call" | custom-call | flops 12000000212992 | bytes 1 | tf_op jit(solution)/shard_map/pallas_call | solution.py:281
  249.7 18.4 %shard_map.274 = (bf16[3,640,1024]{2,1,0:T(8,128)(2,1)}, f32[1,1024]{1,0:T(1,128)S(1)}, f32[1,1024]{1,0:T(1,128)S(1)}) custom-call(bf16[8,2,320,320]{3,2,1,0:T(8,128)(2,1)} %get-tuple-element.427.left_ref, bf16[8,2,320,320]{3,2,1,0:T(8,128)(2,1)} %get-tuple-element.428.right_ref, bf16[640,3072]{1,0:T(8,128)(2,1)} %shard_map.260.q_ref.k_ref.v_ref, ...), custom_call_target="tpu_custom_call" | custom-call | flops 21999998992384 | bytes 1 | tf_op jit(solution)/shard_map/pallas_call | solution.py:125
  268.1 10.0 %shard_map.275 = f32[640,1024]{1,0:T(8,128)} custom-call(s32[20]{0:T(128)S(1)} %copy-done.11, bf16[640,2048]{1,0:T(8,128)(2,1)S(1)} %copy-done.4, bf16[640,2048]{1,0:T(8,128)(2,1)S(1)} %copy-done.2, bf16[2048,1024]{1,0:T(8,128)(2,1)} %shard_map.268.mat_low, bf16[2048,1024]{1,0:T(8,128)(2,1)} %collective-permute-done.26.mat_high, f32[640,1024]{1,0:T(8,128)} %copy-done, ...), custom_call_target="tpu_custom_call" | custom-call | flops 2000000000 | bytes 1 | tf_op jit(solution)/shard_map/pallas_call | solution.py:281
  279.2 4.5 %shard_map.276 = (bf16[128,2560]{1,0:T(8,128)(2,1)S(1)}, bf16[128,2560]{1,0:T(8,128)(2,1)}, bf16[128,2560]{1,0:T(8,128)(2,1)S(1)}, bf16[128,2560]{1,0:T(8,128)(2,1)}) custom-call(s32[20]{0:T(128)S(1)} %copy-done.11, bf16[256,2560]{1,0:T(8,128)(2,1)} %get-tuple-element.451.a0, bf16[256,2560]{1,0:T(8,128)(2,1)} %collective-permute-done.34.a1, ...), custom_call_target="tpu_custom_call" | custom-call | flops 3000000053248 | bytes 1 | tf_op jit(solution)/shard_map/pallas_call | solution.py:281
  286.8 3.8 collective-permute-done.38.refs_3_
  290.5 9.8 %shard_map.277 = (bf16[256,1536]{1,0:T(8,128)(2,1)}, bf16[256,1536]{1,0:T(8,128)(2,1)}, bf16[256,1536]{1,0:T(8,128)(2,1)}, bf16[256,1536]{1,0:T(8,128)(2,1)}) custom-call(s32[20]{0:T(128)S(1)} %copy-done.11, bf16[640,512]{1,0:T(8,128)(2,1)S(1)} %copy-done.27, bf16[640,1536]{1,0:T(8,128)(2,1)} %collective-permute-done.17.refs_3_.refs_1_, ...), custom_call_target="tpu_custom_call" | custom-call | flops 12000000212992 | bytes 1 | tf_op jit(solution)/shard_map/pallas_call | solution.py:281
  307.8 12.7 %shard_map.279 = (f32[640,1024]{1,0:T(8,128)}, f32[32,384]{1,0:T(8,128)S(1)}) custom-call(s32[20]{0:T(128)S(1)} %copy-done.11, bf16[3,640,1024]{2,1,0:T(8,128)(2,1)} %get-tuple-element.471.refs_2_.grad_ref, bf16[512,3328]{1,0:T(8,128)(2,1)} %shard_map.257.low.mat_low, bf16[512,3328]{1,0:T(8,128)(2,1)} %collective-permute-done.10.high.mat_high, ...), custom_call_target="tpu_custom_call" | custom-call | flops 5000000000 | bytes 1 | tf_op jit(solution)/shard_map/pallas_call | solution.py:281
  320.6 4.2 %collective-permute-done.39.a1 = bf16[256,1536]{1,0:T(8,128)(2,1)S(1)} collective-permute-done((bf16[256,1536]{1,0:T(8,128)(2,1)}, bf16[256,1536]{1,0:T(8,128)(2,1)S(1)}, u32[]{:S(2)}, u32[]{:S(2)}) %collective-permute-start.39) | collective-permute-done | bytes 786464 | tf_op jit(solution)/shard_map/ppermute | solution.py:912
  330.6 10.5 %reduce-scatter.5.cloned.1.call-done = bf16[32,5120]{1,0:T(8,128)(2,1)} async-done(((bf16[128,5120]{1,0:T(8,128)(2,1)}), bf16[32,5120]{1,0:T(8,128)(2,1)}) %reduce-scatter.5.cloned.1.call-update) | async-done | bytes 327696 | tf_op jit(solution)/shard_map/reduce_scatter | solution.py:772
  342.0 5.3 %collective-permute-start.44 = (bf16[32,3072]{1,0:T(8,128)(2,1)S(1)}, bf16[32,3072]{1,0:T(8,128)(2,1)S(1)}, u32[]{:S(2)}, u32[]{:S(2)}) collective-permute-start(bf16[32,3072]{1,0:T(8,128)(2,1)S(1)} %get-tuple-element.511), channel_id=1, source_target_pairs={{0,1},{1,2},{2,3},{3,0},{4,5},{5,6},{6,7},{7,4},{8,9},{9,10},{10,1... | collective-permute-start | bytes 589832 | tf_op jit(solution)/shard_map/ppermute | solution.py:915
  351.0 4.0 %collective-permute-done.44 = bf16[32,3072]{1,0:T(8,128)(2,1)S(1)} collective-permute-done((bf16[32,3072]{1,0:T(8,128)(2,1)S(1)}, bf16[32,3072]{1,0:T(8,128)(2,1)S(1)}, u32[]{:S(2)}, u32[]{:S(2)}) %collective-permute-start.44) | collective-permute-done | bytes 196640 | tf_op jit(solution)/shard_map/ppermute | solution.py:915
  356.8 5.2 %collective-permute-done.50 = bf16[32,3072]{1,0:T(8,128)(2,1)S(1)} collective-permute-done((bf16[32,3072]{1,0:T(8,128)(2,1)S(1)}, bf16[32,3072]{1,0:T(8,128)(2,1)S(1)}, u32[]{:S(2)}, u32[]{:S(2)}) %collective-permute-start.50) | collective-permute-done | bytes 196640 | tf_op jit(solution)/shard_map/ppermute | solution.py:915
  362.0 4.7 %collective-permute-start.47 = (f32[1,384]{1,0:T(1,128)S(1)}, f32[1,384]{1,0:T(1,128)S(1)}, u32[]{:S(2)}, u32[]{:S(2)}) collective-permute-start(f32[1,384]{1,0:T(1,128)S(1)} %get-tuple-element.532), channel_id=1, source_target_pairs={{0,1},{1,2},{2,3},{3,0},{4,5},{5,6},{6,7},{7,4},{8,9},{9,10},{10,1... | collective-permute-start | bytes 4616 | tf_op jit(solution)/shard_map/ppermute | solution.py:915
  (241 shorter events, 114.2 us)
Async XLA Ops:
  7.2 95.8 %all-gather.2.cloned.1.call-start = ((), (), s32[]{:S(2)}) async-start(), calls=%async_computation.2 | async-start | bytes 1310720 | tf_op jit(solution)/shard_map/all_gather | solution.py:962
  12.4 16.5 %collective-permute-start.1 = (bf16[32,3328]{1,0:T(8,128)(2,1)S(1)}, bf16[32,3328]{1,0:T(8,128)(2,1)S(1)}, u32[]{:S(2)}, u32[]{:S(2)}) collective-permute-start(bf16[32,3328]{1,0:T(8,128)(2,1)S(1)} %fusion.1.refs_0_), channel_id=1, source_target_pairs={{0,2},{1,3},{2,0},{3,1},{4,6},{5,7},{6,4},{7,5},{8,10},{9,11},{10,... | collective-permute-start | bytes 638984 | tf_op jit(solution)/shard_map/ppermute | solution.py:915
  29.6 20.8 %collective-permute-start.4 = (bf16[128,3328]{1,0:T(8,128)(2,1)S(1)}, bf16[128,3328]{1,0:T(8,128)(2,1)S(1)}, u32[]{:S(2)}, u32[]{:S(2)}) collective-permute-start(bf16[128,3328]{1,0:T(8,128)(2,1)S(1)} %shard_map.254.refs_0_.refs_4_), channel_id=1, source_target_pairs={{0,16},{4,20},{8,24},{12,28},{16,0},{20,4},{24,8},{28,12},{1,17},{... | collective-permute-start | bytes 2555912 | tf_op jit(solution)/shard_map/ppermute | solution.py:912
  31.1 20.6 %collective-permute-start.3 = (bf16[128,3328]{1,0:T(8,128)(2,1)S(1)}, bf16[128,3328]{1,0:T(8,128)(2,1)}, u32[]{:S(2)}, u32[]{:S(2)}) collective-permute-start(bf16[128,3328]{1,0:T(8,128)(2,1)S(1)} %shard_map.254.refs_0_.refs_4_), channel_id=1, source_target_pairs={{0,8},{4,12},{8,0},{12,4},{16,24},{20,28},{24,16},{28,20},{1,9},{5... | collective-permute-start | bytes 2555912 | tf_op jit(solution)/shard_map/ppermute | solution.py:912
  34.8 20.6 %collective-permute-start.9 = (bf16[32,5120]{1,0:T(8,128)(2,1)}, bf16[32,5120]{1,0:T(8,128)(2,1)}, u32[]{:S(2)}, u32[]{:S(2)}) collective-permute-start(bf16[32,5120]{1,0:T(8,128)(2,1)} %pad_maximum_fusion.1.refs_0_), channel_id=1, source_target_pairs={{0,1},{1,2},{2,3},{3,0},{4,5},{5,6},{6,7},{7,4},{8,9},{9,10},{10,1... | collective-permute-start | bytes 983048 | tf_op jit(solution)/shard_map/ppermute | solution.py:915
  39.9 21.8 %collective-permute-start.8 = (bf16[32,5120]{1,0:T(8,128)(2,1)}, bf16[32,5120]{1,0:T(8,128)(2,1)}, u32[]{:S(2)}, u32[]{:S(2)}) collective-permute-start(bf16[32,5120]{1,0:T(8,128)(2,1)} %pad_maximum_fusion.1.refs_0_), channel_id=1, source_target_pairs={{0,2},{1,3},{2,0},{3,1},{4,6},{5,7},{6,4},{7,5},{8,10},{9,11},{10,... | collective-permute-start | bytes 983048 | tf_op jit(solution)/shard_map/ppermute | solution.py:915
  41.5 20.2 %collective-permute-start.7 = (bf16[32,5120]{1,0:T(8,128)(2,1)}, bf16[32,5120]{1,0:T(8,128)(2,1)}, u32[]{:S(2)}, u32[]{:S(2)}) collective-permute-start(bf16[32,5120]{1,0:T(8,128)(2,1)} %pad_maximum_fusion.1.refs_0_), channel_id=1, source_target_pairs={{0,3},{1,0},{2,1},{3,2},{4,7},{5,4},{6,5},{7,6},{8,11},{9,8},{10,9... | collective-permute-start | bytes 983048 | tf_op jit(solution)/shard_map/ppermute | solution.py:915
  69.7 209.5 %reduce-scatter.3.cloned.1.call-start = ((), (), s32[]{:S(2)}) async-start(), calls=%async_computation.3 | async-start | bytes 1310720 | tf_op jit(solution)/shard_map/reduce_scatter | solution.py:772
  71.4 31.6 %collective-permute-start.13 = (bf16[128,2560]{1,0:T(8,128)(2,1)}, bf16[128,2560]{1,0:T(8,128)(2,1)}, u32[]{:S(2)}, u32[]{:S(2)}) collective-permute-start(bf16[128,2560]{1,0:T(8,128)(2,1)} %copy-done.22), channel_id=1, source_target_pairs={{0,16},{4,20},{8,24},{12,28},{16,0},{20,4},{24,8},{28,12},{1,17},{... | collective-permute-start | bytes 1966088 | tf_op jit(solution)/shard_map/ppermute | solution.py:912
  71.9 31.1 %collective-permute-start.11 = (bf16[128,2560]{1,0:T(8,128)(2,1)}, bf16[128,2560]{1,0:T(8,128)(2,1)}, u32[]{:S(2)}, u32[]{:S(2)}) collective-permute-start(bf16[128,2560]{1,0:T(8,128)(2,1)} %copy-done.22), channel_id=1, source_target_pairs={{0,8},{4,12},{8,0},{12,4},{16,24},{20,28},{24,16},{28,20},{1,9},{5... | collective-permute-start | bytes 1966088 | tf_op jit(solution)/shard_map/ppermute | solution.py:912
  72.4 30.5 %collective-permute-start.14 = (bf16[128,2560]{1,0:T(8,128)(2,1)}, bf16[128,2560]{1,0:T(8,128)(2,1)}, u32[]{:S(2)}, u32[]{:S(2)}) collective-permute-start(bf16[128,2560]{1,0:T(8,128)(2,1)} %copy-done.24), channel_id=1, source_target_pairs={{0,16},{4,20},{8,24},{12,28},{16,0},{20,4},{24,8},{28,12},{1,17},{... | collective-permute-start | bytes 1966088 | tf_op jit(solution)/shard_map/ppermute | solution.py:912
  73.9 29.2 %collective-permute-start.12 = (bf16[128,2560]{1,0:T(8,128)(2,1)}, bf16[128,2560]{1,0:T(8,128)(2,1)}, u32[]{:S(2)}, u32[]{:S(2)}) collective-permute-start(bf16[128,2560]{1,0:T(8,128)(2,1)} %copy-done.24), channel_id=1, source_target_pairs={{0,8},{4,12},{8,0},{12,4},{16,24},{20,28},{24,16},{28,20},{1,9},{5... | collective-permute-start | bytes 1966088 | tf_op jit(solution)/shard_map/ppermute | solution.py:912
  103.1 17.8 %collective-permute-start.15 = (bf16[128,2560]{1,0:T(8,128)(2,1)}, bf16[128,2560]{1,0:T(8,128)(2,1)}, u32[]{:S(2)}, u32[]{:S(2)}) collective-permute-start(bf16[128,2560]{1,0:T(8,128)(2,1)} %collective-permute-done.11.refs_1_), channel_id=1, source_target_pairs={{0,16},{4,20},{8,24},{12,28},{16,0},{20,4},{24,8},{28,12},{1,17},{... | collective-permute-start | bytes 1966088 | tf_op jit(solution)/shard_map/ppermute | solution.py:912
  124.6 25.7 %collective-permute-start.21 = (bf16[512,512]{1,0:T(8,128)(2,1)}, bf16[512,512]{1,0:T(8,128)(2,1)}, u32[]{:S(2)}, u32[]{:S(2)}) collective-permute-start(bf16[512,512]{1,0:T(8,128)(2,1)} %get-tuple-element.368.refs_0_), channel_id=1, source_target_pairs={{0,16},{4,20},{8,24},{12,28},{16,0},{20,4},{24,8},{28,12},{1,17},{... | collective-permute-start | bytes 1572872 | tf_op jit(solution)/shard_map/ppermute | solution.py:912
  125.2 25.1 %collective-permute-start.19 = (bf16[512,512]{1,0:T(8,128)(2,1)}, bf16[512,512]{1,0:T(8,128)(2,1)}, u32[]{:S(2)}, u32[]{:S(2)}) collective-permute-start(bf16[512,512]{1,0:T(8,128)(2,1)} %get-tuple-element.368.refs_0_), channel_id=1, source_target_pairs={{0,8},{4,12},{8,0},{12,4},{16,24},{20,28},{24,16},{28,20},{1,9},{5... | collective-permute-start | bytes 1572872 | tf_op jit(solution)/shard_map/ppermute | solution.py:912
  126.7 23.9 %collective-permute-start.22 = (bf16[512,512]{1,0:T(8,128)(2,1)}, bf16[512,512]{1,0:T(8,128)(2,1)}, u32[]{:S(2)}, u32[]{:S(2)}) collective-permute-start(bf16[512,512]{1,0:T(8,128)(2,1)} %get-tuple-element.372.refs_4_), channel_id=1, source_target_pairs={{0,16},{4,20},{8,24},{12,28},{16,0},{20,4},{24,8},{28,12},{1,17},{... | collective-permute-start | bytes 1572872 | tf_op jit(solution)/shard_map/ppermute | solution.py:912
  128.2 22.6 %collective-permute-start.20 = (bf16[512,512]{1,0:T(8,128)(2,1)}, bf16[512,512]{1,0:T(8,128)(2,1)}, u32[]{:S(2)}, u32[]{:S(2)}) collective-permute-start(bf16[512,512]{1,0:T(8,128)(2,1)} %get-tuple-element.372.refs_4_), channel_id=1, source_target_pairs={{0,8},{4,12},{8,0},{12,4},{16,24},{20,28},{24,16},{28,20},{1,9},{5... | collective-permute-start | bytes 1572872 | tf_op jit(solution)/shard_map/ppermute | solution.py:912
  150.8 18.7 %collective-permute-start.23 = (bf16[512,512]{1,0:T(8,128)(2,1)}, bf16[512,512]{1,0:T(8,128)(2,1)}, u32[]{:S(2)}, u32[]{:S(2)}) collective-permute-start(bf16[512,512]{1,0:T(8,128)(2,1)} %collective-permute-done.19.refs_1_), channel_id=1, source_target_pairs={{0,16},{4,20},{8,24},{12,28},{16,0},{20,4},{24,8},{28,12},{1,17},{... | collective-permute-start | bytes 1572872 | tf_op jit(solution)/shard_map/ppermute | solution.py:912
  152.3 17.3 %collective-permute-start.24 = (bf16[512,512]{1,0:T(8,128)(2,1)}, bf16[512,512]{1,0:T(8,128)(2,1)}, u32[]{:S(2)}, u32[]{:S(2)}) collective-permute-start(bf16[512,512]{1,0:T(8,128)(2,1)} %collective-permute-done.22.refs_6_), channel_id=1, source_target_pairs={{0,8},{4,12},{8,0},{12,4},{16,24},{20,28},{24,16},{28,20},{1,9},{5... | collective-permute-start | bytes 1572872 | tf_op jit(solution)/shard_map/ppermute | solution.py:912
  174.9 55.0 %collective-permute-start.29 = (bf16[640,1024]{1,0:T(8,128)(2,1)}, bf16[640,1024]{1,0:T(8,128)(2,1)}, u32[]{:S(2)}, u32[]{:S(2)}) collective-permute-start(bf16[640,1024]{1,0:T(8,128)(2,1)} %copy-done.20), channel_id=1, source_target_pairs={{0,4},{4,0},{8,12},{12,8},{16,20},{20,16},{24,28},{28,24},{1,5},{5... | collective-permute-start | bytes 3932168 | tf_op jit(solution)/shard_map/ppermute | solution.py:912
  175.3 25.5 %collective-permute-start.27 = (bf16[1024,512]{1,0:T(8,128)(2,1)}, bf16[1024,512]{1,0:T(8,128)(2,1)}, u32[]{:S(2)}, u32[]{:S(2)}) collective-permute-start(bf16[1024,512]{1,0:T(8,128)(2,1)} %get-tuple-element.387), channel_id=1, source_target_pairs={{0,16},{4,20},{8,24},{12,28},{16,0},{20,4},{24,8},{28,12},{1,17},{... | collective-permute-start | bytes 3145736 | tf_op jit(solution)/shard_map/ppermute | solution.py:912
  176.8 25.2 %collective-permute-start.28 = (bf16[1024,512]{1,0:T(8,128)(2,1)}, bf16[1024,512]{1,0:T(8,128)(2,1)}, u32[]{:S(2)}, u32[]{:S(2)}) collective-permute-start(bf16[1024,512]{1,0:T(8,128)(2,1)} %get-tuple-element.389), channel_id=1, source_target_pairs={{0,8},{4,12},{8,0},{12,4},{16,24},{20,28},{24,16},{28,20},{1,9},{5... | collective-permute-start | bytes 3145736 | tf_op jit(solution)/shard_map/ppermute | solution.py:912
  206.1 20.0 %collective-permute-start.32 = (bf16[512,512]{1,0:T(8,128)(2,1)}, bf16[512,512]{1,0:T(8,128)(2,1)}, u32[]{:S(2)}, u32[]{:S(2)}) collective-permute-start(bf16[512,512]{1,0:T(8,128)(2,1)} %get-tuple-element.411), channel_id=1, source_target_pairs={{0,8},{4,12},{8,0},{12,4},{16,24},{20,28},{24,16},{28,20},{1,9},{5... | collective-permute-start | bytes 1572872 | tf_op jit(solution)/shard_map/ppermute | solution.py:912
  207.6 18.5 %collective-permute-start.33 = (bf16[512,512]{1,0:T(8,128)(2,1)}, bf16[512,512]{1,0:T(8,128)(2,1)}, u32[]{:S(2)}, u32[]{:S(2)}) collective-permute-start(bf16[512,512]{1,0:T(8,128)(2,1)} %get-tuple-element.413), channel_id=1, source_target_pairs={{0,16},{4,20},{8,24},{12,28},{16,0},{20,4},{24,8},{28,12},{1,17},{... | collective-permute-start | bytes 1572872 | tf_op jit(solution)/shard_map/ppermute | solution.py:912
  208.1 17.9 %collective-permute-start.30 = (bf16[640,4096]{1,0:T(8,128)(2,1)}, bf16[640,4096]{1,0:T(8,128)(2,1)}, u32[]{:S(2)}, u32[]{:S(2)}) collective-permute-start(bf16[640,4096]{1,0:T(8,128)(2,1)} %get-tuple-element.422.grad_ref.refs_4_), channel_id=1, source_target_pairs={{0,4},{4,0},{8,12},{12,8},{16,20},{20,16},{24,28},{28,24},{1,5},{5... | collective-permute-start | bytes 15728648 | tf_op jit(solution)/shard_map/ppermute | solution.py:912
  246.2 95.0 %reduce-scatter.5.cloned.1.call-start = ((), (), s32[]{:S(2)}) async-start(), calls=%async_computation.4 | async-start | bytes 1638400 | tf_op jit(solution)/shard_map/reduce_scatter | solution.py:772
  246.2 33.0 %collective-permute-start.34 = (bf16[256,2560]{1,0:T(8,128)(2,1)}, bf16[256,2560]{1,0:T(8,128)(2,1)}, u32[]{:S(2)}, u32[]{:S(2)}) collective-permute-start(bf16[256,2560]{1,0:T(8,128)(2,1)} %get-tuple-element.446), channel_id=1, source_target_pairs={{0,16},{4,20},{8,24},{12,28},{16,0},{20,4},{24,8},{28,12},{1,17},{... | collective-permute-start | bytes 3932168 | tf_op jit(solution)/shard_map/ppermute | solution.py:912
  247.8 31.4 %collective-permute-start.35 = (bf16[256,2560]{1,0:T(8,128)(2,1)}, bf16[256,2560]{1,0:T(8,128)(2,1)}, u32[]{:S(2)}, u32[]{:S(2)}) collective-permute-start(bf16[256,2560]{1,0:T(8,128)(2,1)} %get-tuple-element.448), channel_id=1, source_target_pairs={{0,8},{4,12},{8,0},{12,4},{16,24},{20,28},{24,16},{28,20},{1,9},{5... | collective-permute-start | bytes 3932168 | tf_op jit(solution)/shard_map/ppermute | solution.py:912
  283.8 17.5 %collective-permute-start.36 = (bf16[128,2560]{1,0:T(8,128)(2,1)}, bf16[128,2560]{1,0:T(8,128)(2,1)}, u32[]{:S(2)}, u32[]{:S(2)}) collective-permute-start(bf16[128,2560]{1,0:T(8,128)(2,1)} %get-tuple-element.458), channel_id=1, source_target_pairs={{0,8},{4,12},{8,0},{12,4},{16,24},{20,28},{24,16},{28,20},{1,9},{5... | collective-permute-start | bytes 1966088 | tf_op jit(solution)/shard_map/ppermute | solution.py:912
  285.3 17.1 %collective-permute-start.37 = (bf16[128,2560]{1,0:T(8,128)(2,1)}, bf16[128,2560]{1,0:T(8,128)(2,1)}, u32[]{:S(2)}, u32[]{:S(2)}) collective-permute-start(bf16[128,2560]{1,0:T(8,128)(2,1)} %get-tuple-element.460), channel_id=1, source_target_pairs={{0,16},{4,20},{8,24},{12,28},{16,0},{20,4},{24,8},{28,12},{1,17},{... | collective-permute-start | bytes 1966088 | tf_op jit(solution)/shard_map/ppermute | solution.py:912
  305.7 19.1 %collective-permute-start.39 = (bf16[256,1536]{1,0:T(8,128)(2,1)}, bf16[256,1536]{1,0:T(8,128)(2,1)S(1)}, u32[]{:S(2)}, u32[]{:S(2)}) collective-permute-start(bf16[256,1536]{1,0:T(8,128)(2,1)} %get-tuple-element.485), channel_id=1, source_target_pairs={{0,16},{4,20},{8,24},{12,28},{16,0},{20,4},{24,8},{28,12},{1,17},{... | collective-permute-start | bytes 2359304 | tf_op jit(solution)/shard_map/ppermute | solution.py:912
  307.2 18.6 %collective-permute-start.40 = (bf16[256,1536]{1,0:T(8,128)(2,1)S(1)}, bf16[256,1536]{1,0:T(8,128)(2,1)}, u32[]{:S(2)}, u32[]{:S(2)}) collective-permute-start(bf16[256,1536]{1,0:T(8,128)(2,1)S(1)} %copy-done.44), channel_id=1, source_target_pairs={{0,8},{4,12},{8,0},{12,4},{16,24},{20,28},{24,16},{28,20},{1,9},{5... | collective-permute-start | bytes 2359304 | tf_op jit(solution)/shard_map/ppermute | solution.py:912
  (69 other events, 787.1 us)
Sparse Core Ops, SparseCore 0:
  69.8 33.1 all-gather.1
  246.3 32.8 reduce-scatter.2
  305.8 35.2 reduce-scatter.4

commit v6 on v5

--- a/solution.py
+++ b/solution.py
@@ -119,8 +119,8 @@
     vector = pl.BlockSpec((1, 128), lambda i: (0, i))
     sums = jax.ShapeDtypeStruct((1, width), f32)
     shape = (pair, seqs, length, length)
-    project, left, right = (
-        pltpu.with_memory_space_constraint(v, pltpu.HBM) for v in (project, *probs)
+    project, grad_mixed, left, right = (
+        pltpu.with_memory_space_constraint(v, pltpu.HBM) for v in (project, grad_mixed, *probs)
     )
     return pl.pallas_call(
         functools.partial(attention_backward_kernel, seqs, length),
@@ -346,6 +346,7 @@
             ((rows, width // 2 + width), bf16, (128, width // 2 + width), index),
         ],
         [pltpu.VMEM((128, width), bf16)],
+        sent=(1,),
     )
 
 
@@ -392,7 +393,10 @@
         [(mixed, *block), (inputs, *block), *[last_columns(m, width) for m in mats]]
         + [whole(v) for v in (shift, gain, bias)],
         [part, ((rows, width), f32, *block), part, ((rows, width), bf16, *block)],
-        [pltpu.VMEM((length, width), bf16)], micros=4)
+        [pltpu.VMEM((length, width), bf16)],
+        micros=4,
+        sent=(3,),
+    )
 
 
 def first_columns(mat, count, at=0):
@@ -586,7 +590,7 @@
         ],
         micros=13 if low else 0.005,
         stream=not low,
-        sent=(0, 1) if low else (),
+        sent=(0, 1, 5) if low else (),
     )
 
 
@@ -786,7 +790,7 @@
 
     def total(self):
         if self.flat:
-            return self.order(lambda share: share.astype(f32), self.share)
+            return self.share.astype(f32)
         return self.order(
             lambda own, *others: sum((piece.astype(f32) for piece in others), own), self.own, *self.shares
         )

time: 384 us -> 386 us (level)
    unnamed x92 -> x90, local copies, waits for them, and re-layouts: 9.41 us -> 9.65 us
  transfers between devices with their start and end apart: 55 -> 55, of which waited for: 26 -> 22; matrix products, arithmetic and copies ran while one was open for 3% -> 3% of each run, Pallas kernels for 41% -> 42%
where the time goes in v6:
time: 386 us; the launch traced here: 381 us
  Pallas kernels  197 us (51%)
  waiting for transfers between devices  80.3 us (21%)
  starting transfers between devices  63.9 us (17%)
  local copies, waits for them, and re-layouts  16.2 us (4%)
  between operations  14.8 us (4%)
  other arithmetic  8.7 us (2%)
    pallas_call x25, Pallas kernels, call(): pl.pallas_call(kernel, grid_spec=pltpu.PrefetchScalarGridSpec(num_scalar_...  159 us
    ppermute x40, waiting for transfers between devices, swap(): return lax.ppermute(value, 'dp', [(i, i ^ bit) for i in range(8)])  40.8 us
    ppermute x40, starting transfers between devices, swap(): return lax.ppermute(value, 'dp', [(i, i ^ bit) for i in range(8)])  35.4 us
    ppermute x12, starting transfers between devices, along(): lax.ppermute(value, 'fsdp', [(i, (i + by) % fsdp_size) for i in range(fsd...  28.2 us
    ppermute x12, waiting for transfers between devices, along(): lax.ppermute(value, 'fsdp', [(i, (i + by) % fsdp_size) for i in range(fsd...  25.9 us
    pallas_call x2, Pallas kernels, attention_forward(): pl.pallas_call(functools.partial(attention_forward_kernel, seqs, length),...  20.5 us
    pallas_call x1, Pallas kernels, attention_backward(): pl.pallas_call(functools.partial(attention_backward_kernel, seqs, length)...  18.1 us
    reduce_scatter x2, waiting for transfers between devices, send(): lax.psum_scatter(self.order.tie(self.own)[0], 'fsdp', scatter_dimension=0...  13.5 us
  transfers between devices with their start and end apart: 55, of which 22 were waited for; matrix products, arithmetic and copies ran while one was open for 3% of the time, Pallas kernels for 42%

profile of v6, /device:TPU:0, one launch (start us, length us, event | category | flops | bytes accessed | tf_op | source)
XLA Modules:
  0.0 381.2 jit_solution(6110181056287351038)
XLA Ops:
  20.6 8.3 %collective-permute-done.1.refs_2_ = bf16[32,3328]{1,0:T(8,128)(2,1)S(1)} collective-permute-done((bf16[32,3328]{1,0:T(8,128)(2,1)S(1)}, bf16[32,3328]{1,0:T(8,128)(2,1)S(1)}, u32[]{:S(2)}, u32[]{:S(2)}) %collective-permute-start.1) | collective-permute-done | bytes 213024 | tf_op jit(solution)/shard_map/ppermute | solution.py:919
  34.8 5.0 %collective-permute-start.9 = (bf16[32,5120]{1,0:T(8,128)(2,1)}, bf16[32,5120]{1,0:T(8,128)(2,1)}, u32[]{:S(2)}, u32[]{:S(2)}) collective-permute-start(bf16[32,5120]{1,0:T(8,128)(2,1)} %pad_maximum_fusion.1.refs_0_), channel_id=1, source_target_pairs={{0,1},{1,2},{2,3},{3,0},{4,5},{5,6},{6,7},{7,4},{8,9},{9,10},{10,1... | collective-permute-start | bytes 983048 | tf_op jit(solution)/shard_map/ppermute | solution.py:919
  42.2 8.2 %collective-permute-done.4.far.refs_2_.refs_6_ = bf16[128,3328]{1,0:T(8,128)(2,1)S(1)} collective-permute-done((bf16[128,3328]{1,0:T(8,128)(2,1)S(1)}, bf16[128,3328]{1,0:T(8,128)(2,1)S(1)}, u32[]{:S(2)}, u32[]{:S(2)}) %collective-permute-start.4) | collective-permute-done | bytes 852000 | tf_op jit(solution)/shard_map/ppermute | solution.py:916
  55.4 6.3 %collective-permute-done.8.refs_2_ = bf16[32,5120]{1,0:T(8,128)(2,1)} collective-permute-done((bf16[32,5120]{1,0:T(8,128)(2,1)}, bf16[32,5120]{1,0:T(8,128)(2,1)}, u32[]{:S(2)}, u32[]{:S(2)}) %collective-permute-start.8) | collective-permute-done | bytes 327712 | tf_op jit(solution)/shard_map/ppermute | solution.py:919
  65.3 3.6 shard_map.257.low.mat_low
  77.4 3.8 %shard_map.259 = (bf16[640,512]{1,0:T(8,128)(2,1)S(1)}, bf16[640,1536]{1,0:T(8,128)(2,1)}) custom-call(s32[20]{0:T(128)S(1)} %stack.90.where, bf16[640,1024]{1,0:T(8,128)(2,1)S(1)} %bitcast.59, bf16[640,1024]{1,0:T(8,128)(2,1)S(1)} %get-tuple-element.397.grad_ref.refs_2_.above_any, f32[1,1024]{1,0:T(1,128)S(1)} %get-tuple-element.297.gain_ref, ...), custom_call_target="tpu_custom_call" | custom-call | flops 3000000053248 | bytes 1 | tf_op jit(solution)/shard_map/pallas_call | solution.py:281
  82.8 9.2 %shard_map.260.q_ref.k_ref.v_ref = bf16[640,3072]{1,0:T(8,128)(2,1)} custom-call(s32[20]{0:T(128)S(1)} %stack.90.where, bf16[640,512]{1,0:T(8,128)(2,1)S(1)} %get-tuple-element.460.low_ref.refs_0_, bf16[640,1536]{1,0:T(8,128)(2,1)S(1)} %copy-done.17, bf16[512,3328]{1,0:T(8,128)(2,1)} %shard_map.257.low.mat_low, ...), custom_call_target="tpu_custom_call" | custom-call | flops 7999999967232 | bytes 1 | tf_op jit(solution)/shard_map/pallas_call | solution.py:281
  92.9 10.2 %shard_map.261 = (bf16[640,512]{1,0:T(8,128)(2,1)S(1)}, bf16[8,2,320,320]{3,2,1,0:T(8,128)(2,1)}) custom-call(s32[2,320,1]{2,1,0:T(8,128)S(1)} %copy.32.keep_ref, bf16[640,3072]{1,0:T(8,128)(2,1)} %shard_map.260.q_ref.k_ref.v_ref, bf16[640,3072]{1,0:T(8,128)(2,1)} %shard_map.260.q_ref.k_ref.v_ref, bf16[640,3072]{1,0:T(8,128)(2,1)} %shard_map.260.q_ref.k_ref.v_ref), custom_call_target="tpu_custom_call" | custom-call | flops 8499999801344 | bytes 1 | tf_op jit(solution)/shard_map/pallas_call | solution.py:92
  106.0 10.3 %shard_map.262 = (bf16[640,512]{1,0:T(8,128)(2,1)S(1)}, bf16[8,2,320,320]{3,2,1,0:T(8,128)(2,1)}) custom-call(s32[2,320,1]{2,1,0:T(8,128)S(1)} %copy.32.keep_ref, bf16[640,3072]{1,0:T(8,128)(2,1)} %shard_map.260.q_ref.k_ref.v_ref, bf16[640,3072]{1,0:T(8,128)(2,1)} %shard_map.260.q_ref.k_ref.v_ref, bf16[640,3072]{1,0:T(8,128)(2,1)} %shard_map.260.q_ref.k_ref.v_ref), custom_call_target="tpu_custom_call" | custom-call | flops 8499999801344 | bytes 1 | tf_op jit(solution)/shard_map/pallas_call | solution.py:92
  128.7 4.4 %collective-permute-done.18.mat_high.rest_1_ = bf16[512,5120]{1,0:T(8,128)(2,1)S(1)} collective-permute-done((bf16[512,5120]{1,0:T(8,128)(2,1)S(1)}, bf16[512,5120]{1,0:T(8,128)(2,1)S(1)}, u32[]{:S(2)}, u32[]{:S(2)}) %collective-permute-start.18) | collective-permute-done | bytes 5242912 | tf_op jit(solution)/shard_map/ppermute | solution.py:916
  133.1 4.4 %shard_map.264 = (bf16[640,512]{1,0:T(8,128)(2,1)S(1)}, f32[640,1024]{1,0:T(8,128)S(1)}, bf16[640,512]{1,0:T(8,128)(2,1)S(1)}, bf16[640,1024]{1,0:T(8,128)(2,1)}) custom-call(s32[20]{0:T(128)S(1)} %copy-done.11, bf16[640,1024]{1,0:T(8,128)(2,1)S(1)} %pad_maximum_fusion.mixed_ref, bf16[640,1024]{1,0:T(8,128)(2,1)S(1)} %bitcast.60, ...), custom_call_target="tpu_custom_call" | custom-call | flops 3999999983616 | bytes 1 | tf_op jit(solution)/shard_map/pallas_call | solution.py:281
  139.7 6.8 %shard_map.265 = (bf16[640,2048]{1,0:T(8,128)(2,1)}, bf16[640,2048]{1,0:T(8,128)(2,1)}) custom-call(s32[20]{0:T(128)S(1)} %copy-done.11, bf16[640,512]{1,0:T(8,128)(2,1)S(1)} %get-tuple-element.416.low_ref.refs_0_, bf16[640,1024]{1,0:T(8,128)(2,1)S(1)} %copy-done.20, bf16[512,5120]{1,0:T(8,128)(2,1)S(1)} %shard_map.263.mat_low.rest_0_, ...), custom_call_target="tpu_custom_call" | custom-call | flops 6999999774720 | bytes 1 | tf_op jit(solution)/shard_map/pallas_call | solution.py:281
  146.6 6.7 %shard_map.266 = (bf16[640,2048]{1,0:T(8,128)(2,1)}, bf16[640,2048]{1,0:T(8,128)(2,1)}) custom-call(s32[20]{0:T(128)S(1)} %copy-done.11, bf16[640,512]{1,0:T(8,128)(2,1)S(1)} %get-tuple-element.416.low_ref.refs_0_, bf16[640,1024]{1,0:T(8,128)(2,1)S(1)} %copy-done.21, bf16[512,5120]{1,0:T(8,128)(2,1)S(1)} %shard_map.263.mat_low.rest_0_, ...), custom_call_target="tpu_custom_call" | custom-call | flops 6999999774720 | bytes 1 | tf_op jit(solution)/shard_map/pallas_call | solution.py:281
  160.1 12.1 %shard_map.267 = (bf16[1024,512]{1,0:T(8,128)(2,1)}, bf16[1024,512]{1,0:T(8,128)(2,1)}, bf16[1024,512]{1,0:T(8,128)(2,1)}, bf16[1024,512]{1,0:T(8,128)(2,1)}) custom-call(s32[20]{0:T(128)S(1)} %copy-done.11, bf16[640,2048]{1,0:T(8,128)(2,1)S(1)} %copy-done.3, bf16[640,2048]{1,0:T(8,128)(2,1)S(1)} %collective-permute-done.25.refs_1_, ...), custom_call_target="tpu_custom_call" | custom-call | flops 12000000212992 | bytes 1 | tf_op jit(solution)/shard_map/pallas_call | solution.py:281
  172.2 4.9 %shard_map.268.mat_low = bf16[2048,1024]{1,0:T(8,128)(2,1)} custom-call(s32[20]{0:T(128)S(1)} %copy-done.11, bf16[512,512]{1,0:T(8,128)(2,1)} %get-tuple-element.366.refs_0_, bf16[512,512]{1,0:T(8,128)(2,1)} %collective-permute-done.19.refs_1_, bf16[512,512]{1,0:T(8,128)(2,1)} %collective-permute-done.21.refs_2_, ...), custom_call_target="tpu_custom_call" | custom-call | flops 3999999983616 | bytes 1 | tf_op jit(solution)/shard_map/pallas_call | solution.py:281
  179.9 4.6 %collective-permute-done.26.mat_high = bf16[2048,1024]{1,0:T(8,128)(2,1)} collective-permute-done((bf16[2048,1024]{1,0:T(8,128)(2,1)}, bf16[2048,1024]{1,0:T(8,128)(2,1)}, u32[]{:S(2)}, u32[]{:S(2)}) %collective-permute-start.26) | collective-permute-done | bytes 4194336 | tf_op jit(solution)/shard_map/ppermute | solution.py:916
  185.9 13.3 %shard_map.269 = (bf16[640,4096]{1,0:T(8,128)(2,1)}, f32[1,4096]{1,0:T(1,128)S(1)}) custom-call(s32[20]{0:T(128)S(1)} %copy-done.11, bf16[640,1024]{1,0:T(8,128)(2,1)S(1)} %copy-done.7, bf16[2048,1024]{1,0:T(8,128)(2,1)} %shard_map.268.mat_low, bf16[2048,1024]{1,0:T(8,128)(2,1)} %collective-permute-done.26.mat_high, ...), custom_call_target="tpu_custom_call" | custom-call | flops 12000000212992 | bytes 1 | tf_op jit(solution)/shard_map/pallas_call | solution.py:281
  199.2 4.2 %collective-permute-done.27.a1 = bf16[1024,512]{1,0:T(8,128)(2,1)} collective-permute-done((bf16[1024,512]{1,0:T(8,128)(2,1)}, bf16[1024,512]{1,0:T(8,128)(2,1)}, u32[]{:S(2)}, u32[]{:S(2)}) %collective-permute-start.27) | collective-permute-done | bytes 1048608 | tf_op jit(solution)/shard_map/ppermute | solution.py:916
  204.1 4.0 %shard_map.270 = (bf16[512,512]{1,0:T(8,128)(2,1)S(1)}, bf16[512,512]{1,0:T(8,128)(2,1)}, bf16[512,512]{1,0:T(8,128)(2,1)S(1)}, bf16[512,512]{1,0:T(8,128)(2,1)}) custom-call(s32[20]{0:T(128)S(1)} %copy-done.11, bf16[1024,512]{1,0:T(8,128)(2,1)} %get-tuple-element.388.a0, bf16[1024,512]{1,0:T(8,128)(2,1)} %collective-permute-done.27.a1, ...), custom_call_target="tpu_custom_call" | custom-call | flops 3000000053248 | bytes 1 | tf_op jit(solution)/shard_map/pallas_call | solution.py:281
  210.7 17.2 %shard_map.271 = (f32[640,1024]{1,0:T(8,128)}, bf16[640,1024]{1,0:T(8,128)(2,1)}, f32[1,1024]{1,0:T(1,128)S(1)}, f32[1,1024]{1,0:T(1,128)S(1)}, f32[1,1024]{1,0:T(1,128)S(1)}, /*index=5*/bf16[640,1024]{1,0:T(8,128)(2,1)}) custom-call(s32[20]{0:T(128)S(1)} %copy-done.11, bf16[640,4096]{1,0:T(8,128)(2,1)} %get-tuple-element.420.grad_ref.refs_4_, ...), custom_call_target="tpu_custom_call" | custom-call | flops 12999999881216 | bytes 1 | tf_op jit(solution)/shard_map/pallas_call | solution.py:281
  231.8 16.3 %shard_map.273 = (bf16[256,2560]{1,0:T(8,128)(2,1)}, bf16[256,2560]{1,0:T(8,128)(2,1)}, bf16[256,2560]{1,0:T(8,128)(2,1)}, bf16[256,2560]{1,0:T(8,128)(2,1)}) custom-call(s32[20]{0:T(128)S(1)} %copy-done.11, bf16[640,512]{1,0:T(8,128)(2,1)S(1)} %copy-done.32, bf16[640,1024]{1,0:T(8,128)(2,1)} %collective-permute-done.29.refs_1_.refs_3_, ...), custom_call_target="tpu_custom_call" | custom-call | flops 12000000212992 | bytes 1 | tf_op jit(solution)/shard_map/pallas_call | solution.py:281
  249.8 18.1 %shard_map.274 = (bf16[3,640,1024]{2,1,0:T(8,128)(2,1)}, f32[1,1024]{1,0:T(1,128)S(1)}, f32[1,1024]{1,0:T(1,128)S(1)}) custom-call(bf16[8,2,320,320]{3,2,1,0:T(8,128)(2,1)} %get-tuple-element.425.left_ref, bf16[8,2,320,320]{3,2,1,0:T(8,128)(2,1)} %get-tuple-element.426.right_ref, bf16[640,3072]{1,0:T(8,128)(2,1)} %shard_map.260.q_ref.k_ref.v_ref, ...), custom_call_target="tpu_custom_call" | custom-call | flops 21999998992384 | bytes 1 | tf_op jit(solution)/shard_map/pallas_call | solution.py:125
  267.9 10.0 %shard_map.275 = f32[640,1024]{1,0:T(8,128)} custom-call(s32[20]{0:T(128)S(1)} %copy-done.11, bf16[640,2048]{1,0:T(8,128)(2,1)S(1)} %copy-done.4, bf16[640,2048]{1,0:T(8,128)(2,1)S(1)} %copy-done.2, bf16[2048,1024]{1,0:T(8,128)(2,1)} %shard_map.268.mat_low, bf16[2048,1024]{1,0:T(8,128)(2,1)} %collective-permute-done.26.mat_high, f32[640,1024]{1,0:T(8,128)} %copy-done, ...), custom_call_target="tpu_custom_call" | custom-call | flops 2000000000 | bytes 1 | tf_op jit(solution)/shard_map/pallas_call | solution.py:281
  280.9 4.5 %shard_map.276 = (bf16[128,2560]{1,0:T(8,128)(2,1)S(1)}, bf16[128,2560]{1,0:T(8,128)(2,1)}, bf16[128,2560]{1,0:T(8,128)(2,1)S(1)}, bf16[128,2560]{1,0:T(8,128)(2,1)}) custom-call(s32[20]{0:T(128)S(1)} %copy-done.11, bf16[256,2560]{1,0:T(8,128)(2,1)} %get-tuple-element.449.a0, bf16[256,2560]{1,0:T(8,128)(2,1)} %collective-permute-done.34.a1, ...), custom_call_target="tpu_custom_call" | custom-call | flops 3000000053248 | bytes 1 | tf_op jit(solution)/shard_map/pallas_call | solution.py:281
  288.4 3.8 collective-permute-done.38.refs_3_
  292.2 9.8 %shard_map.277 = (bf16[256,1536]{1,0:T(8,128)(2,1)}, bf16[256,1536]{1,0:T(8,128)(2,1)}, bf16[256,1536]{1,0:T(8,128)(2,1)}, bf16[256,1536]{1,0:T(8,128)(2,1)}) custom-call(s32[20]{0:T(128)S(1)} %copy-done.11, bf16[640,512]{1,0:T(8,128)(2,1)S(1)} %copy-done.28, bf16[640,1536]{1,0:T(8,128)(2,1)} %collective-permute-done.17.refs_3_.refs_1_, ...), custom_call_target="tpu_custom_call" | custom-call | flops 12000000212992 | bytes 1 | tf_op jit(solution)/shard_map/pallas_call | solution.py:281
  309.5 12.7 %shard_map.279 = (f32[640,1024]{1,0:T(8,128)}, f32[32,384]{1,0:T(8,128)S(1)}) custom-call(s32[20]{0:T(128)S(1)} %copy-done.11, bf16[3,640,1024]{2,1,0:T(8,128)(2,1)} %get-tuple-element.469.refs_2_.grad_ref, bf16[512,3328]{1,0:T(8,128)(2,1)} %shard_map.257.low.mat_low, bf16[512,3328]{1,0:T(8,128)(2,1)} %collective-permute-done.10.high.mat_high, ...), custom_call_target="tpu_custom_call" | custom-call | flops 5000000000 | bytes 1 | tf_op jit(solution)/shard_map/pallas_call | solution.py:281
  322.2 4.2 %collective-permute-done.39.a1 = bf16[256,1536]{1,0:T(8,128)(2,1)S(1)} collective-permute-done((bf16[256,1536]{1,0:T(8,128)(2,1)}, bf16[256,1536]{1,0:T(8,128)(2,1)S(1)}, u32[]{:S(2)}, u32[]{:S(2)}) %collective-permute-start.39) | collective-permute-done | bytes 786464 | tf_op jit(solution)/shard_map/ppermute | solution.py:916
  332.3 10.5 %reduce-scatter.5.cloned.1.call-done = bf16[32,5120]{1,0:T(8,128)(2,1)} async-done(((bf16[128,5120]{1,0:T(8,128)(2,1)}), bf16[32,5120]{1,0:T(8,128)(2,1)}) %reduce-scatter.5.cloned.1.call-update) | async-done | bytes 327696 | tf_op jit(solution)/shard_map/reduce_scatter | solution.py:776
  343.7 5.1 %collective-permute-start.44 = (bf16[32,3072]{1,0:T(8,128)(2,1)S(1)}, bf16[32,3072]{1,0:T(8,128)(2,1)S(1)}, u32[]{:S(2)}, u32[]{:S(2)}) collective-permute-start(bf16[32,3072]{1,0:T(8,128)(2,1)S(1)} %get-tuple-element.509), channel_id=1, source_target_pairs={{0,1},{1,2},{2,3},{3,0},{4,5},{5,6},{6,7},{7,4},{8,9},{9,10},{10,1... | collective-permute-start | bytes 589832 | tf_op jit(solution)/shard_map/ppermute | solution.py:919
  352.4 4.0 %collective-permute-done.44 = bf16[32,3072]{1,0:T(8,128)(2,1)S(1)} collective-permute-done((bf16[32,3072]{1,0:T(8,128)(2,1)S(1)}, bf16[32,3072]{1,0:T(8,128)(2,1)S(1)}, u32[]{:S(2)}, u32[]{:S(2)}) %collective-permute-start.44) | collective-permute-done | bytes 196640 | tf_op jit(solution)/shard_map/ppermute | solution.py:919
  363.5 4.7 %collective-permute-start.47 = (f32[1,384]{1,0:T(1,128)S(1)}, f32[1,384]{1,0:T(1,128)S(1)}, u32[]{:S(2)}, u32[]{:S(2)}) collective-permute-start(f32[1,384]{1,0:T(1,128)S(1)} %get-tuple-element.528), channel_id=1, source_target_pairs={{0,1},{1,2},{2,3},{3,0},{4,5},{5,6},{6,7},{7,4},{8,9},{9,10},{10,1... | collective-permute-start | bytes 4616 | tf_op jit(solution)/shard_map/ppermute | solution.py:919
  (239 shorter events, 115.3 us)
Async XLA Ops:
  7.2 95.9 %all-gather.2.cloned.1.call-start = ((), (), s32[]{:S(2)}) async-start(), calls=%async_computation.2 | async-start | bytes 1310720 | tf_op jit(solution)/shard_map/all_gather | solution.py:966
  12.4 16.5 %collective-permute-start.1 = (bf16[32,3328]{1,0:T(8,128)(2,1)S(1)}, bf16[32,3328]{1,0:T(8,128)(2,1)S(1)}, u32[]{:S(2)}, u32[]{:S(2)}) collective-permute-start(bf16[32,3328]{1,0:T(8,128)(2,1)S(1)} %fusion.1.refs_0_), channel_id=1, source_target_pairs={{0,2},{1,3},{2,0},{3,1},{4,6},{5,7},{6,4},{7,5},{8,10},{9,11},{10,... | collective-permute-start | bytes 638984 | tf_op jit(solution)/shard_map/ppermute | solution.py:919
  29.6 20.8 %collective-permute-start.4 = (bf16[128,3328]{1,0:T(8,128)(2,1)S(1)}, bf16[128,3328]{1,0:T(8,128)(2,1)S(1)}, u32[]{:S(2)}, u32[]{:S(2)}) collective-permute-start(bf16[128,3328]{1,0:T(8,128)(2,1)S(1)} %shard_map.254.refs_0_.refs_4_), channel_id=1, source_target_pairs={{0,16},{4,20},{8,24},{12,28},{16,0},{20,4},{24,8},{28,12},{1,17},{... | collective-permute-start | bytes 2555912 | tf_op jit(solution)/shard_map/ppermute | solution.py:916
  31.1 20.6 %collective-permute-start.3 = (bf16[128,3328]{1,0:T(8,128)(2,1)S(1)}, bf16[128,3328]{1,0:T(8,128)(2,1)}, u32[]{:S(2)}, u32[]{:S(2)}) collective-permute-start(bf16[128,3328]{1,0:T(8,128)(2,1)S(1)} %shard_map.254.refs_0_.refs_4_), channel_id=1, source_target_pairs={{0,8},{4,12},{8,0},{12,4},{16,24},{20,28},{24,16},{28,20},{1,9},{5... | collective-permute-start | bytes 2555912 | tf_op jit(solution)/shard_map/ppermute | solution.py:916
  34.8 20.6 %collective-permute-start.9 = (bf16[32,5120]{1,0:T(8,128)(2,1)}, bf16[32,5120]{1,0:T(8,128)(2,1)}, u32[]{:S(2)}, u32[]{:S(2)}) collective-permute-start(bf16[32,5120]{1,0:T(8,128)(2,1)} %pad_maximum_fusion.1.refs_0_), channel_id=1, source_target_pairs={{0,1},{1,2},{2,3},{3,0},{4,5},{5,6},{6,7},{7,4},{8,9},{9,10},{10,1... | collective-permute-start | bytes 983048 | tf_op jit(solution)/shard_map/ppermute | solution.py:919
  39.9 21.8 %collective-permute-start.8 = (bf16[32,5120]{1,0:T(8,128)(2,1)}, bf16[32,5120]{1,0:T(8,128)(2,1)}, u32[]{:S(2)}, u32[]{:S(2)}) collective-permute-start(bf16[32,5120]{1,0:T(8,128)(2,1)} %pad_maximum_fusion.1.refs_0_), channel_id=1, source_target_pairs={{0,2},{1,3},{2,0},{3,1},{4,6},{5,7},{6,4},{7,5},{8,10},{9,11},{10,... | collective-permute-start | bytes 983048 | tf_op jit(solution)/shard_map/ppermute | solution.py:919
  41.5 20.2 %collective-permute-start.7 = (bf16[32,5120]{1,0:T(8,128)(2,1)}, bf16[32,5120]{1,0:T(8,128)(2,1)}, u32[]{:S(2)}, u32[]{:S(2)}) collective-permute-start(bf16[32,5120]{1,0:T(8,128)(2,1)} %pad_maximum_fusion.1.refs_0_), channel_id=1, source_target_pairs={{0,3},{1,0},{2,1},{3,2},{4,7},{5,4},{6,5},{7,6},{8,11},{9,8},{10,9... | collective-permute-start | bytes 983048 | tf_op jit(solution)/shard_map/ppermute | solution.py:919
  69.7 211.2 %reduce-scatter.3.cloned.1.call-start = ((), (), s32[]{:S(2)}) async-start(), calls=%async_computation.3 | async-start | bytes 1310720 | tf_op jit(solution)/shard_map/reduce_scatter | solution.py:776
  71.4 31.7 %collective-permute-start.13 = (bf16[128,2560]{1,0:T(8,128)(2,1)}, bf16[128,2560]{1,0:T(8,128)(2,1)}, u32[]{:S(2)}, u32[]{:S(2)}) collective-permute-start(bf16[128,2560]{1,0:T(8,128)(2,1)} %copy-done.23), channel_id=1, source_target_pairs={{0,16},{4,20},{8,24},{12,28},{16,0},{20,4},{24,8},{28,12},{1,17},{... | collective-permute-start | bytes 1966088 | tf_op jit(solution)/shard_map/ppermute | solution.py:916
  71.9 31.2 %collective-permute-start.11 = (bf16[128,2560]{1,0:T(8,128)(2,1)}, bf16[128,2560]{1,0:T(8,128)(2,1)}, u32[]{:S(2)}, u32[]{:S(2)}) collective-permute-start(bf16[128,2560]{1,0:T(8,128)(2,1)} %copy-done.23), channel_id=1, source_target_pairs={{0,8},{4,12},{8,0},{12,4},{16,24},{20,28},{24,16},{28,20},{1,9},{5... | collective-permute-start | bytes 1966088 | tf_op jit(solution)/shard_map/ppermute | solution.py:916
  72.4 30.6 %collective-permute-start.14 = (bf16[128,2560]{1,0:T(8,128)(2,1)}, bf16[128,2560]{1,0:T(8,128)(2,1)}, u32[]{:S(2)}, u32[]{:S(2)}) collective-permute-start(bf16[128,2560]{1,0:T(8,128)(2,1)} %copy-done.25), channel_id=1, source_target_pairs={{0,16},{4,20},{8,24},{12,28},{16,0},{20,4},{24,8},{28,12},{1,17},{... | collective-permute-start | bytes 1966088 | tf_op jit(solution)/shard_map/ppermute | solution.py:916
  73.9 29.2 %collective-permute-start.12 = (bf16[128,2560]{1,0:T(8,128)(2,1)}, bf16[128,2560]{1,0:T(8,128)(2,1)}, u32[]{:S(2)}, u32[]{:S(2)}) collective-permute-start(bf16[128,2560]{1,0:T(8,128)(2,1)} %copy-done.25), channel_id=1, source_target_pairs={{0,8},{4,12},{8,0},{12,4},{16,24},{20,28},{24,16},{28,20},{1,9},{5... | collective-permute-start | bytes 1966088 | tf_op jit(solution)/shard_map/ppermute | solution.py:916
  103.1 17.8 %collective-permute-start.15 = (bf16[128,2560]{1,0:T(8,128)(2,1)}, bf16[128,2560]{1,0:T(8,128)(2,1)}, u32[]{:S(2)}, u32[]{:S(2)}) collective-permute-start(bf16[128,2560]{1,0:T(8,128)(2,1)} %collective-permute-done.11.refs_1_), channel_id=1, source_target_pairs={{0,16},{4,20},{8,24},{12,28},{16,0},{20,4},{24,8},{28,12},{1,17},{... | collective-permute-start | bytes 1966088 | tf_op jit(solution)/shard_map/ppermute | solution.py:916
  124.6 28.7 %collective-permute-start.21 = (bf16[512,512]{1,0:T(8,128)(2,1)}, bf16[512,512]{1,0:T(8,128)(2,1)}, u32[]{:S(2)}, u32[]{:S(2)}) collective-permute-start(bf16[512,512]{1,0:T(8,128)(2,1)} %get-tuple-element.366.refs_0_), channel_id=1, source_target_pairs={{0,16},{4,20},{8,24},{12,28},{16,0},{20,4},{24,8},{28,12},{1,17},{... | collective-permute-start | bytes 1572872 | tf_op jit(solution)/shard_map/ppermute | solution.py:916
  125.6 27.7 %collective-permute-start.19 = (bf16[512,512]{1,0:T(8,128)(2,1)}, bf16[512,512]{1,0:T(8,128)(2,1)}, u32[]{:S(2)}, u32[]{:S(2)}) collective-permute-start(bf16[512,512]{1,0:T(8,128)(2,1)} %get-tuple-element.366.refs_0_), channel_id=1, source_target_pairs={{0,8},{4,12},{8,0},{12,4},{16,24},{20,28},{24,16},{28,20},{1,9},{5... | collective-permute-start | bytes 1572872 | tf_op jit(solution)/shard_map/ppermute | solution.py:916
  126.7 26.6 %collective-permute-start.22 = (bf16[512,512]{1,0:T(8,128)(2,1)}, bf16[512,512]{1,0:T(8,128)(2,1)}, u32[]{:S(2)}, u32[]{:S(2)}) collective-permute-start(bf16[512,512]{1,0:T(8,128)(2,1)} %get-tuple-element.370.refs_4_), channel_id=1, source_target_pairs={{0,16},{4,20},{8,24},{12,28},{16,0},{20,4},{24,8},{28,12},{1,17},{... | collective-permute-start | bytes 1572872 | tf_op jit(solution)/shard_map/ppermute | solution.py:916
  128.2 25.2 %collective-permute-start.20 = (bf16[512,512]{1,0:T(8,128)(2,1)}, bf16[512,512]{1,0:T(8,128)(2,1)}, u32[]{:S(2)}, u32[]{:S(2)}) collective-permute-start(bf16[512,512]{1,0:T(8,128)(2,1)} %get-tuple-element.370.refs_4_), channel_id=1, source_target_pairs={{0,8},{4,12},{8,0},{12,4},{16,24},{20,28},{24,16},{28,20},{1,9},{5... | collective-permute-start | bytes 1572872 | tf_op jit(solution)/shard_map/ppermute | solution.py:916
  153.6 18.6 %collective-permute-start.23 = (bf16[512,512]{1,0:T(8,128)(2,1)}, bf16[512,512]{1,0:T(8,128)(2,1)}, u32[]{:S(2)}, u32[]{:S(2)}) collective-permute-start(bf16[512,512]{1,0:T(8,128)(2,1)} %collective-permute-done.19.refs_1_), channel_id=1, source_target_pairs={{0,16},{4,20},{8,24},{12,28},{16,0},{20,4},{24,8},{28,12},{1,17},{... | collective-permute-start | bytes 1572872 | tf_op jit(solution)/shard_map/ppermute | solution.py:916
  154.6 17.6 %collective-permute-start.24 = (bf16[512,512]{1,0:T(8,128)(2,1)}, bf16[512,512]{1,0:T(8,128)(2,1)}, u32[]{:S(2)}, u32[]{:S(2)}) collective-permute-start(bf16[512,512]{1,0:T(8,128)(2,1)} %collective-permute-done.22.refs_6_), channel_id=1, source_target_pairs={{0,8},{4,12},{8,0},{12,4},{16,24},{20,28},{24,16},{28,20},{1,9},{5... | collective-permute-start | bytes 1572872 | tf_op jit(solution)/shard_map/ppermute | solution.py:916
  177.5 54.3 %collective-permute-start.29 = (bf16[640,1024]{1,0:T(8,128)(2,1)}, bf16[640,1024]{1,0:T(8,128)(2,1)}, u32[]{:S(2)}, u32[]{:S(2)}) collective-permute-start(bf16[640,1024]{1,0:T(8,128)(2,1)} %get-tuple-element.401.high_ref), channel_id=1, source_target_pairs={{0,4},{4,0},{8,12},{12,8},{16,20},{20,16},{24,28},{28,24},{1,5},{5... | collective-permute-start | bytes 3932168 | tf_op jit(solution)/shard_map/ppermute | solution.py:916
  177.9 25.5 %collective-permute-start.27 = (bf16[1024,512]{1,0:T(8,128)(2,1)}, bf16[1024,512]{1,0:T(8,128)(2,1)}, u32[]{:S(2)}, u32[]{:S(2)}) collective-permute-start(bf16[1024,512]{1,0:T(8,128)(2,1)} %get-tuple-element.385), channel_id=1, source_target_pairs={{0,16},{4,20},{8,24},{12,28},{16,0},{20,4},{24,8},{28,12},{1,17},{... | collective-permute-start | bytes 3145736 | tf_op jit(solution)/shard_map/ppermute | solution.py:916
  178.9 25.2 %collective-permute-start.28 = (bf16[1024,512]{1,0:T(8,128)(2,1)}, bf16[1024,512]{1,0:T(8,128)(2,1)}, u32[]{:S(2)}, u32[]{:S(2)}) collective-permute-start(bf16[1024,512]{1,0:T(8,128)(2,1)} %get-tuple-element.387), channel_id=1, source_target_pairs={{0,8},{4,12},{8,0},{12,4},{16,24},{20,28},{24,16},{28,20},{1,9},{5... | collective-permute-start | bytes 3145736 | tf_op jit(solution)/shard_map/ppermute | solution.py:916
  208.1 19.8 %collective-permute-start.32 = (bf16[512,512]{1,0:T(8,128)(2,1)}, bf16[512,512]{1,0:T(8,128)(2,1)}, u32[]{:S(2)}, u32[]{:S(2)}) collective-permute-start(bf16[512,512]{1,0:T(8,128)(2,1)} %get-tuple-element.409), channel_id=1, source_target_pairs={{0,8},{4,12},{8,0},{12,4},{16,24},{20,28},{24,16},{28,20},{1,9},{5... | collective-permute-start | bytes 1572872 | tf_op jit(solution)/shard_map/ppermute | solution.py:916
  209.2 18.7 %collective-permute-start.33 = (bf16[512,512]{1,0:T(8,128)(2,1)}, bf16[512,512]{1,0:T(8,128)(2,1)}, u32[]{:S(2)}, u32[]{:S(2)}) collective-permute-start(bf16[512,512]{1,0:T(8,128)(2,1)} %get-tuple-element.411), channel_id=1, source_target_pairs={{0,16},{4,20},{8,24},{12,28},{16,0},{20,4},{24,8},{28,12},{1,17},{... | collective-permute-start | bytes 1572872 | tf_op jit(solution)/shard_map/ppermute | solution.py:916
  210.6 17.3 %collective-permute-start.30 = (bf16[640,4096]{1,0:T(8,128)(2,1)}, bf16[640,4096]{1,0:T(8,128)(2,1)}, u32[]{:S(2)}, u32[]{:S(2)}) collective-permute-start(bf16[640,4096]{1,0:T(8,128)(2,1)} %get-tuple-element.420.grad_ref.refs_4_), channel_id=1, source_target_pairs={{0,4},{4,0},{8,12},{12,8},{16,20},{20,16},{24,28},{28,24},{1,5},{5... | collective-permute-start | bytes 15728648 | tf_op jit(solution)/shard_map/ppermute | solution.py:916
  248.1 94.7 %reduce-scatter.5.cloned.1.call-start = ((), (), s32[]{:S(2)}) async-start(), calls=%async_computation.4 | async-start | bytes 1638400 | tf_op jit(solution)/shard_map/reduce_scatter | solution.py:776
  248.2 32.7 %collective-permute-start.34 = (bf16[256,2560]{1,0:T(8,128)(2,1)}, bf16[256,2560]{1,0:T(8,128)(2,1)}, u32[]{:S(2)}, u32[]{:S(2)}) collective-permute-start(bf16[256,2560]{1,0:T(8,128)(2,1)} %get-tuple-element.444), channel_id=1, source_target_pairs={{0,16},{4,20},{8,24},{12,28},{16,0},{20,4},{24,8},{28,12},{1,17},{... | collective-permute-start | bytes 3932168 | tf_op jit(solution)/shard_map/ppermute | solution.py:916
  248.8 32.0 %collective-permute-start.35 = (bf16[256,2560]{1,0:T(8,128)(2,1)}, bf16[256,2560]{1,0:T(8,128)(2,1)}, u32[]{:S(2)}, u32[]{:S(2)}) collective-permute-start(bf16[256,2560]{1,0:T(8,128)(2,1)} %get-tuple-element.446), channel_id=1, source_target_pairs={{0,8},{4,12},{8,0},{12,4},{16,24},{20,28},{24,16},{28,20},{1,9},{5... | collective-permute-start | bytes 3932168 | tf_op jit(solution)/shard_map/ppermute | solution.py:916
  285.4 17.5 %collective-permute-start.36 = (bf16[128,2560]{1,0:T(8,128)(2,1)}, bf16[128,2560]{1,0:T(8,128)(2,1)}, u32[]{:S(2)}, u32[]{:S(2)}) collective-permute-start(bf16[128,2560]{1,0:T(8,128)(2,1)} %get-tuple-element.456), channel_id=1, source_target_pairs={{0,8},{4,12},{8,0},{12,4},{16,24},{20,28},{24,16},{28,20},{1,9},{5... | collective-permute-start | bytes 1966088 | tf_op jit(solution)/shard_map/ppermute | solution.py:916
  286.9 17.1 %collective-permute-start.37 = (bf16[128,2560]{1,0:T(8,128)(2,1)}, bf16[128,2560]{1,0:T(8,128)(2,1)}, u32[]{:S(2)}, u32[]{:S(2)}) collective-permute-start(bf16[128,2560]{1,0:T(8,128)(2,1)} %get-tuple-element.458), channel_id=1, source_target_pairs={{0,16},{4,20},{8,24},{12,28},{16,0},{20,4},{24,8},{28,12},{1,17},{... | collective-permute-start | bytes 1966088 | tf_op jit(solution)/shard_map/ppermute | solution.py:916
  307.4 19.1 %collective-permute-start.39 = (bf16[256,1536]{1,0:T(8,128)(2,1)}, bf16[256,1536]{1,0:T(8,128)(2,1)S(1)}, u32[]{:S(2)}, u32[]{:S(2)}) collective-permute-start(bf16[256,1536]{1,0:T(8,128)(2,1)} %get-tuple-element.483), channel_id=1, source_target_pairs={{0,16},{4,20},{8,24},{12,28},{16,0},{20,4},{24,8},{28,12},{1,17},{... | collective-permute-start | bytes 2359304 | tf_op jit(solution)/shard_map/ppermute | solution.py:916
  308.9 18.6 %collective-permute-start.40 = (bf16[256,1536]{1,0:T(8,128)(2,1)S(1)}, bf16[256,1536]{1,0:T(8,128)(2,1)}, u32[]{:S(2)}, u32[]{:S(2)}) collective-permute-start(bf16[256,1536]{1,0:T(8,128)(2,1)S(1)} %copy-done.43), channel_id=1, source_target_pairs={{0,8},{4,12},{8,0},{12,4},{16,24},{20,28},{24,16},{28,20},{1,9},{5... | collective-permute-start | bytes 2359304 | tf_op jit(solution)/shard_map/ppermute | solution.py:916
  (68 other events, 787.0 us)
Sparse Core Ops, SparseCore 0:
  69.8 33.1 all-gather.1
  248.2 32.5 reduce-scatter.2
  307.5 35.2 reduce-scatter.4

commit v7 on v6

--- a/solution.py
+++ b/solution.py
@@ -346,7 +346,6 @@
             ((rows, width // 2 + width), bf16, (128, width // 2 + width), index),
         ],
         [pltpu.VMEM((128, width), bf16)],
-        sent=(1,),
     )
 
 
@@ -395,7 +394,6 @@
         [part, ((rows, width), f32, *block), part, ((rows, width), bf16, *block)],
         [pltpu.VMEM((length, width), bf16)],
         micros=4,
-        sent=(3,),
     )
 
 

time: 386 us -> 383 us (level)
    unnamed x90 -> x88, local copies, waits for them, and re-layouts: 9.65 us -> 7.04 us
  transfers between devices with their start and end apart: 55 -> 55, of which waited for: 22 -> 26; matrix products, arithmetic and copies ran while one was open for 3% -> 3% of each run, Pallas kernels for 42% -> 42%
where the time goes in v7:
time: 383 us; the launch traced here: 379 us
  Pallas kernels  195 us (51%)
  waiting for transfers between devices  80.4 us (21%)
  starting transfers between devices  66.1 us (17%)
  between operations  14.8 us (4%)
  local copies, waits for them, and re-layouts  13.6 us (4%)
  other arithmetic  8.72 us (2%)
    pallas_call x25, Pallas kernels, call(): pl.pallas_call(kernel, grid_spec=pltpu.PrefetchScalarGridSpec(num_scalar_...  157 us
    ppermute x40, waiting for transfers between devices, swap(): return lax.ppermute(value, 'dp', [(i, i ^ bit) for i in range(8)])  40.2 us
    ppermute x40, starting transfers between devices, swap(): return lax.ppermute(value, 'dp', [(i, i ^ bit) for i in range(8)])  37.3 us
    ppermute x12, starting transfers between devices, along(): lax.ppermute(value, 'fsdp', [(i, (i + by) % fsdp_size) for i in range(fsd...  28.5 us
    ppermute x12, waiting for transfers between devices, along(): lax.ppermute(value, 'fsdp', [(i, (i + by) % fsdp_size) for i in range(fsd...  25.2 us
    pallas_call x2, Pallas kernels, attention_forward(): pl.pallas_call(functools.partial(attention_forward_kernel, seqs, length),...  20.5 us
    pallas_call x1, Pallas kernels, attention_backward(): pl.pallas_call(functools.partial(attention_backward_kernel, seqs, length)...  18.1 us
    reduce_scatter x2, waiting for transfers between devices, send(): lax.psum_scatter(self.order.tie(self.own)[0], 'fsdp', scatter_dimension=0...  13.3 us
  transfers between devices with their start and end apart: 55, of which 26 were waited for; matrix products, arithmetic and copies ran while one was open for 3% of the time, Pallas kernels for 42%

profile of v7, /device:TPU:0, one launch (start us, length us, event | category | flops | bytes accessed | tf_op | source)
XLA Modules:
  0.0 378.9 jit_solution(3116757563926264721)
XLA Ops:
  20.6 8.3 %collective-permute-done.1.refs_2_ = bf16[32,3328]{1,0:T(8,128)(2,1)S(1)} collective-permute-done((bf16[32,3328]{1,0:T(8,128)(2,1)S(1)}, bf16[32,3328]{1,0:T(8,128)(2,1)S(1)}, u32[]{:S(2)}, u32[]{:S(2)}) %collective-permute-start.1) | collective-permute-done | bytes 213024 | tf_op jit(solution)/shard_map/ppermute | solution.py:917
  34.8 5.0 %collective-permute-start.9 = (bf16[32,5120]{1,0:T(8,128)(2,1)}, bf16[32,5120]{1,0:T(8,128)(2,1)}, u32[]{:S(2)}, u32[]{:S(2)}) collective-permute-start(bf16[32,5120]{1,0:T(8,128)(2,1)} %pad_maximum_fusion.1.refs_0_), channel_id=1, source_target_pairs={{0,1},{1,2},{2,3},{3,0},{4,5},{5,6},{6,7},{7,4},{8,9},{9,10},{10,1... | collective-permute-start | bytes 983048 | tf_op jit(solution)/shard_map/ppermute | solution.py:917
  42.2 8.2 %collective-permute-done.4.far.refs_2_.refs_6_ = bf16[128,3328]{1,0:T(8,128)(2,1)S(1)} collective-permute-done((bf16[128,3328]{1,0:T(8,128)(2,1)S(1)}, bf16[128,3328]{1,0:T(8,128)(2,1)S(1)}, u32[]{:S(2)}, u32[]{:S(2)}) %collective-permute-start.4) | collective-permute-done | bytes 852000 | tf_op jit(solution)/shard_map/ppermute | solution.py:914
  55.4 6.3 %collective-permute-done.8.refs_2_ = bf16[32,5120]{1,0:T(8,128)(2,1)} collective-permute-done((bf16[32,5120]{1,0:T(8,128)(2,1)}, bf16[32,5120]{1,0:T(8,128)(2,1)}, u32[]{:S(2)}, u32[]{:S(2)}) %collective-permute-start.8) | collective-permute-done | bytes 327712 | tf_op jit(solution)/shard_map/ppermute | solution.py:917
  65.3 3.6 shard_map.257.low.mat_low
  79.8 9.2 %shard_map.260.q_ref.k_ref.v_ref = bf16[640,3072]{1,0:T(8,128)(2,1)} custom-call(s32[20]{0:T(128)S(1)} %stack.90.where, bf16[640,512]{1,0:T(8,128)(2,1)S(1)} %get-tuple-element.460.low_ref.refs_0_, bf16[640,1536]{1,0:T(8,128)(2,1)S(1)} %get-tuple-element.319.high_ref, bf16[512,3328]{1,0:T(8,128)(2,1)} %shard_map.257.low.mat_low, ...), custom_call_target="tpu_custom_call" | custom-call | flops 7999999967232 | bytes 1 | tf_op jit(solution)/shard_map/pallas_call | solution.py:281
  91.1 10.2 %shard_map.261 = (bf16[640,512]{1,0:T(8,128)(2,1)S(1)}, bf16[8,2,320,320]{3,2,1,0:T(8,128)(2,1)}) custom-call(s32[2,320,1]{2,1,0:T(8,128)S(1)} %copy.32.keep_ref, bf16[640,3072]{1,0:T(8,128)(2,1)} %shard_map.260.q_ref.k_ref.v_ref, bf16[640,3072]{1,0:T(8,128)(2,1)} %shard_map.260.q_ref.k_ref.v_ref, bf16[640,3072]{1,0:T(8,128)(2,1)} %shard_map.260.q_ref.k_ref.v_ref), custom_call_target="tpu_custom_call" | custom-call | flops 8499999801344 | bytes 1 | tf_op jit(solution)/shard_map/pallas_call | solution.py:92
  106.1 10.3 %shard_map.262 = (bf16[640,512]{1,0:T(8,128)(2,1)S(1)}, bf16[8,2,320,320]{3,2,1,0:T(8,128)(2,1)}) custom-call(s32[2,320,1]{2,1,0:T(8,128)S(1)} %copy.32.keep_ref, bf16[640,3072]{1,0:T(8,128)(2,1)} %shard_map.260.q_ref.k_ref.v_ref, bf16[640,3072]{1,0:T(8,128)(2,1)} %shard_map.260.q_ref.k_ref.v_ref, bf16[640,3072]{1,0:T(8,128)(2,1)} %shard_map.260.q_ref.k_ref.v_ref), custom_call_target="tpu_custom_call" | custom-call | flops 8499999801344 | bytes 1 | tf_op jit(solution)/shard_map/pallas_call | solution.py:92
  117.4 3.5 collective-permute-done.16.refs_7_
  128.7 4.4 %collective-permute-done.18.mat_high.rest_1_ = bf16[512,5120]{1,0:T(8,128)(2,1)S(1)} collective-permute-done((bf16[512,5120]{1,0:T(8,128)(2,1)S(1)}, bf16[512,5120]{1,0:T(8,128)(2,1)S(1)}, u32[]{:S(2)}, u32[]{:S(2)}) %collective-permute-start.18) | collective-permute-done | bytes 5242912 | tf_op jit(solution)/shard_map/ppermute | solution.py:914
  133.1 3.6 shard_map.264
  136.7 6.8 %shard_map.265 = (bf16[640,2048]{1,0:T(8,128)(2,1)}, bf16[640,2048]{1,0:T(8,128)(2,1)}) custom-call(s32[20]{0:T(128)S(1)} %copy-done.11, bf16[640,512]{1,0:T(8,128)(2,1)S(1)} %get-tuple-element.416.low_ref.refs_0_, bf16[640,1024]{1,0:T(8,128)(2,1)S(1)} %get-tuple-element.401.high_ref, bf16[512,5120]{1,0:T(8,128)(2,1)S(1)} %shard_map.263.mat_low.rest_0_, ...), custom_call_target="tpu_custom_call" | custom-call | flops 6999999774720 | bytes 1 | tf_op jit(solution)/shard_map/pallas_call | solution.py:281
  143.6 6.7 %shard_map.266 = (bf16[640,2048]{1,0:T(8,128)(2,1)}, bf16[640,2048]{1,0:T(8,128)(2,1)}) custom-call(s32[20]{0:T(128)S(1)} %copy-done.11, bf16[640,512]{1,0:T(8,128)(2,1)S(1)} %get-tuple-element.416.low_ref.refs_0_, bf16[640,1024]{1,0:T(8,128)(2,1)S(1)} %get-tuple-element.401.high_ref, bf16[512,5120]{1,0:T(8,128)(2,1)S(1)} %shard_map.263.mat_low.rest_0_, ...), custom_call_target="tpu_custom_call" | custom-call | flops 6999999774720 | bytes 1 | tf_op jit(solution)/shard_map/pallas_call | solution.py:281
  157.5 12.1 %shard_map.267 = (bf16[1024,512]{1,0:T(8,128)(2,1)}, bf16[1024,512]{1,0:T(8,128)(2,1)}, bf16[1024,512]{1,0:T(8,128)(2,1)}, bf16[1024,512]{1,0:T(8,128)(2,1)}) custom-call(s32[20]{0:T(128)S(1)} %copy-done.11, bf16[640,2048]{1,0:T(8,128)(2,1)S(1)} %copy-done.3, bf16[640,2048]{1,0:T(8,128)(2,1)S(1)} %collective-permute-done.25.refs_1_, ...), custom_call_target="tpu_custom_call" | custom-call | flops 12000000212992 | bytes 1 | tf_op jit(solution)/shard_map/pallas_call | solution.py:281
  169.6 4.9 %shard_map.268.mat_low = bf16[2048,1024]{1,0:T(8,128)(2,1)} custom-call(s32[20]{0:T(128)S(1)} %copy-done.11, bf16[512,512]{1,0:T(8,128)(2,1)} %get-tuple-element.366.refs_0_, bf16[512,512]{1,0:T(8,128)(2,1)} %collective-permute-done.19.refs_1_, bf16[512,512]{1,0:T(8,128)(2,1)} %collective-permute-done.21.refs_2_, ...), custom_call_target="tpu_custom_call" | custom-call | flops 3999999983616 | bytes 1 | tf_op jit(solution)/shard_map/pallas_call | solution.py:281
  178.3 3.7 collective-permute-done.26.mat_high
  183.3 13.4 %shard_map.269 = (bf16[640,4096]{1,0:T(8,128)(2,1)}, f32[1,4096]{1,0:T(1,128)S(1)}) custom-call(s32[20]{0:T(128)S(1)} %copy-done.11, bf16[640,1024]{1,0:T(8,128)(2,1)S(1)} %copy-done.7, bf16[2048,1024]{1,0:T(8,128)(2,1)} %shard_map.268.mat_low, bf16[2048,1024]{1,0:T(8,128)(2,1)} %collective-permute-done.26.mat_high, ...), custom_call_target="tpu_custom_call" | custom-call | flops 12000000212992 | bytes 1 | tf_op jit(solution)/shard_map/pallas_call | solution.py:281
  196.7 4.2 %collective-permute-done.27.a1 = bf16[1024,512]{1,0:T(8,128)(2,1)} collective-permute-done((bf16[1024,512]{1,0:T(8,128)(2,1)}, bf16[1024,512]{1,0:T(8,128)(2,1)}, u32[]{:S(2)}, u32[]{:S(2)}) %collective-permute-start.27) | collective-permute-done | bytes 1048608 | tf_op jit(solution)/shard_map/ppermute | solution.py:914
  202.0 4.0 %shard_map.270 = (bf16[512,512]{1,0:T(8,128)(2,1)S(1)}, bf16[512,512]{1,0:T(8,128)(2,1)}, bf16[512,512]{1,0:T(8,128)(2,1)S(1)}, bf16[512,512]{1,0:T(8,128)(2,1)}) custom-call(s32[20]{0:T(128)S(1)} %copy-done.11, bf16[1024,512]{1,0:T(8,128)(2,1)} %get-tuple-element.388.a0, bf16[1024,512]{1,0:T(8,128)(2,1)} %collective-permute-done.27.a1, ...), custom_call_target="tpu_custom_call" | custom-call | flops 3000000053248 | bytes 1 | tf_op jit(solution)/shard_map/pallas_call | solution.py:281
  208.1 17.2 %shard_map.271 = (f32[640,1024]{1,0:T(8,128)}, bf16[640,1024]{1,0:T(8,128)(2,1)}, f32[1,1024]{1,0:T(1,128)S(1)}, f32[1,1024]{1,0:T(1,128)S(1)}, f32[1,1024]{1,0:T(1,128)S(1)}, /*index=5*/bf16[640,1024]{1,0:T(8,128)(2,1)}) custom-call(s32[20]{0:T(128)S(1)} %copy-done.11, bf16[640,4096]{1,0:T(8,128)(2,1)} %get-tuple-element.420.grad_ref.refs_4_, ...), custom_call_target="tpu_custom_call" | custom-call | flops 12999999881216 | bytes 1 | tf_op jit(solution)/shard_map/pallas_call | solution.py:281
  229.2 16.3 %shard_map.273 = (bf16[256,2560]{1,0:T(8,128)(2,1)}, bf16[256,2560]{1,0:T(8,128)(2,1)}, bf16[256,2560]{1,0:T(8,128)(2,1)}, bf16[256,2560]{1,0:T(8,128)(2,1)}) custom-call(s32[20]{0:T(128)S(1)} %copy-done.11, bf16[640,512]{1,0:T(8,128)(2,1)S(1)} %copy-done.31, bf16[640,1024]{1,0:T(8,128)(2,1)} %collective-permute-done.29.refs_1_.refs_3_, ...), custom_call_target="tpu_custom_call" | custom-call | flops 12000000212992 | bytes 1 | tf_op jit(solution)/shard_map/pallas_call | solution.py:281
  247.7 18.1 %shard_map.274 = (bf16[3,640,1024]{2,1,0:T(8,128)(2,1)}, f32[1,1024]{1,0:T(1,128)S(1)}, f32[1,1024]{1,0:T(1,128)S(1)}) custom-call(bf16[8,2,320,320]{3,2,1,0:T(8,128)(2,1)} %get-tuple-element.425.left_ref, bf16[8,2,320,320]{3,2,1,0:T(8,128)(2,1)} %get-tuple-element.426.right_ref, bf16[640,3072]{1,0:T(8,128)(2,1)} %shard_map.260.q_ref.k_ref.v_ref, ...), custom_call_target="tpu_custom_call" | custom-call | flops 21999998992384 | bytes 1 | tf_op jit(solution)/shard_map/pallas_call | solution.py:125
  265.8 10.0 %shard_map.275 = f32[640,1024]{1,0:T(8,128)} custom-call(s32[20]{0:T(128)S(1)} %copy-done.11, bf16[640,2048]{1,0:T(8,128)(2,1)S(1)} %copy-done.4, bf16[640,2048]{1,0:T(8,128)(2,1)S(1)} %copy-done.2, bf16[2048,1024]{1,0:T(8,128)(2,1)} %shard_map.268.mat_low, bf16[2048,1024]{1,0:T(8,128)(2,1)} %collective-permute-done.26.mat_high, f32[640,1024]{1,0:T(8,128)} %copy-done, ...), custom_call_target="tpu_custom_call" | custom-call | flops 2000000000 | bytes 1 | tf_op jit(solution)/shard_map/pallas_call | solution.py:281
  278.6 4.5 %shard_map.276 = (bf16[128,2560]{1,0:T(8,128)(2,1)S(1)}, bf16[128,2560]{1,0:T(8,128)(2,1)}, bf16[128,2560]{1,0:T(8,128)(2,1)S(1)}, bf16[128,2560]{1,0:T(8,128)(2,1)}) custom-call(s32[20]{0:T(128)S(1)} %copy-done.11, bf16[256,2560]{1,0:T(8,128)(2,1)} %get-tuple-element.449.a0, bf16[256,2560]{1,0:T(8,128)(2,1)} %collective-permute-done.34.a1, ...), custom_call_target="tpu_custom_call" | custom-call | flops 3000000053248 | bytes 1 | tf_op jit(solution)/shard_map/pallas_call | solution.py:281
  286.2 3.8 collective-permute-done.38.refs_3_
  289.9 9.8 %shard_map.277 = (bf16[256,1536]{1,0:T(8,128)(2,1)}, bf16[256,1536]{1,0:T(8,128)(2,1)}, bf16[256,1536]{1,0:T(8,128)(2,1)}, bf16[256,1536]{1,0:T(8,128)(2,1)}) custom-call(s32[20]{0:T(128)S(1)} %copy-done.11, bf16[640,512]{1,0:T(8,128)(2,1)S(1)} %copy-done.27, bf16[640,1536]{1,0:T(8,128)(2,1)} %collective-permute-done.17.refs_3_.refs_1_, ...), custom_call_target="tpu_custom_call" | custom-call | flops 12000000212992 | bytes 1 | tf_op jit(solution)/shard_map/pallas_call | solution.py:281
  307.3 12.7 %shard_map.279 = (f32[640,1024]{1,0:T(8,128)}, f32[32,384]{1,0:T(8,128)S(1)}) custom-call(s32[20]{0:T(128)S(1)} %copy-done.11, bf16[3,640,1024]{2,1,0:T(8,128)(2,1)} %get-tuple-element.469.refs_2_.grad_ref, bf16[512,3328]{1,0:T(8,128)(2,1)} %shard_map.257.low.mat_low, bf16[512,3328]{1,0:T(8,128)(2,1)} %collective-permute-done.10.high.mat_high, ...), custom_call_target="tpu_custom_call" | custom-call | flops 5000000000 | bytes 1 | tf_op jit(solution)/shard_map/pallas_call | solution.py:281
  320.0 4.2 %collective-permute-done.39.a1 = bf16[256,1536]{1,0:T(8,128)(2,1)S(1)} collective-permute-done((bf16[256,1536]{1,0:T(8,128)(2,1)}, bf16[256,1536]{1,0:T(8,128)(2,1)S(1)}, u32[]{:S(2)}, u32[]{:S(2)}) %collective-permute-start.39) | collective-permute-done | bytes 786464 | tf_op jit(solution)/shard_map/ppermute | solution.py:914
  330.0 10.5 %reduce-scatter.5.cloned.1.call-done = bf16[32,5120]{1,0:T(8,128)(2,1)} async-done(((bf16[128,5120]{1,0:T(8,128)(2,1)}), bf16[32,5120]{1,0:T(8,128)(2,1)}) %reduce-scatter.5.cloned.1.call-update) | async-done | bytes 327696 | tf_op jit(solution)/shard_map/reduce_scatter | solution.py:774
  341.4 4.9 %collective-permute-start.44 = (bf16[32,3072]{1,0:T(8,128)(2,1)S(1)}, bf16[32,3072]{1,0:T(8,128)(2,1)S(1)}, u32[]{:S(2)}, u32[]{:S(2)}) collective-permute-start(bf16[32,3072]{1,0:T(8,128)(2,1)S(1)} %get-tuple-element.509), channel_id=1, source_target_pairs={{0,1},{1,2},{2,3},{3,0},{4,5},{5,6},{6,7},{7,4},{8,9},{9,10},{10,1... | collective-permute-start | bytes 589832 | tf_op jit(solution)/shard_map/ppermute | solution.py:917
  350.2 3.8 %collective-permute-done.44 = bf16[32,3072]{1,0:T(8,128)(2,1)S(1)} collective-permute-done((bf16[32,3072]{1,0:T(8,128)(2,1)S(1)}, bf16[32,3072]{1,0:T(8,128)(2,1)S(1)}, u32[]{:S(2)}, u32[]{:S(2)}) %collective-permute-start.44) | collective-permute-done | bytes 196640 | tf_op jit(solution)/shard_map/ppermute | solution.py:917
  361.1 4.7 %collective-permute-start.47 = (f32[1,384]{1,0:T(1,128)S(1)}, f32[1,384]{1,0:T(1,128)S(1)}, u32[]{:S(2)}, u32[]{:S(2)}) collective-permute-start(f32[1,384]{1,0:T(1,128)S(1)} %get-tuple-element.528), channel_id=1, source_target_pairs={{0,1},{1,2},{2,3},{3,0},{4,5},{5,6},{6,7},{7,4},{8,9},{9,10},{10,1... | collective-permute-start | bytes 4616 | tf_op jit(solution)/shard_map/ppermute | solution.py:917
  (237 shorter events, 115.3 us)
Async XLA Ops:
  7.2 95.8 %all-gather.2.cloned.1.call-start = ((), (), s32[]{:S(2)}) async-start(), calls=%async_computation.2 | async-start | bytes 1310720 | tf_op jit(solution)/shard_map/all_gather | solution.py:964
  12.4 16.5 %collective-permute-start.1 = (bf16[32,3328]{1,0:T(8,128)(2,1)S(1)}, bf16[32,3328]{1,0:T(8,128)(2,1)S(1)}, u32[]{:S(2)}, u32[]{:S(2)}) collective-permute-start(bf16[32,3328]{1,0:T(8,128)(2,1)S(1)} %fusion.1.refs_0_), channel_id=1, source_target_pairs={{0,2},{1,3},{2,0},{3,1},{4,6},{5,7},{6,4},{7,5},{8,10},{9,11},{10,... | collective-permute-start | bytes 638984 | tf_op jit(solution)/shard_map/ppermute | solution.py:917
  29.6 20.8 %collective-permute-start.4 = (bf16[128,3328]{1,0:T(8,128)(2,1)S(1)}, bf16[128,3328]{1,0:T(8,128)(2,1)S(1)}, u32[]{:S(2)}, u32[]{:S(2)}) collective-permute-start(bf16[128,3328]{1,0:T(8,128)(2,1)S(1)} %shard_map.254.refs_0_.refs_4_), channel_id=1, source_target_pairs={{0,16},{4,20},{8,24},{12,28},{16,0},{20,4},{24,8},{28,12},{1,17},{... | collective-permute-start | bytes 2555912 | tf_op jit(solution)/shard_map/ppermute | solution.py:914
  31.1 20.6 %collective-permute-start.3 = (bf16[128,3328]{1,0:T(8,128)(2,1)S(1)}, bf16[128,3328]{1,0:T(8,128)(2,1)}, u32[]{:S(2)}, u32[]{:S(2)}) collective-permute-start(bf16[128,3328]{1,0:T(8,128)(2,1)S(1)} %shard_map.254.refs_0_.refs_4_), channel_id=1, source_target_pairs={{0,8},{4,12},{8,0},{12,4},{16,24},{20,28},{24,16},{28,20},{1,9},{5... | collective-permute-start | bytes 2555912 | tf_op jit(solution)/shard_map/ppermute | solution.py:914
  34.8 20.6 %collective-permute-start.9 = (bf16[32,5120]{1,0:T(8,128)(2,1)}, bf16[32,5120]{1,0:T(8,128)(2,1)}, u32[]{:S(2)}, u32[]{:S(2)}) collective-permute-start(bf16[32,5120]{1,0:T(8,128)(2,1)} %pad_maximum_fusion.1.refs_0_), channel_id=1, source_target_pairs={{0,1},{1,2},{2,3},{3,0},{4,5},{5,6},{6,7},{7,4},{8,9},{9,10},{10,1... | collective-permute-start | bytes 983048 | tf_op jit(solution)/shard_map/ppermute | solution.py:917
  39.9 21.8 %collective-permute-start.8 = (bf16[32,5120]{1,0:T(8,128)(2,1)}, bf16[32,5120]{1,0:T(8,128)(2,1)}, u32[]{:S(2)}, u32[]{:S(2)}) collective-permute-start(bf16[32,5120]{1,0:T(8,128)(2,1)} %pad_maximum_fusion.1.refs_0_), channel_id=1, source_target_pairs={{0,2},{1,3},{2,0},{3,1},{4,6},{5,7},{6,4},{7,5},{8,10},{9,11},{10,... | collective-permute-start | bytes 983048 | tf_op jit(solution)/shard_map/ppermute | solution.py:917
  41.5 20.2 %collective-permute-start.7 = (bf16[32,5120]{1,0:T(8,128)(2,1)}, bf16[32,5120]{1,0:T(8,128)(2,1)}, u32[]{:S(2)}, u32[]{:S(2)}) collective-permute-start(bf16[32,5120]{1,0:T(8,128)(2,1)} %pad_maximum_fusion.1.refs_0_), channel_id=1, source_target_pairs={{0,3},{1,0},{2,1},{3,2},{4,7},{5,4},{6,5},{7,6},{8,11},{9,8},{10,9... | collective-permute-start | bytes 983048 | tf_op jit(solution)/shard_map/ppermute | solution.py:917
  69.7 208.9 %reduce-scatter.3.cloned.1.call-start = ((), (), s32[]{:S(2)}) async-start(), calls=%async_computation.3 | async-start | bytes 1310720 | tf_op jit(solution)/shard_map/reduce_scatter | solution.py:774
  71.4 31.6 %collective-permute-start.13 = (bf16[128,2560]{1,0:T(8,128)(2,1)}, bf16[128,2560]{1,0:T(8,128)(2,1)}, u32[]{:S(2)}, u32[]{:S(2)}) collective-permute-start(bf16[128,2560]{1,0:T(8,128)(2,1)} %copy-done.22), channel_id=1, source_target_pairs={{0,16},{4,20},{8,24},{12,28},{16,0},{20,4},{24,8},{28,12},{1,17},{... | collective-permute-start | bytes 1966088 | tf_op jit(solution)/shard_map/ppermute | solution.py:914
  71.9 31.1 %collective-permute-start.11 = (bf16[128,2560]{1,0:T(8,128)(2,1)}, bf16[128,2560]{1,0:T(8,128)(2,1)}, u32[]{:S(2)}, u32[]{:S(2)}) collective-permute-start(bf16[128,2560]{1,0:T(8,128)(2,1)} %copy-done.22), channel_id=1, source_target_pairs={{0,8},{4,12},{8,0},{12,4},{16,24},{20,28},{24,16},{28,20},{1,9},{5... | collective-permute-start | bytes 1966088 | tf_op jit(solution)/shard_map/ppermute | solution.py:914
  72.5 30.5 %collective-permute-start.14 = (bf16[128,2560]{1,0:T(8,128)(2,1)}, bf16[128,2560]{1,0:T(8,128)(2,1)}, u32[]{:S(2)}, u32[]{:S(2)}) collective-permute-start(bf16[128,2560]{1,0:T(8,128)(2,1)} %copy-done.24), channel_id=1, source_target_pairs={{0,16},{4,20},{8,24},{12,28},{16,0},{20,4},{24,8},{28,12},{1,17},{... | collective-permute-start | bytes 1966088 | tf_op jit(solution)/shard_map/ppermute | solution.py:914
  74.0 29.2 %collective-permute-start.12 = (bf16[128,2560]{1,0:T(8,128)(2,1)}, bf16[128,2560]{1,0:T(8,128)(2,1)}, u32[]{:S(2)}, u32[]{:S(2)}) collective-permute-start(bf16[128,2560]{1,0:T(8,128)(2,1)} %copy-done.24), channel_id=1, source_target_pairs={{0,8},{4,12},{8,0},{12,4},{16,24},{20,28},{24,16},{28,20},{1,9},{5... | collective-permute-start | bytes 1966088 | tf_op jit(solution)/shard_map/ppermute | solution.py:914
  103.1 17.8 %collective-permute-start.15 = (bf16[128,2560]{1,0:T(8,128)(2,1)}, bf16[128,2560]{1,0:T(8,128)(2,1)}, u32[]{:S(2)}, u32[]{:S(2)}) collective-permute-start(bf16[128,2560]{1,0:T(8,128)(2,1)} %collective-permute-done.11.refs_1_), channel_id=1, source_target_pairs={{0,16},{4,20},{8,24},{12,28},{16,0},{20,4},{24,8},{28,12},{1,17},{... | collective-permute-start | bytes 1966088 | tf_op jit(solution)/shard_map/ppermute | solution.py:914
  124.6 25.7 %collective-permute-start.21 = (bf16[512,512]{1,0:T(8,128)(2,1)}, bf16[512,512]{1,0:T(8,128)(2,1)}, u32[]{:S(2)}, u32[]{:S(2)}) collective-permute-start(bf16[512,512]{1,0:T(8,128)(2,1)} %get-tuple-element.366.refs_0_), channel_id=1, source_target_pairs={{0,16},{4,20},{8,24},{12,28},{16,0},{20,4},{24,8},{28,12},{1,17},{... | collective-permute-start | bytes 1572872 | tf_op jit(solution)/shard_map/ppermute | solution.py:914
  125.2 25.1 %collective-permute-start.19 = (bf16[512,512]{1,0:T(8,128)(2,1)}, bf16[512,512]{1,0:T(8,128)(2,1)}, u32[]{:S(2)}, u32[]{:S(2)}) collective-permute-start(bf16[512,512]{1,0:T(8,128)(2,1)} %get-tuple-element.366.refs_0_), channel_id=1, source_target_pairs={{0,8},{4,12},{8,0},{12,4},{16,24},{20,28},{24,16},{28,20},{1,9},{5... | collective-permute-start | bytes 1572872 | tf_op jit(solution)/shard_map/ppermute | solution.py:914
  126.7 23.9 %collective-permute-start.22 = (bf16[512,512]{1,0:T(8,128)(2,1)}, bf16[512,512]{1,0:T(8,128)(2,1)}, u32[]{:S(2)}, u32[]{:S(2)}) collective-permute-start(bf16[512,512]{1,0:T(8,128)(2,1)} %get-tuple-element.370.refs_4_), channel_id=1, source_target_pairs={{0,16},{4,20},{8,24},{12,28},{16,0},{20,4},{24,8},{28,12},{1,17},{... | collective-permute-start | bytes 1572872 | tf_op jit(solution)/shard_map/ppermute | solution.py:914
  128.2 22.6 %collective-permute-start.20 = (bf16[512,512]{1,0:T(8,128)(2,1)}, bf16[512,512]{1,0:T(8,128)(2,1)}, u32[]{:S(2)}, u32[]{:S(2)}) collective-permute-start(bf16[512,512]{1,0:T(8,128)(2,1)} %get-tuple-element.370.refs_4_), channel_id=1, source_target_pairs={{0,8},{4,12},{8,0},{12,4},{16,24},{20,28},{24,16},{28,20},{1,9},{5... | collective-permute-start | bytes 1572872 | tf_op jit(solution)/shard_map/ppermute | solution.py:914
  150.8 18.7 %collective-permute-start.23 = (bf16[512,512]{1,0:T(8,128)(2,1)}, bf16[512,512]{1,0:T(8,128)(2,1)}, u32[]{:S(2)}, u32[]{:S(2)}) collective-permute-start(bf16[512,512]{1,0:T(8,128)(2,1)} %collective-permute-done.19.refs_1_), channel_id=1, source_target_pairs={{0,16},{4,20},{8,24},{12,28},{16,0},{20,4},{24,8},{28,12},{1,17},{... | collective-permute-start | bytes 1572872 | tf_op jit(solution)/shard_map/ppermute | solution.py:914
  152.3 17.2 %collective-permute-start.24 = (bf16[512,512]{1,0:T(8,128)(2,1)}, bf16[512,512]{1,0:T(8,128)(2,1)}, u32[]{:S(2)}, u32[]{:S(2)}) collective-permute-start(bf16[512,512]{1,0:T(8,128)(2,1)} %collective-permute-done.22.refs_6_), channel_id=1, source_target_pairs={{0,8},{4,12},{8,0},{12,4},{16,24},{20,28},{24,16},{28,20},{1,9},{5... | collective-permute-start | bytes 1572872 | tf_op jit(solution)/shard_map/ppermute | solution.py:914
  174.9 54.3 %collective-permute-start.29 = (bf16[640,1024]{1,0:T(8,128)(2,1)}, bf16[640,1024]{1,0:T(8,128)(2,1)}, u32[]{:S(2)}, u32[]{:S(2)}) collective-permute-start(bf16[640,1024]{1,0:T(8,128)(2,1)} %copy-done.20), channel_id=1, source_target_pairs={{0,4},{4,0},{8,12},{12,8},{16,20},{20,16},{24,28},{28,24},{1,5},{5... | collective-permute-start | bytes 3932168 | tf_op jit(solution)/shard_map/ppermute | solution.py:914
  175.3 25.5 %collective-permute-start.27 = (bf16[1024,512]{1,0:T(8,128)(2,1)}, bf16[1024,512]{1,0:T(8,128)(2,1)}, u32[]{:S(2)}, u32[]{:S(2)}) collective-permute-start(bf16[1024,512]{1,0:T(8,128)(2,1)} %get-tuple-element.385), channel_id=1, source_target_pairs={{0,16},{4,20},{8,24},{12,28},{16,0},{20,4},{24,8},{28,12},{1,17},{... | collective-permute-start | bytes 3145736 | tf_op jit(solution)/shard_map/ppermute | solution.py:914
  176.8 25.2 %collective-permute-start.28 = (bf16[1024,512]{1,0:T(8,128)(2,1)}, bf16[1024,512]{1,0:T(8,128)(2,1)}, u32[]{:S(2)}, u32[]{:S(2)}) collective-permute-start(bf16[1024,512]{1,0:T(8,128)(2,1)} %get-tuple-element.387), channel_id=1, source_target_pairs={{0,8},{4,12},{8,0},{12,4},{16,24},{20,28},{24,16},{28,20},{1,9},{5... | collective-permute-start | bytes 3145736 | tf_op jit(solution)/shard_map/ppermute | solution.py:914
  206.0 19.3 %collective-permute-start.32 = (bf16[512,512]{1,0:T(8,128)(2,1)}, bf16[512,512]{1,0:T(8,128)(2,1)}, u32[]{:S(2)}, u32[]{:S(2)}) collective-permute-start(bf16[512,512]{1,0:T(8,128)(2,1)} %get-tuple-element.409), channel_id=1, source_target_pairs={{0,8},{4,12},{8,0},{12,4},{16,24},{20,28},{24,16},{28,20},{1,9},{5... | collective-permute-start | bytes 1572872 | tf_op jit(solution)/shard_map/ppermute | solution.py:914
  207.5 17.8 %collective-permute-start.33 = (bf16[512,512]{1,0:T(8,128)(2,1)}, bf16[512,512]{1,0:T(8,128)(2,1)}, u32[]{:S(2)}, u32[]{:S(2)}) collective-permute-start(bf16[512,512]{1,0:T(8,128)(2,1)} %get-tuple-element.411), channel_id=1, source_target_pairs={{0,16},{4,20},{8,24},{12,28},{16,0},{20,4},{24,8},{28,12},{1,17},{... | collective-permute-start | bytes 1572872 | tf_op jit(solution)/shard_map/ppermute | solution.py:914
  208.1 17.3 %collective-permute-start.30 = (bf16[640,4096]{1,0:T(8,128)(2,1)}, bf16[640,4096]{1,0:T(8,128)(2,1)}, u32[]{:S(2)}, u32[]{:S(2)}) collective-permute-start(bf16[640,4096]{1,0:T(8,128)(2,1)} %get-tuple-element.420.grad_ref.refs_4_), channel_id=1, source_target_pairs={{0,4},{4,0},{8,12},{12,8},{16,20},{20,16},{24,28},{28,24},{1,5},{5... | collective-permute-start | bytes 15728648 | tf_op jit(solution)/shard_map/ppermute | solution.py:914
  245.6 95.0 %reduce-scatter.5.cloned.1.call-start = ((), (), s32[]{:S(2)}) async-start(), calls=%async_computation.4 | async-start | bytes 1638400 | tf_op jit(solution)/shard_map/reduce_scatter | solution.py:774
  245.6 33.0 %collective-permute-start.34 = (bf16[256,2560]{1,0:T(8,128)(2,1)}, bf16[256,2560]{1,0:T(8,128)(2,1)}, u32[]{:S(2)}, u32[]{:S(2)}) collective-permute-start(bf16[256,2560]{1,0:T(8,128)(2,1)} %get-tuple-element.444), channel_id=1, source_target_pairs={{0,16},{4,20},{8,24},{12,28},{16,0},{20,4},{24,8},{28,12},{1,17},{... | collective-permute-start | bytes 3932168 | tf_op jit(solution)/shard_map/ppermute | solution.py:914
  247.2 31.4 %collective-permute-start.35 = (bf16[256,2560]{1,0:T(8,128)(2,1)}, bf16[256,2560]{1,0:T(8,128)(2,1)}, u32[]{:S(2)}, u32[]{:S(2)}) collective-permute-start(bf16[256,2560]{1,0:T(8,128)(2,1)} %get-tuple-element.446), channel_id=1, source_target_pairs={{0,8},{4,12},{8,0},{12,4},{16,24},{20,28},{24,16},{28,20},{1,9},{5... | collective-permute-start | bytes 3932168 | tf_op jit(solution)/shard_map/ppermute | solution.py:914
  283.2 17.5 %collective-permute-start.36 = (bf16[128,2560]{1,0:T(8,128)(2,1)}, bf16[128,2560]{1,0:T(8,128)(2,1)}, u32[]{:S(2)}, u32[]{:S(2)}) collective-permute-start(bf16[128,2560]{1,0:T(8,128)(2,1)} %get-tuple-element.456), channel_id=1, source_target_pairs={{0,8},{4,12},{8,0},{12,4},{16,24},{20,28},{24,16},{28,20},{1,9},{5... | collective-permute-start | bytes 1966088 | tf_op jit(solution)/shard_map/ppermute | solution.py:914
  284.7 17.1 %collective-permute-start.37 = (bf16[128,2560]{1,0:T(8,128)(2,1)}, bf16[128,2560]{1,0:T(8,128)(2,1)}, u32[]{:S(2)}, u32[]{:S(2)}) collective-permute-start(bf16[128,2560]{1,0:T(8,128)(2,1)} %get-tuple-element.458), channel_id=1, source_target_pairs={{0,16},{4,20},{8,24},{12,28},{16,0},{20,4},{24,8},{28,12},{1,17},{... | collective-permute-start | bytes 1966088 | tf_op jit(solution)/shard_map/ppermute | solution.py:914
  305.1 19.1 %collective-permute-start.39 = (bf16[256,1536]{1,0:T(8,128)(2,1)}, bf16[256,1536]{1,0:T(8,128)(2,1)S(1)}, u32[]{:S(2)}, u32[]{:S(2)}) collective-permute-start(bf16[256,1536]{1,0:T(8,128)(2,1)} %get-tuple-element.483), channel_id=1, source_target_pairs={{0,16},{4,20},{8,24},{12,28},{16,0},{20,4},{24,8},{28,12},{1,17},{... | collective-permute-start | bytes 2359304 | tf_op jit(solution)/shard_map/ppermute | solution.py:914
  306.7 18.6 %collective-permute-start.40 = (bf16[256,1536]{1,0:T(8,128)(2,1)S(1)}, bf16[256,1536]{1,0:T(8,128)(2,1)}, u32[]{:S(2)}, u32[]{:S(2)}) collective-permute-start(bf16[256,1536]{1,0:T(8,128)(2,1)S(1)} %copy-done.42), channel_id=1, source_target_pairs={{0,8},{4,12},{8,0},{12,4},{16,24},{20,28},{24,16},{28,20},{1,9},{5... | collective-permute-start | bytes 2359304 | tf_op jit(solution)/shard_map/ppermute | solution.py:914
  (67 other events, 769.5 us)
Sparse Core Ops, SparseCore 0:
  69.8 33.1 all-gather.1
  245.7 32.8 reduce-scatter.2
  305.3 35.2 reduce-scatter.4
